TPU v7x, 32 devices: a whole 2x2x4 slice. The times are simulated.
32 devices in a mesh: dp: 1, tm: 32 (over z, y, x, core).
Axes of the slice: x: 2, y: 2, z: 4, core: 2. Of those that a mesh axis runs over, the one named last changes fastest.
Arguments:
- features: bfloat16 [1, 4096, 1536], P('dp', 'tm'), may hold values from -8 to 8
- start_noise: bfloat16 [1, 4096, 1536], P('dp', 'tm'), may hold values from -1 to 1
- cotangent: bfloat16 [1, 4096, 1536], P('dp', 'tm'), may hold values from -0.09375 to 0.09375
- in_weight: bfloat16 [3072, 1536], P('tm'), may hold values from -0.15625 to 0.15625
- kernel: float32 [31, 1536], replicated, may hold values from -1 to 1
- bn_gain: float32 [1536], replicated, may hold values from 0.25 to 1.75
- bn_shift: float32 [1536], replicated, may hold values from -1 to 1
- ends: int32 [1], replicated, may hold values from 2048 to 4096
Outputs:
- perturbation: float32 [1, 4096, 1536], P('dp', 'tm')
- grad_kernel: float32 [31, 1536], P(None, 'tm')
- grad_norm: float32 [2, 1536], P(None, 'tm')
Inputs may be any that keep to these rules, and one draw needn't show every extreme that they name: `ends`: frames at or after an utterance's end are padding.
All inputs are finite; a program needn't handle non-finite values.
Results may differ from a plain program's by a relative error of at most 0.0059.
Values may be sent and summed in bfloat16 or wider, within the bound.
No kernel may reach another device: no remote copies, remote signals or barrier semaphores. Data moves between devices by JAX's collectives and lax.ppermute only.
A program may use at most 128 MiB of HBM per device.

v0:
```python
import functools

import jax
import jax.numpy as jnp
from jax import lax
from jax.experimental import pallas as pl
from jax.experimental.pallas import tpu as pltpu
from jax.sharding import PartitionSpec as P

ASCENT = 2

noise_scale = 0.5
ascent_rate = 0.5
layer_epsilon = 1e-05
batch_epsilon = 1e-05
ascent_epsilon = 1e-06

HALO = 32
EDGE = 16
PAY = 128
F32 = jnp.float32
BF16 = jnp.bfloat16


def params(limit=56 * 1024 * 1024):
    return pltpu.CompilerParams(vmem_limit_bytes=limit)


def cost(flops, nbytes):
    return pl.CostEstimate(flops=int(flops), bytes_accessed=int(nbytes), transcendentals=0)


def normalize(summed):
    centre = summed - jnp.mean(summed, axis=-1, keepdims=True)
    inverse = lax.rsqrt(jnp.mean(centre * centre, axis=-1, keepdims=True) + layer_epsilon)
    return (centre * inverse, inverse)


def live_rows(first, rows, end):
    ids = first + lax.broadcasted_iota(jnp.int32, (rows, 1), 0)
    return jnp.where((ids >= 0) & (ids < end), 1.0, 0.0).astype(F32)


def forward_kernel(taps_n, scal, nb, wv, wg, taps, value, gate, glu, conv, stats, wide):
    start, end = scal[0], scal[1]
    rows, span = value.shape[0], nb.shape[0]
    half = (taps_n - 1) // 2
    contract = (((1,), (1,)), ((), ()))
    v = lax.dot_general(nb[...], wv[...], contract, preferred_element_type=F32)
    s = jax.nn.sigmoid(lax.dot_general(nb[...], wg[...], contract, preferred_element_type=F32))
    value[...] = v[HALO : HALO + rows]
    gate[...] = s[HALO : HALO + rows]
    gated = (v * s * live_rows(start - HALO, span, end)).astype(BF16)
    glu[...] = gated
    wide[...] = gated.astype(F32)
    count = conv.shape[0]
    shift = HALO - EDGE - half
    block = 32
    for lane in range(0, conv.shape[1], 128):
        lanes = slice(lane, lane + 128)
        for row in range(0, count, block):
            total = jnp.zeros((block, 128), F32)
            for tap in range(taps_n):
                at = row + shift + tap
                total = total + taps[tap : tap + 1, lanes] * wide[at : at + block, lanes]
            conv[row : row + block, lanes] = total
    live = live_rows(start, rows, end)
    own = conv[EDGE : EDGE + rows, :]
    mass = jnp.sum(live * own, axis=0, keepdims=True)
    centre = live * (own - mass / jnp.maximum(jnp.sum(live), 1.0))
    both = jnp.concatenate([mass, jnp.sum(centre * centre, axis=0, keepdims=True)], axis=0)
    for peer in range(stats.shape[0]):
        stats[peer] = both


def forward(scal, nb, weight, taps, rows, peers):
    span, width = nb.shape
    half_width = weight.shape[0] // 2
    chunk = 256 if half_width % 256 == 0 else 128
    steps = half_width // chunk
    col = lambda n: pl.BlockSpec((n, chunk), lambda i: (0, i))
    return pl.pallas_call(
        functools.partial(forward_kernel, taps.shape[0]),
        grid=(steps,),
        in_specs=[
            pl.BlockSpec(memory_space=pltpu.SMEM),
            pl.BlockSpec((span, width), lambda i: (0, 0)),
            pl.BlockSpec((chunk, width), lambda i: (i, 0)),
            pl.BlockSpec((chunk, width), lambda i: (i + steps, 0)),
            col(taps.shape[0]),
        ],
        out_specs=[
            col(rows),
            col(rows),
            col(span),
            col(rows + 2 * EDGE),
            pl.BlockSpec((peers, 2, chunk), lambda i: (0, 0, i)),
        ],
        out_shape=[
            jax.ShapeDtypeStruct((rows, half_width), F32),
            jax.ShapeDtypeStruct((rows, half_width), F32),
            jax.ShapeDtypeStruct((span, half_width), BF16),
            jax.ShapeDtypeStruct((rows + 2 * EDGE, half_width), F32),
            jax.ShapeDtypeStruct((peers, 2, half_width), F32),
        ],
        scratch_shapes=[pltpu.VMEM((span, chunk), F32)],
        compiler_params=params(),
        cost_estimate=cost(2 * span * width * 2 * half_width, 4 * half_width * width + 10 * span * half_width),
        name="project_glu_conv",
    )(scal, nb, weight, weight, taps)


def moments(counts, stats, live_count):
    mass = stats[0, 0:1, :]
    square = stats[0, 1:2, :]
    for peer in range(1, stats.shape[0]):
        mass = mass + stats[peer, 0:1, :]
        square = square + stats[peer, 1:2, :]
    mean = mass / live_count
    for peer in range(stats.shape[0]):
        off = stats[peer, 0:1, :] - counts[0, peer] * mean
        square = square + off * off * counts[1, peer]
    return mean, lax.rsqrt(square / live_count + batch_epsilon)


def swish_grads(scal, counts, stats, conv, cot, gain, shift):
    start, end = scal[0], scal[1]
    live_count = scal[3].astype(F32)
    mean, inv = moments(counts, stats, live_count)
    scaled = (conv[...] - mean) * inv
    pre = gain[...] * scaled + shift[...]
    sig = jax.nn.sigmoid(pre)
    live = live_rows(start - EDGE, conv.shape[0], end)
    upstream = live * cot[...].astype(F32) / ASCENT
    return scaled, upstream * sig * (1.0 + pre * (1.0 - sig)), live, mean, inv


def batch_kernel(scal, counts, stats, conv, cot, gain, shift, scaled_out, grad_out, inv_out, sums):
    scaled, grad, live, mean, inv = swish_grads(scal, counts, stats, conv, cot, gain, shift)
    scaled_out[...] = scaled
    grad_out[...] = grad
    inv_out[...] = inv
    rows = conv.shape[0] - 2 * EDGE
    own = grad[EDGE : EDGE + rows]
    both = jnp.concatenate(
        [
            jnp.sum(own, axis=0, keepdims=True),
            jnp.sum(own * scaled[EDGE : EDGE + rows], axis=0, keepdims=True),
        ],
        axis=0,
    )
    for peer in range(sums.shape[0]):
        sums[peer] = both


def batch(scal, counts, stats, conv, cot, gain, shift, peers):
    span, half_width = conv.shape
    chunk = 256 if half_width % 256 == 0 else 128
    col = lambda n: pl.BlockSpec((n, chunk), lambda i: (0, i))
    smem = pl.BlockSpec(memory_space=pltpu.SMEM)
    return pl.pallas_call(
        batch_kernel,
        grid=(half_width // chunk,),
        in_specs=[
            smem,
            smem,
            pl.BlockSpec((stats.shape[0], 2, chunk), lambda i: (0, 0, i)),
            col(span),
            col(span),
            col(1),
            col(1),
        ],
        out_specs=[col(span), col(span), col(1), pl.BlockSpec((peers, 2, chunk), lambda i: (0, 0, i))],
        out_shape=[
            jax.ShapeDtypeStruct((span, half_width), F32),
            jax.ShapeDtypeStruct((span, half_width), F32),
            jax.ShapeDtypeStruct((1, half_width), F32),
            jax.ShapeDtypeStruct((peers, 2, half_width), F32),
        ],
        compiler_params=params(),
        cost_estimate=cost(40 * span * half_width, 16 * span * half_width),
        name="batch_norm_swish",
    )(scal, counts, stats, conv, cot, gain, shift)


def backward_kernel(taps_n, scal, sums, scaled, grad, inv, gain, taps, value, gate, wv, wg, part, grad_conv, wide):
    start, end = scal[0], scal[1]
    rows, half = value.shape[0], (taps_n - 1) // 2
    live_count = scal[3].astype(F32)
    both = sums[0]
    for peer in range(1, sums.shape[0]):
        both = both + sums[peer]
    shift_sum, gain_sum = both[0:1], both[1:2]
    live = live_rows(start - EDGE, scaled.shape[0], end)
    through = live * (inv[...] * gain[...]) * (
        grad[...] - (shift_sum + scaled[...] * gain_sum) / live_count
    )
    rounded = through.astype(BF16)
    grad_conv[...] = rounded[EDGE : EDGE + rows]
    wide[...] = rounded.astype(F32)
    block = 32
    columns = []
    for lane in range(0, value.shape[1], 128):
        lanes = slice(lane, lane + 128)
        tiles = []
        for row in range(0, rows, block):
            total = jnp.zeros((block, 128), F32)
            for tap in range(taps_n):
                at = row + EDGE + half - tap
                total = total + taps[tap : tap + 1, lanes] * wide[at : at + block, lanes]
            tiles.append(total)
        columns.append(jnp.concatenate(tiles, axis=0))
    grad_glu = jnp.concatenate(columns, axis=1) * live_rows(start, rows, end)
    grad_glu = grad_glu.astype(BF16).astype(F32)
    sig = gate[...]
    to_value = (grad_glu * sig).astype(BF16)
    to_gate = (grad_glu * value[...] * sig * (1.0 - sig)).astype(BF16)
    product = jnp.dot(to_value, wv[...], preferred_element_type=F32) + jnp.dot(
        to_gate, wg[...], preferred_element_type=F32
    )

    @pl.when(pl.program_id(0) == 0)
    def _():
        part[...] = product

    @pl.when(pl.program_id(0) > 0)
    def _():
        part[...] += product


def backward(scal, sums, scaled, grad, inv, gain, taps, value, gate, weight):
    span, half_width = scaled.shape
    rows, width = value.shape[0], weight.shape[1]
    chunk = 256 if half_width % 256 == 0 else 128
    steps = half_width // chunk
    col = lambda n: pl.BlockSpec((n, chunk), lambda i: (0, i))
    return pl.pallas_call(
        functools.partial(backward_kernel, taps.shape[0]),
        grid=(steps,),
        in_specs=[
            pl.BlockSpec(memory_space=pltpu.SMEM),
            pl.BlockSpec((sums.shape[0], 2, chunk), lambda i: (0, 0, i)),
            col(span),
            col(span),
            col(1),
            col(1),
            col(taps.shape[0]),
            col(rows),
            col(rows),
            pl.BlockSpec((chunk, width), lambda i: (i, 0)),
            pl.BlockSpec((chunk, width), lambda i: (i + steps, 0)),
        ],
        out_specs=[pl.BlockSpec((rows, width), lambda i: (0, 0)), col(rows)],
        out_shape=[
            jax.ShapeDtypeStruct((rows, width), F32),
            jax.ShapeDtypeStruct((rows, half_width), BF16),
        ],
        scratch_shapes=[pltpu.VMEM((span, chunk), F32)],
        compiler_params=params(),
        cost_estimate=cost(2 * rows * width * 2 * half_width, 4 * half_width * width + 20 * span * half_width),
        name="grad_conv_project_back",
    )(scal, sums, scaled, grad, inv, gain, taps, value, gate, weight, weight)


def correlate(taps_n, left, wide, first):
    rows = left.shape[0]
    return jnp.concatenate(
        [
            jnp.sum(left * wide[first + tap : first + tap + rows], axis=0, keepdims=True)
            for tap in range(taps_n)
        ],
        axis=0,
    )


def tap_grad_kernel(taps_n, grad_conv, glu, out, wide):
    wide[...] = glu[...].astype(F32)
    first = HALO - (taps_n - 1) // 2
    out[...] = correlate(taps_n, grad_conv[...].astype(F32), wide, first)


def tap_grad(taps_n, grad_conv, glu):
    rows, half_width = grad_conv.shape
    span = glu.shape[0]
    col = lambda n: pl.BlockSpec((n, 128), lambda i: (0, i))
    return pl.pallas_call(
        functools.partial(tap_grad_kernel, taps_n),
        grid=(half_width // 128,),
        in_specs=[col(rows), col(span)],
        out_specs=col(taps_n),
        out_shape=jax.ShapeDtypeStruct((taps_n, half_width), F32),
        scratch_shapes=[pltpu.VMEM((span, 128), F32)],
        compiler_params=params(),
        cost_estimate=cost(2 * taps_n * rows * half_width, 4 * span * half_width),
        name="tap_grad",
    )(grad_conv, glu)


def raw_taps_kernel(taps_n, scal, conv, glu, stats, plain, crossed, wide):
    start, end = scal[0], scal[1]
    rows, span = conv.shape[0] - 2 * EDGE, glu.shape[0]
    wide[...] = glu[...].astype(F32)
    first = HALO - (taps_n - 1) // 2
    live = live_rows(start, rows, end)
    local = stats[0, 0:1, :] / jnp.maximum(jnp.sum(live), 1.0)
    crossed[...] = correlate(taps_n, live * (conv[EDGE : EDGE + rows, :] - local), wide, first)
    tap = lax.broadcasted_iota(jnp.int32, (taps_n, span), 0)
    at = lax.broadcasted_iota(jnp.int32, (taps_n, span), 1) - first - tap
    inside = (at >= 0) & (at < jnp.clip(end - start, 0, rows))
    plain[...] = jnp.dot(
        jnp.where(inside, 1.0, 0.0).astype(BF16), glu[...], preferred_element_type=F32
    )


def raw_taps(taps_n, scal, conv, glu, stats):
    rows, half_width = conv.shape
    span = glu.shape[0]
    col = lambda n: pl.BlockSpec((n, 128), lambda i: (0, i))
    return pl.pallas_call(
        functools.partial(raw_taps_kernel, taps_n),
        grid=(half_width // 128,),
        in_specs=[
            pl.BlockSpec(memory_space=pltpu.SMEM),
            col(rows),
            col(span),
            pl.BlockSpec((1, 2, 128), lambda i: (0, 0, i)),
        ],
        out_specs=[col(taps_n), col(taps_n)],
        out_shape=[jax.ShapeDtypeStruct((taps_n, half_width), F32)] * 2,
        scratch_shapes=[pltpu.VMEM((span, 128), F32)],
        compiler_params=params(),
        cost_estimate=cost(2 * taps_n * rows * half_width, 8 * span * half_width),
        name="raw_taps",
    )(scal, conv, glu, stats)


def last_kernel(taps_n, block, scal, counts, stats, conv, cot, gain, shift, glu, plain, crossed, local_stats, taps_before, sums_before, out, wide, pay):
    step = pl.program_id(0)
    scaled, grad, live, mean, inv = swish_grads(scal, counts, stats, conv, cot, gain, shift)
    rows = conv.shape[0] - 2 * EDGE
    wide[...] = glu[...].astype(F32)
    first = HALO - (taps_n - 1) // 2
    factor = inv * gain[...]
    own = grad[EDGE : EDGE + rows]
    direct = correlate(taps_n, own, wide, first)
    own_live = live[EDGE : EDGE + rows]
    local = local_stats[0, 0:1, :] / jnp.maximum(jnp.sum(own_live), 1.0)
    with_scaled = inv * (crossed[...] + (local - mean) * plain[...])
    both = sums_before[0]
    lanes = 128
    filler = jnp.zeros((PAY - 3 * taps_n - 5, lanes), F32)
    pay[step] = jnp.concatenate(
        [
            taps_before[...] + factor * direct,
            with_scaled,
            plain[...],
            jnp.sum(own, axis=0, keepdims=True),
            jnp.sum(own * scaled[EDGE : EDGE + rows], axis=0, keepdims=True),
            both,
            factor,
            filler,
        ],
        axis=0,
    )

    @pl.when(step == pl.num_programs(0) - 1)
    def _():
        core = scal[2]
        turned = jnp.concatenate([jnp.transpose(pay[s]) for s in range(pay.shape[0])], axis=0)
        for index in range(out.shape[0]):
            out[index, core] = turned[index * block : (index + 1) * block]
            out[index, 1 - core] = jnp.zeros((block, PAY), F32)


def last(taps_n, block, scal, counts, stats, conv, cot, gain, shift, glu, plain, crossed, local_stats, taps_before, sums_before):
    span, half_width = conv.shape
    chunk = 128
    steps = half_width // chunk
    col = lambda n: pl.BlockSpec((n, chunk), lambda i: (0, i))
    one = pl.BlockSpec((1, 2, chunk), lambda i: (0, 0, i))
    smem = pl.BlockSpec(memory_space=pltpu.SMEM)
    blocks = half_width // block
    return pl.pallas_call(
        functools.partial(last_kernel, taps_n, block),
        grid=(steps,),
        in_specs=[
            smem,
            smem,
            pl.BlockSpec((stats.shape[0], 2, chunk), lambda i: (0, 0, i)),
            col(span),
            col(span),
            col(1),
            col(1),
            col(glu.shape[0]),
            col(taps_n),
            col(taps_n),
            one,
            col(taps_n),
            one,
        ],
        out_specs=pl.BlockSpec((blocks, 2, block, PAY), lambda i: (0, 0, 0, 0)),
        out_shape=jax.ShapeDtypeStruct((blocks, 2, block, PAY), F32),
        scratch_shapes=[pltpu.VMEM((glu.shape[0], chunk), F32), pltpu.VMEM((steps, PAY, chunk), F32)],
        compiler_params=params(),
        cost_estimate=cost(100 * span * half_width, 10 * span * half_width),
        name="batch_norm_swish_taps",
    )(scal, counts, stats, conv, cot, gain, shift, glu, plain, crossed, local_stats, taps_before, sums_before)


def finish_kernel(taps_n, sources, scal, received, taps_out, norm_out):
    total = received[0]
    for index in range(1, received.shape[0]):
        total = total + received[index]
    total = jnp.transpose(total)
    at = 3 * taps_n
    shift_sum, gain_sum = total[at : at + 1], total[at + 1 : at + 2]
    factor = total[at + 4 : at + 5] / sources / scal[3].astype(F32)
    taps_out[...] = total[:taps_n] - factor * (
        gain_sum * total[taps_n : 2 * taps_n] + shift_sum * total[2 * taps_n : at]
    )
    norm_out[...] = jnp.concatenate(
        [gain_sum + total[at + 3 : at + 4], shift_sum + total[at + 2 : at + 3]], axis=0
    )


def finish(taps_n, sources, scal, received):
    width = received.shape[1]
    return pl.pallas_call(
        functools.partial(finish_kernel, taps_n, float(sources)),
        in_specs=[pl.BlockSpec(memory_space=pltpu.SMEM), pl.BlockSpec(memory_space=pltpu.VMEM)],
        out_shape=[
            jax.ShapeDtypeStruct((taps_n, width), F32),
            jax.ShapeDtypeStruct((2, width), F32),
        ],
        compiler_params=params(),
        name="finish",
    )(scal, received)


def direction_kernel(scal, mine, other, features, noise, out, squares):
    rows = mine.shape[0]
    first = scal[0] + scal[2] * rows
    block = 32
    total = jnp.zeros((1, 128), F32)
    for row in range(0, rows, block):
        at = slice(row, row + block)
        live = live_rows(first + row, block, scal[1])
        summed = features[at].astype(F32) + noise_scale * noise[at].astype(F32) * live
        normed, inverse = normalize(summed)
        grad = mine[at] + other[at]
        moved = (
            live
            * inverse
            * (
                grad
                - jnp.mean(grad, axis=-1, keepdims=True)
                - normed * jnp.mean(grad * normed, axis=-1, keepdims=True)
            )
        )
        out[at] = moved
        total = total + jnp.sum(moved * moved)
    for peer in range(squares.shape[0]):
        squares[peer] = total


def direction(scal, mine, other, features, noise, peers):
    rows, width = mine.shape
    vmem = pl.BlockSpec(memory_space=pltpu.VMEM)
    return pl.pallas_call(
        direction_kernel,
        in_specs=[pl.BlockSpec(memory_space=pltpu.SMEM)] + [vmem] * 4,
        out_shape=[
            jax.ShapeDtypeStruct((rows, width), F32),
            jax.ShapeDtypeStruct((peers, 1, 128), F32),
        ],
        compiler_params=params(),
        cost_estimate=cost(30 * rows * width, 16 * rows * width),
        name="direction",
    )(scal, mine, other, features, noise)


def ascend_kernel(scal, squares, features, noise, mine, partner, near, far, own_noise, perturbation, normed_out):
    start, end, core = scal[0], scal[1], scal[2]
    rows, width = mine.shape
    total = squares[0]
    for index in range(1, squares.shape[0]):
        total = total + squares[index]
    total = total[0:1, 0:1]
    length = jnp.full((1, 1), 1.0, F32) * end.astype(F32)
    rate = ascent_rate * jnp.sqrt(length * width) / (jnp.sqrt(total) + ascent_epsilon)
    block = 32
    is_first = core == 0

    def place(row, moved):
        at = slice(row, row + block)
        live = live_rows(start - HALO + row, block, end)
        summed = features[at].astype(F32) + (noise_scale * noise[at].astype(F32) * live + moved * rate)
        normed_out[at] = normalize(summed)[0].astype(BF16)

    place(0, jnp.where(is_first, far[...], near[...]))
    for row in range(0, rows, block):
        at = slice(row, row + block)
        place(HALO + row, jnp.where(is_first, mine[at], partner[at]))
        place(HALO + rows + row, jnp.where(is_first, partner[at], mine[at]))
        live = live_rows(start + core * rows + row, block, end)
        perturbation[at] = noise_scale * own_noise[at].astype(F32) * live + mine[at] * rate
    place(HALO + 2 * rows, jnp.where(is_first, near[...], far[...]))


def ascend(scal, squares, features, noise, mine, partner, near, far, own_noise):
    vmem = pl.BlockSpec(memory_space=pltpu.VMEM)
    return pl.pallas_call(
        ascend_kernel,
        in_specs=[pl.BlockSpec(memory_space=pltpu.SMEM)] + [vmem] * 8,
        out_shape=[
            jax.ShapeDtypeStruct(mine.shape, F32),
            jax.ShapeDtypeStruct(features.shape, BF16),
        ],
        compiler_params=params(),
        cost_estimate=cost(30 * features.size, 8 * features.size),
        name="ascend",
    )(scal, squares, features, noise, mine, partner, near, far, own_noise)


def on_device(on_dp, features, start_noise, cotangent, in_weight, kernel, bn_gain, bn_shift, ends):
    rows, width = features.shape[1:]
    taps_n = kernel.shape[0]
    shards = lax.axis_size("tm")
    chips = shards // 2
    index = lax.axis_index("tm")
    group = lax.axis_index("dp")
    chip, core = index // 2, index % 2
    chip_rows = 2 * rows
    block = in_weight.shape[0]
    half_width = width // 2
    end = lax.dynamic_index_in_dim(ends, group, 0, keepdims=False)
    scal = jnp.stack([chip * chip_rows, end, core, jnp.sum(ends)]).astype(jnp.int32)
    held = jnp.clip(
        ends[:, None] - chip_rows * jnp.arange(chips, dtype=jnp.int32)[None, :], 0, chip_rows
    ).reshape(-1).astype(F32)
    counts = jnp.stack([held, jnp.where(held > 0, 1.0 / jnp.maximum(held, 1.0), 0.0)])

    cores = [[2 * c + k for c in range(chips)] for k in range(2)]
    swap = [(i, i ^ 1) for i in range(shards)]
    near_pairs = [(2 * c, 2 * c - 2) for c in range(1, chips)] + [
        (2 * c + 1, 2 * c + 3) for c in range(chips - 1)
    ]
    far_pairs = [(2 * c, 2 * c - 1) for c in range(1, chips)] + [
        (2 * c + 1, 2 * c + 2) for c in range(chips - 1)
    ]

    def edges(array):
        return jnp.where(core == 0, array[..., :HALO, :], array[..., -HALO:, :])

    def across(array):
        edge = edges(array)
        return (
            lax.ppermute(array, "tm", swap),
            lax.ppermute(edge, "tm", near_pairs),
            lax.ppermute(edge, "tm", far_pairs),
        )

    def peers_of(array):
        array = lax.all_to_all(array, "tm", 0, 0, axis_index_groups=cores, tiled=True)
        if on_dp:
            array = lax.all_gather(array, "dp", axis=0, tiled=True)
        return array

    weight = lax.all_gather(in_weight, "tm", axis=0, axis_index_groups=cores, tiled=True)

    packed = jnp.concatenate([features, start_noise, cotangent], axis=0)
    partner, near, far = across(packed)
    first = core == 0
    whole = jnp.concatenate(
        [
            jnp.where(first, far, near),
            jnp.where(first, packed, partner),
            jnp.where(first, partner, packed),
            jnp.where(first, near, far),
        ],
        axis=1,
    )
    wide_features, wide_noise, wide_cot = whole[0], whole[1], whole[2]

    out_channel = jnp.arange(half_width, dtype=jnp.int32)
    source = (2 * (out_channel // block) + core) * block + out_channel % block
    chosen = (jnp.arange(width, dtype=jnp.int32)[:, None] == source[None, :]).astype(BF16)
    cot = jnp.dot(wide_cot[HALO - EDGE : -(HALO - EDGE)], chosen, preferred_element_type=F32).astype(BF16)

    def mine_of(array):
        parts = array.reshape(array.shape[0], width // (2 * block), 2, block)
        return lax.dynamic_index_in_dim(parts, core, 2, keepdims=False).reshape(-1, half_width)

    taps = mine_of(kernel)
    gain, shift = mine_of(bn_gain[None]), mine_of(bn_shift[None])

    frame_ids = chip * chip_rows - HALO + jnp.arange(whole.shape[1], dtype=jnp.int32)
    live = ((frame_ids >= 0) & (frame_ids < end)).astype(F32)
    summed = wide_features.astype(F32) + noise_scale * wide_noise.astype(F32) * live[:, None]
    normed_b = normalize(summed)[0].astype(BF16)

    value, gate, glu, conv, stats = forward(scal, normed_b, weight, taps, chip_rows, chips)
    scaled, grad, inv, sums_before = batch(
        scal, counts, peers_of(stats), conv, cot, gain, shift, chips
    )
    part, grad_conv = backward(
        scal, peers_of(sums_before), scaled, grad, inv, gain, taps, value, gate, weight
    )
    mine = lax.dynamic_slice_in_dim(part, core * rows, rows, 0)
    other = lax.dynamic_slice_in_dim(part, (1 - core) * rows, rows, 0)
    other = lax.ppermute(other, "tm", swap)
    moved, squares = direction(scal, mine, other, features[0], start_noise[0], shards)
    squares = lax.all_to_all(squares, "tm", 0, 0, tiled=True)
    partner, near, far = across(moved)
    taps_before = tap_grad(taps_n, grad_conv, glu)
    perturbation, normed_b = ascend(
        scal, squares, wide_features, wide_noise, moved, partner, near, far, start_noise[0]
    )

    _, _, glu, conv, stats = forward(scal, normed_b, weight, taps, chip_rows, chips)
    plain, crossed = raw_taps(taps_n, scal, conv, glu, stats)
    outgoing = last(
        taps_n, block, scal, counts, peers_of(stats), conv, cot, gain, shift, glu, plain, crossed, stats, taps_before, sums_before
    )
    outgoing = outgoing.reshape(shards, block // 2, PAY)
    if on_dp:
        outgoing = lax.psum(outgoing, "dp")
    received = lax.all_to_all(outgoing, "tm", 0, 0, tiled=True)
    sources = chips * (lax.axis_size("dp") if on_dp else 1)
    kernel_total, norm_total = finish(taps_n, sources, scal, received)
    return (perturbation[None], kernel_total, norm_total)


def solution(mesh):
    return jax.shard_map(
        functools.partial(on_device, mesh.shape["dp"] > 1),
        mesh=mesh,
        in_specs=(
            P("dp", "tm", None),
            P("dp", "tm", None),
            P("dp", "tm", None),
            P("tm", None),
            P(),
            P(),
            P(),
            P(),
        ),
        out_specs=(P("dp", "tm", None), P(None, "tm"), P(None, "tm")),
        check_vma=False,
    )
```

profile of v0, /device:TPU:0, one launch (start us, length us, event | category | flops | bytes accessed | tf_op | source)
XLA Modules:
  0.0 240.0 jit_solution(12189333506778330754)
XLA Ops:
  7.2 0.7 all-gather.2.cloned.1.call-update
  8.0 1.0 constant_dynamic-update-slice_fusion.2
  9.0 1.0 constant_dynamic-update-slice_fusion.1
  10.1 1.3 collective-permute-start.1
  11.4 1.4 collective-permute-start
  12.8 4.3 %collective-permute-start.2 = (bf16[3,128,1536]{2,1,0:T(8,128)(2,1)S(1)}, bf16[3,128,1536]{2,1,0:T(8,128)(2,1)S(1)}, u32[]{:S(2)}, u32[]{:S(2)}) collective-permute-start(bf16[3,128,1536]{2,1,0:T(8,128)(2,1)S(1)} %constant_dynamic-update-slice_fusion), channel_id=1, source_target_pairs={{0,1},{1,0},{2,3},{3,2},{4,5},{5,4},{6,7},{7,6},{8,9},{9,8},{10,11... | collective-permute-start | bytes 3538952 | tf_op jit(solution)/shard_map/ppermute | solution.py:558
  18.4 0.7 reshape.107.shift
  19.1 0.7 reshape.106.gain
  19.7 0.7 reshape.105.taps
  20.5 0.6 pad_maximum_fusion.1.counts
  21.1 0.6 pad_add_fusion.scal
  21.7 0.8 collective-permute-done.1
  22.5 0.7 copy-done.6
  23.2 1.1 broadcast_select_fusion.3
  24.7 0.8 copy-done
  25.9 0.5 fusion.2
  26.4 0.6 multiply_reduce_fusion
  27.0 1.5 multiply_convert_fusion.nb
  28.5 67.1 %all-gather.2.cloned.1.call-done.wv.wg = bf16[1536,1536]{1,0:T(8,128)(2,1)} async-done(((bf16[96,1536]{1,0:T(8,128)(2,1)}), bf16[1536,1536]{1,0:T(8,128)(2,1)}) %all-gather.2.cloned.1.call-update) | async-done | bytes 4718608 | tf_op jit(solution)/shard_map/all_gather | solution.py:569
  95.5 10.0 %project_glu_conv.2 = (f32[256,768]{1,0:T(8,128)}, f32[256,768]{1,0:T(8,128)}, bf16[320,768]{1,0:T(8,128)(2,1)}, f32[288,768]{1,0:T(8,128)}, f32[16,2,768]{2,1,0:T(2,128)}) custom-call(s32[4]{0:T(128)} %pad_add_fusion.scal, bf16[320,1536]{1,0:T(8,128)(2,1)} %multiply_convert_fusion.nb, bf16[1536,1536]{1,0:T(8,128)(2,1)} %all-gather.2.cloned.1.call-done.wv.wg, ...), custom_call_target="tpu_custom_call" | custom-call | flops 1509949440 | bytes 7176192 | tf_op jit(solution)/shard_map/project_glu_conv/pallas_call | solution.py:82
  105.5 4.3 %all-to-all-start = ((f32[16,2,768]{2,1,0:T(2,128)}), f32[16,2,768]{2,1,0:T(2,128)}, u32[]{:S(2)}, u32[]{:S(2)}) async-start(f32[16,2,768]{2,1,0:T(2,128)} %get-tuple-element.25), calls=%async_computation | async-start | bytes 196608 | tf_op jit(solution)/shard_map/all_to_all | solution.py:564
  109.8 3.0 %fusion.3.cot = bf16[288,768]{1,0:T(8,128)(2,1)} fusion(s32[768]{0:T(1024)S(1)} %fusion.19, bf16[3,32,1536]{2,1,0:T(8,128)(2,1)S(1)} %get-tuple-element.54, bf16[3,128,1536]{2,1,0:T(8,128)(2,1)} %copy-done.1, bf16[3,128,1536]{2,1,0:T(8,128)(2,1)} %copy-done, bf16[3,32,1536]{2,1,0:T(8,128)(2,1)S(1)} %get-tuple-element.53), kind=kOutput, calls=%fused_computation.8 | convolution fusion | flops 684417024 | bytes 3394560 | tf_op jit(solution)/shard_map/dot_general | solution.py:588
  112.8 4.7 %all-to-all-done.stats = f32[16,2,768]{2,1,0:T(2,128)} async-done(((f32[16,2,768]{2,1,0:T(2,128)}), f32[16,2,768]{2,1,0:T(2,128)}, u32[]{:S(2)}, u32[]{:S(2)}) %all-to-all-start) | async-done | bytes 98336 | tf_op jit(solution)/shard_map/all_to_all | solution.py:564
  117.5 3.9 %batch_norm_swish.1 = (f32[288,768]{1,0:T(8,128)}, f32[288,768]{1,0:T(8,128)}, f32[1,768]{1,0:T(1,128)}, f32[16,2,768]{2,1,0:T(2,128)}) custom-call(s32[4]{0:T(128)} %pad_add_fusion.scal, f32[2,16]{1,0:T(2,128)} %pad_maximum_fusion.1.counts, f32[16,2,768]{2,1,0:T(2,128)} %all-to-all-done.stats, f32[288,768]{1,0:T(8,128)} %get-tuple-element.26.conv, ...), custom_call_target="tpu_custom_call" | custom-call | flops 8847360 | bytes 3538944 | tf_op jit(solution)/shard_map/batch_norm_swish/pallas_call | solution.py:161
  121.4 3.5 %all-to-all-start.1 = ((f32[16,2,768]{2,1,0:T(2,128)}), f32[16,2,768]{2,1,0:T(2,128)S(1)}, u32[]{:S(2)}, u32[]{:S(2)}) async-start(f32[16,2,768]{2,1,0:T(2,128)} %get-tuple-element.27.sums_before), calls=%async_computation.1 | async-start | bytes 196608 | tf_op jit(solution)/shard_map/all_to_all | solution.py:564
  125.0 7.6 %all-to-all-done.1.sums = f32[16,2,768]{2,1,0:T(2,128)S(1)} async-done(((f32[16,2,768]{2,1,0:T(2,128)}), f32[16,2,768]{2,1,0:T(2,128)S(1)}, u32[]{:S(2)}, u32[]{:S(2)}) %all-to-all-start.1) | async-done | bytes 98336 | tf_op jit(solution)/shard_map/all_to_all | solution.py:564
  132.6 0.6 copy-done.5
  133.2 9.6 %grad_conv_project_back.1 = (f32[256,1536]{1,0:T(8,128)}, bf16[256,768]{1,0:T(8,128)(2,1)}) custom-call(s32[4]{0:T(128)} %pad_add_fusion.scal, f32[16,2,768]{2,1,0:T(2,128)} %copy-done.5, f32[288,768]{1,0:T(8,128)} %get-tuple-element.28.scaled, f32[288,768]{1,0:T(8,128)} %get-tuple-element.29.grad, f32[1,768]{1,0:T(1,128)} %get-tuple-element.30.inv, ...), custom_call_target="tpu_custom_call" | custom-call | flops 1207959552 | bytes 9142272 | tf_op jit(solution)/shard_map/grad_conv_project_back/pallas_call | solution.py:237
  142.8 2.4 constant_dynamic-slice_fusion
  145.2 2.3 collective-permute-done.3.other
  147.5 0.9 copy-done.2
  148.4 3.2 %direction.1 = (f32[128,1536]{1,0:T(8,128)}, f32[32,1,128]{2,1,0:T(1,128)}) custom-call(s32[4]{0:T(128)} %pad_add_fusion.scal, f32[128,1536]{1,0:T(8,128)} %get-tuple-element.52.mine, f32[128,1536]{1,0:T(8,128)} %copy-done.2, bf16[128,1536]{1,0:T(8,128)(2,1)} %bitcast.37, bf16[128,1536]{1,0:T(8,128)(2,1)} %bitcast.34), custom_call_target="tpu_custom_call" | custom-call | flops 5898240 | bytes 3145728 | tf_op jit(solution)/shard_map/direction/pallas_call | solution.py:469
  151.7 1.0 slice_select_fusion.1
  152.7 0.7 collective-permute-start.6
  153.4 1.3 collective-permute-start.5
  154.7 6.3 %all-to-all-start.2 = ((f32[32,1,128]{2,1,0:T(1,128)}), f32[32,1,128]{2,1,0:T(1,128)S(1)}, u32[]{:S(2)}, u32[]{:S(2)}) async-start(f32[32,1,128]{2,1,0:T(1,128)} %get-tuple-element.34), calls=%async_computation.2 | async-start | bytes 32768 | tf_op jit(solution)/shard_map/all_to_all | solution.py:613
  161.0 1.4 slice_bitcast_fusion
  162.4 5.5 %all-to-all-done.2.squares = f32[32,1,128]{2,1,0:T(1,128)S(1)} async-done(((f32[32,1,128]{2,1,0:T(1,128)}), f32[32,1,128]{2,1,0:T(1,128)S(1)}, u32[]{:S(2)}, u32[]{:S(2)}) %all-to-all-start.2) | async-done | bytes 16416 | tf_op jit(solution)/shard_map/all_to_all | solution.py:613
  168.0 0.6 copy-done.10
  168.7 4.4 %ascend.1 = (f32[128,1536]{1,0:T(8,128)}, bf16[320,1536]{1,0:T(8,128)(2,1)}) custom-call(s32[4]{0:T(128)} %pad_add_fusion.scal, f32[32,1,128]{2,1,0:T(1,128)} %copy-done.10, bf16[320,1536]{1,0:T(8,128)(2,1)} %get-tuple-element.48.features, bf16[320,1536]{1,0:T(8,128)(2,1)} %get-tuple-element.47.noise, f32[128,1536]{1,0:T(8,128)} %get-tuple-element.35.mine, ...), custom_call_target="tpu_custom_call" | custom-call | flops 14745600 | bytes 3932160 | tf_op jit(solution)/shard_map/ascend/pallas_call | solution.py:512
  173.1 10.0 %project_glu_conv.3 = (f32[256,768]{1,0:T(8,128)}, f32[256,768]{1,0:T(8,128)}, bf16[320,768]{1,0:T(8,128)(2,1)}, f32[288,768]{1,0:T(8,128)}, f32[16,2,768]{2,1,0:T(2,128)}) custom-call(s32[4]{0:T(128)} %pad_add_fusion.scal, bf16[320,1536]{1,0:T(8,128)(2,1)} %get-tuple-element.37.nb, bf16[1536,1536]{1,0:T(8,128)(2,1)} %all-gather.2.cloned.1.call-done.wv.wg, ...), custom_call_target="tpu_custom_call" | custom-call | flops 1509949440 | bytes 7176192 | tf_op jit(solution)/shard_map/project_glu_conv/pallas_call | solution.py:82
  183.2 3.5 %all-to-all-start.3 = ((f32[16,2,768]{2,1,0:T(2,128)}), f32[16,2,768]{2,1,0:T(2,128)S(1)}, u32[]{:S(2)}, u32[]{:S(2)}) async-start(f32[16,2,768]{2,1,0:T(2,128)} %get-tuple-element.38.stats.local_stats), calls=%async_computation.3 | async-start | bytes 196608 | tf_op jit(solution)/shard_map/all_to_all | solution.py:564
  186.7 5.1 %tap_grad.1.taps_before = f32[31,768]{1,0:T(8,128)} custom-call(bf16[256,768]{1,0:T(8,128)(2,1)} %get-tuple-element.43.grad_conv, bf16[320,768]{1,0:T(8,128)(2,1)} %get-tuple-element.44.glu), custom_call_target="tpu_custom_call" | custom-call | flops 12189696 | bytes 983040 | tf_op jit(solution)/shard_map/tap_grad/pallas_call | solution.py:286
  191.8 5.7 %raw_taps.1 = (f32[31,768]{1,0:T(8,128)}, f32[31,768]{1,0:T(8,128)}) custom-call(s32[4]{0:T(128)} %pad_add_fusion.scal, f32[288,768]{1,0:T(8,128)} %get-tuple-element.39.conv, bf16[320,768]{1,0:T(8,128)(2,1)} %get-tuple-element.40.glu, f32[16,2,768]{2,1,0:T(2,128)} %get-tuple-element.38.stats.local_stats), custom_call_target="tpu_custom_call" | custom-call | flops 13713408 | bytes 1966080 | tf_op jit(solution)/shard_map/raw_taps/pallas_call | solution.py:319
  197.5 0.6 copy-done.3
  198.1 6.6 %batch_norm_swish_taps.1 = f32[8,2,96,128]{3,2,1,0:T(8,128)} custom-call(s32[4]{0:T(128)} %pad_add_fusion.scal, f32[2,16]{1,0:T(2,128)} %pad_maximum_fusion.1.counts, f32[16,2,768]{2,1,0:T(2,128)} %copy-done.3, f32[288,768]{1,0:T(8,128)} %get-tuple-element.39.conv, bf16[288,768]{1,0:T(8,128)(2,1)} %fusion.3.cot, f32[1,768]{1,0:T(1,128)} %reshape.106.gain, ...), custom_call_target="tpu_custom_call" | custom-call | flops 22118400 | bytes 2211840 | tf_op jit(solution)/shard_map/batch_norm_swish_taps/pallas_call | solution.py:383
  204.7 26.6 %all_to_all.25.received = f32[32,48,128]{2,1,0:T(8,128)} all-to-all(f32[32,48,128]{2,1,0:T(8,128)} %bitcast.36), channel_id=1, replica_groups=mesh['dp'=1,'tm'=32] {'tm'}, dimensions={0} | all-to-all | bytes 1572864 | tf_op jit(solution)/shard_map/all_to_all | solution.py:628
  231.3 1.9 finish.1
  (44 shorter events, 1.9 us)
Async XLA Ops:
  7.2 2.9 %copy-start.4 = (bf16[1,128,1536]{2,1,0:T(8,128)(2,1)S(1)}, bf16[1,128,1536]{2,1,0:T(8,128)(2,1)}, u32[]{:S(2)}) copy-start(bf16[1,128,1536]{2,1,0:T(8,128)(2,1)} %param.10) | copy-start | bytes 1179652
  7.2 9.9 %copy-start.9 = (f32[31,1536]{1,0:T(8,128)S(1)}, f32[31,1536]{1,0:T(8,128)}, u32[]{:S(2)}) copy-start(f32[31,1536]{1,0:T(8,128)} %param.12) | copy-start | bytes 571396
  7.2 88.3 %all-gather.2.cloned.1.call-start = ((), (), s32[]{:S(2)}) async-start(), calls=%async_computation.5 | async-start | bytes 5013504 | tf_op jit(solution)/shard_map/all_gather | solution.py:569
  7.9 10.2 %copy-start.11 = (f32[1536]{0:T(1024)S(1)}, f32[1536]{0:T(1024)}, u32[]{:S(2)}) copy-start(f32[1536]{0:T(1024)} %param.13) | copy-start | bytes 18436
  7.9 10.3 %copy-start.12 = (f32[1536]{0:T(1024)S(1)}, f32[1536]{0:T(1024)}, u32[]{:S(2)}) copy-start(f32[1536]{0:T(1024)} %param.14) | copy-start | bytes 18436
  10.1 12.4 %collective-permute-start.1 = (bf16[3,32,1536]{2,1,0:T(8,128)(2,1)S(1)}, bf16[3,32,1536]{2,1,0:T(8,128)(2,1)S(1)}, u32[]{:S(2)}, u32[]{:S(2)}) collective-permute-start(bf16[3,32,1536]{2,1,0:T(8,128)(2,1)S(1)} %slice_select_fusion), channel_id=1, source_target_pairs={{2,0},{4,2},{6,4},{8,6},{10,8},{12,10},{14,12},{16,14},{18,16},{20... | collective-permute-start | bytes 884744 | tf_op jit(solution)/shard_map/ppermute | solution.py:559
  11.4 11.8 %collective-permute-start = (bf16[3,32,1536]{2,1,0:T(8,128)(2,1)S(1)}, bf16[3,32,1536]{2,1,0:T(8,128)(2,1)}, u32[]{:S(2)}, u32[]{:S(2)}) collective-permute-start(bf16[3,32,1536]{2,1,0:T(8,128)(2,1)S(1)} %slice_select_fusion), channel_id=1, source_target_pairs={{2,1},{4,3},{6,5},{8,7},{10,9},{12,11},{14,13},{16,15},{18,17},{20... | collective-permute-start | bytes 884744 | tf_op jit(solution)/shard_map/ppermute | solution.py:560
  12.8 11.5 %collective-permute-start.2 = (bf16[3,128,1536]{2,1,0:T(8,128)(2,1)S(1)}, bf16[3,128,1536]{2,1,0:T(8,128)(2,1)S(1)}, u32[]{:S(2)}, u32[]{:S(2)}) collective-permute-start(bf16[3,128,1536]{2,1,0:T(8,128)(2,1)S(1)} %constant_dynamic-update-slice_fusion), channel_id=1, source_target_pairs={{0,1},{1,0},{2,3},{3,2},{4,5},{5,4},{6,7},{7,6},{8,9},{9,8},{10,11... | collective-permute-start | bytes 3538952 | tf_op jit(solution)/shard_map/ppermute | solution.py:558
  22.5 0.7 copy-start.6
  24.5 1.0 copy-start
  24.5 1.4 copy-start.1
  105.5 12.0 %all-to-all-start = ((f32[16,2,768]{2,1,0:T(2,128)}), f32[16,2,768]{2,1,0:T(2,128)}, u32[]{:S(2)}, u32[]{:S(2)}) async-start(f32[16,2,768]{2,1,0:T(2,128)} %get-tuple-element.25), calls=%async_computation | async-start | bytes 196608 | tf_op jit(solution)/shard_map/all_to_all | solution.py:564
  121.4 11.2 %all-to-all-start.1 = ((f32[16,2,768]{2,1,0:T(2,128)}), f32[16,2,768]{2,1,0:T(2,128)S(1)}, u32[]{:S(2)}, u32[]{:S(2)}) async-start(f32[16,2,768]{2,1,0:T(2,128)} %get-tuple-element.27.sums_before), calls=%async_computation.1 | async-start | bytes 196608 | tf_op jit(solution)/shard_map/all_to_all | solution.py:564
  132.6 0.6 copy-start.5
  145.2 2.3 collective-permute-start.3
  147.5 0.9 copy-start.2
  151.5 16.4 %collective-permute-start.4 = (f32[128,1536]{1,0:T(8,128)}, f32[128,1536]{1,0:T(8,128)}, u32[]{:S(2)}, u32[]{:S(2)}) collective-permute-start(f32[128,1536]{1,0:T(8,128)} %get-tuple-element.35.mine), channel_id=1, source_target_pairs={{0,1},{1,0},{2,3},{3,2},{4,5},{5,4},{6,7},{7,6},{8,9},{9,8},{10,11... | collective-permute-start | bytes 2359304 | tf_op jit(solution)/shard_map/ppermute | solution.py:558
  152.7 15.2 %collective-permute-start.6 = (f32[32,1536]{1,0:T(8,128)S(1)}, f32[32,1536]{1,0:T(8,128)S(1)}, u32[]{:S(2)}, u32[]{:S(2)}) collective-permute-start(f32[32,1536]{1,0:T(8,128)S(1)} %slice_select_fusion.1), channel_id=1, source_target_pairs={{2,1},{4,3},{6,5},{8,7},{10,9},{12,11},{14,13},{16,15},{18,17},{20... | collective-permute-start | bytes 589832 | tf_op jit(solution)/shard_map/ppermute | solution.py:560
  153.4 14.6 %collective-permute-start.5 = (f32[32,1536]{1,0:T(8,128)S(1)}, f32[32,1536]{1,0:T(8,128)S(1)}, u32[]{:S(2)}, u32[]{:S(2)}) collective-permute-start(f32[32,1536]{1,0:T(8,128)S(1)} %slice_select_fusion.1), channel_id=1, source_target_pairs={{2,0},{4,2},{6,4},{8,6},{10,8},{12,10},{14,12},{16,14},{18,16},{20... | collective-permute-start | bytes 589832 | tf_op jit(solution)/shard_map/ppermute | solution.py:559
  154.7 13.2 %all-to-all-start.2 = ((f32[32,1,128]{2,1,0:T(1,128)}), f32[32,1,128]{2,1,0:T(1,128)S(1)}, u32[]{:S(2)}, u32[]{:S(2)}) async-start(f32[32,1,128]{2,1,0:T(1,128)} %get-tuple-element.34), calls=%async_computation.2 | async-start | bytes 32768 | tf_op jit(solution)/shard_map/all_to_all | solution.py:613
  167.9 0.6 copy-start.10
  167.9 0.7 copy-start.7
  168.0 0.7 copy-start.8
  183.2 14.3 %all-to-all-start.3 = ((f32[16,2,768]{2,1,0:T(2,128)}), f32[16,2,768]{2,1,0:T(2,128)S(1)}, u32[]{:S(2)}, u32[]{:S(2)}) async-start(f32[16,2,768]{2,1,0:T(2,128)} %get-tuple-element.38.stats.local_stats), calls=%async_computation.3 | async-start | bytes 196608 | tf_op jit(solution)/shard_map/all_to_all | solution.py:564
  197.5 0.6 copy-start.3
Sparse Core Ops, SparseCore 0:
  10.8 84.6 all-gather.1
where the time goes:
time: 241 us; the launch traced here: 240 us
  waiting for transfers between devices  88.7 us (37%)
  Pallas kernels  60.4 us (25%)
  starting transfers between devices  26.8 us (11%)
  blocking collectives  26.6 us (11%)
  between operations  15 us (6%)
  local copies, waits for them, and re-layouts  13.3 us (6%)
  other arithmetic  6.42 us (3%)
  matrix products  2.99 us (1%)
    all_gather x1, waiting for transfers between devices, on_device(): lax.all_gather(in_weight, 'tm', axis=0, axis_index_groups=cores, tiled=True)  67.1 us
    all_to_all x1, blocking collectives, on_device(): received = lax.all_to_all(outgoing, 'tm', 0, 0, tiled=True)  26.6 us
    pallas_call x2, Pallas kernels, forward(): pl.pallas_call(functools.partial(forward_kernel, taps.shape[0]), grid=(st...  20 us
    all_to_all x3, waiting for transfers between devices, peers_of(): lax.all_to_all(array, 'tm', 0, 0, axis_index_groups=cores, tiled=True)  12.4 us
    all_to_all x3, starting transfers between devices, peers_of(): lax.all_to_all(array, 'tm', 0, 0, axis_index_groups=cores, tiled=True)  11.3 us
    pallas_call x1, Pallas kernels, backward(): pl.pallas_call(functools.partial(backward_kernel, taps.shape[0]), grid=(s...  9.57 us
    unnamed x28, local copies, waits for them, and re-layouts  6.82 us
    pallas_call x1, Pallas kernels, last(): pl.pallas_call(functools.partial(last_kernel, taps_n, block), grid=(steps...  6.59 us
  transfers between devices with their start and end apart: 12, of which 6 were waited for; matrix products, arithmetic and copies ran while one was open for 6% of the time, Pallas kernels for 5%

commit v1 on v0

v1 whole, which is shorter than its diff:
```python
import functools

import jax
import jax.numpy as jnp
from jax import lax
from jax.experimental import pallas as pl
from jax.experimental.pallas import tpu as pltpu
from jax.sharding import PartitionSpec as P

ASCENT = 2

noise_scale = 0.5
ascent_rate = 0.5
layer_epsilon = 1e-05
batch_epsilon = 1e-05
ascent_epsilon = 1e-06

HALO = 32
EDGE = 16
F32 = jnp.float32
BF16 = jnp.bfloat16


def params(limit=56 * 1024 * 1024):
    return pltpu.CompilerParams(vmem_limit_bytes=limit)


def cost(flops, nbytes):
    return pl.CostEstimate(flops=int(flops), bytes_accessed=int(nbytes), transcendentals=0)


def normalize(summed):
    centre = summed - jnp.mean(summed, axis=-1, keepdims=True)
    inverse = lax.rsqrt(jnp.mean(centre * centre, axis=-1, keepdims=True) + layer_epsilon)
    return (centre * inverse, inverse)


def live_rows(first, rows, end):
    ids = first + lax.broadcasted_iota(jnp.int32, (rows, 1), 0)
    return jnp.where((ids >= 0) & (ids < end), 1.0, 0.0).astype(F32)


def spread(plain, shifted, array):
    plain[...] = array
    rows, tiles = shifted.shape[1] * 8, shifted.shape[1]
    for s in range(8):
        shifted[s] = plain[s : s + rows].reshape(tiles, 8, -1)


def tiles_at(shifted, row, tiles, lanes):
    first = (row - row % 8) // 8
    return shifted[row % 8, first : first + tiles, :, lanes]


def convolve(taps, shifted, offsets, rows, most):
    most = max(n for n in range(1, most + 1) if rows // 8 % n == 0)
    columns = []
    for lane in range(0, taps.shape[2], 128):
        lanes = slice(lane, lane + 128)
        parts = []
        for tile in range(0, rows // 8, most):
            total = jnp.zeros((most, 8, 128), F32)
            for tap, offset in enumerate(offsets):
                total = total + taps[tap, :, lanes][None] * tiles_at(
                    shifted, offset + 8 * tile, most, lanes
                )
            parts.append(total.reshape(most * 8, 128))
        columns.append(jnp.concatenate(parts, axis=0))
    return jnp.concatenate(columns, axis=1)


def correlate(taps_n, left, shifted, first):
    rows = left.shape[0]
    lanes = slice(0, 128)
    most = 16
    totals = [None] * taps_n
    for tile in range(0, rows // 8, most):
        part = left[8 * tile : 8 * (tile + most)].reshape(most, 8, 128)
        for tap in range(taps_n):
            product = jnp.sum(
                part * tiles_at(shifted, first + tap + 8 * tile, most, lanes), axis=0, keepdims=True
            )
            totals[tap] = product if totals[tap] is None else totals[tap] + product
    return jnp.sum(jnp.concatenate(totals, axis=0), axis=1)


def place_weights(scal, weights, low, high, steps_a, value_w, gate_w):
    own_v, own_g, x_v, x_g, y_v, y_g, d_v, d_g = weights
    step, spot = pl.program_id(0), scal[4]
    rows = own_v.shape[1]

    @pl.when(step < steps_a)
    def _():
        for other, (v, g) in enumerate(((own_v, own_g), (x_v, x_g), (y_v, y_g), (d_v, d_g))):
            at = pl.ds(pl.multiple_of((spot ^ other) * rows, rows), rows)
            value_w[at, :] = v[0]
            gate_w[at, :] = g[0]

    @pl.when(step >= steps_a)
    def _():
        value_w[...] = low[...]
        gate_w[...] = high[...]


def weight_specs(wide_parts, square):
    own, _, _, d_low, _ = wide_parts
    depth, rows, width = own.shape
    half = depth // 2
    chunk = 4 * rows
    steps_b = square.shape[0] // 2 // chunk
    low = lambda i: (jnp.minimum(i, half - 1), 0, 0)
    high = lambda i: (jnp.minimum(i, half - 1) + half, 0, 0)
    block = (1, rows, width)
    specs = []
    for _ in range(3):
        specs += [pl.BlockSpec(block, low), pl.BlockSpec(block, high)]
    specs += [pl.BlockSpec(block, low), pl.BlockSpec(block, low)]
    specs += [
        pl.BlockSpec((chunk, width), lambda i: (jnp.maximum(i - half, 0), 0)),
        pl.BlockSpec((chunk, width), lambda i: (jnp.maximum(i - half, 0) + steps_b, 0)),
    ]
    own, x, y, d_low, d_high = wide_parts
    operands = [own, own, x, x, y, y, d_low, d_high, square, square]
    scratch = [pltpu.VMEM((chunk, width), BF16)] * 2
    return chunk, half, half + steps_b, specs, operands, scratch


def forward_kernel(steps_a, keep, scal, nb, *refs):
    weights, (low, high, taps), refs = refs[:8], refs[8:11], refs[11:]
    kept, (glu, conv, stats, value_w, gate_w, plain, shifted) = refs[: 2 * keep], refs[2 * keep :]
    place_weights(scal, weights, low, high, steps_a, value_w, gate_w)
    start, end = scal[0], scal[1]
    span, taps_n = nb.shape[0], taps.shape[0]
    rows = conv.shape[0] - 2 * EDGE
    contract = (((1,), (1,)), ((), ()))
    v = lax.dot_general(nb[...], value_w[...], contract, preferred_element_type=F32)
    s = jax.nn.sigmoid(lax.dot_general(nb[...], gate_w[...], contract, preferred_element_type=F32))
    if keep:
        kept[0][...] = v[HALO : HALO + rows]
        kept[1][...] = s[HALO : HALO + rows]
    gated = (v * s * live_rows(start - HALO, span, end)).astype(BF16)
    glu[...] = gated
    spread(plain, shifted, gated.astype(F32))
    shift = HALO - EDGE - (taps_n - 1) // 2
    conv[...] = convolve(taps, shifted, [shift + tap for tap in range(taps_n)], conv.shape[0], 12)
    live = live_rows(start, rows, end)
    own = conv[EDGE : EDGE + rows, :]
    mass = jnp.sum(live * own, axis=0, keepdims=True)
    centre = live * (own - mass / jnp.maximum(jnp.sum(live), 1.0))
    both = jnp.concatenate([mass, jnp.sum(centre * centre, axis=0, keepdims=True)], axis=0)
    for peer in range(stats.shape[0]):
        stats[peer] = both


def forward(scal, nb, wide_parts, square, taps, rows, peers, keep):
    span, width = nb.shape
    taps_n, _, half_width = taps.shape
    chunk, steps_a, steps, specs, operands, scratch = weight_specs(wide_parts, square)
    col = lambda n: pl.BlockSpec((n, chunk), lambda i: (0, i))
    return pl.pallas_call(
        functools.partial(forward_kernel, steps_a, keep),
        grid=(steps,),
        in_specs=[
            pl.BlockSpec(memory_space=pltpu.SMEM),
            pl.BlockSpec((span, width), lambda i: (0, 0)),
            *specs,
            pl.BlockSpec((taps_n, 8, chunk), lambda i: (0, 0, i)),
        ],
        out_specs=[
            *([col(rows)] * (2 * keep)),
            col(span),
            col(rows + 2 * EDGE),
            pl.BlockSpec((peers, 2, chunk), lambda i: (0, 0, i)),
        ],
        out_shape=[
            *([jax.ShapeDtypeStruct((rows, half_width), F32)] * (2 * keep)),
            jax.ShapeDtypeStruct((span, half_width), BF16),
            jax.ShapeDtypeStruct((rows + 2 * EDGE, half_width), F32),
            jax.ShapeDtypeStruct((peers, 2, half_width), F32),
        ],
        scratch_shapes=[
            *scratch,
            pltpu.VMEM((span, chunk), F32),
            pltpu.VMEM((8, span // 8 - 1, 8, chunk), F32),
        ],
        compiler_params=params(),
        cost_estimate=cost(2 * span * width * 2 * half_width, 4 * half_width * width + 10 * span * half_width),
        name="project_glu_conv",
    )(scal, nb, *operands, taps)


def moments(counts, stats, live_count):
    mass = stats[0, 0:1, :]
    square = stats[0, 1:2, :]
    for peer in range(1, stats.shape[0]):
        mass = mass + stats[peer, 0:1, :]
        square = square + stats[peer, 1:2, :]
    mean = mass / live_count
    for peer in range(stats.shape[0]):
        off = stats[peer, 0:1, :] - counts[0, peer] * mean
        square = square + off * off * counts[1, peer]
    return mean, lax.rsqrt(square / live_count + batch_epsilon)


def swish_grads(scal, counts, stats, conv, cot, gain, shift):
    start, end = scal[0], scal[1]
    live_count = scal[3].astype(F32)
    mean, inv = moments(counts, stats, live_count)
    scaled = (conv[...] - mean) * inv
    pre = gain[...] * scaled + shift[...]
    sig = jax.nn.sigmoid(pre)
    live = live_rows(start - EDGE, conv.shape[0], end)
    upstream = live * cot[...].astype(F32) / ASCENT
    return scaled, upstream * sig * (1.0 + pre * (1.0 - sig)), live, mean, inv


def batch_kernel(scal, counts, stats, conv, cot, gain, shift, scaled_out, grad_out, inv_out, sums):
    scaled, grad, live, mean, inv = swish_grads(scal, counts, stats, conv, cot, gain, shift)
    scaled_out[...] = scaled
    grad_out[...] = grad
    inv_out[...] = inv
    rows = conv.shape[0] - 2 * EDGE
    own = grad[EDGE : EDGE + rows]
    both = jnp.concatenate(
        [
            jnp.sum(own, axis=0, keepdims=True),
            jnp.sum(own * scaled[EDGE : EDGE + rows], axis=0, keepdims=True),
        ],
        axis=0,
    )
    for peer in range(sums.shape[0]):
        sums[peer] = both


def batch(scal, counts, stats, conv, cot, gain, shift, peers):
    span, half_width = conv.shape
    chunk = 256 if half_width % 256 == 0 else 128
    col = lambda n: pl.BlockSpec((n, chunk), lambda i: (0, i))
    smem = pl.BlockSpec(memory_space=pltpu.SMEM)
    return pl.pallas_call(
        batch_kernel,
        grid=(half_width // chunk,),
        in_specs=[
            smem,
            smem,
            pl.BlockSpec((stats.shape[0], 2, chunk), lambda i: (0, 0, i)),
            col(span),
            col(span),
            col(1),
            col(1),
        ],
        out_specs=[col(span), col(span), col(1), pl.BlockSpec((peers, 2, chunk), lambda i: (0, 0, i))],
        out_shape=[
            jax.ShapeDtypeStruct((span, half_width), F32),
            jax.ShapeDtypeStruct((span, half_width), F32),
            jax.ShapeDtypeStruct((1, half_width), F32),
            jax.ShapeDtypeStruct((peers, 2, half_width), F32),
        ],
        compiler_params=params(),
        cost_estimate=cost(40 * span * half_width, 16 * span * half_width),
        name="batch_norm_swish",
    )(scal, counts, stats, conv, cot, gain, shift)


def backward_kernel(steps_a, scal, sums, scaled, grad, inv, gain, taps, value, gate, *refs):
    weights, (low, high), refs = refs[:8], refs[8:10], refs[10:]
    mine, other, grad_conv, totals, value_w, gate_w, plain, shifted, part = refs
    place_weights(scal, weights, low, high, steps_a, value_w, gate_w)
    start, end, core = scal[0], scal[1], scal[2]
    rows, taps_n = value.shape[0], taps.shape[0]
    half = (taps_n - 1) // 2
    live_count = scal[3].astype(F32)
    both = sums[0]
    for peer in range(1, sums.shape[0]):
        both = both + sums[peer]
    totals[...] = both
    shift_sum, gain_sum = both[0:1], both[1:2]
    live = live_rows(start - EDGE, scaled.shape[0], end)
    through = live * (inv[...] * gain[...]) * (
        grad[...] - (shift_sum + scaled[...] * gain_sum) / live_count
    )
    rounded = through.astype(BF16)
    grad_conv[...] = rounded[EDGE : EDGE + rows]
    spread(plain, shifted, rounded.astype(F32))
    grad_glu = convolve(taps, shifted, [EDGE + half - tap for tap in range(taps_n)], rows, 16)
    grad_glu = (grad_glu * live_rows(start, rows, end)).astype(BF16).astype(F32)
    sig = gate[...]
    to_value = (grad_glu * sig).astype(BF16)
    to_gate = (grad_glu * value[...] * sig * (1.0 - sig)).astype(BF16)
    product = jnp.dot(to_value, value_w[...], preferred_element_type=F32) + jnp.dot(
        to_gate, gate_w[...], preferred_element_type=F32
    )
    step, last_step = pl.program_id(0), pl.num_programs(0) - 1

    @pl.when(step == 0)
    def _():
        part[...] = product

    @pl.when(step > 0)
    def _():
        part[...] += product

    @pl.when(step == last_step)
    def _():
        count = mine.shape[0]
        mine[...] = part[pl.ds(pl.multiple_of(core * count, count), count), :]
        other[...] = part[pl.ds(pl.multiple_of((1 - core) * count, count), count), :]


def backward(scal, sums, scaled, grad, inv, gain, taps, value, gate, wide_parts, square):
    span, half_width = scaled.shape
    rows, width = value.shape[0], square.shape[1]
    chunk, steps_a, steps, specs, operands, scratch = weight_specs(wide_parts, square)
    taps_n = taps.shape[0]
    col = lambda n: pl.BlockSpec((n, chunk), lambda i: (0, i))
    own = pl.BlockSpec((rows // 2, width), lambda i: (0, 0))
    return pl.pallas_call(
        functools.partial(backward_kernel, steps_a),
        grid=(steps,),
        in_specs=[
            pl.BlockSpec(memory_space=pltpu.SMEM),
            pl.BlockSpec((sums.shape[0], 2, chunk), lambda i: (0, 0, i)),
            col(span),
            col(span),
            col(1),
            col(1),
            pl.BlockSpec((taps_n, 8, chunk), lambda i: (0, 0, i)),
            col(rows),
            col(rows),
            *specs,
        ],
        out_specs=[own, own, col(rows), col(2)],
        out_shape=[
            jax.ShapeDtypeStruct((rows // 2, width), F32),
            jax.ShapeDtypeStruct((rows // 2, width), F32),
            jax.ShapeDtypeStruct((rows, half_width), BF16),
            jax.ShapeDtypeStruct((2, half_width), F32),
        ],
        scratch_shapes=[
            *scratch,
            pltpu.VMEM((span, chunk), F32),
            pltpu.VMEM((8, span // 8 - 1, 8, chunk), F32),
            pltpu.VMEM((rows, width), F32),
        ],
        compiler_params=params(),
        cost_estimate=cost(2 * rows * width * 2 * half_width, 4 * half_width * width + 20 * span * half_width),
        name="grad_conv_project_back",
    )(scal, sums, scaled, grad, inv, gain, taps, value, gate, *operands)


def shifted_scratch(span):
    return [pltpu.VMEM((span, 128), F32), pltpu.VMEM((8, span // 8 - 1, 8, 128), F32)]


def tap_grad_kernel(taps_n, grad_conv, glu, out, plain, shifted):
    spread(plain, shifted, glu[...].astype(F32))
    first = HALO - (taps_n - 1) // 2
    out[...] = correlate(taps_n, grad_conv[...].astype(F32), shifted, first)


def tap_grad(taps_n, grad_conv, glu):
    rows, half_width = grad_conv.shape
    span = glu.shape[0]
    col = lambda n: pl.BlockSpec((n, 128), lambda i: (0, i))
    return pl.pallas_call(
        functools.partial(tap_grad_kernel, taps_n),
        grid=(half_width // 128,),
        in_specs=[col(rows), col(span)],
        out_specs=col(taps_n),
        out_shape=jax.ShapeDtypeStruct((taps_n, half_width), F32),
        scratch_shapes=shifted_scratch(span),
        compiler_params=params(),
        cost_estimate=cost(2 * taps_n * rows * half_width, 4 * span * half_width),
        name="tap_grad",
    )(grad_conv, glu)


def raw_taps_kernel(taps_n, scal, conv, glu, stats, alone, crossed, plain, shifted):
    start, end = scal[0], scal[1]
    rows, span = conv.shape[0] - 2 * EDGE, glu.shape[0]
    spread(plain, shifted, glu[...].astype(F32))
    first = HALO - (taps_n - 1) // 2
    live = live_rows(start, rows, end)
    local = stats[0, 0:1, :] / jnp.maximum(jnp.sum(live), 1.0)
    crossed[...] = correlate(taps_n, live * (conv[EDGE : EDGE + rows, :] - local), shifted, first)
    tap = lax.broadcasted_iota(jnp.int32, (taps_n, span), 0)
    at = lax.broadcasted_iota(jnp.int32, (taps_n, span), 1) - first - tap
    inside = (at >= 0) & (at < jnp.clip(end - start, 0, rows))
    alone[...] = jnp.dot(
        jnp.where(inside, 1.0, 0.0).astype(BF16), glu[...], preferred_element_type=F32
    )


def raw_taps(taps_n, scal, conv, glu, stats):
    rows, half_width = conv.shape
    span = glu.shape[0]
    col = lambda n: pl.BlockSpec((n, 128), lambda i: (0, i))
    return pl.pallas_call(
        functools.partial(raw_taps_kernel, taps_n),
        grid=(half_width // 128,),
        in_specs=[
            pl.BlockSpec(memory_space=pltpu.SMEM),
            col(rows),
            col(span),
            pl.BlockSpec((1, 2, 128), lambda i: (0, 0, i)),
        ],
        out_specs=[col(taps_n), col(taps_n)],
        out_shape=[jax.ShapeDtypeStruct((taps_n, half_width), F32)] * 2,
        scratch_shapes=shifted_scratch(span),
        compiler_params=params(),
        cost_estimate=cost(2 * taps_n * rows * half_width, 8 * span * half_width),
        name="raw_taps",
    )(scal, conv, glu, stats)


def halves(array):
    high = array.astype(BF16).astype(F32)
    return high, array - high


def last_kernel(taps_n, part_a, scal, counts, stats, conv, cot, gain, shift, glu, alone, crossed, local_stats, taps_before, out, factor_out, plain, shifted, pay):
    step = pl.program_id(0)
    scaled, grad, live, mean, inv = swish_grads(scal, counts, stats, conv, cot, gain, shift)
    rows = conv.shape[0] - 2 * EDGE
    spread(plain, shifted, glu[...].astype(F32))
    first = HALO - (taps_n - 1) // 2
    factor = inv * gain[...]
    factor_out[...] = factor
    own = grad[EDGE : EDGE + rows]
    direct = taps_before[...] + factor * correlate(taps_n, own, shifted, first)
    own_live = live[EDGE : EDGE + rows]
    local = local_stats[0, 0:1, :] / jnp.maximum(jnp.sum(own_live), 1.0)
    with_scaled = inv * (crossed[...] + (local - mean) * alone[...])
    sums = jnp.concatenate(
        [
            jnp.sum(own, axis=0, keepdims=True),
            jnp.sum(own * scaled[EDGE : EDGE + rows], axis=0, keepdims=True),
        ],
        axis=0,
    )
    pay[step] = jnp.concatenate([*halves(direct), with_scaled, alone[...], *halves(sums)], axis=0)

    @pl.when(step == pl.num_programs(0) - 1)
    def _():
        turned = jnp.concatenate([jnp.transpose(pay[s]) for s in range(pay.shape[0])], axis=0)
        peers, block = out.shape[0], out.shape[1]
        part_b = block - part_a
        for index in range(peers):
            low, high = index * part_a, peers * part_a + index * part_b
            out[index] = jnp.concatenate(
                [turned[low : low + part_a], turned[high : high + part_b]], axis=0
            ).astype(BF16)


def last(taps_n, part_a, peers, scal, counts, stats, conv, cot, gain, shift, glu, alone, crossed, local_stats, taps_before):
    span, half_width = conv.shape
    chunk = 128
    steps = half_width // chunk
    pay = 4 * taps_n + 4
    col = lambda n: pl.BlockSpec((n, chunk), lambda i: (0, i))
    smem = pl.BlockSpec(memory_space=pltpu.SMEM)
    return pl.pallas_call(
        functools.partial(last_kernel, taps_n, part_a),
        grid=(steps,),
        in_specs=[
            smem,
            smem,
            pl.BlockSpec((stats.shape[0], 2, chunk), lambda i: (0, 0, i)),
            col(span),
            col(span),
            col(1),
            col(1),
            col(glu.shape[0]),
            col(taps_n),
            col(taps_n),
            pl.BlockSpec((1, 2, chunk), lambda i: (0, 0, i)),
            col(taps_n),
        ],
        out_specs=[pl.BlockSpec((peers, half_width // peers, pay), lambda i: (0, 0, 0)), col(1)],
        out_shape=[
            jax.ShapeDtypeStruct((peers, half_width // peers, pay), BF16),
            jax.ShapeDtypeStruct((1, half_width), F32),
        ],
        scratch_shapes=[*shifted_scratch(glu.shape[0]), pltpu.VMEM((steps, pay, chunk), F32)],
        compiler_params=params(),
        cost_estimate=cost(100 * span * half_width, 10 * span * half_width),
        name="batch_norm_swish_taps",
    )(scal, counts, stats, conv, cot, gain, shift, glu, alone, crossed, local_stats, taps_before)


def finish_kernel(taps_n, scal, received, known, taps_out, norm_out):
    total = received[0].astype(F32)
    for index in range(1, received.shape[0]):
        total = total + received[index].astype(F32)
    total = jnp.transpose(total)
    n = taps_n
    sums = total[4 * n : 4 * n + 2] + total[4 * n + 2 : 4 * n + 4]
    shift_sum, gain_sum = sums[0:1], sums[1:2]
    factor = known[0:1] / scal[3].astype(F32)
    taps_out[...] = (total[:n] + total[n : 2 * n]) - factor * (
        gain_sum * total[2 * n : 3 * n] + shift_sum * total[3 * n : 4 * n]
    )
    norm_out[...] = jnp.concatenate([gain_sum + known[2:3], shift_sum + known[1:2]], axis=0)


def finish(taps_n, scal, received, known):
    width = received.shape[1]
    vmem = pl.BlockSpec(memory_space=pltpu.VMEM)
    return pl.pallas_call(
        functools.partial(finish_kernel, taps_n),
        in_specs=[pl.BlockSpec(memory_space=pltpu.SMEM), vmem, vmem],
        out_shape=[
            jax.ShapeDtypeStruct((taps_n, width), F32),
            jax.ShapeDtypeStruct((2, width), F32),
        ],
        compiler_params=params(),
        name="finish",
    )(scal, received, known)


def direction_kernel(scal, mine, other, features, noise, out, edge, squares):
    rows = mine.shape[0]
    first = scal[0] + scal[2] * rows
    block = 32
    total = jnp.zeros((1, 128), F32)
    for row in range(0, rows, block):
        at = slice(row, row + block)
        live = live_rows(first + row, block, scal[1])
        summed = features[at].astype(F32) + noise_scale * noise[at].astype(F32) * live
        normed, inverse = normalize(summed)
        grad = mine[at] + other[at]
        moved = (
            live
            * inverse
            * (
                grad
                - jnp.mean(grad, axis=-1, keepdims=True)
                - normed * jnp.mean(grad * normed, axis=-1, keepdims=True)
            )
        )
        out[at] = moved
        total = total + jnp.sum(moved * moved)
    edge[...] = jnp.where(scal[2] == 0, out[:HALO], out[rows - HALO :])
    for peer in range(squares.shape[0]):
        squares[peer] = total


def direction(scal, mine, other, features, noise, peers):
    rows, width = mine.shape
    vmem = pl.BlockSpec(memory_space=pltpu.VMEM)
    return pl.pallas_call(
        direction_kernel,
        in_specs=[pl.BlockSpec(memory_space=pltpu.SMEM)] + [vmem] * 4,
        out_shape=[
            jax.ShapeDtypeStruct((rows, width), F32),
            jax.ShapeDtypeStruct((HALO, width), F32),
            jax.ShapeDtypeStruct((peers, 1, 128), F32),
        ],
        compiler_params=params(),
        cost_estimate=cost(30 * rows * width, 16 * rows * width),
        name="direction",
    )(scal, mine, other, features, noise)


def ascend_kernel(scal, squares, features, noise, mine, partner, near, far, own_noise, perturbation, normed_out):
    start, end, core = scal[0], scal[1], scal[2]
    rows, width = mine.shape
    total = squares[0]
    for index in range(1, squares.shape[0]):
        total = total + squares[index]
    total = total[0:1, 0:1]
    length = jnp.full((1, 1), 1.0, F32) * end.astype(F32)
    rate = ascent_rate * jnp.sqrt(length * width) / (jnp.sqrt(total) + ascent_epsilon)
    block = 32
    is_first = core == 0

    def place(row, moved):
        at = slice(row, row + block)
        live = live_rows(start - HALO + row, block, end)
        summed = features[at].astype(F32) + (noise_scale * noise[at].astype(F32) * live + moved * rate)
        normed_out[at] = normalize(summed)[0].astype(BF16)

    place(0, jnp.where(is_first, far[...], near[...]))
    for row in range(0, rows, block):
        at = slice(row, row + block)
        place(HALO + row, jnp.where(is_first, mine[at], partner[at]))
        place(HALO + rows + row, jnp.where(is_first, partner[at], mine[at]))
        live = live_rows(start + core * rows + row, block, end)
        perturbation[at] = noise_scale * own_noise[at].astype(F32) * live + mine[at] * rate
    place(HALO + 2 * rows, jnp.where(is_first, near[...], far[...]))


def ascend(scal, squares, features, noise, mine, partner, near, far, own_noise):
    vmem = pl.BlockSpec(memory_space=pltpu.VMEM)
    return pl.pallas_call(
        ascend_kernel,
        in_specs=[pl.BlockSpec(memory_space=pltpu.SMEM)] + [vmem] * 8,
        out_shape=[
            jax.ShapeDtypeStruct(mine.shape, F32),
            jax.ShapeDtypeStruct(features.shape, BF16),
        ],
        compiler_params=params(),
        cost_estimate=cost(30 * features.size, 8 * features.size),
        name="ascend",
    )(scal, squares, features, noise, mine, partner, near, far, own_noise)


def on_device(on_dp, features, start_noise, cotangent, in_weight, kernel, bn_gain, bn_shift, ends):
    rows, width = features.shape[1:]
    taps_n = kernel.shape[0]
    shards = lax.axis_size("tm")
    chips = shards // 2
    index = lax.axis_index("tm")
    group = lax.axis_index("dp")
    chip, core = index // 2, index % 2
    chip_rows = 2 * rows
    half_width = width // 2
    end = lax.dynamic_index_in_dim(ends, group, 0, keepdims=False)
    scal = jnp.stack([chip * chip_rows, end, core, jnp.sum(ends), chip % 4]).astype(jnp.int32)
    held = jnp.clip(
        ends[:, None] - chip_rows * jnp.arange(chips, dtype=jnp.int32)[None, :], 0, chip_rows
    ).reshape(-1).astype(F32)
    counts = jnp.stack([held, jnp.where(held > 0, 1.0 / jnp.maximum(held, 1.0), 0.0)])

    cores = [[2 * c + k for c in range(chips)] for k in range(2)]
    columns = [[8 * z + k for z in range(shards // 8)] for k in range(8)]
    swap = [(i, i ^ 1) for i in range(shards)]
    swap_x = [(i, i ^ 2) for i in range(shards)]
    swap_y = [(i, i ^ 4) for i in range(shards)]
    near_pairs = [(2 * c, 2 * c - 2) for c in range(1, chips)] + [
        (2 * c + 1, 2 * c + 3) for c in range(chips - 1)
    ]
    far_pairs = [(2 * c, 2 * c - 1) for c in range(1, chips)] + [
        (2 * c + 1, 2 * c + 2) for c in range(chips - 1)
    ]
    first = core == 0

    def across(array, edge):
        return (
            lax.ppermute(array, "tm", swap),
            lax.ppermute(edge, "tm", near_pairs),
            lax.ppermute(edge, "tm", far_pairs),
        )

    def peers_of(array):
        array = lax.all_to_all(array, "tm", 0, 0, axis_index_groups=cores, tiled=True)
        if on_dp:
            array = lax.all_gather(array, "dp", axis=0, tiled=True)
        return array

    def around(array):
        half = array.shape[0] // 2
        from_x = lax.ppermute(array, "tm", swap_x)
        from_y = lax.ppermute(array, "tm", swap_y)
        return (
            from_x,
            from_y,
            lax.ppermute(from_y[:half], "tm", swap_x),
            lax.ppermute(from_x[half:], "tm", swap_y),
        )

    slice_width = width // shards
    part_a = 2 * slice_width // 3
    pair = in_weight.reshape(2, slice_width, width)
    kept = lax.dynamic_index_in_dim(pair, core, 0, keepdims=False)
    given = lax.ppermute(lax.dynamic_index_in_dim(pair, 1 - core, 0, keepdims=False), "tm", swap)
    one, two = jnp.where(first, kept, given), jnp.where(first, given, kept)
    weight_a = jnp.concatenate([one[:part_a], two[:part_a]], axis=0)
    weight_b = jnp.concatenate([one[part_a:], two[part_a:]], axis=0)
    column = lax.all_gather(weight_a, "tm", axis=0, axis_index_groups=columns, tiled=False)
    x_b, y_b, d_low, d_high = around(weight_b)
    four = (weight_b, x_b, y_b, jnp.concatenate([d_low, d_high], axis=0))
    spot = chip % 4
    square = jnp.stack(
        [
            jnp.where(spot == s, four[0], jnp.where(spot == s ^ 1, four[1], jnp.where(spot == s ^ 2, four[2], four[3])))
            for s in range(4)
        ]
    ).reshape(-1, width)
    square = lax.all_gather(square, "tm", axis=0, axis_index_groups=columns, tiled=True)
    wide_parts = (column, *around(column))

    packed = jnp.concatenate([features, start_noise, cotangent], axis=0)
    partner, near, far = across(
        packed, jnp.where(first, packed[:, :HALO], packed[:, rows - HALO :])
    )
    whole = jnp.concatenate(
        [
            jnp.where(first, far, near),
            jnp.where(first, packed, partner),
            jnp.where(first, partner, packed),
            jnp.where(first, near, far),
        ],
        axis=1,
    )
    wide_features, wide_noise, wide_cot = whole[0], whole[1], whole[2]

    place = jnp.arange(half_width, dtype=jnp.int32)
    part_b = slice_width - part_a
    in_a = place < chips * part_a
    rest = place - chips * part_a
    at = jnp.where(in_a, place // part_a, rest // part_b)
    within = jnp.where(in_a, place % part_a, part_a + rest % part_b)
    source = (2 * at + core) * slice_width + within
    chosen = (jnp.arange(width, dtype=jnp.int32)[:, None] == source[None, :]).astype(BF16)
    cot = jnp.dot(wide_cot[HALO - EDGE : -(HALO - EDGE)], chosen, preferred_element_type=F32).astype(BF16)

    def mine_of(array):
        parts = array.reshape(array.shape[0], chips, 2, slice_width)
        own = lax.dynamic_index_in_dim(parts, core, 2, keepdims=False)
        return jnp.concatenate(
            [
                own[..., :part_a].reshape(array.shape[0], -1),
                own[..., part_a:].reshape(array.shape[0], -1),
            ],
            axis=1,
        )

    channel = mine_of(jnp.concatenate([kernel, bn_gain[None], bn_shift[None]], axis=0))
    gain, shift = channel[taps_n : taps_n + 1], channel[taps_n + 1 :]
    taps = jnp.broadcast_to(channel[:taps_n, None], (taps_n, 8, half_width))

    frame_ids = chip * chip_rows - HALO + jnp.arange(whole.shape[1], dtype=jnp.int32)
    live = ((frame_ids >= 0) & (frame_ids < end)).astype(F32)
    summed = wide_features.astype(F32) + noise_scale * wide_noise.astype(F32) * live[:, None]
    normed_b = normalize(summed)[0].astype(BF16)

    value, gate, glu, conv, stats = forward(
        scal, normed_b, wide_parts, square, taps, chip_rows, chips, True
    )
    scaled, grad, inv, sums = batch(scal, counts, peers_of(stats), conv, cot, gain, shift, chips)
    mine, other, grad_conv, totals = backward(
        scal, peers_of(sums), scaled, grad, inv, gain, taps, value, gate, wide_parts, square
    )
    other = lax.ppermute(other, "tm", swap)
    moved, edge, squares = direction(scal, mine, other, features[0], start_noise[0], shards)
    squares = lax.all_to_all(squares, "tm", 0, 0, tiled=True)
    partner, near, far = across(moved, edge)
    taps_before = tap_grad(taps_n, grad_conv, glu)
    squares, taps_before = lax.optimization_barrier((squares, taps_before))
    perturbation, normed_b = ascend(
        scal, squares, wide_features, wide_noise, moved, partner, near, far, start_noise[0]
    )

    glu, conv, stats = forward(scal, normed_b, wide_parts, square, taps, chip_rows, chips, False)
    alone, crossed = raw_taps(taps_n, scal, conv, glu, stats)
    outgoing, factor = last(
        taps_n, part_a, chips, scal, counts, peers_of(stats), conv, cot, gain, shift, glu, alone, crossed, stats, taps_before
    )
    received = peers_of(outgoing)
    known = jnp.concatenate([factor, totals], axis=0)
    known = jnp.concatenate(
        [
            lax.dynamic_slice_in_dim(known[:, : chips * part_a], chip * part_a, part_a, 1),
            lax.dynamic_slice_in_dim(known[:, chips * part_a :], chip * part_b, part_b, 1),
        ],
        axis=1,
    )
    kernel_total, norm_total = finish(taps_n, scal, received, known)
    return (perturbation[None], kernel_total, norm_total)


def solution(mesh):
    return jax.shard_map(
        functools.partial(on_device, mesh.shape["dp"] > 1),
        mesh=mesh,
        in_specs=(
            P("dp", "tm", None),
            P("dp", "tm", None),
            P("dp", "tm", None),
            P("tm", None),
            P(),
            P(),
            P(),
            P(),
        ),
        out_specs=(P("dp", "tm", None), P(None, "tm"), P(None, "tm")),
        check_vma=False,
    )
```

time: 241 us -> 236 us (0.979)
  waiting for transfers between devices: 88.7 us -> 60.4 us
  starting transfers between devices: 26.8 us -> 44.9 us
  blocking collectives: 26.6 us -> 31.4 us
  other arithmetic: 6.42 us -> 10.8 us
  Pallas kernels: 60.4 us -> 56.8 us
    all_gather x1, waiting for transfers between devices: 67.1 us -> 11.7 us  [on_device(): lax.all_gather(square, 'tm', axis=0, axis_index_groups=columns, tiled=True)]
    ppermute x0 -> x9, waiting for transfers between devices: none -> 32.4 us  [the longest x2 16.5 us: around(): lax.ppermute(from_x[half:], 'tm', swap_y)]
    all_gather x0 -> x1, blocking collectives: none -> 19.6 us  [on_device(): lax.all_gather(weight_a, 'tm', axis=0, axis_index_groups=columns, tiled=F...]
    all_to_all x1, blocking collectives: 26.6 us -> 11.8 us  [peers_of(): lax.all_to_all(array, 'tm', 0, 0, axis_index_groups=cores, tiled=True)]
    ppermute x0 -> x9, starting transfers between devices: none -> 13.9 us  [the longest x2 5.02 us: around(): lax.ppermute(from_y[:half], 'tm', swap_x)]
    all_to_all x1, waiting for transfers between devices: 5.5 us -> 0.71 us  [on_device(): squares = lax.all_to_all(squares, 'tm', 0, 0, tiled=True)]
    all_to_all x3, starting transfers between devices: 11.3 us -> 15.6 us  [peers_of(): lax.all_to_all(array, 'tm', 0, 0, axis_index_groups=cores, tiled=True)]
    pallas_call x5, Pallas kernels: 38.1 us -> 34.8 us  [the longest x2 17.9 us: forward(): pl.pallas_call(functools.partial(forward_kernel, steps_a, keep), grid=(st...]
  transfers between devices with their start and end apart: 12 -> 21, of which waited for: 6 -> 10; matrix products, arithmetic and copies ran while one was open for 6% -> 7% of each run, Pallas kernels for 5% -> 4%
where the time goes in v1:
time: 236 us; the launch traced here: 235 us
  waiting for transfers between devices  60.4 us (26%)
  Pallas kernels  56.8 us (24%)
  starting transfers between devices  44.9 us (19%)
  blocking collectives  31.4 us (13%)
  between operations  15.2 us (6%)
  local copies, waits for them, and re-layouts  12.5 us (5%)
  other arithmetic  10.8 us (5%)
  matrix products  2.99 us (1%)
    all_gather x1, blocking collectives, on_device(): lax.all_gather(weight_a, 'tm', axis=0, axis_index_groups=columns, tiled=F...  19.6 us
    pallas_call x2, Pallas kernels, forward(): pl.pallas_call(functools.partial(forward_kernel, steps_a, keep), grid=(st...  17.9 us
    ppermute x2, waiting for transfers between devices, around(): lax.ppermute(from_x[half:], 'tm', swap_y)  16.5 us
    all_to_all x3, starting transfers between devices, peers_of(): lax.all_to_all(array, 'tm', 0, 0, axis_index_groups=cores, tiled=True)  15.6 us
    ppermute x2, waiting for transfers between devices, around(): from_x = lax.ppermute(array, 'tm', swap_x)  14.7 us
    all_to_all x3, waiting for transfers between devices, peers_of(): lax.all_to_all(array, 'tm', 0, 0, axis_index_groups=cores, tiled=True)  13.1 us
    all_to_all x1, blocking collectives, peers_of(): lax.all_to_all(array, 'tm', 0, 0, axis_index_groups=cores, tiled=True)  11.8 us
    all_gather x1, waiting for transfers between devices, on_device(): lax.all_gather(square, 'tm', axis=0, axis_index_groups=columns, tiled=True)  11.7 us
  transfers between devices with their start and end apart: 21, of which 10 were waited for; matrix products, arithmetic and copies ran while one was open for 7% of the time, Pallas kernels for 4%

profile of v1, /device:TPU:0, one launch (start us, length us, event | category | flops | bytes accessed | tf_op | source)
XLA Modules:
  0.0 235.0 jit_solution(3828144430326507415)
XLA Ops:
  7.3 1.1 constant_dynamic-update-slice_fusion.2
  8.4 1.0 constant_dynamic-update-slice_fusion.1
  9.4 1.0 constant_dynamic-update-slice_fusion
  10.5 0.7 slice_select_fusion
  11.2 1.3 collective-permute-start.1
  12.5 1.4 collective-permute-start
  13.9 4.4 %collective-permute-start.2 = (bf16[3,128,1536]{2,1,0:T(8,128)(2,1)S(1)}, bf16[3,128,1536]{2,1,0:T(8,128)(2,1)}, u32[]{:S(2)}, u32[]{:S(2)}) collective-permute-start(bf16[3,128,1536]{2,1,0:T(8,128)(2,1)S(1)} %constant_dynamic-update-slice_fusion), channel_id=1, source_target_pairs={{0,1},{1,0},{2,3},{3,2},{4,5},{5,4},{6,7},{7,6},{8,9},{9,8},{10,11... | collective-permute-start | bytes 3538952 | tf_op jit(solution)/shard_map/ppermute | solution.py:640
  18.6 0.8 concatenate.39
  23.6 2.4 %collective-permute-start.9 = (bf16[32,1536]{1,0:T(8,128)(2,1)S(1)}, bf16[32,1536]{1,0:T(8,128)(2,1)S(1)}, u32[]{:S(2)}, u32[]{:S(2)}) collective-permute-start(bf16[32,1536]{1,0:T(8,128)(2,1)S(1)} %pad_maximum_fusion.3), channel_id=1, source_target_pairs={{0,4},{1,5},{2,6},{3,7},{4,0},{5,1},{6,2},{7,3},{8,12},{9,13},{10,... | collective-permute-start | bytes 294920 | tf_op jit(solution)/shard_map/ppermute | solution.py:654
  26.0 2.9 %collective-permute-start.8 = (bf16[32,1536]{1,0:T(8,128)(2,1)S(1)}, bf16[32,1536]{1,0:T(8,128)(2,1)S(1)}, u32[]{:S(2)}, u32[]{:S(2)}) collective-permute-start(bf16[32,1536]{1,0:T(8,128)(2,1)S(1)} %pad_maximum_fusion.3), channel_id=1, source_target_pairs={{0,2},{1,3},{2,0},{3,1},{4,6},{5,7},{6,4},{7,5},{8,10},{9,11},{10,... | collective-permute-start | bytes 294920 | tf_op jit(solution)/shard_map/ppermute | solution.py:653
  28.9 1.2 collective-permute-done.9
  30.1 3.8 %collective-permute-start.10 = (bf16[16,1536]{1,0:T(8,128)(2,1)S(1)}, bf16[16,1536]{1,0:T(8,128)(2,1)S(1)}, u32[]{:S(2)}, u32[]{:S(2)}) collective-permute-start(bf16[16,1536]{1,0:T(8,128)(2,1)S(1)} %slice.96), channel_id=1, source_target_pairs={{0,2},{1,3},{2,0},{3,1},{4,6},{5,7},{6,4},{7,5},{8,10},{9,11},{10,... | collective-permute-start | bytes 147464 | tf_op jit(solution)/shard_map/ppermute | solution.py:658
  33.9 19.6 %all-gather = bf16[256,1536]{1,0:T(8,128)(2,1)S(1)} all-gather(bf16[64,1536]{1,0:T(8,128)(2,1)S(1)} %pad_maximum_fusion.2), channel_id=2, replica_groups={{0,8,16,24},{1,9,17,25},{2,10,18,26},{3,11,19,27},{4,12,20,28},{5,13,21..., dimensions={0}, use_global_device_ids=true | all-gather | bytes 983040 | tf_op jit(solution)/shard_map/all_gather | solution.py:670
  53.5 2.1 collective-permute-start.11
  55.6 14.5 %collective-permute-done.11 = bf16[16,1536]{1,0:T(8,128)(2,1)S(1)} collective-permute-done((bf16[16,1536]{1,0:T(8,128)(2,1)S(1)}, bf16[16,1536]{1,0:T(8,128)(2,1)S(1)}, u32[]{:S(2)}, u32[]{:S(2)}) %collective-permute-start.11) | collective-permute-done | bytes 49184 | tf_op jit(solution)/shard_map/ppermute | solution.py:659
  70.1 0.9 collective-permute-start.4
  71.1 0.8 pad_maximum_fusion.1
  72.0 1.1 broadcast_select_fusion.3
  73.1 1.2 collective-permute-start.6
  74.4 14.7 %collective-permute-done.4.refs_2_.refs_3_ = bf16[4,64,1536]{2,1,0:T(8,128)(2,1)S(1)} collective-permute-done((bf16[4,64,1536]{2,1,0:T(8,128)(2,1)S(1)}, bf16[4,64,1536]{2,1,0:T(8,128)(2,1)S(1)}, u32[]{:S(2)}, u32[]{:S(2)}) %collective-permute-start.4) | collective-permute-done | bytes 786464 | tf_op jit(solution)/shard_map/ppermute | solution.py:653
  89.7 1.4 broadcast_select_fusion.1
  93.6 1.5 multiply_convert_fusion.nb
  95.1 1.9 collective-permute-done.7.refs_7_
  97.1 11.7 %all-gather.3.cloned.1.call-done.refs_8_.refs_9_ = bf16[512,1536]{1,0:T(8,128)(2,1)} async-done(((bf16[128,1536]{1,0:T(8,128)(2,1)}), bf16[512,1536]{1,0:T(8,128)(2,1)}) %all-gather.3.cloned.1.call-update) | async-done | bytes 1572880 | tf_op jit(solution)/shard_map/all_gather | solution.py:680
  108.7 0.9 broadcast_in_dim.6.refs_10_.taps
  109.6 8.9 %project_glu_conv.2 = (f32[256,768]{1,0:T(8,128)}, f32[256,768]{1,0:T(8,128)}, bf16[320,768]{1,0:T(8,128)(2,1)}, f32[288,768]{1,0:T(8,128)}, f32[16,2,768]{2,1,0:T(2,128)}) custom-call(s32[5]{0:T(128)} %stack.37.scal, bf16[320,1536]{1,0:T(8,128)(2,1)} %multiply_convert_fusion.nb, bf16[4,64,1536]{2,1,0:T(8,128)(2,1)} %bitcast.50, ...), custom_call_target="tpu_custom_call" | custom-call | flops 1509949440 | bytes 7176192 | tf_op jit(solution)/shard_map/project_glu_conv/pallas_call | solution.py:160
  118.6 4.5 %all-to-all-start = ((f32[16,2,768]{2,1,0:T(2,128)}), f32[16,2,768]{2,1,0:T(2,128)}, u32[]{:S(2)}, u32[]{:S(2)}) async-start(f32[16,2,768]{2,1,0:T(2,128)} %get-tuple-element.32), calls=%async_computation | async-start | bytes 196608 | tf_op jit(solution)/shard_map/all_to_all | solution.py:646
  123.1 3.0 %fusion.3.cot = bf16[288,768]{1,0:T(8,128)(2,1)} fusion(s32[768]{0:T(1024)S(1)} %fusion.28, bf16[3,32,1536]{2,1,0:T(8,128)(2,1)S(1)} %copy-done.8, bf16[3,128,1536]{2,1,0:T(8,128)(2,1)} %copy-done.4, bf16[3,128,1536]{2,1,0:T(8,128)(2,1)} %copy-done.3, bf16[3,32,1536]{2,1,0:T(8,128)(2,1)S(1)} %copy-done.6), kind=kOutput, calls=%fused_computation.8 | convolution fusion | flops 684417024 | bytes 3394560 | tf_op jit(solution)/shard_map/dot_general | solution.py:706
  126.1 4.7 %all-to-all-done.stats = f32[16,2,768]{2,1,0:T(2,128)} async-done(((f32[16,2,768]{2,1,0:T(2,128)}), f32[16,2,768]{2,1,0:T(2,128)}, u32[]{:S(2)}, u32[]{:S(2)}) %all-to-all-start) | async-done | bytes 98336 | tf_op jit(solution)/shard_map/all_to_all | solution.py:646
  130.8 3.9 %batch_norm_swish.1 = (f32[288,768]{1,0:T(8,128)}, f32[288,768]{1,0:T(8,128)}, f32[1,768]{1,0:T(1,128)}, f32[16,2,768]{2,1,0:T(2,128)}) custom-call(s32[5]{0:T(128)} %stack.37.scal, f32[2,16]{1,0:T(2,128)} %pad_maximum_fusion.6.counts, f32[16,2,768]{2,1,0:T(2,128)} %all-to-all-done.stats, f32[288,768]{1,0:T(8,128)} %get-tuple-element.33.conv, ...), custom_call_target="tpu_custom_call" | custom-call | flops 8847360 | bytes 3538944 | tf_op jit(solution)/shard_map/batch_norm_swish/pallas_call | solution.py:240
  134.7 11.8 %all_to_all.25.sums = f32[16,2,768]{2,1,0:T(2,128)} all-to-all(f32[16,2,768]{2,1,0:T(2,128)} %get-tuple-element.34), channel_id=1, replica_groups={{0,2,4,6,8,10,12,14,16,18,20,22,24,26,28,30},{1,3,5,7,9,11,13,15,17,19,..., dimensions={0} | all-to-all | bytes 196608 | tf_op jit(solution)/shard_map/all_to_all | solution.py:646
  146.6 9.0 %grad_conv_project_back.1 = (f32[128,1536]{1,0:T(8,128)}, f32[128,1536]{1,0:T(8,128)}, bf16[256,768]{1,0:T(8,128)(2,1)}, f32[2,768]{1,0:T(2,128)}) custom-call(s32[5]{0:T(128)} %stack.37.scal, f32[16,2,768]{2,1,0:T(2,128)} %all_to_all.25.sums, f32[288,768]{1,0:T(8,128)} %get-tuple-element.35.scaled, f32[288,768]{1,0:T(8,128)} %get-tuple-element.36.grad, ...), custom_call_target="tpu_custom_call" | custom-call | flops 1207959552 | bytes 9142272 | tf_op jit(solution)/shard_map/grad_conv_project_back/pallas_call | solution.py:317
  155.6 2.5 %collective-permute-done.12.other = f32[128,1536]{1,0:T(8,128)S(1)} collective-permute-done((f32[128,1536]{1,0:T(8,128)}, f32[128,1536]{1,0:T(8,128)S(1)}, u32[]{:S(2)}, u32[]{:S(2)}) %collective-permute-start.12) | collective-permute-done | bytes 786464 | tf_op jit(solution)/shard_map/ppermute | solution.py:735
  158.1 0.9 copy-done.9
  159.0 3.2 %direction.1 = (f32[128,1536]{1,0:T(8,128)}, f32[32,1536]{1,0:T(8,128)}, f32[32,1,128]{2,1,0:T(1,128)}) custom-call(s32[5]{0:T(128)} %stack.37.scal, f32[128,1536]{1,0:T(8,128)} %get-tuple-element.40.mine, f32[128,1536]{1,0:T(8,128)} %copy-done.9, bf16[128,1536]{1,0:T(8,128)(2,1)} %bitcast.58, bf16[128,1536]{1,0:T(8,128)(2,1)} %bitcast.56), custom_call_target="tpu_custom_call" | custom-call | flops 5898240 | bytes 3145728 | tf_op jit(solution)/shard_map/direction/pallas_call | solution.py:551
  163.0 1.3 collective-permute-start.14
  164.3 6.2 %all-to-all-start.2 = ((f32[32,1,128]{2,1,0:T(1,128)}), f32[32,1,128]{2,1,0:T(1,128)S(1)}, u32[]{:S(2)}, u32[]{:S(2)}) async-start(f32[32,1,128]{2,1,0:T(1,128)} %get-tuple-element.42), calls=%async_computation.2 | async-start | bytes 32768 | tf_op jit(solution)/shard_map/all_to_all | solution.py:737
  170.4 1.4 slice_bitcast_fusion
  171.9 4.9 %tap_grad.1.taps_before = f32[31,768]{1,0:T(8,128)} custom-call(bf16[256,768]{1,0:T(8,128)(2,1)} %get-tuple-element.43.grad_conv, bf16[320,768]{1,0:T(8,128)(2,1)} %get-tuple-element.44.glu), custom_call_target="tpu_custom_call" | custom-call | flops 12189696 | bytes 983040 | tf_op jit(solution)/shard_map/tap_grad/pallas_call | solution.py:365
  178.2 4.4 %ascend.1 = (f32[128,1536]{1,0:T(8,128)}, bf16[320,1536]{1,0:T(8,128)(2,1)}) custom-call(s32[5]{0:T(128)} %stack.37.scal, f32[32,1,128]{2,1,0:T(1,128)} %copy-done.17, bf16[320,1536]{1,0:T(8,128)(2,1)} %get-tuple-element.62.features, bf16[320,1536]{1,0:T(8,128)(2,1)} %get-tuple-element.61.noise, f32[128,1536]{1,0:T(8,128)} %get-tuple-element.46.mine, ...), custom_call_target="tpu_custom_call" | custom-call | flops 14745600 | bytes 3932160 | tf_op jit(solution)/shard_map/ascend/pallas_call | solution.py:595
  182.7 8.9 %project_glu_conv.3 = (bf16[320,768]{1,0:T(8,128)(2,1)}, f32[288,768]{1,0:T(8,128)}, f32[16,2,768]{2,1,0:T(2,128)}) custom-call(s32[5]{0:T(128)} %stack.37.scal, bf16[320,1536]{1,0:T(8,128)(2,1)} %get-tuple-element.49.nb, bf16[4,64,1536]{2,1,0:T(8,128)(2,1)} %bitcast.54, bf16[4,64,1536]{2,1,0:T(8,128)(2,1)} %bitcast.55, bf16[4,64,1536]{2,1,0:T(8,128)(2,1)} %copy-done.2, ...), custom_call_target="tpu_custom_call" | custom-call | flops 1509949440 | bytes 7176192 | tf_op jit(solution)/shard_map/project_glu_conv/pallas_call | solution.py:160
  191.6 6.2 %all-to-all-start.3 = ((f32[16,2,768]{2,1,0:T(2,128)}), f32[16,2,768]{2,1,0:T(2,128)S(1)}, u32[]{:S(2)}, u32[]{:S(2)}) async-start(f32[16,2,768]{2,1,0:T(2,128)} %get-tuple-element.50.stats.local_stats), calls=%async_computation.3 | async-start | bytes 196608 | tf_op jit(solution)/shard_map/all_to_all | solution.py:646
  197.8 5.6 %raw_taps.1 = (f32[31,768]{1,0:T(8,128)}, f32[31,768]{1,0:T(8,128)}) custom-call(s32[5]{0:T(128)} %stack.37.scal, f32[288,768]{1,0:T(8,128)} %get-tuple-element.51.conv, bf16[320,768]{1,0:T(8,128)(2,1)} %get-tuple-element.52.glu, f32[16,2,768]{2,1,0:T(2,128)} %get-tuple-element.50.stats.local_stats), custom_call_target="tpu_custom_call" | custom-call | flops 13713408 | bytes 1966080 | tf_op jit(solution)/shard_map/raw_taps/pallas_call | solution.py:398
  203.4 2.0 all-to-all-done.3.stats
  206.0 6.3 %batch_norm_swish_taps.1 = (bf16[16,48,128]{2,1,0:T(8,128)(2,1)}, f32[1,768]{1,0:T(1,128)}) custom-call(s32[5]{0:T(128)} %stack.37.scal, f32[2,16]{1,0:T(2,128)} %pad_maximum_fusion.6.counts, f32[16,2,768]{2,1,0:T(2,128)} %copy-done.11, f32[288,768]{1,0:T(8,128)} %get-tuple-element.51.conv, bf16[288,768]{1,0:T(8,128)(2,1)} %fusion.3.cot, ...), custom_call_target="tpu_custom_call" | custom-call | flops 22118400 | bytes 2211840 | tf_op jit(solution)/shard_map/batch_norm_swish_taps/pallas_call | solution.py:462
  212.4 4.9 %all-to-all-start.4 = ((bf16[16,48,128]{2,1,0:T(8,128)(2,1)}), bf16[16,48,128]{2,1,0:T(8,128)(2,1)S(1)}, u32[]{:S(2)}, u32[]{:S(2)}) async-start(bf16[16,48,128]{2,1,0:T(8,128)(2,1)} %get-tuple-element.56), calls=%async_computation.4 | async-start | bytes 393216 | tf_op jit(solution)/shard_map/all_to_all | solution.py:646
  219.4 6.4 %all-to-all-done.4.received = bf16[16,48,128]{2,1,0:T(8,128)(2,1)S(1)} async-done(((bf16[16,48,128]{2,1,0:T(8,128)(2,1)}), bf16[16,48,128]{2,1,0:T(8,128)(2,1)S(1)}, u32[]{:S(2)}, u32[]{:S(2)}) %all-to-all-start.4) | async-done | bytes 196640 | tf_op jit(solution)/shard_map/all_to_all | solution.py:646
  226.5 1.7 finish.1
  (102 shorter events, 12.7 us)
Async XLA Ops:
  7.2 11.1 %copy-start.13 = (bf16[96,1536]{1,0:T(8,128)(2,1)S(1)}, bf16[96,1536]{1,0:T(8,128)(2,1)}, u32[]{:S(2)}) copy-start(bf16[96,1536]{1,0:T(8,128)(2,1)} %param.11) | copy-start | bytes 884740
  7.2 11.3 %copy-start.19 = (f32[1536]{0:T(1024)S(1)}, f32[1536]{0:T(1024)}, u32[]{:S(2)}) copy-start(f32[1536]{0:T(1024)} %param.13) | copy-start | bytes 18436
  7.2 11.3 %copy-start.20 = (f32[1536]{0:T(1024)S(1)}, f32[1536]{0:T(1024)}, u32[]{:S(2)}) copy-start(f32[1536]{0:T(1024)} %param.14) | copy-start | bytes 18436
  7.2 11.4 %copy-start.16 = (f32[31,1536]{1,0:T(8,128)S(1)}, f32[31,1536]{1,0:T(8,128)}, u32[]{:S(2)}) copy-start(f32[31,1536]{1,0:T(8,128)} %param.12) | copy-start | bytes 571396
  7.2 101.5 %all-gather.3.cloned.1.call-start = ((), (), s32[]{:S(2)}) async-start(), calls=%async_computation.5 | async-start | bytes 1966080 | tf_op jit(solution)/shard_map/all_gather | solution.py:680
  11.2 60.7 %collective-permute-start.1 = (bf16[3,32,1536]{2,1,0:T(8,128)(2,1)}, bf16[3,32,1536]{2,1,0:T(8,128)(2,1)}, u32[]{:S(2)}, u32[]{:S(2)}) collective-permute-start(bf16[3,32,1536]{2,1,0:T(8,128)(2,1)} %slice_select_fusion), channel_id=1, source_target_pairs={{2,0},{4,2},{6,4},{8,6},{10,8},{12,10},{14,12},{16,14},{18,16},{20... | collective-permute-start | bytes 884744 | tf_op jit(solution)/shard_map/ppermute | solution.py:641
  12.5 59.5 %collective-permute-start = (bf16[3,32,1536]{2,1,0:T(8,128)(2,1)}, bf16[3,32,1536]{2,1,0:T(8,128)(2,1)}, u32[]{:S(2)}, u32[]{:S(2)}) collective-permute-start(bf16[3,32,1536]{2,1,0:T(8,128)(2,1)} %slice_select_fusion), channel_id=1, source_target_pairs={{2,1},{4,3},{6,5},{8,7},{10,9},{12,11},{14,13},{16,15},{18,17},{20... | collective-permute-start | bytes 884744 | tf_op jit(solution)/shard_map/ppermute | solution.py:642
  13.9 75.8 %collective-permute-start.2 = (bf16[3,128,1536]{2,1,0:T(8,128)(2,1)S(1)}, bf16[3,128,1536]{2,1,0:T(8,128)(2,1)}, u32[]{:S(2)}, u32[]{:S(2)}) collective-permute-start(bf16[3,128,1536]{2,1,0:T(8,128)(2,1)S(1)} %constant_dynamic-update-slice_fusion), channel_id=1, source_target_pairs={{0,1},{1,0},{2,3},{3,2},{4,5},{5,4},{6,7},{7,6},{8,9},{9,8},{10,11... | collective-permute-start | bytes 3538952 | tf_op jit(solution)/shard_map/ppermute | solution.py:640
  18.3 5.2 %collective-permute-start.3 = (bf16[48,1536]{1,0:T(8,128)(2,1)S(1)}, bf16[48,1536]{1,0:T(8,128)(2,1)S(1)}, u32[]{:S(2)}, u32[]{:S(2)}) collective-permute-start(bf16[48,1536]{1,0:T(8,128)(2,1)S(1)} %dynamic-slice_bitcast_fusion), channel_id=1, source_target_pairs={{0,1},{1,0},{2,3},{3,2},{4,5},{5,4},{6,7},{7,6},{8,9},{9,8},{10,11... | collective-permute-start | bytes 442376 | tf_op jit(solution)/shard_map/ppermute | solution.py:666
  23.6 6.5 %collective-permute-start.9 = (bf16[32,1536]{1,0:T(8,128)(2,1)S(1)}, bf16[32,1536]{1,0:T(8,128)(2,1)S(1)}, u32[]{:S(2)}, u32[]{:S(2)}) collective-permute-start(bf16[32,1536]{1,0:T(8,128)(2,1)S(1)} %pad_maximum_fusion.3), channel_id=1, source_target_pairs={{0,4},{1,5},{2,6},{3,7},{4,0},{5,1},{6,2},{7,3},{8,12},{9,13},{10,... | collective-permute-start | bytes 294920 | tf_op jit(solution)/shard_map/ppermute | solution.py:654
  26.0 27.5 %collective-permute-start.8 = (bf16[32,1536]{1,0:T(8,128)(2,1)S(1)}, bf16[32,1536]{1,0:T(8,128)(2,1)S(1)}, u32[]{:S(2)}, u32[]{:S(2)}) collective-permute-start(bf16[32,1536]{1,0:T(8,128)(2,1)S(1)} %pad_maximum_fusion.3), channel_id=1, source_target_pairs={{0,2},{1,3},{2,0},{3,1},{4,6},{5,7},{6,4},{7,5},{8,10},{9,11},{10,... | collective-permute-start | bytes 294920 | tf_op jit(solution)/shard_map/ppermute | solution.py:653
  30.1 23.4 %collective-permute-start.10 = (bf16[16,1536]{1,0:T(8,128)(2,1)S(1)}, bf16[16,1536]{1,0:T(8,128)(2,1)S(1)}, u32[]{:S(2)}, u32[]{:S(2)}) collective-permute-start(bf16[16,1536]{1,0:T(8,128)(2,1)S(1)} %slice.96), channel_id=1, source_target_pairs={{0,2},{1,3},{2,0},{3,1},{4,6},{5,7},{6,4},{7,5},{8,10},{9,11},{10,... | collective-permute-start | bytes 147464 | tf_op jit(solution)/shard_map/ppermute | solution.py:658
  53.5 19.7 %copy-start = (bf16[256,1536]{1,0:T(8,128)(2,1)}, bf16[256,1536]{1,0:T(8,128)(2,1)S(1)}, u32[]{:S(2)}) copy-start(bf16[256,1536]{1,0:T(8,128)(2,1)S(1)} %all-gather) | copy-start | bytes 2359300
  53.5 19.6 %collective-permute-start.5 = (bf16[4,64,1536]{2,1,0:T(8,128)(2,1)S(1)}, bf16[4,64,1536]{2,1,0:T(8,128)(2,1)S(1)}, u32[]{:S(2)}, u32[]{:S(2)}) collective-permute-start(bf16[4,64,1536]{2,1,0:T(8,128)(2,1)S(1)} %bitcast.48), channel_id=1, source_target_pairs={{0,4},{1,5},{2,6},{3,7},{4,0},{5,1},{6,2},{7,3},{8,12},{9,13},{10,... | collective-permute-start | bytes 2359304 | tf_op jit(solution)/shard_map/ppermute | solution.py:654
  53.5 16.6 %collective-permute-start.11 = (bf16[16,1536]{1,0:T(8,128)(2,1)S(1)}, bf16[16,1536]{1,0:T(8,128)(2,1)S(1)}, u32[]{:S(2)}, u32[]{:S(2)}) collective-permute-start(bf16[16,1536]{1,0:T(8,128)(2,1)S(1)} %slice.97), channel_id=1, source_target_pairs={{0,4},{1,5},{2,6},{3,7},{4,0},{5,1},{6,2},{7,3},{8,12},{9,13},{10,... | collective-permute-start | bytes 147464 | tf_op jit(solution)/shard_map/ppermute | solution.py:659
  70.1 19.0 %collective-permute-start.4 = (bf16[4,64,1536]{2,1,0:T(8,128)(2,1)S(1)}, bf16[4,64,1536]{2,1,0:T(8,128)(2,1)S(1)}, u32[]{:S(2)}, u32[]{:S(2)}) collective-permute-start(bf16[4,64,1536]{2,1,0:T(8,128)(2,1)S(1)} %bitcast.49), channel_id=1, source_target_pairs={{0,2},{1,3},{2,0},{3,1},{4,6},{5,7},{6,4},{7,5},{8,10},{9,11},{10,... | collective-permute-start | bytes 2359304 | tf_op jit(solution)/shard_map/ppermute | solution.py:653
  73.1 18.1 %copy-start.5 = (bf16[3,32,1536]{2,1,0:T(8,128)(2,1)}, bf16[3,32,1536]{2,1,0:T(8,128)(2,1)S(1)}, u32[]{:S(2)}) copy-start(bf16[3,32,1536]{2,1,0:T(8,128)(2,1)S(1)} %get-tuple-element.65) | copy-start | bytes 884740
  73.1 18.1 %copy-start.7 = (bf16[3,32,1536]{2,1,0:T(8,128)(2,1)}, bf16[3,32,1536]{2,1,0:T(8,128)(2,1)S(1)}, u32[]{:S(2)}) copy-start(bf16[3,32,1536]{2,1,0:T(8,128)(2,1)S(1)} %get-tuple-element.66) | copy-start | bytes 884740
  73.1 18.0 %copy-start.1 = (bf16[4,64,1536]{2,1,0:T(8,128)(2,1)}, bf16[4,64,1536]{2,1,0:T(8,128)(2,1)S(1)}, u32[]{:S(2)}) copy-start(bf16[4,64,1536]{2,1,0:T(8,128)(2,1)S(1)} %collective-permute-done.5.refs_4_.refs_5_) | copy-start | bytes 2359300
  73.1 22.0 %collective-permute-start.6 = (bf16[2,64,1536]{2,1,0:T(8,128)(2,1)S(1)}, bf16[2,64,1536]{2,1,0:T(8,128)(2,1)}, u32[]{:S(2)}, u32[]{:S(2)}) collective-permute-start(bf16[2,64,1536]{2,1,0:T(8,128)(2,1)S(1)} %slice.92), channel_id=1, source_target_pairs={{0,2},{1,3},{2,0},{3,1},{4,6},{5,7},{6,4},{7,5},{8,10},{9,11},{10,... | collective-permute-start | bytes 1179656 | tf_op jit(solution)/shard_map/ppermute | solution.py:658
  89.1 2.0 copy-start.2
  89.1 7.9 %collective-permute-start.7 = (bf16[2,64,1536]{2,1,0:T(8,128)(2,1)S(1)}, bf16[2,64,1536]{2,1,0:T(8,128)(2,1)}, u32[]{:S(2)}, u32[]{:S(2)}) collective-permute-start(bf16[2,64,1536]{2,1,0:T(8,128)(2,1)S(1)} %slice.93), channel_id=1, source_target_pairs={{0,4},{1,5},{2,6},{3,7},{4,0},{5,1},{6,2},{7,3},{8,12},{9,13},{10,... | collective-permute-start | bytes 1179656 | tf_op jit(solution)/shard_map/ppermute | solution.py:659
  91.1 1.0 copy-start.3
  91.1 1.4 copy-start.4
  93.6 15.1 %copy-start.12 = (f32[31,768]{1,0:T(8,128)S(1)}, f32[31,768]{1,0:T(8,128)}, u32[]{:S(2)}) copy-start(f32[31,768]{1,0:T(8,128)} %fusion.12) | copy-start | bytes 285700
  109.6 13.5 %copy-start.6 = (bf16[3,32,1536]{2,1,0:T(8,128)(2,1)S(1)}, bf16[3,32,1536]{2,1,0:T(8,128)(2,1)}, u32[]{:S(2)}) copy-start(bf16[3,32,1536]{2,1,0:T(8,128)(2,1)} %copy-done.5) | copy-start | bytes 884740
  109.6 13.5 %copy-start.8 = (bf16[3,32,1536]{2,1,0:T(8,128)(2,1)S(1)}, bf16[3,32,1536]{2,1,0:T(8,128)(2,1)}, u32[]{:S(2)}) copy-start(bf16[3,32,1536]{2,1,0:T(8,128)(2,1)} %copy-done.7) | copy-start | bytes 884740
  118.6 12.3 %all-to-all-start = ((f32[16,2,768]{2,1,0:T(2,128)}), f32[16,2,768]{2,1,0:T(2,128)}, u32[]{:S(2)}, u32[]{:S(2)}) async-start(f32[16,2,768]{2,1,0:T(2,128)} %get-tuple-element.32), calls=%async_computation | async-start | bytes 196608 | tf_op jit(solution)/shard_map/all_to_all | solution.py:646
  155.5 2.6 %collective-permute-start.12 = (f32[128,1536]{1,0:T(8,128)}, f32[128,1536]{1,0:T(8,128)S(1)}, u32[]{:S(2)}, u32[]{:S(2)}) collective-permute-start(f32[128,1536]{1,0:T(8,128)} %get-tuple-element.41), channel_id=1, source_target_pairs={{0,1},{1,0},{2,3},{3,2},{4,5},{5,4},{6,7},{7,6},{8,9},{9,8},{10,11... | collective-permute-start | bytes 2359304 | tf_op jit(solution)/shard_map/ppermute | solution.py:735
  158.1 0.9 copy-start.9
  162.2 15.4 %collective-permute-start.13 = (f32[128,1536]{1,0:T(8,128)}, f32[128,1536]{1,0:T(8,128)}, u32[]{:S(2)}, u32[]{:S(2)}) collective-permute-start(f32[128,1536]{1,0:T(8,128)} %get-tuple-element.46.mine), channel_id=1, source_target_pairs={{0,1},{1,0},{2,3},{3,2},{4,5},{5,4},{6,7},{7,6},{8,9},{9,8},{10,11... | collective-permute-start | bytes 2359304 | tf_op jit(solution)/shard_map/ppermute | solution.py:640
  162.3 15.2 %collective-permute-start.15 = (f32[32,1536]{1,0:T(8,128)}, f32[32,1536]{1,0:T(8,128)S(1)}, u32[]{:S(2)}, u32[]{:S(2)}) collective-permute-start(f32[32,1536]{1,0:T(8,128)} %get-tuple-element.47), channel_id=1, source_target_pairs={{2,1},{4,3},{6,5},{8,7},{10,9},{12,11},{14,13},{16,15},{18,17},{20... | collective-permute-start | bytes 589832 | tf_op jit(solution)/shard_map/ppermute | solution.py:642
  163.0 14.6 %collective-permute-start.14 = (f32[32,1536]{1,0:T(8,128)}, f32[32,1536]{1,0:T(8,128)S(1)}, u32[]{:S(2)}, u32[]{:S(2)}) collective-permute-start(f32[32,1536]{1,0:T(8,128)} %get-tuple-element.47), channel_id=1, source_target_pairs={{2,0},{4,2},{6,4},{8,6},{10,8},{12,10},{14,12},{16,14},{18,16},{20... | collective-permute-start | bytes 589832 | tf_op jit(solution)/shard_map/ppermute | solution.py:641
  164.3 13.2 %all-to-all-start.2 = ((f32[32,1,128]{2,1,0:T(1,128)}), f32[32,1,128]{2,1,0:T(1,128)S(1)}, u32[]{:S(2)}, u32[]{:S(2)}) async-start(f32[32,1,128]{2,1,0:T(1,128)} %get-tuple-element.42), calls=%async_computation.2 | async-start | bytes 32768 | tf_op jit(solution)/shard_map/all_to_all | solution.py:737
  177.5 0.6 copy-start.17
  177.5 0.7 copy-start.14
  177.5 0.7 copy-start.15
  182.7 15.1 %copy-start.18 = (f32[2,768]{1,0:T(2,128)S(1)}, f32[2,768]{1,0:T(2,128)}, u32[]{:S(2)}) copy-start(f32[2,768]{1,0:T(2,128)} %get-tuple-element.58) | copy-start | bytes 18436
  191.6 13.8 %all-to-all-start.3 = ((f32[16,2,768]{2,1,0:T(2,128)}), f32[16,2,768]{2,1,0:T(2,128)S(1)}, u32[]{:S(2)}, u32[]{:S(2)}) async-start(f32[16,2,768]{2,1,0:T(2,128)} %get-tuple-element.50.stats.local_stats), calls=%async_computation.3 | async-start | bytes 196608 | tf_op jit(solution)/shard_map/all_to_all | solution.py:646
  205.4 0.6 copy-start.11
  212.4 13.4 %all-to-all-start.4 = ((bf16[16,48,128]{2,1,0:T(8,128)(2,1)}), bf16[16,48,128]{2,1,0:T(8,128)(2,1)S(1)}, u32[]{:S(2)}, u32[]{:S(2)}) async-start(bf16[16,48,128]{2,1,0:T(8,128)(2,1)} %get-tuple-element.56), calls=%async_computation.4 | async-start | bytes 393216 | tf_op jit(solution)/shard_map/all_to_all | solution.py:646
  225.8 0.7 copy-start.10
Sparse Core Ops, SparseCore 0:
  72.1 36.6 all-gather.2

commit v2 on v1

--- a/solution.py
+++ b/solution.py
@@ -84,51 +84,49 @@
     return jnp.sum(jnp.concatenate(totals, axis=0), axis=1)
 
 
-def place_weights(scal, weights, low, high, steps_a, value_w, gate_w):
-    own_v, own_g, x_v, x_g, y_v, y_g, d_v, d_g = weights
-    step, spot = pl.program_id(0), scal[4]
-    rows = own_v.shape[1]
-
-    @pl.when(step < steps_a)
-    def _():
-        for other, (v, g) in enumerate(((own_v, own_g), (x_v, x_g), (y_v, y_g), (d_v, d_g))):
-            at = pl.ds(pl.multiple_of((spot ^ other) * rows, rows), rows)
-            value_w[at, :] = v[0]
-            gate_w[at, :] = g[0]
-
-    @pl.when(step >= steps_a)
-    def _():
-        value_w[...] = low[...]
-        gate_w[...] = high[...]
-
-
-def weight_specs(wide_parts, square):
-    own, _, _, d_low, _ = wide_parts
-    depth, rows, width = own.shape
-    half = depth // 2
-    chunk = 4 * rows
-    steps_b = square.shape[0] // 2 // chunk
-    low = lambda i: (jnp.minimum(i, half - 1), 0, 0)
-    high = lambda i: (jnp.minimum(i, half - 1) + half, 0, 0)
-    block = (1, rows, width)
-    specs = []
-    for _ in range(3):
-        specs += [pl.BlockSpec(block, low), pl.BlockSpec(block, high)]
-    specs += [pl.BlockSpec(block, low), pl.BlockSpec(block, low)]
-    specs += [
-        pl.BlockSpec((chunk, width), lambda i: (jnp.maximum(i - half, 0), 0)),
-        pl.BlockSpec((chunk, width), lambda i: (jnp.maximum(i - half, 0) + steps_b, 0)),
-    ]
-    own, x, y, d_low, d_high = wide_parts
-    operands = [own, own, x, x, y, y, d_low, d_high, square, square]
-    scratch = [pltpu.VMEM((chunk, width), BF16)] * 2
-    return chunk, half, half + steps_b, specs, operands, scratch
-
-
-def forward_kernel(steps_a, keep, scal, nb, *refs):
-    weights, (low, high, taps), refs = refs[:8], refs[8:11], refs[11:]
-    kept, (glu, conv, stats, value_w, gate_w, plain, shifted) = refs[: 2 * keep], refs[2 * keep :]
-    place_weights(scal, weights, low, high, steps_a, value_w, gate_w)
+def place_kernel(depth, scal, *refs):
+    blocks, out, sems = refs[:-2], refs[-2], refs[-1]
+    spot, layer = scal[4], scal[5]
+    copies = []
+    for number, (shift, other, first, ref) in enumerate(blocks_of(blocks, depth)):
+        layer_of = lax.rem(layer - shift + depth, depth)
+        chip = layer_of * 4 + (spot ^ other)
+        size = blocks[0].shape[0]
+        row = pl.multiple_of(chip * size + first, 16)
+        copies.append(
+            pltpu.make_async_copy(ref, out.at[pl.ds(row, ref.shape[0]), :], sems.at[number])
+        )
+    for copy in copies:
+        copy.start()
+    for copy in copies:
+        copy.wait()
+
+
+def blocks_of(refs, depth):
+    cut = refs[3].shape[0]
+    for shift in range(depth):
+        group = refs[5 * shift : 5 * shift + 5]
+        for other, first, ref in zip((0, 1, 2, 3, 3), (0, 0, 0, 0, cut), group):
+            yield shift, other, first, ref
+
+
+def place(scal, pieces, depth):
+    rows, width = pieces[0].shape
+    hbm = pl.BlockSpec(memory_space=pl.ANY)
+    return pl.pallas_call(
+        functools.partial(place_kernel, depth),
+        in_specs=[pl.BlockSpec(memory_space=pltpu.SMEM)] + [hbm] * len(pieces),
+        out_specs=hbm,
+        out_shape=jax.ShapeDtypeStruct((4 * depth * rows, width), BF16),
+        scratch_shapes=[pltpu.SemaphoreType.DMA((len(pieces),))],
+        compiler_params=params(),
+        cost_estimate=cost(0, 16 * depth * rows * width),
+        name="place_weights",
+    )(scal, *pieces)
+
+
+def forward_kernel(keep, scal, nb, value_w, gate_w, taps, *refs):
+    kept, (glu, conv, stats, plain, shifted) = refs[: 2 * keep], refs[2 * keep :]
     start, end = scal[0], scal[1]
     span, taps_n = nb.shape[0], taps.shape[0]
     rows = conv.shape[0] - 2 * EDGE
@@ -152,18 +150,20 @@
         stats[peer] = both
 
 
-def forward(scal, nb, wide_parts, square, taps, rows, peers, keep):
+def forward(scal, nb, weight, taps, rows, peers, keep):
     span, width = nb.shape
     taps_n, _, half_width = taps.shape
-    chunk, steps_a, steps, specs, operands, scratch = weight_specs(wide_parts, square)
+    chunk = 256 if half_width % 256 == 0 else 128
+    steps = half_width // chunk
     col = lambda n: pl.BlockSpec((n, chunk), lambda i: (0, i))
     return pl.pallas_call(
-        functools.partial(forward_kernel, steps_a, keep),
+        functools.partial(forward_kernel, keep),
         grid=(steps,),
         in_specs=[
             pl.BlockSpec(memory_space=pltpu.SMEM),
             pl.BlockSpec((span, width), lambda i: (0, 0)),
-            *specs,
+            pl.BlockSpec((chunk, width), lambda i: (i, 0)),
+            pl.BlockSpec((chunk, width), lambda i: (i + steps, 0)),
             pl.BlockSpec((taps_n, 8, chunk), lambda i: (0, 0, i)),
         ],
         out_specs=[
@@ -179,14 +179,13 @@
             jax.ShapeDtypeStruct((peers, 2, half_width), F32),
         ],
         scratch_shapes=[
-            *scratch,
             pltpu.VMEM((span, chunk), F32),
             pltpu.VMEM((8, span // 8 - 1, 8, chunk), F32),
         ],
         compiler_params=params(),
         cost_estimate=cost(2 * span * width * 2 * half_width, 4 * half_width * width + 10 * span * half_width),
         name="project_glu_conv",
-    )(scal, nb, *operands, taps)
+    )(scal, nb, weight, weight, taps)
 
 
 def moments(counts, stats, live_count):
@@ -262,10 +261,7 @@
     )(scal, counts, stats, conv, cot, gain, shift)
 
 
-def backward_kernel(steps_a, scal, sums, scaled, grad, inv, gain, taps, value, gate, *refs):
-    weights, (low, high), refs = refs[:8], refs[8:10], refs[10:]
-    mine, other, grad_conv, totals, value_w, gate_w, plain, shifted, part = refs
-    place_weights(scal, weights, low, high, steps_a, value_w, gate_w)
+def backward_kernel(scal, sums, scaled, grad, inv, gain, taps, value, gate, value_w, gate_w, mine, other, grad_conv, totals, plain, shifted, part):
     start, end, core = scal[0], scal[1], scal[2]
     rows, taps_n = value.shape[0], taps.shape[0]
     half = (taps_n - 1) // 2
@@ -307,15 +303,16 @@
         other[...] = part[pl.ds(pl.multiple_of((1 - core) * count, count), count), :]
 
 
-def backward(scal, sums, scaled, grad, inv, gain, taps, value, gate, wide_parts, square):
+def backward(scal, sums, scaled, grad, inv, gain, taps, value, gate, weight):
     span, half_width = scaled.shape
-    rows, width = value.shape[0], square.shape[1]
-    chunk, steps_a, steps, specs, operands, scratch = weight_specs(wide_parts, square)
+    rows, width = value.shape[0], weight.shape[1]
+    chunk = 256 if half_width % 256 == 0 else 128
+    steps = half_width // chunk
     taps_n = taps.shape[0]
     col = lambda n: pl.BlockSpec((n, chunk), lambda i: (0, i))
     own = pl.BlockSpec((rows // 2, width), lambda i: (0, 0))
     return pl.pallas_call(
-        functools.partial(backward_kernel, steps_a),
+        backward_kernel,
         grid=(steps,),
         in_specs=[
             pl.BlockSpec(memory_space=pltpu.SMEM),
@@ -327,7 +324,8 @@
             pl.BlockSpec((taps_n, 8, chunk), lambda i: (0, 0, i)),
             col(rows),
             col(rows),
-            *specs,
+            pl.BlockSpec((chunk, width), lambda i: (i, 0)),
+            pl.BlockSpec((chunk, width), lambda i: (i + steps, 0)),
         ],
         out_specs=[own, own, col(rows), col(2)],
         out_shape=[
@@ -337,7 +335,6 @@
             jax.ShapeDtypeStruct((2, half_width), F32),
         ],
         scratch_shapes=[
-            *scratch,
             pltpu.VMEM((span, chunk), F32),
             pltpu.VMEM((8, span // 8 - 1, 8, chunk), F32),
             pltpu.VMEM((rows, width), F32),
@@ -345,7 +342,7 @@
         compiler_params=params(),
         cost_estimate=cost(2 * rows * width * 2 * half_width, 4 * half_width * width + 20 * span * half_width),
         name="grad_conv_project_back",
-    )(scal, sums, scaled, grad, inv, gain, taps, value, gate, *operands)
+    )(scal, sums, scaled, grad, inv, gain, taps, value, gate, weight, weight)
 
 
 def shifted_scratch(span):
@@ -418,7 +415,7 @@
     return high, array - high
 
 
-def last_kernel(taps_n, part_a, scal, counts, stats, conv, cot, gain, shift, glu, alone, crossed, local_stats, taps_before, out, factor_out, plain, shifted, pay):
+def last_kernel(taps_n, scal, counts, stats, conv, cot, gain, shift, glu, alone, crossed, local_stats, taps_before, out, factor_out, plain, shifted, pay):
     step = pl.program_id(0)
     scaled, grad, live, mean, inv = swish_grads(scal, counts, stats, conv, cot, gain, shift)
     rows = conv.shape[0] - 2 * EDGE
@@ -443,16 +440,12 @@
     @pl.when(step == pl.num_programs(0) - 1)
     def _():
         turned = jnp.concatenate([jnp.transpose(pay[s]) for s in range(pay.shape[0])], axis=0)
-        peers, block = out.shape[0], out.shape[1]
-        part_b = block - part_a
-        for index in range(peers):
-            low, high = index * part_a, peers * part_a + index * part_b
-            out[index] = jnp.concatenate(
-                [turned[low : low + part_a], turned[high : high + part_b]], axis=0
-            ).astype(BF16)
-
-
-def last(taps_n, part_a, peers, scal, counts, stats, conv, cot, gain, shift, glu, alone, crossed, local_stats, taps_before):
+        block = out.shape[1]
+        for index in range(out.shape[0]):
+            out[index] = turned[index * block : (index + 1) * block].astype(BF16)
+
+
+def last(taps_n, peers, scal, counts, stats, conv, cot, gain, shift, glu, alone, crossed, local_stats, taps_before):
     span, half_width = conv.shape
     chunk = 128
     steps = half_width // chunk
@@ -460,7 +453,7 @@
     col = lambda n: pl.BlockSpec((n, chunk), lambda i: (0, i))
     smem = pl.BlockSpec(memory_space=pltpu.SMEM)
     return pl.pallas_call(
-        functools.partial(last_kernel, taps_n, part_a),
+        functools.partial(last_kernel, taps_n),
         grid=(steps,),
         in_specs=[
             smem,
@@ -616,14 +609,15 @@
     chip_rows = 2 * rows
     half_width = width // 2
     end = lax.dynamic_index_in_dim(ends, group, 0, keepdims=False)
-    scal = jnp.stack([chip * chip_rows, end, core, jnp.sum(ends), chip % 4]).astype(jnp.int32)
+    scal = jnp.stack([chip * chip_rows, end, core, jnp.sum(ends), chip % 4, chip // 4]).astype(jnp.int32)
     held = jnp.clip(
         ends[:, None] - chip_rows * jnp.arange(chips, dtype=jnp.int32)[None, :], 0, chip_rows
     ).reshape(-1).astype(F32)
     counts = jnp.stack([held, jnp.where(held > 0, 1.0 / jnp.maximum(held, 1.0), 0.0)])
 
     cores = [[2 * c + k for c in range(chips)] for k in range(2)]
-    columns = [[8 * z + k for z in range(shards // 8)] for k in range(8)]
+    depth = chips // 4
+    onward = [(i, (i + 8) % shards) for i in range(shards)]
     swap = [(i, i ^ 1) for i in range(shards)]
     swap_x = [(i, i ^ 2) for i in range(shards)]
     swap_y = [(i, i ^ 4) for i in range(shards)]
@@ -648,39 +642,29 @@
             array = lax.all_gather(array, "dp", axis=0, tiled=True)
         return array
 
-    def around(array):
-        half = array.shape[0] // 2
-        from_x = lax.ppermute(array, "tm", swap_x)
-        from_y = lax.ppermute(array, "tm", swap_y)
-        return (
-            from_x,
-            from_y,
-            lax.ppermute(from_y[:half], "tm", swap_x),
-            lax.ppermute(from_x[half:], "tm", swap_y),
-        )
-
     slice_width = width // shards
-    part_a = 2 * slice_width // 3
     pair = in_weight.reshape(2, slice_width, width)
     kept = lax.dynamic_index_in_dim(pair, core, 0, keepdims=False)
     given = lax.ppermute(lax.dynamic_index_in_dim(pair, 1 - core, 0, keepdims=False), "tm", swap)
-    one, two = jnp.where(first, kept, given), jnp.where(first, given, kept)
-    weight_a = jnp.concatenate([one[:part_a], two[:part_a]], axis=0)
-    weight_b = jnp.concatenate([one[part_a:], two[part_a:]], axis=0)
-    column = lax.all_gather(weight_a, "tm", axis=0, axis_index_groups=columns, tiled=False)
-    x_b, y_b, d_low, d_high = around(weight_b)
-    four = (weight_b, x_b, y_b, jnp.concatenate([d_low, d_high], axis=0))
-    spot = chip % 4
-    square = jnp.stack(
-        [
-            jnp.where(spot == s, four[0], jnp.where(spot == s ^ 1, four[1], jnp.where(spot == s ^ 2, four[2], four[3])))
-            for s in range(4)
+    block = jnp.concatenate([jnp.where(first, kept, given), jnp.where(first, given, kept)], axis=0)
+    cut = (slice_width + 15) // 16 * 16
+    pieces = []
+    for shift in range(depth):
+        if shift:
+            block = lax.ppermute(block, "tm", onward)
+        from_x = lax.ppermute(block, "tm", swap_x)
+        from_y = lax.ppermute(block, "tm", swap_y)
+        pieces += [
+            block,
+            from_x,
+            from_y,
+            lax.ppermute(from_y[:cut], "tm", swap_x),
+            lax.ppermute(from_x[cut:], "tm", swap_y),
         ]
-    ).reshape(-1, width)
-    square = lax.all_gather(square, "tm", axis=0, axis_index_groups=columns, tiled=True)
-    wide_parts = (column, *around(column))
+    weight = place(scal, pieces, depth)
 
     packed = jnp.concatenate([features, start_noise, cotangent], axis=0)
+    packed, _ = lax.optimization_barrier((packed, given))
     partner, near, far = across(
         packed, jnp.where(first, packed[:, :HALO], packed[:, rows - HALO :])
     )
@@ -695,26 +679,14 @@
     )
     wide_features, wide_noise, wide_cot = whole[0], whole[1], whole[2]
 
-    place = jnp.arange(half_width, dtype=jnp.int32)
-    part_b = slice_width - part_a
-    in_a = place < chips * part_a
-    rest = place - chips * part_a
-    at = jnp.where(in_a, place // part_a, rest // part_b)
-    within = jnp.where(in_a, place % part_a, part_a + rest % part_b)
-    source = (2 * at + core) * slice_width + within
+    place_of = jnp.arange(half_width, dtype=jnp.int32)
+    source = (2 * (place_of // slice_width) + core) * slice_width + place_of % slice_width
     chosen = (jnp.arange(width, dtype=jnp.int32)[:, None] == source[None, :]).astype(BF16)
     cot = jnp.dot(wide_cot[HALO - EDGE : -(HALO - EDGE)], chosen, preferred_element_type=F32).astype(BF16)
 
     def mine_of(array):
         parts = array.reshape(array.shape[0], chips, 2, slice_width)
-        own = lax.dynamic_index_in_dim(parts, core, 2, keepdims=False)
-        return jnp.concatenate(
-            [
-                own[..., :part_a].reshape(array.shape[0], -1),
-                own[..., part_a:].reshape(array.shape[0], -1),
-            ],
-            axis=1,
-        )
+        return lax.dynamic_index_in_dim(parts, core, 2, keepdims=False).reshape(-1, half_width)
 
     channel = mine_of(jnp.concatenate([kernel, bn_gain[None], bn_shift[None]], axis=0))
     gain, shift = channel[taps_n : taps_n + 1], channel[taps_n + 1 :]
@@ -726,11 +698,11 @@
     normed_b = normalize(summed)[0].astype(BF16)
 
     value, gate, glu, conv, stats = forward(
-        scal, normed_b, wide_parts, square, taps, chip_rows, chips, True
+        scal, normed_b, weight, taps, chip_rows, chips, True
     )
     scaled, grad, inv, sums = batch(scal, counts, peers_of(stats), conv, cot, gain, shift, chips)
     mine, other, grad_conv, totals = backward(
-        scal, peers_of(sums), scaled, grad, inv, gain, taps, value, gate, wide_parts, square
+        scal, peers_of(sums), scaled, grad, inv, gain, taps, value, gate, weight
     )
     other = lax.ppermute(other, "tm", swap)
     moved, edge, squares = direction(scal, mine, other, features[0], start_noise[0], shards)
@@ -742,20 +714,14 @@
         scal, squares, wide_features, wide_noise, moved, partner, near, far, start_noise[0]
     )
 
-    glu, conv, stats = forward(scal, normed_b, wide_parts, square, taps, chip_rows, chips, False)
+    glu, conv, stats = forward(scal, normed_b, weight, taps, chip_rows, chips, False)
     alone, crossed = raw_taps(taps_n, scal, conv, glu, stats)
     outgoing, factor = last(
-        taps_n, part_a, chips, scal, counts, peers_of(stats), conv, cot, gain, shift, glu, alone, crossed, stats, taps_before
+        taps_n, chips, scal, counts, peers_of(stats), conv, cot, gain, shift, glu, alone, crossed, stats, taps_before
     )
     received = peers_of(outgoing)
     known = jnp.concatenate([factor, totals], axis=0)
-    known = jnp.concatenate(
-        [
-            lax.dynamic_slice_in_dim(known[:, : chips * part_a], chip * part_a, part_a, 1),
-            lax.dynamic_slice_in_dim(known[:, chips * part_a :], chip * part_b, part_b, 1),
-        ],
-        axis=1,
-    )
+    known = lax.dynamic_slice_in_dim(known, chip * slice_width, slice_width, 1)
     kernel_total, norm_total = finish(taps_n, scal, received, known)
     return (perturbation[None], kernel_total, norm_total)
 

time: 236 us -> 334 us (1.42)
  Pallas kernels: 56.8 us -> 199 us
  blocking collectives: 31.4 us -> 11.8 us
  between operations: 15.2 us -> 2 us
  waiting for transfers between devices: 60.4 us -> 47.6 us
  other arithmetic: 10.8 us -> 5.4 us
  starting transfers between devices: 44.9 us -> 49.3 us
    pallas_call x4 -> x5, Pallas kernels: 33.1 us -> 175 us  [the longest x1 145 us: place(): pl.pallas_call(functools.partial(place_kernel, depth), in_specs=[pl.Block...]
    all_gather x1 -> x0, blocking collectives: 19.6 us -> none  [on_device(): lax.all_gather(weight_a, 'tm', axis=0, axis_index_groups=columns, tiled=F...]
    all_gather x1 -> x0, waiting for transfers between devices: 11.7 us -> none  [on_device(): lax.all_gather(square, 'tm', axis=0, axis_index_groups=columns, tiled=True)]
    ppermute x8 -> x19, starting transfers between devices: 13.8 us -> 22.8 us  [the longest x3 7.12 us: on_device(): block = lax.ppermute(block, 'tm', onward)]
    ppermute x2, starting transfers between devices: 4.56 us -> 0.14 us  [across(): lax.ppermute(array, 'tm', swap)]
    ppermute x8 -> x19, waiting for transfers between devices: 32.4 us -> 28.6 us  [the longest x3 12.7 us: on_device(): block = lax.ppermute(block, 'tm', onward)]
  transfers between devices with their start and end apart: 21 -> 31, of which waited for: 10 -> 18; matrix products, arithmetic and copies ran while one was open for 7% -> 5% of each run, Pallas kernels for 4% -> 3%
where the time goes in v2:
time: 334 us; the launch traced here: 332 us
  Pallas kernels  199 us (60%)
  starting transfers between devices  49.3 us (15%)
  waiting for transfers between devices  47.6 us (14%)
  local copies, waits for them, and re-layouts  14.4 us (4%)
  blocking collectives  11.8 us (4%)
  other arithmetic  5.4 us (2%)
    pallas_call x1, Pallas kernels, place(): pl.pallas_call(functools.partial(place_kernel, depth), in_specs=[pl.Block...  145 us
    all_to_all x3, starting transfers between devices, peers_of(): lax.all_to_all(array, 'tm', 0, 0, axis_index_groups=cores, tiled=True)  15.7 us
    pallas_call x2, Pallas kernels, forward(): pl.pallas_call(functools.partial(forward_kernel, keep), grid=(steps,), in...  15.5 us
    all_to_all x3, waiting for transfers between devices, peers_of(): lax.all_to_all(array, 'tm', 0, 0, axis_index_groups=cores, tiled=True)  13.9 us
    ppermute x3, waiting for transfers between devices, on_device(): block = lax.ppermute(block, 'tm', onward)  12.7 us
    all_to_all x1, blocking collectives, peers_of(): lax.all_to_all(array, 'tm', 0, 0, axis_index_groups=cores, tiled=True)  11.8 us
    pallas_call x1, Pallas kernels, backward(): pl.pallas_call(backward_kernel, grid=(steps,), in_specs=[pl.BlockSpec(mem...  8.24 us
    ppermute x3, starting transfers between devices, on_device(): block = lax.ppermute(block, 'tm', onward)  7.12 us
  transfers between devices with their start and end apart: 31, of which 18 were waited for; matrix products, arithmetic and copies ran while one was open for 5% of the time, Pallas kernels for 3%

profile of v2, /device:TPU:0, one launch (start us, length us, event | category | flops | bytes accessed | tf_op | source)
XLA Modules:
  0.0 332.3 jit_solution(3863773300166331977)
XLA Ops:
  4.5 1.8 concatenate.25
  9.5 2.6 collective-permute-start.8
  12.1 1.5 collective-permute-start.5
  13.6 1.5 collective-permute-start.4
  15.2 1.3 collective-permute-start.2
  16.5 5.4 %collective-permute-done.8.refs_5_ = bf16[96,1536]{1,0:T(8,128)(2,1)S(1)} collective-permute-done((bf16[96,1536]{1,0:T(8,128)(2,1)S(1)}, bf16[96,1536]{1,0:T(8,128)(2,1)S(1)}, u32[]{:S(2)}, u32[]{:S(2)}) %collective-permute-start.8) | collective-permute-done | bytes 294944 | tf_op jit(solution)/shard_map/ppermute | solution.py:654
  22.6 4.5 %collective-permute-start.13 = (bf16[96,1536]{1,0:T(8,128)(2,1)S(1)}, bf16[96,1536]{1,0:T(8,128)(2,1)S(1)}, u32[]{:S(2)}, u32[]{:S(2)}) collective-permute-start(bf16[96,1536]{1,0:T(8,128)(2,1)S(1)} %collective-permute-done.8.refs_5_), channel_id=1, source_target_pairs={{0,8},{1,9},{2,10},{3,11},{4,12},{5,13},{6,14},{7,15},{8,16},{9,17... | collective-permute-start | bytes 884744 | tf_op jit(solution)/shard_map/ppermute | solution.py:654
  27.8 2.1 collective-permute-done.2
  29.8 1.4 collective-permute-start.9
  31.3 6.9 %collective-permute-done.13.refs_10_ = bf16[96,1536]{1,0:T(8,128)(2,1)S(1)} collective-permute-done((bf16[96,1536]{1,0:T(8,128)(2,1)S(1)}, bf16[96,1536]{1,0:T(8,128)(2,1)S(1)}, u32[]{:S(2)}, u32[]{:S(2)}) %collective-permute-start.13) | collective-permute-done | bytes 294944 | tf_op jit(solution)/shard_map/ppermute | solution.py:654
  38.2 1.6 collective-permute-start.14
  40.0 2.5 collective-permute-done.9.refs_6_
  42.5 2.7 collective-permute-done.15.refs_12_
  45.2 1.3 collective-permute-start.7
  47.7 1.1 collective-permute-done.14.refs_11_
  49.0 1.9 collective-permute-start.19
  53.6 3.1 collective-permute-done.20.refs_17_
  56.7 1.2 collective-permute-start.12
  57.9 2.5 collective-permute-done.19.refs_16_
  60.4 1.5 collective-permute-start.16
  62.6 1.9 collective-permute-start.22
  64.6 1.5 multiply_convert_fusion.nb
  67.1 1.5 collective-permute-done.17.refs_14_
  68.7 1.5 collective-permute-done.22.refs_19_
  70.8 144.9 %place_weights.1.value_w.gate_w = bf16[1536,1536]{1,0:T(8,128)(2,1)} custom-call(s32[6]{0:T(128)} %stack.26.scal, bf16[96,1536]{1,0:T(8,128)(2,1)} %copy-done.4, bf16[96,1536]{1,0:T(8,128)(2,1)} %copy-done.8, bf16[96,1536]{1,0:T(8,128)(2,1)} %copy-done.7, bf16[48,1536]{1,0:T(8,128)(2,1)} %copy-done.24, bf16[48,1536]{1,0:T(8,128)(2,1)} %copy-done.25, ...), custom_call_target="tpu_custom_call" | custom-call | bytes 9437184 | tf_op jit(solution)/shard_map/place_weights/pallas_call | solution.py:116
  216.7 7.8 %project_glu_conv.2 = (f32[256,768]{1,0:T(8,128)}, f32[256,768]{1,0:T(8,128)}, bf16[320,768]{1,0:T(8,128)(2,1)}, f32[288,768]{1,0:T(8,128)}, f32[16,2,768]{2,1,0:T(2,128)}) custom-call(s32[6]{0:T(128)} %stack.26.scal, bf16[320,1536]{1,0:T(8,128)(2,1)} %multiply_convert_fusion.nb, bf16[1536,1536]{1,0:T(8,128)(2,1)} %place_weights.1.value_w.gate_w, ...), custom_call_target="tpu_custom_call" | custom-call | flops 1509949440 | bytes 7176192 | tf_op jit(solution)/shard_map/project_glu_conv/pallas_call | solution.py:159
  224.5 4.6 %all-to-all-start = ((f32[16,2,768]{2,1,0:T(2,128)}), f32[16,2,768]{2,1,0:T(2,128)}, u32[]{:S(2)}, u32[]{:S(2)}) async-start(f32[16,2,768]{2,1,0:T(2,128)} %get-tuple-element.34), calls=%async_computation | async-start | bytes 196608 | tf_op jit(solution)/shard_map/all_to_all | solution.py:640
  229.1 3.0 fusion.3.cot
  232.1 4.7 %all-to-all-done.stats = f32[16,2,768]{2,1,0:T(2,128)} async-done(((f32[16,2,768]{2,1,0:T(2,128)}), f32[16,2,768]{2,1,0:T(2,128)}, u32[]{:S(2)}, u32[]{:S(2)}) %all-to-all-start) | async-done | bytes 98336 | tf_op jit(solution)/shard_map/all_to_all | solution.py:640
  236.8 3.9 %batch_norm_swish.1 = (f32[288,768]{1,0:T(8,128)}, f32[288,768]{1,0:T(8,128)}, f32[1,768]{1,0:T(1,128)}, f32[16,2,768]{2,1,0:T(2,128)}) custom-call(s32[6]{0:T(128)} %stack.26.scal, f32[2,16]{1,0:T(2,128)} %pad_maximum_fusion.3.counts, f32[16,2,768]{2,1,0:T(2,128)} %all-to-all-done.stats, f32[288,768]{1,0:T(8,128)} %get-tuple-element.35.conv, ...), custom_call_target="tpu_custom_call" | custom-call | flops 8847360 | bytes 3538944 | tf_op jit(solution)/shard_map/batch_norm_swish/pallas_call | solution.py:239
  240.7 11.8 %all_to_all.25.sums = f32[16,2,768]{2,1,0:T(2,128)} all-to-all(f32[16,2,768]{2,1,0:T(2,128)} %get-tuple-element.36), channel_id=1, replica_groups={{0,2,4,6,8,10,12,14,16,18,20,22,24,26,28,30},{1,3,5,7,9,11,13,15,17,19,..., dimensions={0} | all-to-all | bytes 196608 | tf_op jit(solution)/shard_map/all_to_all | solution.py:640
  252.5 8.2 %grad_conv_project_back.1 = (f32[128,1536]{1,0:T(8,128)}, f32[128,1536]{1,0:T(8,128)}, bf16[256,768]{1,0:T(8,128)(2,1)}, f32[2,768]{1,0:T(2,128)}) custom-call(s32[6]{0:T(128)} %stack.26.scal, f32[16,2,768]{2,1,0:T(2,128)} %all_to_all.25.sums, f32[288,768]{1,0:T(8,128)} %get-tuple-element.37.scaled, f32[288,768]{1,0:T(8,128)} %get-tuple-element.38.grad, ...), custom_call_target="tpu_custom_call" | custom-call | flops 1207959552 | bytes 9142272 | tf_op jit(solution)/shard_map/grad_conv_project_back/pallas_call | solution.py:314
  260.9 2.5 collective-permute-done.23.other
  264.2 3.2 direction.1
  268.3 1.3 collective-permute-start.25
  269.6 6.2 %all-to-all-start.2 = ((f32[32,1,128]{2,1,0:T(1,128)}), f32[32,1,128]{2,1,0:T(1,128)S(1)}, u32[]{:S(2)}, u32[]{:S(2)}) async-start(f32[32,1,128]{2,1,0:T(1,128)} %get-tuple-element.44), calls=%async_computation.2 | async-start | bytes 32768 | tf_op jit(solution)/shard_map/all_to_all | solution.py:709
  275.7 1.5 slice_bitcast_fusion
  277.2 4.9 %tap_grad.1.taps_before = f32[31,768]{1,0:T(8,128)} custom-call(bf16[256,768]{1,0:T(8,128)(2,1)} %get-tuple-element.45.grad_conv, bf16[320,768]{1,0:T(8,128)(2,1)} %get-tuple-element.46.glu), custom_call_target="tpu_custom_call" | custom-call | flops 12189696 | bytes 983040 | tf_op jit(solution)/shard_map/tap_grad/pallas_call | solution.py:362
  283.6 4.4 %ascend.1 = (f32[128,1536]{1,0:T(8,128)}, bf16[320,1536]{1,0:T(8,128)(2,1)}) custom-call(s32[6]{0:T(128)} %stack.26.scal, f32[32,1,128]{2,1,0:T(1,128)} %copy-done.32, bf16[320,1536]{1,0:T(8,128)(2,1)} %get-tuple-element.64.features, bf16[320,1536]{1,0:T(8,128)(2,1)} %get-tuple-element.63.noise, f32[128,1536]{1,0:T(8,128)} %get-tuple-element.48.mine, ...), custom_call_target="tpu_custom_call" | custom-call | flops 14745600 | bytes 3932160 | tf_op jit(solution)/shard_map/ascend/pallas_call | solution.py:588
  288.0 7.7 %project_glu_conv.3 = (bf16[320,768]{1,0:T(8,128)(2,1)}, f32[288,768]{1,0:T(8,128)}, f32[16,2,768]{2,1,0:T(2,128)}) custom-call(s32[6]{0:T(128)} %stack.26.scal, bf16[320,1536]{1,0:T(8,128)(2,1)} %get-tuple-element.51.nb, bf16[1536,1536]{1,0:T(8,128)(2,1)} %place_weights.1.value_w.gate_w, bf16[1536,1536]{1,0:T(8,128)(2,1)} %place_weights.1.value_w.gate_w, ...), custom_call_target="tpu_custom_call" | custom-call | flops 1509949440 | bytes 7176192 | tf_op jit(solution)/shard_map/project_glu_conv/pallas_call | solution.py:159
  295.6 6.2 %all-to-all-start.3 = ((f32[16,2,768]{2,1,0:T(2,128)}), f32[16,2,768]{2,1,0:T(2,128)S(1)}, u32[]{:S(2)}, u32[]{:S(2)}) async-start(f32[16,2,768]{2,1,0:T(2,128)} %get-tuple-element.52.stats.local_stats), calls=%async_computation.3 | async-start | bytes 196608 | tf_op jit(solution)/shard_map/all_to_all | solution.py:640
  301.9 5.7 %raw_taps.1 = (f32[31,768]{1,0:T(8,128)}, f32[31,768]{1,0:T(8,128)}) custom-call(s32[6]{0:T(128)} %stack.26.scal, f32[288,768]{1,0:T(8,128)} %get-tuple-element.53.conv, bf16[320,768]{1,0:T(8,128)(2,1)} %get-tuple-element.54.glu, f32[16,2,768]{2,1,0:T(2,128)} %get-tuple-element.52.stats.local_stats), custom_call_target="tpu_custom_call" | custom-call | flops 13713408 | bytes 1966080 | tf_op jit(solution)/shard_map/raw_taps/pallas_call | solution.py:395
  307.5 2.0 all-to-all-done.3.stats
  310.2 6.3 %batch_norm_swish_taps.1 = (bf16[16,48,128]{2,1,0:T(8,128)(2,1)}, f32[1,768]{1,0:T(1,128)}) custom-call(s32[6]{0:T(128)} %stack.26.scal, f32[2,16]{1,0:T(2,128)} %pad_maximum_fusion.3.counts, f32[16,2,768]{2,1,0:T(2,128)} %copy-done.15, f32[288,768]{1,0:T(8,128)} %get-tuple-element.53.conv, bf16[288,768]{1,0:T(8,128)(2,1)} %fusion.3.cot, ...), custom_call_target="tpu_custom_call" | custom-call | flops 22118400 | bytes 2211840 | tf_op jit(solution)/shard_map/batch_norm_swish_taps/pallas_call | solution.py:455
  316.5 4.9 %all-to-all-start.4 = ((bf16[16,48,128]{2,1,0:T(8,128)(2,1)}), bf16[16,48,128]{2,1,0:T(8,128)(2,1)S(1)}, u32[]{:S(2)}, u32[]{:S(2)}) async-start(bf16[16,48,128]{2,1,0:T(8,128)(2,1)} %get-tuple-element.58), calls=%async_computation.4 | async-start | bytes 393216 | tf_op jit(solution)/shard_map/all_to_all | solution.py:640
  321.5 1.3 fusion.23.known
  322.8 7.1 %all-to-all-done.4.received = bf16[16,48,128]{2,1,0:T(8,128)(2,1)S(1)} async-done(((bf16[16,48,128]{2,1,0:T(8,128)(2,1)}), bf16[16,48,128]{2,1,0:T(8,128)(2,1)S(1)}, u32[]{:S(2)}, u32[]{:S(2)}) %all-to-all-start.4) | async-done | bytes 196640 | tf_op jit(solution)/shard_map/all_to_all | solution.py:640
  330.6 1.7 finish.1
  (137 shorter events, 19.7 us)
Async XLA Ops:
  0.6 5.7 %copy-start.2 = (bf16[1,128,1536]{2,1,0:T(8,128)(2,1)S(1)}, bf16[1,128,1536]{2,1,0:T(8,128)(2,1)}, u32[]{:S(2)}) copy-start(bf16[1,128,1536]{2,1,0:T(8,128)(2,1)} %param.9) | copy-start | bytes 1179652
  0.6 5.7 %copy-start.3 = (bf16[1,128,1536]{2,1,0:T(8,128)(2,1)S(1)}, bf16[1,128,1536]{2,1,0:T(8,128)(2,1)}, u32[]{:S(2)}) copy-start(bf16[1,128,1536]{2,1,0:T(8,128)(2,1)} %param.8) | copy-start | bytes 1179652
  1.7 7.7 %collective-permute-start = (bf16[48,1536]{1,0:T(8,128)(2,1)S(1)}, bf16[48,1536]{1,0:T(8,128)(2,1)S(1)}, u32[]{:S(2)}, u32[]{:S(2)}) collective-permute-start(bf16[48,1536]{1,0:T(8,128)(2,1)S(1)} %dynamic-slice_bitcast_fusion), channel_id=1, source_target_pairs={{0,1},{1,0},{2,3},{3,2},{4,5},{5,4},{6,7},{7,6},{8,9},{9,8},{10,11... | collective-permute-start | bytes 442376 | tf_op jit(solution)/shard_map/ppermute | solution.py:648
  9.5 41.6 %copy-start.4 = (bf16[96,1536]{1,0:T(8,128)(2,1)}, bf16[96,1536]{1,0:T(8,128)(2,1)S(1)}, u32[]{:S(2)}) copy-start(bf16[96,1536]{1,0:T(8,128)(2,1)S(1)} %pad_maximum_fusion.2.refs_0_) | copy-start | bytes 884740
  9.5 12.4 %collective-permute-start.8 = (bf16[96,1536]{1,0:T(8,128)(2,1)S(1)}, bf16[96,1536]{1,0:T(8,128)(2,1)S(1)}, u32[]{:S(2)}, u32[]{:S(2)}) collective-permute-start(bf16[96,1536]{1,0:T(8,128)(2,1)S(1)} %pad_maximum_fusion.2.refs_0_), channel_id=1, source_target_pairs={{0,8},{1,9},{2,10},{3,11},{4,12},{5,13},{6,14},{7,15},{8,16},{9,17... | collective-permute-start | bytes 884744 | tf_op jit(solution)/shard_map/ppermute | solution.py:654
  12.1 10.5 %collective-permute-start.5 = (bf16[96,1536]{1,0:T(8,128)(2,1)S(1)}, bf16[96,1536]{1,0:T(8,128)(2,1)S(1)}, u32[]{:S(2)}, u32[]{:S(2)}) collective-permute-start(bf16[96,1536]{1,0:T(8,128)(2,1)S(1)} %pad_maximum_fusion.2.refs_0_), channel_id=1, source_target_pairs={{0,4},{1,5},{2,6},{3,7},{4,0},{5,1},{6,2},{7,3},{8,12},{9,13},{10,... | collective-permute-start | bytes 884744 | tf_op jit(solution)/shard_map/ppermute | solution.py:656
  13.6 13.5 %collective-permute-start.4 = (bf16[96,1536]{1,0:T(8,128)(2,1)S(1)}, bf16[96,1536]{1,0:T(8,128)(2,1)S(1)}, u32[]{:S(2)}, u32[]{:S(2)}) collective-permute-start(bf16[96,1536]{1,0:T(8,128)(2,1)S(1)} %pad_maximum_fusion.2.refs_0_), channel_id=1, source_target_pairs={{0,2},{1,3},{2,0},{3,1},{4,6},{5,7},{6,4},{7,5},{8,10},{9,11},{10,... | collective-permute-start | bytes 884744 | tf_op jit(solution)/shard_map/ppermute | solution.py:655
  15.1 33.9 %collective-permute-start.3 = (bf16[3,128,1536]{2,1,0:T(8,128)(2,1)S(1)}, bf16[3,128,1536]{2,1,0:T(8,128)(2,1)S(1)}, u32[]{:S(2)}, u32[]{:S(2)}) collective-permute-start(bf16[3,128,1536]{2,1,0:T(8,128)(2,1)S(1)} %pad_maximum_fusion.1), channel_id=1, source_target_pairs={{0,1},{1,0},{2,3},{3,2},{4,5},{5,4},{6,7},{7,6},{8,9},{9,8},{10,11... | collective-permute-start | bytes 3538952 | tf_op jit(solution)/shard_map/ppermute | solution.py:634
  15.2 14.7 %collective-permute-start.2 = (bf16[3,32,1536]{2,1,0:T(8,128)(2,1)S(1)}, bf16[3,32,1536]{2,1,0:T(8,128)(2,1)S(1)}, u32[]{:S(2)}, u32[]{:S(2)}) collective-permute-start(bf16[3,32,1536]{2,1,0:T(8,128)(2,1)S(1)} %slice_select_fusion), channel_id=1, source_target_pairs={{2,0},{4,2},{6,4},{8,6},{10,8},{12,10},{14,12},{16,14},{18,16},{20... | collective-permute-start | bytes 884744 | tf_op jit(solution)/shard_map/ppermute | solution.py:635
  21.9 29.1 %copy-start.18 = (bf16[96,1536]{1,0:T(8,128)(2,1)}, bf16[96,1536]{1,0:T(8,128)(2,1)S(1)}, u32[]{:S(2)}) copy-start(bf16[96,1536]{1,0:T(8,128)(2,1)S(1)} %collective-permute-done.8.refs_5_) | copy-start | bytes 884740
  21.9 16.2 %collective-permute-start.1 = (bf16[3,32,1536]{2,1,0:T(8,128)(2,1)S(1)}, bf16[3,32,1536]{2,1,0:T(8,128)(2,1)S(1)}, u32[]{:S(2)}, u32[]{:S(2)}) collective-permute-start(bf16[3,32,1536]{2,1,0:T(8,128)(2,1)S(1)} %slice_select_fusion), channel_id=1, source_target_pairs={{2,1},{4,3},{6,5},{8,7},{10,9},{12,11},{14,13},{16,15},{18,17},{20... | collective-permute-start | bytes 884744 | tf_op jit(solution)/shard_map/ppermute | solution.py:636
  22.6 28.5 %copy-start.7 = (bf16[96,1536]{1,0:T(8,128)(2,1)}, bf16[96,1536]{1,0:T(8,128)(2,1)S(1)}, u32[]{:S(2)}) copy-start(bf16[96,1536]{1,0:T(8,128)(2,1)S(1)} %collective-permute-done.5.refs_2_) | copy-start | bytes 884740
  22.6 15.5 %collective-permute-start.13 = (bf16[96,1536]{1,0:T(8,128)(2,1)S(1)}, bf16[96,1536]{1,0:T(8,128)(2,1)S(1)}, u32[]{:S(2)}, u32[]{:S(2)}) collective-permute-start(bf16[96,1536]{1,0:T(8,128)(2,1)S(1)} %collective-permute-done.8.refs_5_), channel_id=1, source_target_pairs={{0,8},{1,9},{2,10},{3,11},{4,12},{5,13},{6,14},{7,15},{8,16},{9,17... | collective-permute-start | bytes 884744 | tf_op jit(solution)/shard_map/ppermute | solution.py:654
  27.1 24.0 %copy-start.8 = (bf16[96,1536]{1,0:T(8,128)(2,1)}, bf16[96,1536]{1,0:T(8,128)(2,1)S(1)}, u32[]{:S(2)}) copy-start(bf16[96,1536]{1,0:T(8,128)(2,1)S(1)} %collective-permute-done.4.refs_1_) | copy-start | bytes 884740
  27.1 11.1 %collective-permute-start.10 = (bf16[96,1536]{1,0:T(8,128)(2,1)S(1)}, bf16[96,1536]{1,0:T(8,128)(2,1)S(1)}, u32[]{:S(2)}, u32[]{:S(2)}) collective-permute-start(bf16[96,1536]{1,0:T(8,128)(2,1)S(1)} %collective-permute-done.8.refs_5_), channel_id=1, source_target_pairs={{0,4},{1,5},{2,6},{3,7},{4,0},{5,1},{6,2},{7,3},{8,12},{9,13},{10,... | collective-permute-start | bytes 884744 | tf_op jit(solution)/shard_map/ppermute | solution.py:656
  29.8 12.6 %collective-permute-start.9 = (bf16[96,1536]{1,0:T(8,128)(2,1)S(1)}, bf16[96,1536]{1,0:T(8,128)(2,1)S(1)}, u32[]{:S(2)}, u32[]{:S(2)}) collective-permute-start(bf16[96,1536]{1,0:T(8,128)(2,1)S(1)} %collective-permute-done.8.refs_5_), channel_id=1, source_target_pairs={{0,2},{1,3},{2,0},{3,1},{4,6},{5,7},{6,4},{7,5},{8,10},{9,11},{10,... | collective-permute-start | bytes 884744 | tf_op jit(solution)/shard_map/ppermute | solution.py:655
  38.1 12.9 %copy-start.19 = (bf16[96,1536]{1,0:T(8,128)(2,1)}, bf16[96,1536]{1,0:T(8,128)(2,1)S(1)}, u32[]{:S(2)}) copy-start(bf16[96,1536]{1,0:T(8,128)(2,1)S(1)} %collective-permute-done.13.refs_10_) | copy-start | bytes 884740
  38.1 8.8 %collective-permute-start.18 = (bf16[96,1536]{1,0:T(8,128)(2,1)S(1)}, bf16[96,1536]{1,0:T(8,128)(2,1)S(1)}, u32[]{:S(2)}, u32[]{:S(2)}) collective-permute-start(bf16[96,1536]{1,0:T(8,128)(2,1)S(1)} %collective-permute-done.13.refs_10_), channel_id=1, source_target_pairs={{0,8},{1,9},{2,10},{3,11},{4,12},{5,13},{6,14},{7,15},{8,16},{9,17... | collective-permute-start | bytes 884744 | tf_op jit(solution)/shard_map/ppermute | solution.py:654
  38.1 7.1 %collective-permute-start.15 = (bf16[96,1536]{1,0:T(8,128)(2,1)S(1)}, bf16[96,1536]{1,0:T(8,128)(2,1)S(1)}, u32[]{:S(2)}, u32[]{:S(2)}) collective-permute-start(bf16[96,1536]{1,0:T(8,128)(2,1)S(1)} %collective-permute-done.13.refs_10_), channel_id=1, source_target_pairs={{0,4},{1,5},{2,6},{3,7},{4,0},{5,1},{6,2},{7,3},{8,12},{9,13},{10,... | collective-permute-start | bytes 884744 | tf_op jit(solution)/shard_map/ppermute | solution.py:656
  38.2 12.8 %copy-start.9 = (bf16[96,1536]{1,0:T(8,128)(2,1)}, bf16[96,1536]{1,0:T(8,128)(2,1)S(1)}, u32[]{:S(2)}) copy-start(bf16[96,1536]{1,0:T(8,128)(2,1)S(1)} %collective-permute-done.10.refs_7_) | copy-start | bytes 884740
  38.2 10.5 %collective-permute-start.14 = (bf16[96,1536]{1,0:T(8,128)(2,1)S(1)}, bf16[96,1536]{1,0:T(8,128)(2,1)S(1)}, u32[]{:S(2)}, u32[]{:S(2)}) collective-permute-start(bf16[96,1536]{1,0:T(8,128)(2,1)S(1)} %collective-permute-done.13.refs_10_), channel_id=1, source_target_pairs={{0,2},{1,3},{2,0},{3,1},{4,6},{5,7},{6,4},{7,5},{8,10},{9,11},{10,... | collective-permute-start | bytes 884744 | tf_op jit(solution)/shard_map/ppermute | solution.py:655
  42.5 8.6 %copy-start.10 = (bf16[96,1536]{1,0:T(8,128)(2,1)}, bf16[96,1536]{1,0:T(8,128)(2,1)S(1)}, u32[]{:S(2)}) copy-start(bf16[96,1536]{1,0:T(8,128)(2,1)S(1)} %collective-permute-done.9.refs_6_) | copy-start | bytes 884740
  42.5 19.4 %collective-permute-start.6 = (bf16[48,1536]{1,0:T(8,128)(2,1)S(1)}, bf16[48,1536]{1,0:T(8,128)(2,1)S(1)}, u32[]{:S(2)}, u32[]{:S(2)}) collective-permute-start(bf16[48,1536]{1,0:T(8,128)(2,1)S(1)} %slice.81), channel_id=1, source_target_pairs={{0,2},{1,3},{2,0},{3,1},{4,6},{5,7},{6,4},{7,5},{8,10},{9,11},{10,... | collective-permute-start | bytes 442376 | tf_op jit(solution)/shard_map/ppermute | solution.py:661
  45.2 5.9 %copy-start.11 = (bf16[96,1536]{1,0:T(8,128)(2,1)}, bf16[96,1536]{1,0:T(8,128)(2,1)S(1)}, u32[]{:S(2)}) copy-start(bf16[96,1536]{1,0:T(8,128)(2,1)S(1)} %collective-permute-done.15.refs_12_) | copy-start | bytes 884740
  45.2 17.3 %collective-permute-start.7 = (bf16[48,1536]{1,0:T(8,128)(2,1)S(1)}, bf16[48,1536]{1,0:T(8,128)(2,1)S(1)}, u32[]{:S(2)}, u32[]{:S(2)}) collective-permute-start(bf16[48,1536]{1,0:T(8,128)(2,1)S(1)} %slice.82), channel_id=1, source_target_pairs={{0,4},{1,5},{2,6},{3,7},{4,0},{5,1},{6,2},{7,3},{8,12},{9,13},{10,... | collective-permute-start | bytes 442376 | tf_op jit(solution)/shard_map/ppermute | solution.py:662
  46.9 15.7 %collective-permute-start.11 = (bf16[48,1536]{1,0:T(8,128)(2,1)S(1)}, bf16[48,1536]{1,0:T(8,128)(2,1)S(1)}, u32[]{:S(2)}, u32[]{:S(2)}) collective-permute-start(bf16[48,1536]{1,0:T(8,128)(2,1)S(1)} %slice.83), channel_id=1, source_target_pairs={{0,2},{1,3},{2,0},{3,1},{4,6},{5,7},{6,4},{7,5},{8,10},{9,11},{10,... | collective-permute-start | bytes 442376 | tf_op jit(solution)/shard_map/ppermute | solution.py:661
  48.8 7.9 %collective-permute-start.20 = (bf16[96,1536]{1,0:T(8,128)(2,1)S(1)}, bf16[96,1536]{1,0:T(8,128)(2,1)S(1)}, u32[]{:S(2)}, u32[]{:S(2)}) collective-permute-start(bf16[96,1536]{1,0:T(8,128)(2,1)S(1)} %collective-permute-done.18.refs_15_), channel_id=1, source_target_pairs={{0,4},{1,5},{2,6},{3,7},{4,0},{5,1},{6,2},{7,3},{8,12},{9,13},{10,... | collective-permute-start | bytes 884744 | tf_op jit(solution)/shard_map/ppermute | solution.py:656
  49.0 11.4 %collective-permute-start.19 = (bf16[96,1536]{1,0:T(8,128)(2,1)S(1)}, bf16[96,1536]{1,0:T(8,128)(2,1)S(1)}, u32[]{:S(2)}, u32[]{:S(2)}) collective-permute-start(bf16[96,1536]{1,0:T(8,128)(2,1)S(1)} %collective-permute-done.18.refs_15_), channel_id=1, source_target_pairs={{0,2},{1,3},{2,0},{3,1},{4,6},{5,7},{6,4},{7,5},{8,10},{9,11},{10,... | collective-permute-start | bytes 884744 | tf_op jit(solution)/shard_map/ppermute | solution.py:655
  56.7 13.4 %copy-start.13 = (bf16[96,1536]{1,0:T(8,128)(2,1)}, bf16[96,1536]{1,0:T(8,128)(2,1)S(1)}, u32[]{:S(2)}) copy-start(bf16[96,1536]{1,0:T(8,128)(2,1)S(1)} %collective-permute-done.20.refs_17_) | copy-start | bytes 884740
  56.7 9.4 %collective-permute-start.12 = (bf16[48,1536]{1,0:T(8,128)(2,1)S(1)}, bf16[48,1536]{1,0:T(8,128)(2,1)S(1)}, u32[]{:S(2)}, u32[]{:S(2)}) collective-permute-start(bf16[48,1536]{1,0:T(8,128)(2,1)S(1)} %slice.84), channel_id=1, source_target_pairs={{0,4},{1,5},{2,6},{3,7},{4,0},{5,1},{6,2},{7,3},{8,12},{9,13},{10,... | collective-permute-start | bytes 442376 | tf_op jit(solution)/shard_map/ppermute | solution.py:662
  60.4 9.7 %copy-start.14 = (bf16[96,1536]{1,0:T(8,128)(2,1)}, bf16[96,1536]{1,0:T(8,128)(2,1)S(1)}, u32[]{:S(2)}) copy-start(bf16[96,1536]{1,0:T(8,128)(2,1)S(1)} %collective-permute-done.19.refs_16_) | copy-start | bytes 884740
  60.4 6.7 %collective-permute-start.16 = (bf16[48,1536]{1,0:T(8,128)(2,1)S(1)}, bf16[48,1536]{1,0:T(8,128)(2,1)S(1)}, u32[]{:S(2)}, u32[]{:S(2)}) collective-permute-start(bf16[48,1536]{1,0:T(8,128)(2,1)S(1)} %slice.85), channel_id=1, source_target_pairs={{0,2},{1,3},{2,0},{3,1},{4,6},{5,7},{6,4},{7,5},{8,10},{9,11},{10,... | collective-permute-start | bytes 442376 | tf_op jit(solution)/shard_map/ppermute | solution.py:661
  61.9 8.2 %copy-start.24 = (bf16[48,1536]{1,0:T(8,128)(2,1)}, bf16[48,1536]{1,0:T(8,128)(2,1)S(1)}, u32[]{:S(2)}) copy-start(bf16[48,1536]{1,0:T(8,128)(2,1)S(1)} %collective-permute-done.6.refs_3_) | copy-start | bytes 442372
  61.9 6.6 %collective-permute-start.17 = (bf16[48,1536]{1,0:T(8,128)(2,1)S(1)}, bf16[48,1536]{1,0:T(8,128)(2,1)S(1)}, u32[]{:S(2)}, u32[]{:S(2)}) collective-permute-start(bf16[48,1536]{1,0:T(8,128)(2,1)S(1)} %slice.86), channel_id=1, source_target_pairs={{0,4},{1,5},{2,6},{3,7},{4,0},{5,1},{6,2},{7,3},{8,12},{9,13},{10,... | collective-permute-start | bytes 442376 | tf_op jit(solution)/shard_map/ppermute | solution.py:662
  62.5 6.2 %copy-start.25 = (bf16[48,1536]{1,0:T(8,128)(2,1)}, bf16[48,1536]{1,0:T(8,128)(2,1)S(1)}, u32[]{:S(2)}) copy-start(bf16[48,1536]{1,0:T(8,128)(2,1)S(1)} %collective-permute-done.7.refs_4_) | copy-start | bytes 442372
  62.5 6.2 %collective-permute-start.21 = (bf16[48,1536]{1,0:T(8,128)(2,1)S(1)}, bf16[48,1536]{1,0:T(8,128)(2,1)S(1)}, u32[]{:S(2)}, u32[]{:S(2)}) collective-permute-start(bf16[48,1536]{1,0:T(8,128)(2,1)S(1)} %slice.87), channel_id=1, source_target_pairs={{0,2},{1,3},{2,0},{3,1},{4,6},{5,7},{6,4},{7,5},{8,10},{9,11},{10,... | collective-permute-start | bytes 442376 | tf_op jit(solution)/shard_map/ppermute | solution.py:661
  62.6 6.0 %copy-start.26 = (bf16[48,1536]{1,0:T(8,128)(2,1)}, bf16[48,1536]{1,0:T(8,128)(2,1)S(1)}, u32[]{:S(2)}) copy-start(bf16[48,1536]{1,0:T(8,128)(2,1)S(1)} %collective-permute-done.11.refs_8_) | copy-start | bytes 442372
  62.6 7.5 %collective-permute-start.22 = (bf16[48,1536]{1,0:T(8,128)(2,1)S(1)}, bf16[48,1536]{1,0:T(8,128)(2,1)S(1)}, u32[]{:S(2)}, u32[]{:S(2)}) collective-permute-start(bf16[48,1536]{1,0:T(8,128)(2,1)S(1)} %slice.88), channel_id=1, source_target_pairs={{0,4},{1,5},{2,6},{3,7},{4,0},{5,1},{6,2},{7,3},{8,12},{9,13},{10,... | collective-permute-start | bytes 442376 | tf_op jit(solution)/shard_map/ppermute | solution.py:662
  66.1 149.7 %copy-start.17 = (f32[31,768]{1,0:T(8,128)S(1)}, f32[31,768]{1,0:T(8,128)}, u32[]{:S(2)}) copy-start(f32[31,768]{1,0:T(8,128)} %broadcast_in_dim.8) | copy-start | bytes 285700
  224.5 12.3 %all-to-all-start = ((f32[16,2,768]{2,1,0:T(2,128)}), f32[16,2,768]{2,1,0:T(2,128)}, u32[]{:S(2)}, u32[]{:S(2)}) async-start(f32[16,2,768]{2,1,0:T(2,128)} %get-tuple-element.34), calls=%async_computation | async-start | bytes 196608 | tf_op jit(solution)/shard_map/all_to_all | solution.py:640
  260.8 2.6 collective-permute-start.23
  267.5 15.4 %collective-permute-start.24 = (f32[128,1536]{1,0:T(8,128)}, f32[128,1536]{1,0:T(8,128)}, u32[]{:S(2)}, u32[]{:S(2)}) collective-permute-start(f32[128,1536]{1,0:T(8,128)} %get-tuple-element.48.mine), channel_id=1, source_target_pairs={{0,1},{1,0},{2,3},{3,2},{4,5},{5,4},{6,7},{7,6},{8,9},{9,8},{10,11... | collective-permute-start | bytes 2359304 | tf_op jit(solution)/shard_map/ppermute | solution.py:634
  267.6 15.2 %collective-permute-start.26 = (f32[32,1536]{1,0:T(8,128)}, f32[32,1536]{1,0:T(8,128)S(1)}, u32[]{:S(2)}, u32[]{:S(2)}) collective-permute-start(f32[32,1536]{1,0:T(8,128)} %get-tuple-element.49), channel_id=1, source_target_pairs={{2,1},{4,3},{6,5},{8,7},{10,9},{12,11},{14,13},{16,15},{18,17},{20... | collective-permute-start | bytes 589832 | tf_op jit(solution)/shard_map/ppermute | solution.py:636
  268.3 14.6 %collective-permute-start.25 = (f32[32,1536]{1,0:T(8,128)}, f32[32,1536]{1,0:T(8,128)S(1)}, u32[]{:S(2)}, u32[]{:S(2)}) collective-permute-start(f32[32,1536]{1,0:T(8,128)} %get-tuple-element.49), channel_id=1, source_target_pairs={{2,0},{4,2},{6,4},{8,6},{10,8},{12,10},{14,12},{16,14},{18,16},{20... | collective-permute-start | bytes 589832 | tf_op jit(solution)/shard_map/ppermute | solution.py:635
  269.6 13.2 %all-to-all-start.2 = ((f32[32,1,128]{2,1,0:T(1,128)}), f32[32,1,128]{2,1,0:T(1,128)S(1)}, u32[]{:S(2)}, u32[]{:S(2)}) async-start(f32[32,1,128]{2,1,0:T(1,128)} %get-tuple-element.44), calls=%async_computation.2 | async-start | bytes 32768 | tf_op jit(solution)/shard_map/all_to_all | solution.py:709
  295.6 13.9 %all-to-all-start.3 = ((f32[16,2,768]{2,1,0:T(2,128)}), f32[16,2,768]{2,1,0:T(2,128)S(1)}, u32[]{:S(2)}, u32[]{:S(2)}) async-start(f32[16,2,768]{2,1,0:T(2,128)} %get-tuple-element.52.stats.local_stats), calls=%async_computation.3 | async-start | bytes 196608 | tf_op jit(solution)/shard_map/all_to_all | solution.py:640
  301.9 19.6 %copy-start.33 = (f32[2,768]{1,0:T(2,128)S(1)}, f32[2,768]{1,0:T(2,128)}, u32[]{:S(2)}) copy-start(f32[2,768]{1,0:T(2,128)} %get-tuple-element.60) | copy-start | bytes 18436
  316.5 13.4 %all-to-all-start.4 = ((bf16[16,48,128]{2,1,0:T(8,128)(2,1)}), bf16[16,48,128]{2,1,0:T(8,128)(2,1)S(1)}, u32[]{:S(2)}, u32[]{:S(2)}) async-start(bf16[16,48,128]{2,1,0:T(8,128)(2,1)} %get-tuple-element.58), calls=%async_computation.4 | async-start | bytes 393216 | tf_op jit(solution)/shard_map/all_to_all | solution.py:640
  (17 other events, 32.9 us)

commit v3 on v2

--- a/solution.py
+++ b/solution.py
@@ -84,43 +84,43 @@
     return jnp.sum(jnp.concatenate(totals, axis=0), axis=1)
 
 
-def place_kernel(depth, scal, *refs):
-    blocks, out, sems = refs[:-2], refs[-2], refs[-1]
+def place_kernel(shifts, size, scal, *refs):
+    pieces, out = refs[:-1], refs[-1]
     spot, layer = scal[4], scal[5]
-    copies = []
-    for number, (shift, other, first, ref) in enumerate(blocks_of(blocks, depth)):
-        layer_of = lax.rem(layer - shift + depth, depth)
-        chip = layer_of * 4 + (spot ^ other)
-        size = blocks[0].shape[0]
+    depth = out.shape[0] // (4 * size)
+
+    def put(ref, start, stop, shift, other, first):
+        chip = lax.rem(layer - shift + depth, depth) * 4 + (spot ^ other)
         row = pl.multiple_of(chip * size + first, 16)
-        copies.append(
-            pltpu.make_async_copy(ref, out.at[pl.ds(row, ref.shape[0]), :], sems.at[number])
-        )
-    for copy in copies:
-        copy.start()
-    for copy in copies:
-        copy.wait()
-
-
-def blocks_of(refs, depth):
-    cut = refs[3].shape[0]
-    for shift in range(depth):
-        group = refs[5 * shift : 5 * shift + 5]
-        for other, first, ref in zip((0, 1, 2, 3, 3), (0, 0, 0, 0, cut), group):
-            yield shift, other, first, ref
-
-
-def place(scal, pieces, depth):
-    rows, width = pieces[0].shape
-    hbm = pl.BlockSpec(memory_space=pl.ANY)
-    return pl.pallas_call(
-        functools.partial(place_kernel, depth),
-        in_specs=[pl.BlockSpec(memory_space=pltpu.SMEM)] + [hbm] * len(pieces),
-        out_specs=hbm,
-        out_shape=jax.ShapeDtypeStruct((4 * depth * rows, width), BF16),
-        scratch_shapes=[pltpu.SemaphoreType.DMA((len(pieces),))],
-        compiler_params=params(),
-        cost_estimate=cost(0, 16 * depth * rows * width),
+        out[pl.ds(row, stop - start), :] = ref[start:stop, :]
+
+    for number, group in enumerate(shifts):
+        for other, ref in enumerate(pieces[5 * number : 5 * number + 3]):
+            for nth, shift in enumerate(group):
+                put(ref, nth * size, (nth + 1) * size, shift, other, 0)
+        at = 0
+        for ref in pieces[5 * number + 3 : 5 * number + 5]:
+            rows = ref.shape[0]
+            start = 0
+            while start < rows:
+                nth, first = (at + start) // size, (at + start) % size
+                stop = min(rows, start + size - first)
+                put(ref, start, stop, group[nth], 3, first)
+                start = stop
+            at += rows
+
+
+def place(scal, pieces, shifts, size):
+    width = pieces[0].shape[1]
+    chips = 4 * sum(len(group) for group in shifts)
+    vmem = pl.BlockSpec(memory_space=pltpu.VMEM)
+    return pl.pallas_call(
+        functools.partial(place_kernel, shifts, size),
+        in_specs=[pl.BlockSpec(memory_space=pltpu.SMEM)] + [vmem] * len(pieces),
+        out_specs=vmem,
+        out_shape=jax.ShapeDtypeStruct((chips * size, width), BF16),
+        compiler_params=params(),
+        cost_estimate=cost(0, 4 * chips * size * width),
         name="place_weights",
     )(scal, *pieces)
 
@@ -617,7 +617,6 @@
 
     cores = [[2 * c + k for c in range(chips)] for k in range(2)]
     depth = chips // 4
-    onward = [(i, (i + 8) % shards) for i in range(shards)]
     swap = [(i, i ^ 1) for i in range(shards)]
     swap_x = [(i, i ^ 2) for i in range(shards)]
     swap_y = [(i, i ^ 4) for i in range(shards)]
@@ -647,24 +646,29 @@
     kept = lax.dynamic_index_in_dim(pair, core, 0, keepdims=False)
     given = lax.ppermute(lax.dynamic_index_in_dim(pair, 1 - core, 0, keepdims=False), "tm", swap)
     block = jnp.concatenate([jnp.where(first, kept, given), jnp.where(first, given, kept)], axis=0)
-    cut = (slice_width + 15) // 16 * 16
+    shifts = [(0,)] + [(k, depth - k) if 2 * k < depth else (k,) for k in range(1, depth // 2 + 1)]
+    along = {0: block}
+    for k in [k for group in shifts[1:] for k in group]:
+        along[k] = lax.ppermute(block, "tm", [(i, (i + 8 * k) % shards) for i in range(shards)])
     pieces = []
-    for shift in range(depth):
-        if shift:
-            block = lax.ppermute(block, "tm", onward)
-        from_x = lax.ppermute(block, "tm", swap_x)
-        from_y = lax.ppermute(block, "tm", swap_y)
+    for group in shifts:
+        blocks = jnp.concatenate([along[k] for k in group], axis=0)
+        cut = (blocks.shape[0] // 2 + 15) // 16 * 16
+        from_x = lax.ppermute(blocks, "tm", swap_x)
+        from_y = lax.ppermute(blocks, "tm", swap_y)
         pieces += [
-            block,
+            blocks,
             from_x,
             from_y,
             lax.ppermute(from_y[:cut], "tm", swap_x),
             lax.ppermute(from_x[cut:], "tm", swap_y),
         ]
-    weight = place(scal, pieces, depth)
-
+    weight = place(scal, pieces, shifts, block.shape[0])
+
+    features, start_noise, cotangent, kernel, bn_gain, bn_shift, _ = lax.optimization_barrier(
+        (features, start_noise, cotangent, kernel, bn_gain, bn_shift, pieces[5])
+    )
     packed = jnp.concatenate([features, start_noise, cotangent], axis=0)
-    packed, _ = lax.optimization_barrier((packed, given))
     partner, near, far = across(
         packed, jnp.where(first, packed[:, :HALO], packed[:, rows - HALO :])
     )

time: 334 us -> 209 us (0.63)
  Pallas kernels: 199 us -> 58.7 us
  waiting for transfers between devices: 47.6 us -> 53.8 us
  other arithmetic: 5.4 us -> 9.89 us
    pallas_call x1, Pallas kernels: 145 us -> 4.81 us  [place(): pl.pallas_call(functools.partial(place_kernel, shifts, size), in_specs=[p...]
    ppermute x4 -> x3, waiting for transfers between devices: 1.09 us -> 14.3 us  [on_device(): lax.ppermute(from_y[:cut], 'tm', swap_x)]
    ppermute x11 -> x9, waiting for transfers between devices: 24.5 us -> 22.4 us  [the longest x3 16.5 us: on_device(): lax.ppermute(block, 'tm', [(i, (i + 8 * k) % shards) for i in range(shard...]
    ppermute x11 -> x9, starting transfers between devices: 15.4 us -> 14.7 us  [the longest x3 5.67 us: on_device(): lax.ppermute(block, 'tm', [(i, (i + 8 * k) % shards) for i in range(shard...]
  transfers between devices with their start and end apart: 31 -> 27, of which waited for: 18 -> 14; matrix products, arithmetic and copies ran while one was open for 5% -> 8% of each run, Pallas kernels for 3% -> 7%
where the time goes in v3:
time: 209 us; the launch traced here: 208 us
  Pallas kernels  58.7 us (28%)
  waiting for transfers between devices  53.8 us (26%)
  starting transfers between devices  51 us (24%)
  local copies, waits for them, and re-layouts  17.6 us (8%)
  blocking collectives  11.8 us (6%)
  other arithmetic  9.89 us (5%)
  matrix products  2.99 us (1%)
    ppermute x3, waiting for transfers between devices, on_device(): lax.ppermute(block, 'tm', [(i, (i + 8 * k) % shards) for i in range(shard...  16.5 us
    pallas_call x2, Pallas kernels, forward(): pl.pallas_call(functools.partial(forward_kernel, keep), grid=(steps,), in...  15.5 us
    all_to_all x3, starting transfers between devices, peers_of(): lax.all_to_all(array, 'tm', 0, 0, axis_index_groups=cores, tiled=True)  15.2 us
    ppermute x3, waiting for transfers between devices, on_device(): lax.ppermute(from_y[:cut], 'tm', swap_x)  14.3 us
    all_to_all x3, waiting for transfers between devices, peers_of(): lax.all_to_all(array, 'tm', 0, 0, axis_index_groups=cores, tiled=True)  13.9 us
    all_to_all x1, blocking collectives, peers_of(): lax.all_to_all(array, 'tm', 0, 0, axis_index_groups=cores, tiled=True)  11.8 us
    pallas_call x1, Pallas kernels, backward(): pl.pallas_call(backward_kernel, grid=(steps,), in_specs=[pl.BlockSpec(mem...  8.31 us
    all_to_all x1, starting transfers between devices, on_device(): squares = lax.all_to_all(squares, 'tm', 0, 0, tiled=True)  6.34 us
  transfers between devices with their start and end apart: 27, of which 14 were waited for; matrix products, arithmetic and copies ran while one was open for 8% of the time, Pallas kernels for 7%

profile of v3, /device:TPU:0, one launch (start us, length us, event | category | flops | bytes accessed | tf_op | source)
XLA Modules:
  0.0 207.7 jit_solution(10122714323657808680)
XLA Ops:
  5.4 2.6 %collective-permute-start.1 = (bf16[96,1536]{1,0:T(8,128)(2,1)}, bf16[96,1536]{1,0:T(8,128)(2,1)S(1)}, u32[]{:S(2)}, u32[]{:S(2)}) collective-permute-start(bf16[96,1536]{1,0:T(8,128)(2,1)} %pad_maximum_fusion.1.refs_0_), channel_id=1, source_target_pairs={{0,8},{1,9},{2,10},{3,11},{4,12},{5,13},{6,14},{7,15},{8,16},{9,17... | collective-permute-start | bytes 884744 | tf_op jit(solution)/shard_map/ppermute | solution.py:652
  8.0 2.1 %collective-permute-start.2 = (bf16[96,1536]{1,0:T(8,128)(2,1)}, bf16[96,1536]{1,0:T(8,128)(2,1)S(1)}, u32[]{:S(2)}, u32[]{:S(2)}) collective-permute-start(bf16[96,1536]{1,0:T(8,128)(2,1)} %pad_maximum_fusion.1.refs_0_), channel_id=1, source_target_pairs={{0,24},{1,25},{2,26},{3,27},{4,28},{5,29},{6,30},{7,31},{8,0},{9,1... | collective-permute-start | bytes 884744 | tf_op jit(solution)/shard_map/ppermute | solution.py:652
  11.6 1.5 collective-permute-start.7
  13.2 1.5 collective-permute-start.6
  14.7 3.4 %collective-permute-done.1 = bf16[96,1536]{1,0:T(8,128)(2,1)S(1)} collective-permute-done((bf16[96,1536]{1,0:T(8,128)(2,1)}, bf16[96,1536]{1,0:T(8,128)(2,1)S(1)}, u32[]{:S(2)}, u32[]{:S(2)}) %collective-permute-start.1) | collective-permute-done | bytes 294944 | tf_op jit(solution)/shard_map/ppermute | solution.py:652
  18.8 4.9 %collective-permute-done.2 = bf16[96,1536]{1,0:T(8,128)(2,1)S(1)} collective-permute-done((bf16[96,1536]{1,0:T(8,128)(2,1)}, bf16[96,1536]{1,0:T(8,128)(2,1)S(1)}, u32[]{:S(2)}, u32[]{:S(2)}) %collective-permute-start.2) | collective-permute-done | bytes 294944 | tf_op jit(solution)/shard_map/ppermute | solution.py:652
  24.4 1.5 collective-permute-start.11
  26.0 1.5 collective-permute-start.10
  28.7 8.2 %collective-permute-done.14.refs_10_ = bf16[96,1536]{1,0:T(8,128)(2,1)} collective-permute-done((bf16[96,1536]{1,0:T(8,128)(2,1)}, bf16[96,1536]{1,0:T(8,128)(2,1)}, u32[]{:S(2)}, u32[]{:S(2)}) %collective-permute-start.14) | collective-permute-done | bytes 294944 | tf_op jit(solution)/shard_map/ppermute | solution.py:652
  37.0 1.5 collective-permute-start.16
  38.5 1.5 collective-permute-start.15
  40.7 5.8 %collective-permute-done.16.refs_12_ = bf16[96,1536]{1,0:T(8,128)(2,1)S(1)} collective-permute-done((bf16[96,1536]{1,0:T(8,128)(2,1)}, bf16[96,1536]{1,0:T(8,128)(2,1)S(1)}, u32[]{:S(2)}, u32[]{:S(2)}) %collective-permute-start.16) | collective-permute-done | bytes 294944 | tf_op jit(solution)/shard_map/ppermute | solution.py:658
  46.6 1.3 collective-permute-start.4
  47.9 1.4 collective-permute-start.3
  50.2 1.6 slice.75
  52.7 4.5 %collective-permute-start.8 = (bf16[48,1536]{1,0:T(8,128)(2,1)}, bf16[48,1536]{1,0:T(8,128)(2,1)}, u32[]{:S(2)}, u32[]{:S(2)}) collective-permute-start(bf16[48,1536]{1,0:T(8,128)(2,1)} %slice.75), channel_id=1, source_target_pairs={{0,2},{1,3},{2,0},{3,1},{4,6},{5,7},{6,4},{7,5},{8,10},{9,11},{10,... | collective-permute-start | bytes 442376 | tf_op jit(solution)/shard_map/ppermute | solution.py:663
  60.4 7.5 %collective-permute-done.8.refs_3_ = bf16[48,1536]{1,0:T(8,128)(2,1)} collective-permute-done((bf16[48,1536]{1,0:T(8,128)(2,1)}, bf16[48,1536]{1,0:T(8,128)(2,1)}, u32[]{:S(2)}, u32[]{:S(2)}) %collective-permute-start.8) | collective-permute-done | bytes 147488 | tf_op jit(solution)/shard_map/ppermute | solution.py:663
  67.9 2.1 collective-permute-start.18
  70.0 2.0 collective-permute-start.13
  72.0 1.1 broadcast_select_fusion.3
  73.1 1.6 collective-permute-done.17.refs_13_
  74.6 5.2 %collective-permute-done.12.refs_8_ = bf16[96,1536]{1,0:T(8,128)(2,1)S(1)} collective-permute-done((bf16[96,1536]{1,0:T(8,128)(2,1)S(1)}, bf16[96,1536]{1,0:T(8,128)(2,1)S(1)}, u32[]{:S(2)}, u32[]{:S(2)}) %collective-permute-start.12) | collective-permute-done | bytes 294944 | tf_op jit(solution)/shard_map/ppermute | solution.py:663
  81.3 4.8 %place_weights.1.value_w.gate_w = bf16[1536,1536]{1,0:T(8,128)(2,1)} custom-call(s32[6]{0:T(128)} %stack.26.scal, bf16[96,1536]{1,0:T(8,128)(2,1)} %pad_maximum_fusion.1.refs_0_, bf16[96,1536]{1,0:T(8,128)(2,1)} %collective-permute-done.6.refs_1_, bf16[96,1536]{1,0:T(8,128)(2,1)} %collective-permute-done.7.refs_2_, ...), custom_call_target="tpu_custom_call" | custom-call | bytes 9437184 | tf_op jit(solution)/shard_map/place_weights/pallas_call | solution.py:117
  86.1 1.4 broadcast_select_fusion.1
  90.1 1.5 multiply_convert_fusion.nb
  92.5 7.8 %project_glu_conv.2 = (f32[256,768]{1,0:T(8,128)}, f32[256,768]{1,0:T(8,128)}, bf16[320,768]{1,0:T(8,128)(2,1)}, f32[288,768]{1,0:T(8,128)}, f32[16,2,768]{2,1,0:T(2,128)}) custom-call(s32[6]{0:T(128)} %stack.26.scal, bf16[320,1536]{1,0:T(8,128)(2,1)} %multiply_convert_fusion.nb, bf16[1536,1536]{1,0:T(8,128)(2,1)} %place_weights.1.value_w.gate_w, ...), custom_call_target="tpu_custom_call" | custom-call | flops 1509949440 | bytes 7176192 | tf_op jit(solution)/shard_map/project_glu_conv/pallas_call | solution.py:159
  100.3 4.2 %all-to-all-start = ((f32[16,2,768]{2,1,0:T(2,128)}), f32[16,2,768]{2,1,0:T(2,128)}, u32[]{:S(2)}, u32[]{:S(2)}) async-start(f32[16,2,768]{2,1,0:T(2,128)} %get-tuple-element.44), calls=%async_computation | async-start | bytes 196608 | tf_op jit(solution)/shard_map/all_to_all | solution.py:639
  104.5 3.0 %fusion.3.cot = bf16[288,768]{1,0:T(8,128)(2,1)} fusion(s32[768]{0:T(1024)S(1)} %fusion.21, bf16[3,32,1536]{2,1,0:T(8,128)(2,1)S(1)} %get-tuple-element.78, bf16[3,128,1536]{2,1,0:T(8,128)(2,1)} %copy-done.1, bf16[3,128,1536]{2,1,0:T(8,128)(2,1)} %copy-done, bf16[3,32,1536]{2,1,0:T(8,128)(2,1)S(1)} %get-tuple-element.77), kind=kOutput, calls=%fused_computation.8 | convolution fusion | flops 684417024 | bytes 3394560 | tf_op jit(solution)/shard_map/dot_general | solution.py:689
  107.5 4.7 %all-to-all-done.stats = f32[16,2,768]{2,1,0:T(2,128)} async-done(((f32[16,2,768]{2,1,0:T(2,128)}), f32[16,2,768]{2,1,0:T(2,128)}, u32[]{:S(2)}, u32[]{:S(2)}) %all-to-all-start) | async-done | bytes 98336 | tf_op jit(solution)/shard_map/all_to_all | solution.py:639
  112.1 3.9 %batch_norm_swish.1 = (f32[288,768]{1,0:T(8,128)}, f32[288,768]{1,0:T(8,128)}, f32[1,768]{1,0:T(1,128)}, f32[16,2,768]{2,1,0:T(2,128)}) custom-call(s32[6]{0:T(128)} %stack.26.scal, f32[2,16]{1,0:T(2,128)} %pad_maximum_fusion.2.counts, f32[16,2,768]{2,1,0:T(2,128)} %all-to-all-done.stats, f32[288,768]{1,0:T(8,128)} %get-tuple-element.45.conv, ...), custom_call_target="tpu_custom_call" | custom-call | flops 8847360 | bytes 3538944 | tf_op jit(solution)/shard_map/batch_norm_swish/pallas_call | solution.py:239
  116.0 11.8 %all_to_all.25.sums = f32[16,2,768]{2,1,0:T(2,128)} all-to-all(f32[16,2,768]{2,1,0:T(2,128)} %get-tuple-element.46), channel_id=1, replica_groups={{0,2,4,6,8,10,12,14,16,18,20,22,24,26,28,30},{1,3,5,7,9,11,13,15,17,19,..., dimensions={0} | all-to-all | bytes 196608 | tf_op jit(solution)/shard_map/all_to_all | solution.py:639
  127.9 8.3 %grad_conv_project_back.1 = (f32[128,1536]{1,0:T(8,128)}, f32[128,1536]{1,0:T(8,128)}, bf16[256,768]{1,0:T(8,128)(2,1)}, f32[2,768]{1,0:T(2,128)}) custom-call(s32[6]{0:T(128)} %stack.26.scal, f32[16,2,768]{2,1,0:T(2,128)} %all_to_all.25.sums, f32[288,768]{1,0:T(8,128)} %get-tuple-element.47.scaled, f32[288,768]{1,0:T(8,128)} %get-tuple-element.48.grad, ...), custom_call_target="tpu_custom_call" | custom-call | flops 1207959552 | bytes 9142272 | tf_op jit(solution)/shard_map/grad_conv_project_back/pallas_call | solution.py:314
  136.3 2.5 %collective-permute-done.19.other = f32[128,1536]{1,0:T(8,128)S(1)} collective-permute-done((f32[128,1536]{1,0:T(8,128)}, f32[128,1536]{1,0:T(8,128)S(1)}, u32[]{:S(2)}, u32[]{:S(2)}) %collective-permute-start.19) | collective-permute-done | bytes 786464 | tf_op jit(solution)/shard_map/ppermute | solution.py:711
  139.6 3.2 %direction.1 = (f32[128,1536]{1,0:T(8,128)}, f32[32,1536]{1,0:T(8,128)}, f32[32,1,128]{2,1,0:T(1,128)}) custom-call(s32[6]{0:T(128)} %stack.26.scal, f32[128,1536]{1,0:T(8,128)} %get-tuple-element.52.mine, f32[128,1536]{1,0:T(8,128)} %copy-done.6, bf16[128,1536]{1,0:T(8,128)(2,1)} %bitcast.50, bf16[128,1536]{1,0:T(8,128)(2,1)} %bitcast.48), custom_call_target="tpu_custom_call" | custom-call | flops 5898240 | bytes 3145728 | tf_op jit(solution)/shard_map/direction/pallas_call | solution.py:544
  143.7 1.3 collective-permute-start.21
  145.0 6.3 %all-to-all-start.2 = ((f32[32,1,128]{2,1,0:T(1,128)}), f32[32,1,128]{2,1,0:T(1,128)S(1)}, u32[]{:S(2)}, u32[]{:S(2)}) async-start(f32[32,1,128]{2,1,0:T(1,128)} %get-tuple-element.54), calls=%async_computation.2 | async-start | bytes 32768 | tf_op jit(solution)/shard_map/all_to_all | solution.py:713
  151.3 1.4 slice_bitcast_fusion
  152.8 4.9 %tap_grad.1.taps_before = f32[31,768]{1,0:T(8,128)} custom-call(bf16[256,768]{1,0:T(8,128)(2,1)} %get-tuple-element.55.grad_conv, bf16[320,768]{1,0:T(8,128)(2,1)} %get-tuple-element.56.glu), custom_call_target="tpu_custom_call" | custom-call | flops 12189696 | bytes 983040 | tf_op jit(solution)/shard_map/tap_grad/pallas_call | solution.py:362
  159.0 4.4 %ascend.1 = (f32[128,1536]{1,0:T(8,128)}, bf16[320,1536]{1,0:T(8,128)(2,1)}) custom-call(s32[6]{0:T(128)} %stack.26.scal, f32[32,1,128]{2,1,0:T(1,128)} %copy-done.19, bf16[320,1536]{1,0:T(8,128)(2,1)} %get-tuple-element.74.features, bf16[320,1536]{1,0:T(8,128)(2,1)} %get-tuple-element.73.noise, f32[128,1536]{1,0:T(8,128)} %get-tuple-element.58.mine, ...), custom_call_target="tpu_custom_call" | custom-call | flops 14745600 | bytes 3932160 | tf_op jit(solution)/shard_map/ascend/pallas_call | solution.py:588
  163.4 7.7 %project_glu_conv.3 = (bf16[320,768]{1,0:T(8,128)(2,1)}, f32[288,768]{1,0:T(8,128)}, f32[16,2,768]{2,1,0:T(2,128)}) custom-call(s32[6]{0:T(128)} %stack.26.scal, bf16[320,1536]{1,0:T(8,128)(2,1)} %get-tuple-element.61.nb, bf16[1536,1536]{1,0:T(8,128)(2,1)} %place_weights.1.value_w.gate_w, bf16[1536,1536]{1,0:T(8,128)(2,1)} %place_weights.1.value_w.gate_w, ...), custom_call_target="tpu_custom_call" | custom-call | flops 1509949440 | bytes 7176192 | tf_op jit(solution)/shard_map/project_glu_conv/pallas_call | solution.py:159
  171.1 6.2 %all-to-all-start.3 = ((f32[16,2,768]{2,1,0:T(2,128)}), f32[16,2,768]{2,1,0:T(2,128)S(1)}, u32[]{:S(2)}, u32[]{:S(2)}) async-start(f32[16,2,768]{2,1,0:T(2,128)} %get-tuple-element.62.stats.local_stats), calls=%async_computation.3 | async-start | bytes 196608 | tf_op jit(solution)/shard_map/all_to_all | solution.py:639
  177.3 5.6 %raw_taps.1 = (f32[31,768]{1,0:T(8,128)}, f32[31,768]{1,0:T(8,128)}) custom-call(s32[6]{0:T(128)} %stack.26.scal, f32[288,768]{1,0:T(8,128)} %get-tuple-element.63.conv, bf16[320,768]{1,0:T(8,128)(2,1)} %get-tuple-element.64.glu, f32[16,2,768]{2,1,0:T(2,128)} %get-tuple-element.62.stats.local_stats), custom_call_target="tpu_custom_call" | custom-call | flops 13713408 | bytes 1966080 | tf_op jit(solution)/shard_map/raw_taps/pallas_call | solution.py:395
  182.9 2.0 all-to-all-done.3.stats
  185.6 6.3 %batch_norm_swish_taps.1 = (bf16[16,48,128]{2,1,0:T(8,128)(2,1)}, f32[1,768]{1,0:T(1,128)}) custom-call(s32[6]{0:T(128)} %stack.26.scal, f32[2,16]{1,0:T(2,128)} %pad_maximum_fusion.2.counts, f32[16,2,768]{2,1,0:T(2,128)} %copy-done.9, f32[288,768]{1,0:T(8,128)} %get-tuple-element.63.conv, bf16[288,768]{1,0:T(8,128)(2,1)} %fusion.3.cot, ...), custom_call_target="tpu_custom_call" | custom-call | flops 22118400 | bytes 2211840 | tf_op jit(solution)/shard_map/batch_norm_swish_taps/pallas_call | solution.py:455
  191.9 4.9 %all-to-all-start.4 = ((bf16[16,48,128]{2,1,0:T(8,128)(2,1)}), bf16[16,48,128]{2,1,0:T(8,128)(2,1)S(1)}, u32[]{:S(2)}, u32[]{:S(2)}) async-start(bf16[16,48,128]{2,1,0:T(8,128)(2,1)} %get-tuple-element.68), calls=%async_computation.4 | async-start | bytes 393216 | tf_op jit(solution)/shard_map/all_to_all | solution.py:639
  196.8 1.4 fusion.23.known
  198.2 7.1 %all-to-all-done.4.received = bf16[16,48,128]{2,1,0:T(8,128)(2,1)S(1)} async-done(((bf16[16,48,128]{2,1,0:T(8,128)(2,1)}), bf16[16,48,128]{2,1,0:T(8,128)(2,1)S(1)}, u32[]{:S(2)}, u32[]{:S(2)}) %all-to-all-start.4) | async-done | bytes 196640 | tf_op jit(solution)/shard_map/all_to_all | solution.py:639
  206.0 1.7 finish.1
  (109 shorter events, 23.2 us)
Async XLA Ops:
  0.6 26.9 %copy-start.2 = (bf16[1,128,1536]{2,1,0:T(8,128)(2,1)S(1)}, bf16[1,128,1536]{2,1,0:T(8,128)(2,1)}, u32[]{:S(2)}) copy-start(bf16[1,128,1536]{2,1,0:T(8,128)(2,1)} %param.9) | copy-start | bytes 1179652
  0.6 26.8 %copy-start.3 = (bf16[1,128,1536]{2,1,0:T(8,128)(2,1)S(1)}, bf16[1,128,1536]{2,1,0:T(8,128)(2,1)}, u32[]{:S(2)}) copy-start(bf16[1,128,1536]{2,1,0:T(8,128)(2,1)} %param.8) | copy-start | bytes 1179652
  1.7 1.9 collective-permute-start
  3.6 23.9 %copy-start.10 = (bf16[1,128,1536]{2,1,0:T(8,128)(2,1)S(1)}, bf16[1,128,1536]{2,1,0:T(8,128)(2,1)}, u32[]{:S(2)}) copy-start(bf16[1,128,1536]{2,1,0:T(8,128)(2,1)} %param.10) | copy-start | bytes 1179652
  4.6 23.0 %copy-start.20 = (f32[1536]{0:T(1024)S(1)}, f32[1536]{0:T(1024)}, u32[]{:S(2)}) copy-start(f32[1536]{0:T(1024)} %param.13) | copy-start | bytes 18436
  4.6 23.1 %copy-start.21 = (f32[1536]{0:T(1024)S(1)}, f32[1536]{0:T(1024)}, u32[]{:S(2)}) copy-start(f32[1536]{0:T(1024)} %param.14) | copy-start | bytes 18436
  5.4 22.4 %copy-start.16 = (f32[31,1536]{1,0:T(8,128)S(1)}, f32[31,1536]{1,0:T(8,128)}, u32[]{:S(2)}) copy-start(f32[31,1536]{1,0:T(8,128)} %param.12) | copy-start | bytes 571396
  5.4 12.7 %collective-permute-start.1 = (bf16[96,1536]{1,0:T(8,128)(2,1)}, bf16[96,1536]{1,0:T(8,128)(2,1)S(1)}, u32[]{:S(2)}, u32[]{:S(2)}) collective-permute-start(bf16[96,1536]{1,0:T(8,128)(2,1)} %pad_maximum_fusion.1.refs_0_), channel_id=1, source_target_pairs={{0,8},{1,9},{2,10},{3,11},{4,12},{5,13},{6,14},{7,15},{8,16},{9,17... | collective-permute-start | bytes 884744 | tf_op jit(solution)/shard_map/ppermute | solution.py:652
  8.0 15.7 %collective-permute-start.2 = (bf16[96,1536]{1,0:T(8,128)(2,1)}, bf16[96,1536]{1,0:T(8,128)(2,1)S(1)}, u32[]{:S(2)}, u32[]{:S(2)}) collective-permute-start(bf16[96,1536]{1,0:T(8,128)(2,1)} %pad_maximum_fusion.1.refs_0_), channel_id=1, source_target_pairs={{0,24},{1,25},{2,26},{3,27},{4,28},{5,29},{6,30},{7,31},{8,0},{9,1... | collective-permute-start | bytes 884744 | tf_op jit(solution)/shard_map/ppermute | solution.py:652
  10.6 26.3 %collective-permute-start.14 = (bf16[96,1536]{1,0:T(8,128)(2,1)}, bf16[96,1536]{1,0:T(8,128)(2,1)}, u32[]{:S(2)}, u32[]{:S(2)}) collective-permute-start(bf16[96,1536]{1,0:T(8,128)(2,1)} %pad_maximum_fusion.1.refs_0_), channel_id=1, source_target_pairs={{0,16},{1,17},{2,18},{3,19},{4,20},{5,21},{6,22},{7,23},{8,24},{9,... | collective-permute-start | bytes 884744 | tf_op jit(solution)/shard_map/ppermute | solution.py:652
  11.6 25.3 %collective-permute-start.7 = (bf16[96,1536]{1,0:T(8,128)(2,1)}, bf16[96,1536]{1,0:T(8,128)(2,1)}, u32[]{:S(2)}, u32[]{:S(2)}) collective-permute-start(bf16[96,1536]{1,0:T(8,128)(2,1)} %pad_maximum_fusion.1.refs_0_), channel_id=1, source_target_pairs={{0,4},{1,5},{2,6},{3,7},{4,0},{5,1},{6,2},{7,3},{8,12},{9,13},{10,... | collective-permute-start | bytes 884744 | tf_op jit(solution)/shard_map/ppermute | solution.py:658
  13.2 25.3 %collective-permute-start.6 = (bf16[96,1536]{1,0:T(8,128)(2,1)}, bf16[96,1536]{1,0:T(8,128)(2,1)}, u32[]{:S(2)}, u32[]{:S(2)}) collective-permute-start(bf16[96,1536]{1,0:T(8,128)(2,1)} %pad_maximum_fusion.1.refs_0_), channel_id=1, source_target_pairs={{0,2},{1,3},{2,0},{3,1},{4,6},{5,7},{6,4},{7,5},{8,10},{9,11},{10,... | collective-permute-start | bytes 884744 | tf_op jit(solution)/shard_map/ppermute | solution.py:657
  24.4 28.2 %collective-permute-start.11 = (bf16[192,1536]{1,0:T(8,128)(2,1)}, bf16[192,1536]{1,0:T(8,128)(2,1)S(1)}, u32[]{:S(2)}, u32[]{:S(2)}) collective-permute-start(bf16[192,1536]{1,0:T(8,128)(2,1)} %constant_dynamic-update-slice_fusion.refs_5_), channel_id=1, source_target_pairs={{0,4},{1,5},{2,6},{3,7},{4,0},{5,1},{6,2},{7,3},{8,12},{9,13},{10,... | collective-permute-start | bytes 1769480 | tf_op jit(solution)/shard_map/ppermute | solution.py:658
  26.0 31.2 %collective-permute-start.10 = (bf16[192,1536]{1,0:T(8,128)(2,1)}, bf16[192,1536]{1,0:T(8,128)(2,1)S(1)}, u32[]{:S(2)}, u32[]{:S(2)}) collective-permute-start(bf16[192,1536]{1,0:T(8,128)(2,1)} %constant_dynamic-update-slice_fusion.refs_5_), channel_id=1, source_target_pairs={{0,2},{1,3},{2,0},{3,1},{4,6},{5,7},{6,4},{7,5},{8,10},{9,11},{10,... | collective-permute-start | bytes 1769480 | tf_op jit(solution)/shard_map/ppermute | solution.py:657
  36.9 49.2 %collective-permute-start.5 = (bf16[3,128,1536]{2,1,0:T(8,128)(2,1)S(1)}, bf16[3,128,1536]{2,1,0:T(8,128)(2,1)}, u32[]{:S(2)}, u32[]{:S(2)}) collective-permute-start(bf16[3,128,1536]{2,1,0:T(8,128)(2,1)S(1)} %constant_dynamic-update-slice_fusion.2), channel_id=1, source_target_pairs={{0,1},{1,0},{2,3},{3,2},{4,5},{5,4},{6,7},{7,6},{8,9},{9,8},{10,11... | collective-permute-start | bytes 3538952 | tf_op jit(solution)/shard_map/ppermute | solution.py:633
  37.0 9.6 %collective-permute-start.16 = (bf16[96,1536]{1,0:T(8,128)(2,1)}, bf16[96,1536]{1,0:T(8,128)(2,1)S(1)}, u32[]{:S(2)}, u32[]{:S(2)}) collective-permute-start(bf16[96,1536]{1,0:T(8,128)(2,1)} %collective-permute-done.14.refs_10_), channel_id=1, source_target_pairs={{0,4},{1,5},{2,6},{3,7},{4,0},{5,1},{6,2},{7,3},{8,12},{9,13},{10,... | collective-permute-start | bytes 884744 | tf_op jit(solution)/shard_map/ppermute | solution.py:658
  38.5 9.4 %collective-permute-start.15 = (bf16[96,1536]{1,0:T(8,128)(2,1)}, bf16[96,1536]{1,0:T(8,128)(2,1)}, u32[]{:S(2)}, u32[]{:S(2)}) collective-permute-start(bf16[96,1536]{1,0:T(8,128)(2,1)} %collective-permute-done.14.refs_10_), channel_id=1, source_target_pairs={{0,2},{1,3},{2,0},{3,1},{4,6},{5,7},{6,4},{7,5},{8,10},{9,11},{10,... | collective-permute-start | bytes 884744 | tf_op jit(solution)/shard_map/ppermute | solution.py:657
  46.6 13.8 %copy-start.8 = (bf16[96,1536]{1,0:T(8,128)(2,1)}, bf16[96,1536]{1,0:T(8,128)(2,1)S(1)}, u32[]{:S(2)}) copy-start(bf16[96,1536]{1,0:T(8,128)(2,1)S(1)} %collective-permute-done.16.refs_12_) | copy-start | bytes 884740
  46.6 23.4 %collective-permute-start.4 = (bf16[3,32,1536]{2,1,0:T(8,128)(2,1)}, bf16[3,32,1536]{2,1,0:T(8,128)(2,1)}, u32[]{:S(2)}, u32[]{:S(2)}) collective-permute-start(bf16[3,32,1536]{2,1,0:T(8,128)(2,1)} %slice_select_fusion), channel_id=1, source_target_pairs={{2,0},{4,2},{6,4},{8,6},{10,8},{12,10},{14,12},{16,14},{18,16},{20... | collective-permute-start | bytes 884744 | tf_op jit(solution)/shard_map/ppermute | solution.py:634
  47.9 22.1 %collective-permute-start.3 = (bf16[3,32,1536]{2,1,0:T(8,128)(2,1)}, bf16[3,32,1536]{2,1,0:T(8,128)(2,1)}, u32[]{:S(2)}, u32[]{:S(2)}) collective-permute-start(bf16[3,32,1536]{2,1,0:T(8,128)(2,1)} %slice_select_fusion), channel_id=1, source_target_pairs={{2,1},{4,3},{6,5},{8,7},{10,9},{12,11},{14,13},{16,15},{18,17},{20... | collective-permute-start | bytes 884744 | tf_op jit(solution)/shard_map/ppermute | solution.py:635
  52.7 27.4 %copy-start.4 = (bf16[192,1536]{1,0:T(8,128)(2,1)}, bf16[192,1536]{1,0:T(8,128)(2,1)S(1)}, u32[]{:S(2)}) copy-start(bf16[192,1536]{1,0:T(8,128)(2,1)S(1)} %collective-permute-done.11.refs_7_) | copy-start | bytes 1769476
  52.7 15.2 %collective-permute-start.8 = (bf16[48,1536]{1,0:T(8,128)(2,1)}, bf16[48,1536]{1,0:T(8,128)(2,1)}, u32[]{:S(2)}, u32[]{:S(2)}) collective-permute-start(bf16[48,1536]{1,0:T(8,128)(2,1)} %slice.75), channel_id=1, source_target_pairs={{0,2},{1,3},{2,0},{3,1},{4,6},{5,7},{6,4},{7,5},{8,10},{9,11},{10,... | collective-permute-start | bytes 442376 | tf_op jit(solution)/shard_map/ppermute | solution.py:663
  57.2 22.9 %copy-start.5 = (bf16[192,1536]{1,0:T(8,128)(2,1)}, bf16[192,1536]{1,0:T(8,128)(2,1)S(1)}, u32[]{:S(2)}) copy-start(bf16[192,1536]{1,0:T(8,128)(2,1)S(1)} %collective-permute-done.10.refs_6_) | copy-start | bytes 1769476
  57.2 10.7 %collective-permute-start.9 = (bf16[48,1536]{1,0:T(8,128)(2,1)S(1)}, bf16[48,1536]{1,0:T(8,128)(2,1)}, u32[]{:S(2)}, u32[]{:S(2)}) collective-permute-start(bf16[48,1536]{1,0:T(8,128)(2,1)S(1)} %slice.76), channel_id=1, source_target_pairs={{0,4},{1,5},{2,6},{3,7},{4,0},{5,1},{6,2},{7,3},{8,12},{9,13},{10,... | collective-permute-start | bytes 442376 | tf_op jit(solution)/shard_map/ppermute | solution.py:664
  67.9 6.7 %collective-permute-start.17 = (bf16[48,1536]{1,0:T(8,128)(2,1)S(1)}, bf16[48,1536]{1,0:T(8,128)(2,1)S(1)}, u32[]{:S(2)}, u32[]{:S(2)}) collective-permute-start(bf16[48,1536]{1,0:T(8,128)(2,1)S(1)} %slice.79), channel_id=1, source_target_pairs={{0,2},{1,3},{2,0},{3,1},{4,6},{5,7},{6,4},{7,5},{8,10},{9,11},{10,... | collective-permute-start | bytes 442376 | tf_op jit(solution)/shard_map/ppermute | solution.py:663
  67.9 6.7 %collective-permute-start.18 = (bf16[48,1536]{1,0:T(8,128)(2,1)S(1)}, bf16[48,1536]{1,0:T(8,128)(2,1)S(1)}, u32[]{:S(2)}, u32[]{:S(2)}) collective-permute-start(bf16[48,1536]{1,0:T(8,128)(2,1)S(1)} %slice.80), channel_id=1, source_target_pairs={{0,4},{1,5},{2,6},{3,7},{4,0},{5,1},{6,2},{7,3},{8,12},{9,13},{10,... | collective-permute-start | bytes 442376 | tf_op jit(solution)/shard_map/ppermute | solution.py:664
  70.0 9.9 %collective-permute-start.12 = (bf16[96,1536]{1,0:T(8,128)(2,1)S(1)}, bf16[96,1536]{1,0:T(8,128)(2,1)S(1)}, u32[]{:S(2)}, u32[]{:S(2)}) collective-permute-start(bf16[96,1536]{1,0:T(8,128)(2,1)S(1)} %slice.77), channel_id=1, source_target_pairs={{0,2},{1,3},{2,0},{3,1},{4,6},{5,7},{6,4},{7,5},{8,10},{9,11},{10,... | collective-permute-start | bytes 884744 | tf_op jit(solution)/shard_map/ppermute | solution.py:663
  70.0 10.0 %collective-permute-start.13 = (bf16[96,1536]{1,0:T(8,128)(2,1)S(1)}, bf16[96,1536]{1,0:T(8,128)(2,1)S(1)}, u32[]{:S(2)}, u32[]{:S(2)}) collective-permute-start(bf16[96,1536]{1,0:T(8,128)(2,1)S(1)} %slice.78), channel_id=1, source_target_pairs={{0,4},{1,5},{2,6},{3,7},{4,0},{5,1},{6,2},{7,3},{8,12},{9,13},{10,... | collective-permute-start | bytes 884744 | tf_op jit(solution)/shard_map/ppermute | solution.py:664
  74.6 5.4 %copy-start.17 = (bf16[48,1536]{1,0:T(8,128)(2,1)}, bf16[48,1536]{1,0:T(8,128)(2,1)S(1)}, u32[]{:S(2)}) copy-start(bf16[48,1536]{1,0:T(8,128)(2,1)S(1)} %collective-permute-done.17.refs_13_) | copy-start | bytes 442372
  74.6 5.4 %copy-start.18 = (bf16[48,1536]{1,0:T(8,128)(2,1)}, bf16[48,1536]{1,0:T(8,128)(2,1)S(1)}, u32[]{:S(2)}) copy-start(bf16[48,1536]{1,0:T(8,128)(2,1)S(1)} %collective-permute-done.18.refs_14_) | copy-start | bytes 442372
  79.9 0.7 copy-start.12
  80.6 0.7 copy-start.13
  87.6 1.0 copy-start
  87.6 1.4 copy-start.1
  90.0 1.5 copy-start.11
  100.3 11.8 %all-to-all-start = ((f32[16,2,768]{2,1,0:T(2,128)}), f32[16,2,768]{2,1,0:T(2,128)}, u32[]{:S(2)}, u32[]{:S(2)}) async-start(f32[16,2,768]{2,1,0:T(2,128)} %get-tuple-element.44), calls=%async_computation | async-start | bytes 196608 | tf_op jit(solution)/shard_map/all_to_all | solution.py:639
  136.2 2.6 %collective-permute-start.19 = (f32[128,1536]{1,0:T(8,128)}, f32[128,1536]{1,0:T(8,128)S(1)}, u32[]{:S(2)}, u32[]{:S(2)}) collective-permute-start(f32[128,1536]{1,0:T(8,128)} %get-tuple-element.53), channel_id=1, source_target_pairs={{0,1},{1,0},{2,3},{3,2},{4,5},{5,4},{6,7},{7,6},{8,9},{9,8},{10,11... | collective-permute-start | bytes 2359304 | tf_op jit(solution)/shard_map/ppermute | solution.py:711
  138.7 0.9 copy-start.6
  142.9 15.4 %collective-permute-start.20 = (f32[128,1536]{1,0:T(8,128)}, f32[128,1536]{1,0:T(8,128)}, u32[]{:S(2)}, u32[]{:S(2)}) collective-permute-start(f32[128,1536]{1,0:T(8,128)} %get-tuple-element.58.mine), channel_id=1, source_target_pairs={{0,1},{1,0},{2,3},{3,2},{4,5},{5,4},{6,7},{7,6},{8,9},{9,8},{10,11... | collective-permute-start | bytes 2359304 | tf_op jit(solution)/shard_map/ppermute | solution.py:633
  143.0 15.2 %collective-permute-start.22 = (f32[32,1536]{1,0:T(8,128)}, f32[32,1536]{1,0:T(8,128)S(1)}, u32[]{:S(2)}, u32[]{:S(2)}) collective-permute-start(f32[32,1536]{1,0:T(8,128)} %get-tuple-element.59), channel_id=1, source_target_pairs={{2,1},{4,3},{6,5},{8,7},{10,9},{12,11},{14,13},{16,15},{18,17},{20... | collective-permute-start | bytes 589832 | tf_op jit(solution)/shard_map/ppermute | solution.py:635
  143.7 14.6 %collective-permute-start.21 = (f32[32,1536]{1,0:T(8,128)}, f32[32,1536]{1,0:T(8,128)S(1)}, u32[]{:S(2)}, u32[]{:S(2)}) collective-permute-start(f32[32,1536]{1,0:T(8,128)} %get-tuple-element.59), channel_id=1, source_target_pairs={{2,0},{4,2},{6,4},{8,6},{10,8},{12,10},{14,12},{16,14},{18,16},{20... | collective-permute-start | bytes 589832 | tf_op jit(solution)/shard_map/ppermute | solution.py:634
  145.0 13.2 %all-to-all-start.2 = ((f32[32,1,128]{2,1,0:T(1,128)}), f32[32,1,128]{2,1,0:T(1,128)S(1)}, u32[]{:S(2)}, u32[]{:S(2)}) async-start(f32[32,1,128]{2,1,0:T(1,128)} %get-tuple-element.54), calls=%async_computation.2 | async-start | bytes 32768 | tf_op jit(solution)/shard_map/all_to_all | solution.py:713
  158.2 0.7 copy-start.14
  158.2 0.7 copy-start.15
  171.1 13.8 %all-to-all-start.3 = ((f32[16,2,768]{2,1,0:T(2,128)}), f32[16,2,768]{2,1,0:T(2,128)S(1)}, u32[]{:S(2)}, u32[]{:S(2)}) async-start(f32[16,2,768]{2,1,0:T(2,128)} %get-tuple-element.62.stats.local_stats), calls=%async_computation.3 | async-start | bytes 196608 | tf_op jit(solution)/shard_map/all_to_all | solution.py:639
  177.3 19.5 %copy-start.22 = (f32[2,768]{1,0:T(2,128)S(1)}, f32[2,768]{1,0:T(2,128)}, u32[]{:S(2)}) copy-start(f32[2,768]{1,0:T(2,128)} %get-tuple-element.70) | copy-start | bytes 18436
  191.9 13.4 %all-to-all-start.4 = ((bf16[16,48,128]{2,1,0:T(8,128)(2,1)}), bf16[16,48,128]{2,1,0:T(8,128)(2,1)S(1)}, u32[]{:S(2)}, u32[]{:S(2)}) async-start(bf16[16,48,128]{2,1,0:T(8,128)(2,1)} %get-tuple-element.68), calls=%async_computation.4 | async-start | bytes 393216 | tf_op jit(solution)/shard_map/all_to_all | solution.py:639
  205.3 0.7 copy-start.7
  (2 other events, 1.2 us)

commit v4 on v3

--- a/solution.py
+++ b/solution.py
@@ -89,25 +89,12 @@
     spot, layer = scal[4], scal[5]
     depth = out.shape[0] // (4 * size)
 
-    def put(ref, start, stop, shift, other, first):
-        chip = lax.rem(layer - shift + depth, depth) * 4 + (spot ^ other)
-        row = pl.multiple_of(chip * size + first, 16)
-        out[pl.ds(row, stop - start), :] = ref[start:stop, :]
-
     for number, group in enumerate(shifts):
-        for other, ref in enumerate(pieces[5 * number : 5 * number + 3]):
+        for other, ref in enumerate(pieces[4 * number : 4 * number + 4]):
             for nth, shift in enumerate(group):
-                put(ref, nth * size, (nth + 1) * size, shift, other, 0)
-        at = 0
-        for ref in pieces[5 * number + 3 : 5 * number + 5]:
-            rows = ref.shape[0]
-            start = 0
-            while start < rows:
-                nth, first = (at + start) // size, (at + start) % size
-                stop = min(rows, start + size - first)
-                put(ref, start, stop, group[nth], 3, first)
-                start = stop
-            at += rows
+                chip = lax.rem(layer - shift + depth, depth) * 4 + (spot ^ other)
+                row = pl.multiple_of(chip * size, 16)
+                out[pl.ds(row, size), :] = ref[nth * size : (nth + 1) * size, :]
 
 
 def place(scal, pieces, shifts, size):
@@ -650,23 +637,22 @@
     along = {0: block}
     for k in [k for group in shifts[1:] for k in group]:
         along[k] = lax.ppermute(block, "tm", [(i, (i + 8 * k) % shards) for i in range(shards)])
-    pieces = []
-    for group in shifts:
+    corner = [(i, i ^ (4 if i % 2 else 2)) for i in range(shards)]
+    pieces, relayed = [], None
+    for number, group in enumerate(shifts):
         blocks = jnp.concatenate([along[k] for k in group], axis=0)
-        cut = (blocks.shape[0] // 2 + 15) // 16 * 16
+        if number == 1:
+            blocks, relayed = lax.optimization_barrier((blocks, relayed))
+        elif number > 1:
+            blocks, _ = lax.optimization_barrier((blocks, pieces[4 * number - 5]))
         from_x = lax.ppermute(blocks, "tm", swap_x)
         from_y = lax.ppermute(blocks, "tm", swap_y)
-        pieces += [
-            blocks,
-            from_x,
-            from_y,
-            lax.ppermute(from_y[:cut], "tm", swap_x),
-            lax.ppermute(from_x[cut:], "tm", swap_y),
-        ]
-    weight = place(scal, pieces, shifts, block.shape[0])
-
+        relayed = jnp.where(first, from_y, from_x)
+        pieces += [blocks, from_x, from_y]
+        if number + 1 < len(shifts):
+            pieces.append(lax.ppermute(relayed, "tm", corner))
     features, start_noise, cotangent, kernel, bn_gain, bn_shift, _ = lax.optimization_barrier(
-        (features, start_noise, cotangent, kernel, bn_gain, bn_shift, pieces[5])
+        (features, start_noise, cotangent, kernel, bn_gain, bn_shift, pieces[4])
     )
     packed = jnp.concatenate([features, start_noise, cotangent], axis=0)
     partner, near, far = across(
@@ -700,6 +686,12 @@
     live = ((frame_ids >= 0) & (frame_ids < end)).astype(F32)
     summed = wide_features.astype(F32) + noise_scale * wide_noise.astype(F32) * live[:, None]
     normed_b = normalize(summed)[0].astype(BF16)
+
+    relayed, normed_b, taps, gain, shift = lax.optimization_barrier(
+        (relayed, normed_b, taps, gain, shift)
+    )
+    pieces.append(lax.ppermute(relayed, "tm", corner))
+    weight = place(scal, pieces, shifts, block.shape[0])
 
     value, gate, glu, conv, stats = forward(
         scal, normed_b, weight, taps, chip_rows, chips, True

time: 209 us -> 205 us (0.981)
  local copies, waits for them, and re-layouts: 17.6 us -> 13.7 us
    ppermute x3, waiting for transfers between devices: 0.06 us -> 14.9 us  [on_device(): from_x = lax.ppermute(blocks, 'tm', swap_x)]
    ppermute x6 -> x3, waiting for transfers between devices: 14.5 us -> 4.08 us  [on_device(): pieces.append(lax.ppermute(relayed, 'tm', corner))]
    ppermute x6 -> x3, starting transfers between devices: 9.38 us -> 4.27 us  [on_device(): pieces.append(lax.ppermute(relayed, 'tm', corner))]
    ppermute x3, waiting for transfers between devices: 5.83 us -> 1.47 us  [on_device(): from_y = lax.ppermute(blocks, 'tm', swap_y)]
    all_to_all x3, starting transfers between devices: 15.2 us -> 19 us  [peers_of(): lax.all_to_all(array, 'tm', 0, 0, axis_index_groups=cores, tiled=True)]
    slice x6 -> x0, local copies, waits for them, and re-layouts: 3.47 us -> none  [the longest x3 1.86 us: on_device(): from_x[cut:]]
    unnamed x49 -> x58, local copies, waits for them, and re-layouts: 6.11 us -> 5.59 us
  transfers between devices with their start and end apart: 27 -> 24, of which waited for: 14 -> 14; matrix products, arithmetic and copies ran while one was open for 8% -> 9% of each run, Pallas kernels for 7% -> 5%
where the time goes in v4:
time: 205 us; the launch traced here: 204 us
  Pallas kernels  58.8 us (29%)
  waiting for transfers between devices  53.2 us (26%)
  starting transfers between devices  52.2 us (25%)
  local copies, waits for them, and re-layouts  13.7 us (7%)
  blocking collectives  11.8 us (6%)
  other arithmetic  9.4 us (5%)
  matrix products  2.98 us (1%)
    all_to_all x3, starting transfers between devices, peers_of(): lax.all_to_all(array, 'tm', 0, 0, axis_index_groups=cores, tiled=True)  19 us
    pallas_call x2, Pallas kernels, forward(): pl.pallas_call(functools.partial(forward_kernel, keep), grid=(steps,), in...  15.6 us
    ppermute x3, waiting for transfers between devices, on_device(): lax.ppermute(block, 'tm', [(i, (i + 8 * k) % shards) for i in range(shard...  15.1 us
    ppermute x3, waiting for transfers between devices, on_device(): from_x = lax.ppermute(blocks, 'tm', swap_x)  14.9 us
    all_to_all x3, waiting for transfers between devices, peers_of(): lax.all_to_all(array, 'tm', 0, 0, axis_index_groups=cores, tiled=True)  13.9 us
    all_to_all x1, blocking collectives, peers_of(): lax.all_to_all(array, 'tm', 0, 0, axis_index_groups=cores, tiled=True)  11.8 us
    pallas_call x1, Pallas kernels, backward(): pl.pallas_call(backward_kernel, grid=(steps,), in_specs=[pl.BlockSpec(mem...  8.23 us
    all_to_all x1, starting transfers between devices, on_device(): squares = lax.all_to_all(squares, 'tm', 0, 0, tiled=True)  6.59 us
  transfers between devices with their start and end apart: 24, of which 14 were waited for; matrix products, arithmetic and copies ran while one was open for 9% of the time, Pallas kernels for 5%

profile of v4, /device:TPU:0, one launch (start us, length us, event | category | flops | bytes accessed | tf_op | source)
XLA Modules:
  0.0 203.8 jit_solution(7057566995450953963)
XLA Ops:
  0.7 1.0 dynamic-slice_bitcast_fusion
  2.2 1.0 collective-permute-done
  3.2 0.9 bitcast_select_fusion.1
  4.8 2.9 %collective-permute-start.3 = (bf16[96,1536]{1,0:T(8,128)(2,1)}, bf16[96,1536]{1,0:T(8,128)(2,1)S(1)}, u32[]{:S(2)}, u32[]{:S(2)}) collective-permute-start(bf16[96,1536]{1,0:T(8,128)(2,1)} %pad_maximum_fusion.2.refs_0_), channel_id=1, source_target_pairs={{0,2},{1,3},{2,0},{3,1},{4,6},{5,7},{6,4},{7,5},{8,10},{9,11},{10,... | collective-permute-start | bytes 884744 | tf_op jit(solution)/shard_map/ppermute | solution.py:648
  7.7 1.5 collective-permute-start.2
  10.5 3.7 %collective-permute-start.8 = (bf16[96,1536]{1,0:T(8,128)(2,1)}, bf16[96,1536]{1,0:T(8,128)(2,1)S(1)}, u32[]{:S(2)}, u32[]{:S(2)}) collective-permute-start(bf16[96,1536]{1,0:T(8,128)(2,1)} %pad_maximum_fusion.2.refs_0_), channel_id=1, source_target_pairs={{0,24},{1,25},{2,26},{3,27},{4,28},{5,29},{6,30},{7,31},{8,0},{9,1... | collective-permute-start | bytes 884744 | tf_op jit(solution)/shard_map/ppermute | solution.py:639
  14.1 1.0 collective-permute-start.1
  15.2 1.5 collective-permute-done.2.refs_2_
  17.9 4.0 %collective-permute-done.8 = bf16[96,1536]{1,0:T(8,128)(2,1)S(1)} collective-permute-done((bf16[96,1536]{1,0:T(8,128)(2,1)}, bf16[96,1536]{1,0:T(8,128)(2,1)S(1)}, u32[]{:S(2)}, u32[]{:S(2)}) %collective-permute-start.8) | collective-permute-done | bytes 294944 | tf_op jit(solution)/shard_map/ppermute | solution.py:639
  21.9 7.2 %collective-permute-done.7 = bf16[96,1536]{1,0:T(8,128)(2,1)S(1)} collective-permute-done((bf16[96,1536]{1,0:T(8,128)(2,1)}, bf16[96,1536]{1,0:T(8,128)(2,1)S(1)}, u32[]{:S(2)}, u32[]{:S(2)}) %collective-permute-start.7) | collective-permute-done | bytes 294944 | tf_op jit(solution)/shard_map/ppermute | solution.py:639
  29.9 1.0 constant_dynamic-update-slice_fusion
  31.6 1.3 collective-permute-start.10
  32.9 1.4 collective-permute-start.9
  35.5 3.9 %collective-permute-done.1.refs_8_ = bf16[96,1536]{1,0:T(8,128)(2,1)} collective-permute-done((bf16[96,1536]{1,0:T(8,128)(2,1)}, bf16[96,1536]{1,0:T(8,128)(2,1)}, u32[]{:S(2)}, u32[]{:S(2)}) %collective-permute-start.1) | collective-permute-done | bytes 294944 | tf_op jit(solution)/shard_map/ppermute | solution.py:639
  42.2 1.4 collective-permute-start.6
  43.6 4.4 %collective-permute-start.5 = (bf16[96,1536]{1,0:T(8,128)(2,1)}, bf16[96,1536]{1,0:T(8,128)(2,1)S(1)}, u32[]{:S(2)}, u32[]{:S(2)}) collective-permute-start(bf16[96,1536]{1,0:T(8,128)(2,1)} %collective-permute-done.1.refs_8_), channel_id=1, source_target_pairs={{0,4},{1,5},{2,6},{3,7},{4,0},{5,1},{6,2},{7,3},{8,12},{9,13},{10,... | collective-permute-start | bytes 884744 | tf_op jit(solution)/shard_map/ppermute | solution.py:649
  48.0 1.1 broadcast_select_fusion.4
  49.2 10.8 %collective-permute-done.12.refs_5_ = bf16[192,1536]{1,0:T(8,128)(2,1)S(1)} collective-permute-done((bf16[192,1536]{1,0:T(8,128)(2,1)S(1)}, bf16[192,1536]{1,0:T(8,128)(2,1)S(1)}, u32[]{:S(2)}, u32[]{:S(2)}) %collective-permute-start.12) | collective-permute-done | bytes 589856 | tf_op jit(solution)/shard_map/ppermute | solution.py:648
  60.0 1.8 collective-permute-start.14
  61.8 4.1 %collective-permute-done.6.refs_9_ = bf16[96,1536]{1,0:T(8,128)(2,1)S(1)} collective-permute-done((bf16[96,1536]{1,0:T(8,128)(2,1)}, bf16[96,1536]{1,0:T(8,128)(2,1)S(1)}, u32[]{:S(2)}, u32[]{:S(2)}) %collective-permute-start.6) | collective-permute-done | bytes 294944 | tf_op jit(solution)/shard_map/ppermute | solution.py:648
  69.3 1.5 multiply_convert_fusion.nb
  70.8 1.0 broadcast_in_dim.9.taps
  71.7 2.1 %collective-permute-start.15 = (bf16[96,1536]{1,0:T(8,128)(2,1)S(1)}, bf16[96,1536]{1,0:T(8,128)(2,1)S(1)}, u32[]{:S(2)}, u32[]{:S(2)}) collective-permute-start(bf16[96,1536]{1,0:T(8,128)(2,1)S(1)} %broadcast_select_fusion.5), channel_id=1, source_target_pairs={{0,2},{1,5},{2,0},{3,7},{4,6},{5,1},{6,4},{7,3},{8,10},{9,13},{10,... | collective-permute-start | bytes 884744 | tf_op jit(solution)/shard_map/ppermute | solution.py:693
  74.5 4.1 %collective-permute-done.15.refs_11_ = bf16[96,1536]{1,0:T(8,128)(2,1)S(1)} collective-permute-done((bf16[96,1536]{1,0:T(8,128)(2,1)S(1)}, bf16[96,1536]{1,0:T(8,128)(2,1)S(1)}, u32[]{:S(2)}, u32[]{:S(2)}) %collective-permute-start.15) | collective-permute-done | bytes 294944 | tf_op jit(solution)/shard_map/ppermute | solution.py:693
  79.3 4.8 %place_weights.1.value_w.gate_w = bf16[1536,1536]{1,0:T(8,128)(2,1)} custom-call(s32[6]{0:T(128)} %stack.26.scal, bf16[96,1536]{1,0:T(8,128)(2,1)} %pad_maximum_fusion.2.refs_0_, bf16[96,1536]{1,0:T(8,128)(2,1)} %copy-done.7, bf16[96,1536]{1,0:T(8,128)(2,1)} %copy-done.8, bf16[96,1536]{1,0:T(8,128)(2,1)} %collective-permute-done.4.refs_3_, ...), custom_call_target="tpu_custom_call" | custom-call | bytes 9437184 | tf_op jit(solution)/shard_map/place_weights/pallas_call | solution.py:104
  84.1 7.9 %project_glu_conv.2 = (f32[256,768]{1,0:T(8,128)}, f32[256,768]{1,0:T(8,128)}, bf16[320,768]{1,0:T(8,128)(2,1)}, f32[288,768]{1,0:T(8,128)}, f32[16,2,768]{2,1,0:T(2,128)}) custom-call(s32[6]{0:T(128)} %stack.26.scal, bf16[320,1536]{1,0:T(8,128)(2,1)} %multiply_convert_fusion.nb, bf16[1536,1536]{1,0:T(8,128)(2,1)} %place_weights.1.value_w.gate_w, ...), custom_call_target="tpu_custom_call" | custom-call | flops 1509949440 | bytes 7176192 | tf_op jit(solution)/shard_map/project_glu_conv/pallas_call | solution.py:146
  92.0 8.0 %all-to-all-start = ((f32[16,2,768]{2,1,0:T(2,128)}), f32[16,2,768]{2,1,0:T(2,128)}, u32[]{:S(2)}, u32[]{:S(2)}) async-start(f32[16,2,768]{2,1,0:T(2,128)} %get-tuple-element.56), calls=%async_computation | async-start | bytes 196608 | tf_op jit(solution)/shard_map/all_to_all | solution.py:626
  99.9 3.0 %fusion.3.cot = bf16[288,768]{1,0:T(8,128)(2,1)} fusion(s32[768]{0:T(1024)S(1)} %fusion.21, bf16[3,32,1536]{2,1,0:T(8,128)(2,1)S(1)} %copy-done.14, bf16[3,128,1536]{2,1,0:T(8,128)(2,1)} %copy-done.1, bf16[3,128,1536]{2,1,0:T(8,128)(2,1)} %copy-done, bf16[3,32,1536]{2,1,0:T(8,128)(2,1)S(1)} %copy-done.12), kind=kOutput, calls=%fused_computation.8 | convolution fusion | flops 684417024 | bytes 3394560 | tf_op jit(solution)/shard_map/dot_general | solution.py:675
  102.9 4.7 %all-to-all-done.stats = f32[16,2,768]{2,1,0:T(2,128)} async-done(((f32[16,2,768]{2,1,0:T(2,128)}), f32[16,2,768]{2,1,0:T(2,128)}, u32[]{:S(2)}, u32[]{:S(2)}) %all-to-all-start) | async-done | bytes 98336 | tf_op jit(solution)/shard_map/all_to_all | solution.py:626
  107.7 3.9 %batch_norm_swish.1 = (f32[288,768]{1,0:T(8,128)}, f32[288,768]{1,0:T(8,128)}, f32[1,768]{1,0:T(1,128)}, f32[16,2,768]{2,1,0:T(2,128)}) custom-call(s32[6]{0:T(128)} %stack.26.scal, f32[2,16]{1,0:T(2,128)} %pad_maximum_fusion.3.counts, f32[16,2,768]{2,1,0:T(2,128)} %all-to-all-done.stats, f32[288,768]{1,0:T(8,128)} %get-tuple-element.57.conv, ...), custom_call_target="tpu_custom_call" | custom-call | flops 8847360 | bytes 3538944 | tf_op jit(solution)/shard_map/batch_norm_swish/pallas_call | solution.py:226
  111.6 11.8 %all_to_all.25.sums = f32[16,2,768]{2,1,0:T(2,128)} all-to-all(f32[16,2,768]{2,1,0:T(2,128)} %get-tuple-element.60), channel_id=1, replica_groups={{0,2,4,6,8,10,12,14,16,18,20,22,24,26,28,30},{1,3,5,7,9,11,13,15,17,19,..., dimensions={0} | all-to-all | bytes 196608 | tf_op jit(solution)/shard_map/all_to_all | solution.py:626
  123.4 8.2 %grad_conv_project_back.1 = (f32[128,1536]{1,0:T(8,128)}, f32[128,1536]{1,0:T(8,128)}, bf16[256,768]{1,0:T(8,128)(2,1)}, f32[2,768]{1,0:T(2,128)}) custom-call(s32[6]{0:T(128)} %stack.26.scal, f32[16,2,768]{2,1,0:T(2,128)} %all_to_all.25.sums, f32[288,768]{1,0:T(8,128)} %get-tuple-element.61.scaled, f32[288,768]{1,0:T(8,128)} %get-tuple-element.62.grad, ...), custom_call_target="tpu_custom_call" | custom-call | flops 1207959552 | bytes 9142272 | tf_op jit(solution)/shard_map/grad_conv_project_back/pallas_call | solution.py:301
  132.3 2.1 %collective-permute-done.16.other = f32[128,1536]{1,0:T(8,128)S(1)} collective-permute-done((f32[128,1536]{1,0:T(8,128)}, f32[128,1536]{1,0:T(8,128)S(1)}, u32[]{:S(2)}, u32[]{:S(2)}) %collective-permute-start.16) | collective-permute-done | bytes 786464 | tf_op jit(solution)/shard_map/ppermute | solution.py:703
  135.3 3.2 %direction.1 = (f32[128,1536]{1,0:T(8,128)}, f32[32,1536]{1,0:T(8,128)}, f32[32,1,128]{2,1,0:T(1,128)}) custom-call(s32[6]{0:T(128)} %stack.26.scal, f32[128,1536]{1,0:T(8,128)} %get-tuple-element.66.mine, f32[128,1536]{1,0:T(8,128)} %copy-done.15, bf16[128,1536]{1,0:T(8,128)(2,1)} %bitcast.50, bf16[128,1536]{1,0:T(8,128)(2,1)} %bitcast.48), custom_call_target="tpu_custom_call" | custom-call | flops 5898240 | bytes 3145728 | tf_op jit(solution)/shard_map/direction/pallas_call | solution.py:531
  139.5 1.3 collective-permute-start.18
  140.8 6.6 %all-to-all-start.2 = ((f32[32,1,128]{2,1,0:T(1,128)}), f32[32,1,128]{2,1,0:T(1,128)S(1)}, u32[]{:S(2)}, u32[]{:S(2)}) async-start(f32[32,1,128]{2,1,0:T(1,128)} %get-tuple-element.68), calls=%async_computation.2 | async-start | bytes 32768 | tf_op jit(solution)/shard_map/all_to_all | solution.py:705
  147.4 1.4 slice_bitcast_fusion
  148.8 4.9 %tap_grad.1.taps_before = f32[31,768]{1,0:T(8,128)} custom-call(bf16[256,768]{1,0:T(8,128)(2,1)} %get-tuple-element.69.grad_conv, bf16[320,768]{1,0:T(8,128)(2,1)} %get-tuple-element.70.glu), custom_call_target="tpu_custom_call" | custom-call | flops 12189696 | bytes 983040 | tf_op jit(solution)/shard_map/tap_grad/pallas_call | solution.py:349
  155.1 4.5 %ascend.1 = (f32[128,1536]{1,0:T(8,128)}, bf16[320,1536]{1,0:T(8,128)(2,1)}) custom-call(s32[6]{0:T(128)} %stack.26.scal, f32[32,1,128]{2,1,0:T(1,128)} %copy-done.24, bf16[320,1536]{1,0:T(8,128)(2,1)} %get-tuple-element.88.features, bf16[320,1536]{1,0:T(8,128)(2,1)} %get-tuple-element.87.noise, f32[128,1536]{1,0:T(8,128)} %get-tuple-element.72.mine, ...), custom_call_target="tpu_custom_call" | custom-call | flops 14745600 | bytes 3932160 | tf_op jit(solution)/shard_map/ascend/pallas_call | solution.py:575
  159.6 7.7 %project_glu_conv.3 = (bf16[320,768]{1,0:T(8,128)(2,1)}, f32[288,768]{1,0:T(8,128)}, f32[16,2,768]{2,1,0:T(2,128)}) custom-call(s32[6]{0:T(128)} %stack.26.scal, bf16[320,1536]{1,0:T(8,128)(2,1)} %get-tuple-element.75.nb, bf16[1536,1536]{1,0:T(8,128)(2,1)} %place_weights.1.value_w.gate_w, bf16[1536,1536]{1,0:T(8,128)(2,1)} %place_weights.1.value_w.gate_w, ...), custom_call_target="tpu_custom_call" | custom-call | flops 1509949440 | bytes 7176192 | tf_op jit(solution)/shard_map/project_glu_conv/pallas_call | solution.py:146
  167.3 6.1 %all-to-all-start.3 = ((f32[16,2,768]{2,1,0:T(2,128)}), f32[16,2,768]{2,1,0:T(2,128)S(1)}, u32[]{:S(2)}, u32[]{:S(2)}) async-start(f32[16,2,768]{2,1,0:T(2,128)} %get-tuple-element.76.stats.local_stats), calls=%async_computation.3 | async-start | bytes 196608 | tf_op jit(solution)/shard_map/all_to_all | solution.py:626
  173.4 5.6 %raw_taps.1 = (f32[31,768]{1,0:T(8,128)}, f32[31,768]{1,0:T(8,128)}) custom-call(s32[6]{0:T(128)} %stack.26.scal, f32[288,768]{1,0:T(8,128)} %get-tuple-element.77.conv, bf16[320,768]{1,0:T(8,128)(2,1)} %get-tuple-element.78.glu, f32[16,2,768]{2,1,0:T(2,128)} %get-tuple-element.76.stats.local_stats), custom_call_target="tpu_custom_call" | custom-call | flops 13713408 | bytes 1966080 | tf_op jit(solution)/shard_map/raw_taps/pallas_call | solution.py:382
  179.1 2.0 all-to-all-done.3.stats
  181.7 6.3 %batch_norm_swish_taps.1 = (bf16[16,48,128]{2,1,0:T(8,128)(2,1)}, f32[1,768]{1,0:T(1,128)}) custom-call(s32[6]{0:T(128)} %stack.26.scal, f32[2,16]{1,0:T(2,128)} %pad_maximum_fusion.3.counts, f32[16,2,768]{2,1,0:T(2,128)} %copy-done.18, f32[288,768]{1,0:T(8,128)} %get-tuple-element.77.conv, bf16[288,768]{1,0:T(8,128)(2,1)} %fusion.3.cot, ...), custom_call_target="tpu_custom_call" | custom-call | flops 22118400 | bytes 2211840 | tf_op jit(solution)/shard_map/batch_norm_swish_taps/pallas_call | solution.py:442
  188.1 4.9 %all-to-all-start.4 = ((bf16[16,48,128]{2,1,0:T(8,128)(2,1)}), bf16[16,48,128]{2,1,0:T(8,128)(2,1)S(1)}, u32[]{:S(2)}, u32[]{:S(2)}) async-start(bf16[16,48,128]{2,1,0:T(8,128)(2,1)} %get-tuple-element.82), calls=%async_computation.4 | async-start | bytes 393216 | tf_op jit(solution)/shard_map/all_to_all | solution.py:626
  193.0 1.3 fusion.23.known
  194.3 7.2 %all-to-all-done.4.received = bf16[16,48,128]{2,1,0:T(8,128)(2,1)S(1)} async-done(((bf16[16,48,128]{2,1,0:T(8,128)(2,1)}), bf16[16,48,128]{2,1,0:T(8,128)(2,1)S(1)}, u32[]{:S(2)}, u32[]{:S(2)}) %all-to-all-start.4) | async-done | bytes 196640 | tf_op jit(solution)/shard_map/all_to_all | solution.py:626
  202.2 1.7 finish.1
  (109 shorter events, 18.5 us)
Async XLA Ops:
  0.6 29.2 %copy-start.6 = (bf16[1,128,1536]{2,1,0:T(8,128)(2,1)S(1)}, bf16[1,128,1536]{2,1,0:T(8,128)(2,1)}, u32[]{:S(2)}) copy-start(bf16[1,128,1536]{2,1,0:T(8,128)(2,1)} %param.8) | copy-start | bytes 1179652
  1.6 1.5 collective-permute-start
  2.2 27.7 %copy-start.2 = (bf16[1,128,1536]{2,1,0:T(8,128)(2,1)S(1)}, bf16[1,128,1536]{2,1,0:T(8,128)(2,1)}, u32[]{:S(2)}) copy-start(bf16[1,128,1536]{2,1,0:T(8,128)(2,1)} %param.9) | copy-start | bytes 1179652
  4.8 10.4 %collective-permute-start.3 = (bf16[96,1536]{1,0:T(8,128)(2,1)}, bf16[96,1536]{1,0:T(8,128)(2,1)S(1)}, u32[]{:S(2)}, u32[]{:S(2)}) collective-permute-start(bf16[96,1536]{1,0:T(8,128)(2,1)} %pad_maximum_fusion.2.refs_0_), channel_id=1, source_target_pairs={{0,2},{1,3},{2,0},{3,1},{4,6},{5,7},{6,4},{7,5},{8,10},{9,11},{10,... | collective-permute-start | bytes 884744 | tf_op jit(solution)/shard_map/ppermute | solution.py:648
  7.7 9.0 %collective-permute-start.2 = (bf16[96,1536]{1,0:T(8,128)(2,1)}, bf16[96,1536]{1,0:T(8,128)(2,1)S(1)}, u32[]{:S(2)}, u32[]{:S(2)}) collective-permute-start(bf16[96,1536]{1,0:T(8,128)(2,1)} %pad_maximum_fusion.2.refs_0_), channel_id=1, source_target_pairs={{0,4},{1,5},{2,6},{3,7},{4,0},{5,1},{6,2},{7,3},{8,12},{9,13},{10,... | collective-permute-start | bytes 884744 | tf_op jit(solution)/shard_map/ppermute | solution.py:649
  10.5 11.4 %collective-permute-start.8 = (bf16[96,1536]{1,0:T(8,128)(2,1)}, bf16[96,1536]{1,0:T(8,128)(2,1)S(1)}, u32[]{:S(2)}, u32[]{:S(2)}) collective-permute-start(bf16[96,1536]{1,0:T(8,128)(2,1)} %pad_maximum_fusion.2.refs_0_), channel_id=1, source_target_pairs={{0,24},{1,25},{2,26},{3,27},{4,28},{5,29},{6,30},{7,31},{8,0},{9,1... | collective-permute-start | bytes 884744 | tf_op jit(solution)/shard_map/ppermute | solution.py:639
  14.1 15.0 %collective-permute-start.7 = (bf16[96,1536]{1,0:T(8,128)(2,1)}, bf16[96,1536]{1,0:T(8,128)(2,1)S(1)}, u32[]{:S(2)}, u32[]{:S(2)}) collective-permute-start(bf16[96,1536]{1,0:T(8,128)(2,1)} %pad_maximum_fusion.2.refs_0_), channel_id=1, source_target_pairs={{0,8},{1,9},{2,10},{3,11},{4,12},{5,13},{6,14},{7,15},{8,16},{9,17... | collective-permute-start | bytes 884744 | tf_op jit(solution)/shard_map/ppermute | solution.py:639
  14.1 25.2 %collective-permute-start.1 = (bf16[96,1536]{1,0:T(8,128)(2,1)}, bf16[96,1536]{1,0:T(8,128)(2,1)}, u32[]{:S(2)}, u32[]{:S(2)}) collective-permute-start(bf16[96,1536]{1,0:T(8,128)(2,1)} %pad_maximum_fusion.2.refs_0_), channel_id=1, source_target_pairs={{0,16},{1,17},{2,18},{3,19},{4,20},{5,21},{6,22},{7,23},{8,24},{9,... | collective-permute-start | bytes 884744 | tf_op jit(solution)/shard_map/ppermute | solution.py:639
  15.2 14.0 %copy-start.7 = (bf16[96,1536]{1,0:T(8,128)(2,1)}, bf16[96,1536]{1,0:T(8,128)(2,1)S(1)}, u32[]{:S(2)}) copy-start(bf16[96,1536]{1,0:T(8,128)(2,1)S(1)} %collective-permute-done.3.refs_1_) | copy-start | bytes 884740
  16.7 12.5 %copy-start.8 = (bf16[96,1536]{1,0:T(8,128)(2,1)}, bf16[96,1536]{1,0:T(8,128)(2,1)S(1)}, u32[]{:S(2)}) copy-start(bf16[96,1536]{1,0:T(8,128)(2,1)S(1)} %collective-permute-done.2.refs_2_) | copy-start | bytes 884740
  17.5 16.8 %copy-start.25 = (f32[1536]{0:T(1024)S(1)}, f32[1536]{0:T(1024)}, u32[]{:S(2)}) copy-start(f32[1536]{0:T(1024)} %param.13) | copy-start | bytes 18436
  17.5 16.9 %copy-start.26 = (f32[1536]{0:T(1024)S(1)}, f32[1536]{0:T(1024)}, u32[]{:S(2)}) copy-start(f32[1536]{0:T(1024)} %param.14) | copy-start | bytes 18436
  17.5 24.5 %collective-permute-start.4 = (bf16[96,1536]{1,0:T(8,128)(2,1)}, bf16[96,1536]{1,0:T(8,128)(2,1)}, u32[]{:S(2)}, u32[]{:S(2)}) collective-permute-start(bf16[96,1536]{1,0:T(8,128)(2,1)} %broadcast_select_fusion.6), channel_id=1, source_target_pairs={{0,2},{1,5},{2,0},{3,7},{4,6},{5,1},{6,4},{7,3},{8,10},{9,13},{10,... | collective-permute-start | bytes 884744 | tf_op jit(solution)/shard_map/ppermute | solution.py:653
  29.2 10.1 %copy-start.3 = (bf16[192,1536]{1,0:T(8,128)(2,1)}, bf16[192,1536]{1,0:T(8,128)(2,1)S(1)}, u32[]{:S(2)}) copy-start(bf16[192,1536]{1,0:T(8,128)(2,1)S(1)} %pad_maximum_fusion.1.refs_4_) | copy-start | bytes 1769476
  29.2 5.3 %copy-start.23 = (f32[31,1536]{1,0:T(8,128)S(1)}, f32[31,1536]{1,0:T(8,128)}, u32[]{:S(2)}) copy-start(f32[31,1536]{1,0:T(8,128)} %param.12) | copy-start | bytes 571396
  29.2 19.9 %collective-permute-start.13 = (bf16[192,1536]{1,0:T(8,128)(2,1)S(1)}, bf16[192,1536]{1,0:T(8,128)(2,1)S(1)}, u32[]{:S(2)}, u32[]{:S(2)}) collective-permute-start(bf16[192,1536]{1,0:T(8,128)(2,1)S(1)} %pad_maximum_fusion.1.refs_4_), channel_id=1, source_target_pairs={{0,4},{1,5},{2,6},{3,7},{4,0},{5,1},{6,2},{7,3},{8,12},{9,13},{10,... | collective-permute-start | bytes 1769480 | tf_op jit(solution)/shard_map/ppermute | solution.py:649
  31.6 10.5 %collective-permute-start.10 = (bf16[3,32,1536]{2,1,0:T(8,128)(2,1)}, bf16[3,32,1536]{2,1,0:T(8,128)(2,1)}, u32[]{:S(2)}, u32[]{:S(2)}) collective-permute-start(bf16[3,32,1536]{2,1,0:T(8,128)(2,1)} %slice_select_fusion), channel_id=1, source_target_pairs={{2,0},{4,2},{6,4},{8,6},{10,8},{12,10},{14,12},{16,14},{18,16},{20... | collective-permute-start | bytes 884744 | tf_op jit(solution)/shard_map/ppermute | solution.py:621
  32.9 10.7 %collective-permute-start.9 = (bf16[3,32,1536]{2,1,0:T(8,128)(2,1)}, bf16[3,32,1536]{2,1,0:T(8,128)(2,1)}, u32[]{:S(2)}, u32[]{:S(2)}) collective-permute-start(bf16[3,32,1536]{2,1,0:T(8,128)(2,1)} %slice_select_fusion), channel_id=1, source_target_pairs={{2,1},{4,3},{6,5},{8,7},{10,9},{12,11},{14,13},{16,15},{18,17},{20... | collective-permute-start | bytes 884744 | tf_op jit(solution)/shard_map/ppermute | solution.py:622
  39.3 20.6 %collective-permute-start.12 = (bf16[192,1536]{1,0:T(8,128)(2,1)S(1)}, bf16[192,1536]{1,0:T(8,128)(2,1)S(1)}, u32[]{:S(2)}, u32[]{:S(2)}) collective-permute-start(bf16[192,1536]{1,0:T(8,128)(2,1)S(1)} %pad_maximum_fusion.1.refs_4_), channel_id=1, source_target_pairs={{0,2},{1,3},{2,0},{3,1},{4,6},{5,7},{6,4},{7,5},{8,10},{9,11},{10,... | collective-permute-start | bytes 1769480 | tf_op jit(solution)/shard_map/ppermute | solution.py:648
  42.0 23.9 %collective-permute-start.11 = (bf16[3,128,1536]{2,1,0:T(8,128)(2,1)S(1)}, bf16[3,128,1536]{2,1,0:T(8,128)(2,1)S(1)}, u32[]{:S(2)}, u32[]{:S(2)}) collective-permute-start(bf16[3,128,1536]{2,1,0:T(8,128)(2,1)S(1)} %constant_dynamic-update-slice_fusion), channel_id=1, source_target_pairs={{0,1},{1,0},{2,3},{3,2},{4,5},{5,4},{6,7},{7,6},{8,9},{9,8},{10,11... | collective-permute-start | bytes 3538952 | tf_op jit(solution)/shard_map/ppermute | solution.py:620
  42.2 23.7 %collective-permute-start.6 = (bf16[96,1536]{1,0:T(8,128)(2,1)}, bf16[96,1536]{1,0:T(8,128)(2,1)S(1)}, u32[]{:S(2)}, u32[]{:S(2)}) collective-permute-start(bf16[96,1536]{1,0:T(8,128)(2,1)} %collective-permute-done.1.refs_8_), channel_id=1, source_target_pairs={{0,2},{1,3},{2,0},{3,1},{4,6},{5,7},{6,4},{7,5},{8,10},{9,11},{10,... | collective-permute-start | bytes 884744 | tf_op jit(solution)/shard_map/ppermute | solution.py:648
  43.6 22.3 %collective-permute-start.5 = (bf16[96,1536]{1,0:T(8,128)(2,1)}, bf16[96,1536]{1,0:T(8,128)(2,1)S(1)}, u32[]{:S(2)}, u32[]{:S(2)}) collective-permute-start(bf16[96,1536]{1,0:T(8,128)(2,1)} %collective-permute-done.1.refs_8_), channel_id=1, source_target_pairs={{0,4},{1,5},{2,6},{3,7},{4,0},{5,1},{6,2},{7,3},{8,12},{9,13},{10,... | collective-permute-start | bytes 884744 | tf_op jit(solution)/shard_map/ppermute | solution.py:649
  49.1 17.6 %copy-start.11 = (bf16[3,32,1536]{2,1,0:T(8,128)(2,1)}, bf16[3,32,1536]{2,1,0:T(8,128)(2,1)S(1)}, u32[]{:S(2)}) copy-start(bf16[3,32,1536]{2,1,0:T(8,128)(2,1)S(1)} %get-tuple-element.91) | copy-start | bytes 884740
  49.1 17.6 %copy-start.13 = (bf16[3,32,1536]{2,1,0:T(8,128)(2,1)}, bf16[3,32,1536]{2,1,0:T(8,128)(2,1)S(1)}, u32[]{:S(2)}) copy-start(bf16[3,32,1536]{2,1,0:T(8,128)(2,1)S(1)} %get-tuple-element.92) | copy-start | bytes 884740
  49.1 16.9 %copy-start.4 = (bf16[192,1536]{1,0:T(8,128)(2,1)}, bf16[192,1536]{1,0:T(8,128)(2,1)S(1)}, u32[]{:S(2)}) copy-start(bf16[192,1536]{1,0:T(8,128)(2,1)S(1)} %collective-permute-done.13.refs_6_) | copy-start | bytes 1769476
  59.9 6.1 %copy-start.5 = (bf16[192,1536]{1,0:T(8,128)(2,1)}, bf16[192,1536]{1,0:T(8,128)(2,1)S(1)}, u32[]{:S(2)}) copy-start(bf16[192,1536]{1,0:T(8,128)(2,1)S(1)} %collective-permute-done.12.refs_5_) | copy-start | bytes 1769476
  60.0 14.5 %collective-permute-start.14 = (bf16[192,1536]{1,0:T(8,128)(2,1)S(1)}, bf16[192,1536]{1,0:T(8,128)(2,1)S(1)}, u32[]{:S(2)}, u32[]{:S(2)}) collective-permute-start(bf16[192,1536]{1,0:T(8,128)(2,1)S(1)} %broadcast_select_fusion.2), channel_id=1, source_target_pairs={{0,2},{1,5},{2,0},{3,7},{4,6},{5,1},{6,4},{7,3},{8,10},{9,13},{10,... | collective-permute-start | bytes 1769480 | tf_op jit(solution)/shard_map/ppermute | solution.py:653
  65.8 0.7 copy-start.9
  65.8 0.9 copy-start.10
  66.7 1.0 copy-start
  66.7 1.5 copy-start.1
  69.3 1.5 copy-start.19
  71.7 6.8 %collective-permute-start.15 = (bf16[96,1536]{1,0:T(8,128)(2,1)S(1)}, bf16[96,1536]{1,0:T(8,128)(2,1)S(1)}, u32[]{:S(2)}, u32[]{:S(2)}) collective-permute-start(bf16[96,1536]{1,0:T(8,128)(2,1)S(1)} %broadcast_select_fusion.5), channel_id=1, source_target_pairs={{0,2},{1,5},{2,0},{3,7},{4,6},{5,1},{6,4},{7,3},{8,10},{9,13},{10,... | collective-permute-start | bytes 884744 | tf_op jit(solution)/shard_map/ppermute | solution.py:693
  74.5 4.1 %copy-start.17 = (bf16[192,1536]{1,0:T(8,128)(2,1)}, bf16[192,1536]{1,0:T(8,128)(2,1)S(1)}, u32[]{:S(2)}) copy-start(bf16[192,1536]{1,0:T(8,128)(2,1)S(1)} %collective-permute-done.14.refs_7_) | copy-start | bytes 1769476
  78.6 0.7 copy-start.20
  84.1 15.9 %copy-start.12 = (bf16[3,32,1536]{2,1,0:T(8,128)(2,1)S(1)}, bf16[3,32,1536]{2,1,0:T(8,128)(2,1)}, u32[]{:S(2)}) copy-start(bf16[3,32,1536]{2,1,0:T(8,128)(2,1)} %copy-done.11) | copy-start | bytes 884740
  84.1 15.9 %copy-start.14 = (bf16[3,32,1536]{2,1,0:T(8,128)(2,1)S(1)}, bf16[3,32,1536]{2,1,0:T(8,128)(2,1)}, u32[]{:S(2)}) copy-start(bf16[3,32,1536]{2,1,0:T(8,128)(2,1)} %copy-done.13) | copy-start | bytes 884740
  92.0 15.7 %all-to-all-start = ((f32[16,2,768]{2,1,0:T(2,128)}), f32[16,2,768]{2,1,0:T(2,128)}, u32[]{:S(2)}, u32[]{:S(2)}) async-start(f32[16,2,768]{2,1,0:T(2,128)} %get-tuple-element.56), calls=%async_computation | async-start | bytes 196608 | tf_op jit(solution)/shard_map/all_to_all | solution.py:626
  131.6 2.8 %collective-permute-start.16 = (f32[128,1536]{1,0:T(8,128)}, f32[128,1536]{1,0:T(8,128)S(1)}, u32[]{:S(2)}, u32[]{:S(2)}) collective-permute-start(f32[128,1536]{1,0:T(8,128)} %get-tuple-element.67), channel_id=1, source_target_pairs={{0,1},{1,0},{2,3},{3,2},{4,5},{5,4},{6,7},{7,6},{8,9},{9,8},{10,11... | collective-permute-start | bytes 2359304 | tf_op jit(solution)/shard_map/ppermute | solution.py:703
  134.4 0.9 copy-start.15
  138.5 15.9 %collective-permute-start.17 = (f32[128,1536]{1,0:T(8,128)}, f32[128,1536]{1,0:T(8,128)}, u32[]{:S(2)}, u32[]{:S(2)}) collective-permute-start(f32[128,1536]{1,0:T(8,128)} %get-tuple-element.72.mine), channel_id=1, source_target_pairs={{0,1},{1,0},{2,3},{3,2},{4,5},{5,4},{6,7},{7,6},{8,9},{9,8},{10,11... | collective-permute-start | bytes 2359304 | tf_op jit(solution)/shard_map/ppermute | solution.py:620
  138.9 15.5 %collective-permute-start.19 = (f32[32,1536]{1,0:T(8,128)}, f32[32,1536]{1,0:T(8,128)S(1)}, u32[]{:S(2)}, u32[]{:S(2)}) collective-permute-start(f32[32,1536]{1,0:T(8,128)} %get-tuple-element.73), channel_id=1, source_target_pairs={{2,1},{4,3},{6,5},{8,7},{10,9},{12,11},{14,13},{16,15},{18,17},{20... | collective-permute-start | bytes 589832 | tf_op jit(solution)/shard_map/ppermute | solution.py:622
  139.5 14.8 %collective-permute-start.18 = (f32[32,1536]{1,0:T(8,128)}, f32[32,1536]{1,0:T(8,128)S(1)}, u32[]{:S(2)}, u32[]{:S(2)}) collective-permute-start(f32[32,1536]{1,0:T(8,128)} %get-tuple-element.73), channel_id=1, source_target_pairs={{2,0},{4,2},{6,4},{8,6},{10,8},{12,10},{14,12},{16,14},{18,16},{20... | collective-permute-start | bytes 589832 | tf_op jit(solution)/shard_map/ppermute | solution.py:621
  140.8 13.5 %all-to-all-start.2 = ((f32[32,1,128]{2,1,0:T(1,128)}), f32[32,1,128]{2,1,0:T(1,128)S(1)}, u32[]{:S(2)}, u32[]{:S(2)}) async-start(f32[32,1,128]{2,1,0:T(1,128)} %get-tuple-element.68), calls=%async_computation.2 | async-start | bytes 32768 | tf_op jit(solution)/shard_map/all_to_all | solution.py:705
  154.3 0.7 copy-start.22
  167.3 13.8 %all-to-all-start.3 = ((f32[16,2,768]{2,1,0:T(2,128)}), f32[16,2,768]{2,1,0:T(2,128)S(1)}, u32[]{:S(2)}, u32[]{:S(2)}) async-start(f32[16,2,768]{2,1,0:T(2,128)} %get-tuple-element.76.stats.local_stats), calls=%async_computation.3 | async-start | bytes 196608 | tf_op jit(solution)/shard_map/all_to_all | solution.py:626
  173.4 19.5 %copy-start.27 = (f32[2,768]{1,0:T(2,128)S(1)}, f32[2,768]{1,0:T(2,128)}, u32[]{:S(2)}) copy-start(f32[2,768]{1,0:T(2,128)} %get-tuple-element.84) | copy-start | bytes 18436
  188.1 13.4 %all-to-all-start.4 = ((bf16[16,48,128]{2,1,0:T(8,128)(2,1)}), bf16[16,48,128]{2,1,0:T(8,128)(2,1)S(1)}, u32[]{:S(2)}, u32[]{:S(2)}) async-start(bf16[16,48,128]{2,1,0:T(8,128)(2,1)} %get-tuple-element.82), calls=%async_computation.4 | async-start | bytes 393216 | tf_op jit(solution)/shard_map/all_to_all | solution.py:626
  (4 other events, 2.6 us)

commit v5 on v4

--- a/solution.py
+++ b/solution.py
@@ -84,25 +84,45 @@
     return jnp.sum(jnp.concatenate(totals, axis=0), axis=1)
 
 
-def place_kernel(shifts, size, scal, *refs):
+def block_row(scal, size, depth, shift, other):
+    chip = lax.rem(scal[5] - shift + depth, depth) * 4 + (scal[4] ^ other)
+    return pl.multiple_of(chip * size, 16)
+
+
+def place_kernel(kinds, size, scal, *refs):
     pieces, out = refs[:-1], refs[-1]
-    spot, layer = scal[4], scal[5]
     depth = out.shape[0] // (4 * size)
-
-    for number, group in enumerate(shifts):
-        for other, ref in enumerate(pieces[4 * number : 4 * number + 4]):
-            for nth, shift in enumerate(group):
-                chip = lax.rem(layer - shift + depth, depth) * 4 + (spot ^ other)
-                row = pl.multiple_of(chip * size, 16)
-                out[pl.ds(row, size), :] = ref[nth * size : (nth + 1) * size, :]
-
-
-def place(scal, pieces, shifts, size):
+    for (group, other), ref in zip(kinds, pieces):
+        for nth, shift in enumerate(group):
+            row = block_row(scal, size, depth, shift, other)
+            out[pl.ds(row, size), :] = ref[nth * size : (nth + 1) * size, :]
+
+
+def place_late_kernel(kinds, size, scal, *refs):
+    pieces, out, sems = refs[: len(kinds)], refs[-2], refs[-1]
+    depth = out.shape[0] // (4 * size)
+    copies = []
+    for (group, other), ref in zip(kinds, pieces):
+        for nth, shift in enumerate(group):
+            row = block_row(scal, size, depth, shift, other)
+            copies.append(
+                pltpu.make_async_copy(
+                    ref.at[pl.ds(nth * size, size), :],
+                    out.at[pl.ds(row, size), :],
+                    sems.at[len(copies)],
+                )
+            )
+    for copy in copies:
+        copy.start()
+    for copy in copies:
+        copy.wait()
+
+
+def place(scal, kinds, pieces, size, chips):
     width = pieces[0].shape[1]
-    chips = 4 * sum(len(group) for group in shifts)
     vmem = pl.BlockSpec(memory_space=pltpu.VMEM)
     return pl.pallas_call(
-        functools.partial(place_kernel, shifts, size),
+        functools.partial(place_kernel, kinds, size),
         in_specs=[pl.BlockSpec(memory_space=pltpu.SMEM)] + [vmem] * len(pieces),
         out_specs=vmem,
         out_shape=jax.ShapeDtypeStruct((chips * size, width), BF16),
@@ -110,6 +130,23 @@
         cost_estimate=cost(0, 4 * chips * size * width),
         name="place_weights",
     )(scal, *pieces)
+
+
+def place_late(scal, kinds, pieces, size, weight):
+    count = sum(len(group) for group, _ in kinds)
+    vmem = pl.BlockSpec(memory_space=pltpu.VMEM)
+    hbm = pl.BlockSpec(memory_space=pl.ANY)
+    return pl.pallas_call(
+        functools.partial(place_late_kernel, kinds, size),
+        in_specs=[pl.BlockSpec(memory_space=pltpu.SMEM)] + [vmem] * len(pieces) + [hbm],
+        out_specs=hbm,
+        out_shape=jax.ShapeDtypeStruct(weight.shape, BF16),
+        scratch_shapes=[pltpu.SemaphoreType.DMA((count,))],
+        input_output_aliases={len(pieces) + 1: 0},
+        compiler_params=params(),
+        cost_estimate=cost(0, 4 * count * size * weight.shape[1]),
+        name="place_last_weights",
+    )(scal, *pieces, weight)
 
 
 def forward_kernel(keep, scal, nb, value_w, gate_w, taps, *refs):
@@ -634,25 +671,35 @@
     given = lax.ppermute(lax.dynamic_index_in_dim(pair, 1 - core, 0, keepdims=False), "tm", swap)
     block = jnp.concatenate([jnp.where(first, kept, given), jnp.where(first, given, kept)], axis=0)
     shifts = [(0,)] + [(k, depth - k) if 2 * k < depth else (k,) for k in range(1, depth // 2 + 1)]
-    along = {0: block}
-    for k in [k for group in shifts[1:] for k in group]:
-        along[k] = lax.ppermute(block, "tm", [(i, (i + 8 * k) % shards) for i in range(shards)])
+    forth = [(i, (i + 8) % shards) for i in range(shards)]
+    back = [(i, (i - 8) % shards) for i in range(shards)]
     corner = [(i, i ^ (4 if i % 2 else 2)) for i in range(shards)]
-    pieces, relayed = [], None
+    along = {0: block, depth: block}
+    kinds, pieces, late_kinds, late_pieces = [], [], [], []
     for number, group in enumerate(shifts):
         blocks = jnp.concatenate([along[k] for k in group], axis=0)
-        if number == 1:
-            blocks, relayed = lax.optimization_barrier((blocks, relayed))
-        elif number > 1:
-            blocks, _ = lax.optimization_barrier((blocks, pieces[4 * number - 5]))
-        from_x = lax.ppermute(blocks, "tm", swap_x)
-        from_y = lax.ppermute(blocks, "tm", swap_y)
+        sent = [lax.ppermute(blocks, "tm", swap_x), lax.ppermute(blocks, "tm", swap_y)]
+        if number:
+            sent.append(lax.ppermute(relayed, "tm", corner))
+        if number + 1 < len(shifts):
+            for k in shifts[number + 1]:
+                from_before = 2 * k <= depth
+                sent.append(lax.ppermute(along[k - 1 if from_before else k + 1], "tm", forth if from_before else back))
+        sent = list(lax.optimization_barrier(tuple(sent)))
+        from_x, from_y = sent[:2]
         relayed = jnp.where(first, from_y, from_x)
+        kinds += [(group, 0), (group, 1), (group, 2)]
         pieces += [blocks, from_x, from_y]
+        late_kinds.append((group, 3))
+        if number:
+            late_pieces.append(sent[2])
+        else:
+            square_done = from_x
         if number + 1 < len(shifts):
-            pieces.append(lax.ppermute(relayed, "tm", corner))
+            for k, arrived in zip(shifts[number + 1], sent[-len(shifts[number + 1]) :]):
+                along[k] = arrived
     features, start_noise, cotangent, kernel, bn_gain, bn_shift, _ = lax.optimization_barrier(
-        (features, start_noise, cotangent, kernel, bn_gain, bn_shift, pieces[4])
+        (features, start_noise, cotangent, kernel, bn_gain, bn_shift, square_done)
     )
     packed = jnp.concatenate([features, start_noise, cotangent], axis=0)
     partner, near, far = across(
@@ -690,8 +737,10 @@
     relayed, normed_b, taps, gain, shift = lax.optimization_barrier(
         (relayed, normed_b, taps, gain, shift)
     )
-    pieces.append(lax.ppermute(relayed, "tm", corner))
-    weight = place(scal, pieces, shifts, block.shape[0])
+    late_pieces.append(lax.ppermute(relayed, "tm", corner))
+    kinds, pieces = kinds + late_kinds[:1], pieces + late_pieces[:1]
+    weight = place(scal, kinds, pieces, block.shape[0], chips)
+    weight = place_late(scal, late_kinds[1:], late_pieces[1:], block.shape[0], weight)
 
     value, gate, glu, conv, stats = forward(
         scal, normed_b, weight, taps, chip_rows, chips, True

time: 205 us -> 206 us (level)
  starting transfers between devices: 52.2 us -> 47.8 us
  local copies, waits for them, and re-layouts: 13.7 us -> 17.1 us
    all_to_all x3, starting transfers between devices: 19 us -> 15.2 us  [peers_of(): lax.all_to_all(array, 'tm', 0, 0, axis_index_groups=cores, tiled=True)]
    ppermute x2, starting transfers between devices: 0.52 us -> 3.34 us  [across(): lax.ppermute(array, 'tm', swap)]
    ppermute x12, starting transfers between devices: 20.3 us -> 17.7 us  [the longest x3 6.69 us: on_device(): lax.ppermute(along[k - 1 if from_before else k + 1], 'tm', forth if from_...]
    pallas_call x1 -> x2, Pallas kernels: 4.81 us -> 6.59 us  [the longest x1 4.5 us: place(): pl.pallas_call(functools.partial(place_kernel, kinds, size), in_specs=[pl...]
    unnamed x58 -> x61, local copies, waits for them, and re-layouts: 5.59 us -> 6.55 us
  transfers between devices with their start and end apart: 24 -> 24, of which waited for: 14 -> 11; matrix products, arithmetic and copies ran while one was open for 9% -> 10% of each run, Pallas kernels for 5% -> 7%
where the time goes in v5:
time: 206 us; the launch traced here: 204 us
  Pallas kernels  60.4 us (29%)
  waiting for transfers between devices  51.6 us (25%)
  starting transfers between devices  47.8 us (23%)
  local copies, waits for them, and re-layouts  17.1 us (8%)
  blocking collectives  11.8 us (6%)
  other arithmetic  10.7 us (5%)
  matrix products  2.99 us (1%)
    ppermute x2, waiting for transfers between devices, on_device(): sent.append(lax.ppermute(relayed, 'tm', corner))  15.6 us
    pallas_call x2, Pallas kernels, forward(): pl.pallas_call(functools.partial(forward_kernel, keep), grid=(steps,), in...  15.6 us
    all_to_all x3, starting transfers between devices, peers_of(): lax.all_to_all(array, 'tm', 0, 0, axis_index_groups=cores, tiled=True)  15.2 us
    all_to_all x3, waiting for transfers between devices, peers_of(): lax.all_to_all(array, 'tm', 0, 0, axis_index_groups=cores, tiled=True)  13.8 us
    all_to_all x1, blocking collectives, peers_of(): lax.all_to_all(array, 'tm', 0, 0, axis_index_groups=cores, tiled=True)  11.8 us
    ppermute x3, waiting for transfers between devices, on_device(): lax.ppermute(along[k - 1 if from_before else k + 1], 'tm', forth if from_...  8.51 us
    pallas_call x1, Pallas kernels, backward(): pl.pallas_call(backward_kernel, grid=(steps,), in_specs=[pl.BlockSpec(mem...  8.2 us
    ppermute x3, waiting for transfers between devices, on_device(): lax.ppermute(blocks, 'tm', swap_y)  7.01 us
  transfers between devices with their start and end apart: 24, of which 11 were waited for; matrix products, arithmetic and copies ran while one was open for 10% of the time, Pallas kernels for 7%

profile of v5, /device:TPU:0, one launch (start us, length us, event | category | flops | bytes accessed | tf_op | source)
XLA Modules:
  0.0 204.2 jit_solution(732165544414737395)
XLA Ops:
  2.2 1.0 collective-permute-done
  4.1 5.0 %collective-permute-start.4 = (bf16[96,1536]{1,0:T(8,128)(2,1)S(1)}, bf16[96,1536]{1,0:T(8,128)(2,1)S(1)}, u32[]{:S(2)}, u32[]{:S(2)}) collective-permute-start(bf16[96,1536]{1,0:T(8,128)(2,1)S(1)} %pad_maximum_fusion.1.refs_0_), channel_id=1, source_target_pairs={{0,24},{1,25},{2,26},{3,27},{4,28},{5,29},{6,30},{7,31},{8,0},{9,1... | collective-permute-start | bytes 884744 | tf_op jit(solution)/shard_map/ppermute | solution.py:687
  9.2 1.5 collective-permute-start.2
  10.7 1.5 collective-permute-start.1
  14.5 2.0 collective-permute-done.4
  16.6 6.5 %collective-permute-done.3 = bf16[96,1536]{1,0:T(8,128)(2,1)} collective-permute-done((bf16[96,1536]{1,0:T(8,128)(2,1)S(1)}, bf16[96,1536]{1,0:T(8,128)(2,1)}, u32[]{:S(2)}, u32[]{:S(2)}) %collective-permute-start.3) | collective-permute-done | bytes 294944 | tf_op jit(solution)/shard_map/ppermute | solution.py:687
  23.1 1.7 collective-permute-start.8
  24.8 1.7 constant_dynamic-update-slice_fusion.1
  27.2 1.5 collective-permute-start.6
  28.7 1.5 collective-permute-start.5
  31.7 1.0 constant_dynamic-update-slice_fusion.2
  34.6 1.3 collective-permute-start.13
  35.9 15.6 %collective-permute-done.7.refs_9_ = bf16[96,1536]{1,0:T(8,128)(2,1)} collective-permute-done((bf16[96,1536]{1,0:T(8,128)(2,1)}, bf16[96,1536]{1,0:T(8,128)(2,1)}, u32[]{:S(2)}, u32[]{:S(2)}) %collective-permute-start.7) | collective-permute-done | bytes 294944 | tf_op jit(solution)/shard_map/ppermute | solution.py:683
  51.5 1.4 collective-permute-start.12
  52.9 3.2 %collective-permute-start.14 = (bf16[3,128,1536]{2,1,0:T(8,128)(2,1)S(1)}, bf16[3,128,1536]{2,1,0:T(8,128)(2,1)S(1)}, u32[]{:S(2)}, u32[]{:S(2)}) collective-permute-start(bf16[3,128,1536]{2,1,0:T(8,128)(2,1)S(1)} %constant_dynamic-update-slice_fusion.2), channel_id=1, source_target_pairs={{0,1},{1,0},{2,3},{3,2},{4,5},{5,4},{6,7},{7,6},{8,9},{9,8},{10,11... | collective-permute-start | bytes 3538952 | tf_op jit(solution)/shard_map/ppermute | solution.py:657
  56.1 1.0 broadcast_select_fusion.2
  57.9 1.7 broadcast_in_dim.8
  61.8 1.2 collective-permute-start.9
  63.0 1.1 broadcast_select_fusion.4
  64.1 7.0 %collective-permute-done.10.refs_8_ = bf16[96,1536]{1,0:T(8,128)(2,1)S(1)} collective-permute-done((bf16[96,1536]{1,0:T(8,128)(2,1)}, bf16[96,1536]{1,0:T(8,128)(2,1)S(1)}, u32[]{:S(2)}, u32[]{:S(2)}) %collective-permute-start.10) | collective-permute-done | bytes 294944 | tf_op jit(solution)/shard_map/ppermute | solution.py:681
  71.1 2.5 %collective-permute-done.9.refs_7_ = bf16[96,1536]{1,0:T(8,128)(2,1)S(1)} collective-permute-done((bf16[96,1536]{1,0:T(8,128)(2,1)}, bf16[96,1536]{1,0:T(8,128)(2,1)S(1)}, u32[]{:S(2)}, u32[]{:S(2)}) %collective-permute-start.9) | collective-permute-done | bytes 294944 | tf_op jit(solution)/shard_map/ppermute | solution.py:681
  76.3 1.5 multiply_convert_fusion.nb
  78.8 2.4 %collective-permute-start.15 = (bf16[96,1536]{1,0:T(8,128)(2,1)S(1)}, bf16[96,1536]{1,0:T(8,128)(2,1)S(1)}, u32[]{:S(2)}, u32[]{:S(2)}) collective-permute-start(bf16[96,1536]{1,0:T(8,128)(2,1)S(1)} %broadcast_select_fusion.5), channel_id=1, source_target_pairs={{0,2},{1,5},{2,0},{3,7},{4,6},{5,1},{6,4},{7,3},{8,10},{9,13},{10,... | collective-permute-start | bytes 884744 | tf_op jit(solution)/shard_map/ppermute | solution.py:740
  81.8 4.5 %place_weights.1.refs_2_ = bf16[1536,1536]{1,0:T(8,128)(2,1)} custom-call(s32[6]{0:T(128)} %stack.26.scal, bf16[96,1536]{1,0:T(8,128)(2,1)} %copy-done.10, bf16[96,1536]{1,0:T(8,128)(2,1)} %copy-done.7, bf16[96,1536]{1,0:T(8,128)(2,1)} %copy-done.6, bf16[192,1536]{1,0:T(8,128)(2,1)} %constant_dynamic-update-slice_fusion.refs_3_, ...), custom_call_target="tpu_custom_call" | custom-call | bytes 9437184 | tf_op jit(solution)/shard_map/place_weights/pallas_call | solution.py:124
  87.0 2.1 %place_last_weights.1.value_w.gate_w = bf16[1536,1536]{1,0:T(8,128)(2,1)} custom-call(s32[6]{0:T(128)} %stack.26.scal, bf16[192,1536]{1,0:T(8,128)(2,1)} %collective-permute-done.11.refs_0_, bf16[96,1536]{1,0:T(8,128)(2,1)} %copy-done.19, bf16[1536,1536]{1,0:T(8,128)(2,1)} %place_weights.1.refs_2_), custom_call_target="tpu_custom_call", output_to_operand_aliasing={{}: (3, {})} | custom-call | bytes 1769472 | tf_op jit(solution)/shard_map/place_last_weights/pallas_call | solution.py:139
  89.2 7.9 %project_glu_conv.2 = (f32[256,768]{1,0:T(8,128)}, f32[256,768]{1,0:T(8,128)}, bf16[320,768]{1,0:T(8,128)(2,1)}, f32[288,768]{1,0:T(8,128)}, f32[16,2,768]{2,1,0:T(2,128)}) custom-call(s32[6]{0:T(128)} %stack.26.scal, bf16[320,1536]{1,0:T(8,128)(2,1)} %multiply_convert_fusion.nb, bf16[1536,1536]{1,0:T(8,128)(2,1)} %place_last_weights.1.value_w.gate_w, ...), custom_call_target="tpu_custom_call" | custom-call | flops 1509949440 | bytes 7176192 | tf_op jit(solution)/shard_map/project_glu_conv/pallas_call | solution.py:183
  97.0 4.1 %all-to-all-start = ((f32[16,2,768]{2,1,0:T(2,128)}), f32[16,2,768]{2,1,0:T(2,128)}, u32[]{:S(2)}, u32[]{:S(2)}) async-start(f32[16,2,768]{2,1,0:T(2,128)} %get-tuple-element.74), calls=%async_computation | async-start | bytes 196608 | tf_op jit(solution)/shard_map/all_to_all | solution.py:663
  101.2 3.0 %fusion.3.cot = bf16[288,768]{1,0:T(8,128)(2,1)} fusion(s32[768]{0:T(1024)S(1)} %fusion.21, bf16[3,32,1536]{2,1,0:T(8,128)(2,1)S(1)} %copy-done.14, bf16[3,128,1536]{2,1,0:T(8,128)(2,1)} %copy-done.1, bf16[3,128,1536]{2,1,0:T(8,128)(2,1)} %copy-done, bf16[3,32,1536]{2,1,0:T(8,128)(2,1)S(1)} %copy-done.12), kind=kOutput, calls=%fused_computation.8 | convolution fusion | flops 684417024 | bytes 3394560 | tf_op jit(solution)/shard_map/dot_general | solution.py:722
  104.2 4.7 %all-to-all-done.stats = f32[16,2,768]{2,1,0:T(2,128)} async-done(((f32[16,2,768]{2,1,0:T(2,128)}), f32[16,2,768]{2,1,0:T(2,128)}, u32[]{:S(2)}, u32[]{:S(2)}) %all-to-all-start) | async-done | bytes 98336 | tf_op jit(solution)/shard_map/all_to_all | solution.py:663
  108.9 3.9 %batch_norm_swish.1 = (f32[288,768]{1,0:T(8,128)}, f32[288,768]{1,0:T(8,128)}, f32[1,768]{1,0:T(1,128)}, f32[16,2,768]{2,1,0:T(2,128)}) custom-call(s32[6]{0:T(128)} %stack.26.scal, f32[2,16]{1,0:T(2,128)} %pad_maximum_fusion.2.counts, f32[16,2,768]{2,1,0:T(2,128)} %all-to-all-done.stats, f32[288,768]{1,0:T(8,128)} %get-tuple-element.75.conv, ...), custom_call_target="tpu_custom_call" | custom-call | flops 8847360 | bytes 3538944 | tf_op jit(solution)/shard_map/batch_norm_swish/pallas_call | solution.py:263
  112.8 11.8 %all_to_all.25.sums = f32[16,2,768]{2,1,0:T(2,128)} all-to-all(f32[16,2,768]{2,1,0:T(2,128)} %get-tuple-element.78), channel_id=1, replica_groups={{0,2,4,6,8,10,12,14,16,18,20,22,24,26,28,30},{1,3,5,7,9,11,13,15,17,19,..., dimensions={0} | all-to-all | bytes 196608 | tf_op jit(solution)/shard_map/all_to_all | solution.py:663
  124.6 8.2 %grad_conv_project_back.1 = (f32[128,1536]{1,0:T(8,128)}, f32[128,1536]{1,0:T(8,128)}, bf16[256,768]{1,0:T(8,128)(2,1)}, f32[2,768]{1,0:T(2,128)}) custom-call(s32[6]{0:T(128)} %stack.26.scal, f32[16,2,768]{2,1,0:T(2,128)} %all_to_all.25.sums, f32[288,768]{1,0:T(8,128)} %get-tuple-element.79.scaled, f32[288,768]{1,0:T(8,128)} %get-tuple-element.80.grad, ...), custom_call_target="tpu_custom_call" | custom-call | flops 1207959552 | bytes 9142272 | tf_op jit(solution)/shard_map/grad_conv_project_back/pallas_call | solution.py:338
  132.9 2.5 %collective-permute-done.16.other = f32[128,1536]{1,0:T(8,128)S(1)} collective-permute-done((f32[128,1536]{1,0:T(8,128)}, f32[128,1536]{1,0:T(8,128)S(1)}, u32[]{:S(2)}, u32[]{:S(2)}) %collective-permute-start.16) | collective-permute-done | bytes 786464 | tf_op jit(solution)/shard_map/ppermute | solution.py:752
  136.2 3.2 %direction.1 = (f32[128,1536]{1,0:T(8,128)}, f32[32,1536]{1,0:T(8,128)}, f32[32,1,128]{2,1,0:T(1,128)}) custom-call(s32[6]{0:T(128)} %stack.26.scal, f32[128,1536]{1,0:T(8,128)} %get-tuple-element.84.mine, f32[128,1536]{1,0:T(8,128)} %copy-done.15, bf16[128,1536]{1,0:T(8,128)(2,1)} %bitcast.50, bf16[128,1536]{1,0:T(8,128)(2,1)} %bitcast.48), custom_call_target="tpu_custom_call" | custom-call | flops 5898240 | bytes 3145728 | tf_op jit(solution)/shard_map/direction/pallas_call | solution.py:568
  140.2 1.3 collective-permute-start.18
  141.5 6.3 %all-to-all-start.2 = ((f32[32,1,128]{2,1,0:T(1,128)}), f32[32,1,128]{2,1,0:T(1,128)S(1)}, u32[]{:S(2)}, u32[]{:S(2)}) async-start(f32[32,1,128]{2,1,0:T(1,128)} %get-tuple-element.86), calls=%async_computation.2 | async-start | bytes 32768 | tf_op jit(solution)/shard_map/all_to_all | solution.py:754
  147.8 1.4 slice_bitcast_fusion
  149.2 4.9 %tap_grad.1.taps_before = f32[31,768]{1,0:T(8,128)} custom-call(bf16[256,768]{1,0:T(8,128)(2,1)} %get-tuple-element.87.grad_conv, bf16[320,768]{1,0:T(8,128)(2,1)} %get-tuple-element.88.glu), custom_call_target="tpu_custom_call" | custom-call | flops 12189696 | bytes 983040 | tf_op jit(solution)/shard_map/tap_grad/pallas_call | solution.py:386
  155.5 4.5 %ascend.1 = (f32[128,1536]{1,0:T(8,128)}, bf16[320,1536]{1,0:T(8,128)(2,1)}) custom-call(s32[6]{0:T(128)} %stack.26.scal, f32[32,1,128]{2,1,0:T(1,128)} %copy-done.23, bf16[320,1536]{1,0:T(8,128)(2,1)} %get-tuple-element.106.features, bf16[320,1536]{1,0:T(8,128)(2,1)} %get-tuple-element.105.noise, f32[128,1536]{1,0:T(8,128)} %get-tuple-element.90.mine, ...), custom_call_target="tpu_custom_call" | custom-call | flops 14745600 | bytes 3932160 | tf_op jit(solution)/shard_map/ascend/pallas_call | solution.py:612
  160.0 7.7 %project_glu_conv.3 = (bf16[320,768]{1,0:T(8,128)(2,1)}, f32[288,768]{1,0:T(8,128)}, f32[16,2,768]{2,1,0:T(2,128)}) custom-call(s32[6]{0:T(128)} %stack.26.scal, bf16[320,1536]{1,0:T(8,128)(2,1)} %get-tuple-element.93.nb, bf16[1536,1536]{1,0:T(8,128)(2,1)} %place_last_weights.1.value_w.gate_w, bf16[1536,1536]{1,0:T(8,128)(2,1)} %place_last_weights.1.value_w.gate_w, ...), custom_call_target="tpu_custom_call" | custom-call | flops 1509949440 | bytes 7176192 | tf_op jit(solution)/shard_map/project_glu_conv/pallas_call | solution.py:183
  167.7 6.1 %all-to-all-start.3 = ((f32[16,2,768]{2,1,0:T(2,128)}), f32[16,2,768]{2,1,0:T(2,128)S(1)}, u32[]{:S(2)}, u32[]{:S(2)}) async-start(f32[16,2,768]{2,1,0:T(2,128)} %get-tuple-element.94.stats.local_stats), calls=%async_computation.3 | async-start | bytes 196608 | tf_op jit(solution)/shard_map/all_to_all | solution.py:663
  173.8 5.6 %raw_taps.1 = (f32[31,768]{1,0:T(8,128)}, f32[31,768]{1,0:T(8,128)}) custom-call(s32[6]{0:T(128)} %stack.26.scal, f32[288,768]{1,0:T(8,128)} %get-tuple-element.95.conv, bf16[320,768]{1,0:T(8,128)(2,1)} %get-tuple-element.96.glu, f32[16,2,768]{2,1,0:T(2,128)} %get-tuple-element.94.stats.local_stats), custom_call_target="tpu_custom_call" | custom-call | flops 13713408 | bytes 1966080 | tf_op jit(solution)/shard_map/raw_taps/pallas_call | solution.py:419
  179.4 2.0 all-to-all-done.3.stats
  182.1 6.3 %batch_norm_swish_taps.1 = (bf16[16,48,128]{2,1,0:T(8,128)(2,1)}, f32[1,768]{1,0:T(1,128)}) custom-call(s32[6]{0:T(128)} %stack.26.scal, f32[2,16]{1,0:T(2,128)} %pad_maximum_fusion.2.counts, f32[16,2,768]{2,1,0:T(2,128)} %copy-done.17, f32[288,768]{1,0:T(8,128)} %get-tuple-element.95.conv, bf16[288,768]{1,0:T(8,128)(2,1)} %fusion.3.cot, ...), custom_call_target="tpu_custom_call" | custom-call | flops 22118400 | bytes 2211840 | tf_op jit(solution)/shard_map/batch_norm_swish_taps/pallas_call | solution.py:479
  188.4 4.9 %all-to-all-start.4 = ((bf16[16,48,128]{2,1,0:T(8,128)(2,1)}), bf16[16,48,128]{2,1,0:T(8,128)(2,1)S(1)}, u32[]{:S(2)}, u32[]{:S(2)}) async-start(bf16[16,48,128]{2,1,0:T(8,128)(2,1)} %get-tuple-element.100), calls=%async_computation.4 | async-start | bytes 393216 | tf_op jit(solution)/shard_map/all_to_all | solution.py:663
  193.4 1.3 fusion.23.known
  194.7 7.1 %all-to-all-done.4.received = bf16[16,48,128]{2,1,0:T(8,128)(2,1)S(1)} async-done(((bf16[16,48,128]{2,1,0:T(8,128)(2,1)}), bf16[16,48,128]{2,1,0:T(8,128)(2,1)S(1)}, u32[]{:S(2)}, u32[]{:S(2)}) %all-to-all-start.4) | async-done | bytes 196640 | tf_op jit(solution)/shard_map/all_to_all | solution.py:663
  202.5 1.7 finish.1
  (113 shorter events, 20.4 us)
Async XLA Ops:
  0.6 31.0 %copy-start.5 = (bf16[1,128,1536]{2,1,0:T(8,128)(2,1)S(1)}, bf16[1,128,1536]{2,1,0:T(8,128)(2,1)}, u32[]{:S(2)}) copy-start(bf16[1,128,1536]{2,1,0:T(8,128)(2,1)} %param.8) | copy-start | bytes 1179652
  1.6 1.5 collective-permute-start
  2.2 29.5 %copy-start.2 = (bf16[1,128,1536]{2,1,0:T(8,128)(2,1)S(1)}, bf16[1,128,1536]{2,1,0:T(8,128)(2,1)}, u32[]{:S(2)}) copy-start(bf16[1,128,1536]{2,1,0:T(8,128)(2,1)} %param.9) | copy-start | bytes 1179652
  4.1 26.9 %copy-start.10 = (bf16[96,1536]{1,0:T(8,128)(2,1)}, bf16[96,1536]{1,0:T(8,128)(2,1)S(1)}, u32[]{:S(2)}) copy-start(bf16[96,1536]{1,0:T(8,128)(2,1)S(1)} %pad_maximum_fusion.1.refs_0_) | copy-start | bytes 884740
  4.1 12.4 %collective-permute-start.4 = (bf16[96,1536]{1,0:T(8,128)(2,1)S(1)}, bf16[96,1536]{1,0:T(8,128)(2,1)S(1)}, u32[]{:S(2)}, u32[]{:S(2)}) collective-permute-start(bf16[96,1536]{1,0:T(8,128)(2,1)S(1)} %pad_maximum_fusion.1.refs_0_), channel_id=1, source_target_pairs={{0,24},{1,25},{2,26},{3,27},{4,28},{5,29},{6,30},{7,31},{8,0},{9,1... | collective-permute-start | bytes 884744 | tf_op jit(solution)/shard_map/ppermute | solution.py:687
  9.1 13.9 %collective-permute-start.3 = (bf16[96,1536]{1,0:T(8,128)(2,1)S(1)}, bf16[96,1536]{1,0:T(8,128)(2,1)}, u32[]{:S(2)}, u32[]{:S(2)}) collective-permute-start(bf16[96,1536]{1,0:T(8,128)(2,1)S(1)} %pad_maximum_fusion.1.refs_0_), channel_id=1, source_target_pairs={{0,8},{1,9},{2,10},{3,11},{4,12},{5,13},{6,14},{7,15},{8,16},{9,17... | collective-permute-start | bytes 884744 | tf_op jit(solution)/shard_map/ppermute | solution.py:687
  9.2 13.9 %collective-permute-start.2 = (bf16[96,1536]{1,0:T(8,128)(2,1)S(1)}, bf16[96,1536]{1,0:T(8,128)(2,1)S(1)}, u32[]{:S(2)}, u32[]{:S(2)}) collective-permute-start(bf16[96,1536]{1,0:T(8,128)(2,1)S(1)} %pad_maximum_fusion.1.refs_0_), channel_id=1, source_target_pairs={{0,4},{1,5},{2,6},{3,7},{4,0},{5,1},{6,2},{7,3},{8,12},{9,13},{10,... | collective-permute-start | bytes 884744 | tf_op jit(solution)/shard_map/ppermute | solution.py:681
  10.7 12.4 %collective-permute-start.1 = (bf16[96,1536]{1,0:T(8,128)(2,1)S(1)}, bf16[96,1536]{1,0:T(8,128)(2,1)S(1)}, u32[]{:S(2)}, u32[]{:S(2)}) collective-permute-start(bf16[96,1536]{1,0:T(8,128)(2,1)S(1)} %pad_maximum_fusion.1.refs_0_), channel_id=1, source_target_pairs={{0,2},{1,3},{2,0},{3,1},{4,6},{5,7},{6,4},{7,5},{8,10},{9,11},{10,... | collective-permute-start | bytes 884744 | tf_op jit(solution)/shard_map/ppermute | solution.py:681
  23.1 7.9 %copy-start.6 = (bf16[96,1536]{1,0:T(8,128)(2,1)}, bf16[96,1536]{1,0:T(8,128)(2,1)S(1)}, u32[]{:S(2)}) copy-start(bf16[96,1536]{1,0:T(8,128)(2,1)S(1)} %collective-permute-done.2.refs_2_) | copy-start | bytes 884740
  23.1 7.9 %copy-start.7 = (bf16[96,1536]{1,0:T(8,128)(2,1)}, bf16[96,1536]{1,0:T(8,128)(2,1)S(1)}, u32[]{:S(2)}) copy-start(bf16[96,1536]{1,0:T(8,128)(2,1)S(1)} %collective-permute-done.1.refs_1_) | copy-start | bytes 884740
  23.1 29.8 %collective-permute-start.8 = (bf16[96,1536]{1,0:T(8,128)(2,1)}, bf16[96,1536]{1,0:T(8,128)(2,1)}, u32[]{:S(2)}, u32[]{:S(2)}) collective-permute-start(bf16[96,1536]{1,0:T(8,128)(2,1)} %collective-permute-done.3), channel_id=1, source_target_pairs={{0,8},{1,9},{2,10},{3,11},{4,12},{5,13},{6,14},{7,15},{8,16},{9,17... | collective-permute-start | bytes 884744 | tf_op jit(solution)/shard_map/ppermute | solution.py:687
  27.2 6.2 %copy-start.25 = (f32[1536]{0:T(1024)S(1)}, f32[1536]{0:T(1024)}, u32[]{:S(2)}) copy-start(f32[1536]{0:T(1024)} %param.13) | copy-start | bytes 18436
  27.2 6.4 %copy-start.26 = (f32[1536]{0:T(1024)S(1)}, f32[1536]{0:T(1024)}, u32[]{:S(2)}) copy-start(f32[1536]{0:T(1024)} %param.14) | copy-start | bytes 18436
  27.2 6.5 %copy-start.22 = (f32[31,1536]{1,0:T(8,128)S(1)}, f32[31,1536]{1,0:T(8,128)}, u32[]{:S(2)}) copy-start(f32[31,1536]{1,0:T(8,128)} %param.12) | copy-start | bytes 571396
  27.2 28.9 %collective-permute-start.6 = (bf16[192,1536]{1,0:T(8,128)(2,1)}, bf16[192,1536]{1,0:T(8,128)(2,1)S(1)}, u32[]{:S(2)}, u32[]{:S(2)}) collective-permute-start(bf16[192,1536]{1,0:T(8,128)(2,1)} %constant_dynamic-update-slice_fusion.refs_3_), channel_id=1, source_target_pairs={{0,4},{1,5},{2,6},{3,7},{4,0},{5,1},{6,2},{7,3},{8,12},{9,13},{10,... | collective-permute-start | bytes 1769480 | tf_op jit(solution)/shard_map/ppermute | solution.py:681
  28.7 27.4 %collective-permute-start.5 = (bf16[192,1536]{1,0:T(8,128)(2,1)}, bf16[192,1536]{1,0:T(8,128)(2,1)S(1)}, u32[]{:S(2)}, u32[]{:S(2)}) collective-permute-start(bf16[192,1536]{1,0:T(8,128)(2,1)} %constant_dynamic-update-slice_fusion.refs_3_), channel_id=1, source_target_pairs={{0,2},{1,3},{2,0},{3,1},{4,6},{5,7},{6,4},{7,5},{8,10},{9,11},{10,... | collective-permute-start | bytes 1769480 | tf_op jit(solution)/shard_map/ppermute | solution.py:681
  31.0 20.5 %collective-permute-start.7 = (bf16[96,1536]{1,0:T(8,128)(2,1)}, bf16[96,1536]{1,0:T(8,128)(2,1)}, u32[]{:S(2)}, u32[]{:S(2)}) collective-permute-start(bf16[96,1536]{1,0:T(8,128)(2,1)} %broadcast_select_fusion.6), channel_id=1, source_target_pairs={{0,2},{1,5},{2,0},{3,7},{4,6},{5,1},{6,4},{7,3},{8,10},{9,13},{10,... | collective-permute-start | bytes 884744 | tf_op jit(solution)/shard_map/ppermute | solution.py:683
  34.6 27.2 %collective-permute-start.13 = (bf16[3,32,1536]{2,1,0:T(8,128)(2,1)}, bf16[3,32,1536]{2,1,0:T(8,128)(2,1)}, u32[]{:S(2)}, u32[]{:S(2)}) collective-permute-start(bf16[3,32,1536]{2,1,0:T(8,128)(2,1)} %slice_select_fusion), channel_id=1, source_target_pairs={{2,0},{4,2},{6,4},{8,6},{10,8},{12,10},{14,12},{16,14},{18,16},{20... | collective-permute-start | bytes 884744 | tf_op jit(solution)/shard_map/ppermute | solution.py:658
  51.5 11.4 %collective-permute-start.12 = (bf16[3,32,1536]{2,1,0:T(8,128)(2,1)}, bf16[3,32,1536]{2,1,0:T(8,128)(2,1)}, u32[]{:S(2)}, u32[]{:S(2)}) collective-permute-start(bf16[3,32,1536]{2,1,0:T(8,128)(2,1)} %slice_select_fusion), channel_id=1, source_target_pairs={{2,1},{4,3},{6,5},{8,7},{10,9},{12,11},{14,13},{16,15},{18,17},{20... | collective-permute-start | bytes 884744 | tf_op jit(solution)/shard_map/ppermute | solution.py:659
  52.9 20.7 %collective-permute-start.14 = (bf16[3,128,1536]{2,1,0:T(8,128)(2,1)S(1)}, bf16[3,128,1536]{2,1,0:T(8,128)(2,1)S(1)}, u32[]{:S(2)}, u32[]{:S(2)}) collective-permute-start(bf16[3,128,1536]{2,1,0:T(8,128)(2,1)S(1)} %constant_dynamic-update-slice_fusion.2), channel_id=1, source_target_pairs={{0,1},{1,0},{2,3},{3,2},{4,5},{5,4},{6,7},{7,6},{8,9},{9,8},{10,11... | collective-permute-start | bytes 3538952 | tf_op jit(solution)/shard_map/ppermute | solution.py:657
  56.1 17.7 %copy-start.3 = (bf16[192,1536]{1,0:T(8,128)(2,1)}, bf16[192,1536]{1,0:T(8,128)(2,1)S(1)}, u32[]{:S(2)}) copy-start(bf16[192,1536]{1,0:T(8,128)(2,1)S(1)} %collective-permute-done.6.refs_5_) | copy-start | bytes 1769476
  56.1 17.7 %copy-start.4 = (bf16[192,1536]{1,0:T(8,128)(2,1)}, bf16[192,1536]{1,0:T(8,128)(2,1)S(1)}, u32[]{:S(2)}) copy-start(bf16[192,1536]{1,0:T(8,128)(2,1)S(1)} %collective-permute-done.5.refs_4_) | copy-start | bytes 1769476
  57.1 16.5 %collective-permute-start.11 = (bf16[192,1536]{1,0:T(8,128)(2,1)}, bf16[192,1536]{1,0:T(8,128)(2,1)}, u32[]{:S(2)}, u32[]{:S(2)}) collective-permute-start(bf16[192,1536]{1,0:T(8,128)(2,1)} %broadcast_select_fusion.2), channel_id=1, source_target_pairs={{0,2},{1,5},{2,0},{3,7},{4,6},{5,1},{6,4},{7,3},{8,10},{9,13},{10,... | collective-permute-start | bytes 1769480 | tf_op jit(solution)/shard_map/ppermute | solution.py:683
  60.9 10.2 %collective-permute-start.10 = (bf16[96,1536]{1,0:T(8,128)(2,1)}, bf16[96,1536]{1,0:T(8,128)(2,1)S(1)}, u32[]{:S(2)}, u32[]{:S(2)}) collective-permute-start(bf16[96,1536]{1,0:T(8,128)(2,1)} %collective-permute-done.8.refs_6_), channel_id=1, source_target_pairs={{0,4},{1,5},{2,6},{3,7},{4,0},{5,1},{6,2},{7,3},{8,12},{9,13},{10,... | collective-permute-start | bytes 884744 | tf_op jit(solution)/shard_map/ppermute | solution.py:681
  61.8 11.9 %collective-permute-start.9 = (bf16[96,1536]{1,0:T(8,128)(2,1)}, bf16[96,1536]{1,0:T(8,128)(2,1)S(1)}, u32[]{:S(2)}, u32[]{:S(2)}) collective-permute-start(bf16[96,1536]{1,0:T(8,128)(2,1)} %collective-permute-done.8.refs_6_), channel_id=1, source_target_pairs={{0,2},{1,3},{2,0},{3,1},{4,6},{5,7},{6,4},{7,5},{8,10},{9,11},{10,... | collective-permute-start | bytes 884744 | tf_op jit(solution)/shard_map/ppermute | solution.py:681
  64.0 9.8 %copy-start.11 = (bf16[3,32,1536]{2,1,0:T(8,128)(2,1)}, bf16[3,32,1536]{2,1,0:T(8,128)(2,1)S(1)}, u32[]{:S(2)}) copy-start(bf16[3,32,1536]{2,1,0:T(8,128)(2,1)S(1)} %get-tuple-element.109) | copy-start | bytes 884740
  64.1 9.8 %copy-start.13 = (bf16[3,32,1536]{2,1,0:T(8,128)(2,1)}, bf16[3,32,1536]{2,1,0:T(8,128)(2,1)S(1)}, u32[]{:S(2)}) copy-start(bf16[3,32,1536]{2,1,0:T(8,128)(2,1)S(1)} %get-tuple-element.110) | copy-start | bytes 884740
  71.1 6.8 %copy-start.8 = (bf16[96,1536]{1,0:T(8,128)(2,1)}, bf16[96,1536]{1,0:T(8,128)(2,1)S(1)}, u32[]{:S(2)}) copy-start(bf16[96,1536]{1,0:T(8,128)(2,1)S(1)} %collective-permute-done.10.refs_8_) | copy-start | bytes 884740
  73.6 4.2 %copy-start.9 = (bf16[96,1536]{1,0:T(8,128)(2,1)}, bf16[96,1536]{1,0:T(8,128)(2,1)S(1)}, u32[]{:S(2)}) copy-start(bf16[96,1536]{1,0:T(8,128)(2,1)S(1)} %collective-permute-done.9.refs_7_) | copy-start | bytes 884740
  73.8 1.0 copy-start
  73.8 1.4 copy-start.1
  73.9 1.3 copy-start.24
  76.3 1.6 copy-start.18
  76.3 4.9 %copy-start.28 = (f32[1,16]{1,0:T(1,128)S(1)}, f32[1,16]{1,0:T(1,128)}, u32[]{:S(2)}) copy-start(f32[1,16]{1,0:T(1,128)} %clamp_convert_fusion) | copy-start | bytes 196
  78.8 7.5 %collective-permute-start.15 = (bf16[96,1536]{1,0:T(8,128)(2,1)S(1)}, bf16[96,1536]{1,0:T(8,128)(2,1)S(1)}, u32[]{:S(2)}, u32[]{:S(2)}) collective-permute-start(bf16[96,1536]{1,0:T(8,128)(2,1)S(1)} %broadcast_select_fusion.5), channel_id=1, source_target_pairs={{0,2},{1,5},{2,0},{3,7},{4,6},{5,1},{6,4},{7,3},{8,10},{9,13},{10,... | collective-permute-start | bytes 884744 | tf_op jit(solution)/shard_map/ppermute | solution.py:740
  89.1 12.0 %copy-start.12 = (bf16[3,32,1536]{2,1,0:T(8,128)(2,1)S(1)}, bf16[3,32,1536]{2,1,0:T(8,128)(2,1)}, u32[]{:S(2)}) copy-start(bf16[3,32,1536]{2,1,0:T(8,128)(2,1)} %copy-done.11) | copy-start | bytes 884740
  89.2 12.0 %copy-start.14 = (bf16[3,32,1536]{2,1,0:T(8,128)(2,1)S(1)}, bf16[3,32,1536]{2,1,0:T(8,128)(2,1)}, u32[]{:S(2)}) copy-start(bf16[3,32,1536]{2,1,0:T(8,128)(2,1)} %copy-done.13) | copy-start | bytes 884740
  97.0 11.8 %all-to-all-start = ((f32[16,2,768]{2,1,0:T(2,128)}), f32[16,2,768]{2,1,0:T(2,128)}, u32[]{:S(2)}, u32[]{:S(2)}) async-start(f32[16,2,768]{2,1,0:T(2,128)} %get-tuple-element.74), calls=%async_computation | async-start | bytes 196608 | tf_op jit(solution)/shard_map/all_to_all | solution.py:663
  132.8 2.6 %collective-permute-start.16 = (f32[128,1536]{1,0:T(8,128)}, f32[128,1536]{1,0:T(8,128)S(1)}, u32[]{:S(2)}, u32[]{:S(2)}) collective-permute-start(f32[128,1536]{1,0:T(8,128)} %get-tuple-element.85), channel_id=1, source_target_pairs={{0,1},{1,0},{2,3},{3,2},{4,5},{5,4},{6,7},{7,6},{8,9},{9,8},{10,11... | collective-permute-start | bytes 2359304 | tf_op jit(solution)/shard_map/ppermute | solution.py:752
  135.4 0.9 copy-start.15
  139.4 15.4 %collective-permute-start.17 = (f32[128,1536]{1,0:T(8,128)}, f32[128,1536]{1,0:T(8,128)}, u32[]{:S(2)}, u32[]{:S(2)}) collective-permute-start(f32[128,1536]{1,0:T(8,128)} %get-tuple-element.90.mine), channel_id=1, source_target_pairs={{0,1},{1,0},{2,3},{3,2},{4,5},{5,4},{6,7},{7,6},{8,9},{9,8},{10,11... | collective-permute-start | bytes 2359304 | tf_op jit(solution)/shard_map/ppermute | solution.py:657
  139.5 15.2 %collective-permute-start.19 = (f32[32,1536]{1,0:T(8,128)}, f32[32,1536]{1,0:T(8,128)S(1)}, u32[]{:S(2)}, u32[]{:S(2)}) collective-permute-start(f32[32,1536]{1,0:T(8,128)} %get-tuple-element.91), channel_id=1, source_target_pairs={{2,1},{4,3},{6,5},{8,7},{10,9},{12,11},{14,13},{16,15},{18,17},{20... | collective-permute-start | bytes 589832 | tf_op jit(solution)/shard_map/ppermute | solution.py:659
  140.2 14.6 %collective-permute-start.18 = (f32[32,1536]{1,0:T(8,128)}, f32[32,1536]{1,0:T(8,128)S(1)}, u32[]{:S(2)}, u32[]{:S(2)}) collective-permute-start(f32[32,1536]{1,0:T(8,128)} %get-tuple-element.91), channel_id=1, source_target_pairs={{2,0},{4,2},{6,4},{8,6},{10,8},{12,10},{14,12},{16,14},{18,16},{20... | collective-permute-start | bytes 589832 | tf_op jit(solution)/shard_map/ppermute | solution.py:658
  141.5 13.2 %all-to-all-start.2 = ((f32[32,1,128]{2,1,0:T(1,128)}), f32[32,1,128]{2,1,0:T(1,128)S(1)}, u32[]{:S(2)}, u32[]{:S(2)}) async-start(f32[32,1,128]{2,1,0:T(1,128)} %get-tuple-element.86), calls=%async_computation.2 | async-start | bytes 32768 | tf_op jit(solution)/shard_map/all_to_all | solution.py:754
  154.8 0.7 copy-start.21
  167.7 13.8 %all-to-all-start.3 = ((f32[16,2,768]{2,1,0:T(2,128)}), f32[16,2,768]{2,1,0:T(2,128)S(1)}, u32[]{:S(2)}, u32[]{:S(2)}) async-start(f32[16,2,768]{2,1,0:T(2,128)} %get-tuple-element.94.stats.local_stats), calls=%async_computation.3 | async-start | bytes 196608 | tf_op jit(solution)/shard_map/all_to_all | solution.py:663
  173.8 19.6 %copy-start.27 = (f32[2,768]{1,0:T(2,128)S(1)}, f32[2,768]{1,0:T(2,128)}, u32[]{:S(2)}) copy-start(f32[2,768]{1,0:T(2,128)} %get-tuple-element.102) | copy-start | bytes 18436
  188.4 13.4 %all-to-all-start.4 = ((bf16[16,48,128]{2,1,0:T(8,128)(2,1)}), bf16[16,48,128]{2,1,0:T(8,128)(2,1)S(1)}, u32[]{:S(2)}, u32[]{:S(2)}) async-start(bf16[16,48,128]{2,1,0:T(8,128)(2,1)} %get-tuple-element.100), calls=%async_computation.4 | async-start | bytes 393216 | tf_op jit(solution)/shard_map/all_to_all | solution.py:663
  (5 other events, 3.3 us)

commit v6 on v5

--- a/solution.py
+++ b/solution.py
@@ -674,78 +674,104 @@
     forth = [(i, (i + 8) % shards) for i in range(shards)]
     back = [(i, (i - 8) % shards) for i in range(shards)]
     corner = [(i, i ^ (4 if i % 2 else 2)) for i in range(shards)]
+    def mine_of(array):
+        parts = array.reshape(array.shape[0], chips, 2, slice_width)
+        return lax.dynamic_index_in_dim(parts, core, 2, keepdims=False).reshape(-1, half_width)
+
+    def prepare_first():
+        own_ids = chip * chip_rows + core * rows + jnp.arange(rows, dtype=jnp.int32)
+        own_live = (own_ids < end).astype(F32)[:, None]
+        summed = features[0].astype(F32) + noise_scale * start_noise[0].astype(F32) * own_live
+        return [normalize(summed)[0].astype(BF16)]
+
+    def prepare_second():
+        channel = mine_of(jnp.concatenate([kernel, bn_gain[None], bn_shift[None]], axis=0))
+        taps = jnp.broadcast_to(channel[:taps_n, None], (taps_n, 8, half_width))
+        return [taps, channel[taps_n : taps_n + 1], channel[taps_n + 1 :], counts, scal]
+
+    def assemble(own, partner, near, far):
+        return jnp.concatenate(
+            [
+                jnp.where(first, far, near),
+                jnp.where(first, own, partner),
+                jnp.where(first, partner, own),
+                jnp.where(first, near, far),
+            ],
+            axis=0,
+        )
+
     along = {0: block, depth: block}
-    kinds, pieces, late_kinds, late_pieces = [], [], [], []
+    kinds, pieces = [], []
+    cot_own = cotangent[0]
+    final = len(shifts) - 1
     for number, group in enumerate(shifts):
         blocks = jnp.concatenate([along[k] for k in group], axis=0)
+        kinds.append((group, 0))
+        pieces.append(blocks)
         sent = [lax.ppermute(blocks, "tm", swap_x), lax.ppermute(blocks, "tm", swap_y)]
+        sent_kinds = [(group, 1), (group, 2)]
         if number:
             sent.append(lax.ppermute(relayed, "tm", corner))
-        if number + 1 < len(shifts):
-            for k in shifts[number + 1]:
-                from_before = 2 * k <= depth
-                sent.append(lax.ppermute(along[k - 1 if from_before else k + 1], "tm", forth if from_before else back))
-        sent = list(lax.optimization_barrier(tuple(sent)))
-        from_x, from_y = sent[:2]
-        relayed = jnp.where(first, from_y, from_x)
-        kinds += [(group, 0), (group, 1), (group, 2)]
-        pieces += [blocks, from_x, from_y]
-        late_kinds.append((group, 3))
-        if number:
-            late_pieces.append(sent[2])
+            sent_kinds.append((shifts[number - 1], 3))
+        onward = shifts[number + 1] if number < final else ()
+        for k in onward:
+            from_before = 2 * k <= depth
+            sent.append(lax.ppermute(along[k - 1 if from_before else k + 1], "tm", forth if from_before else back))
+        beside = []
+        if number == 0:
+            beside = prepare_first()
+        elif number == 1:
+            both = jnp.stack([normed_own, cot_own])
+            edge = jnp.concatenate(
+                [
+                    jnp.where(first, normed_own[:HALO], normed_own[rows - HALO :]),
+                    jnp.where(first, cot_own[:EDGE], cot_own[rows - EDGE :]),
+                ],
+                axis=0,
+            )
+            beside = [*across(both, edge), *prepare_second()]
+        if number == final:
+            (partner, near, far), ready = (beside or crossing)[:3], beside[3:]
+            beside = [
+                assemble(normed_own, partner[0], near[:HALO], far[:HALO]),
+                assemble(cot_own, partner[1], near[HALO:], far[HALO:]),
+                place(scal, kinds, pieces, block.shape[0], chips),
+                *ready,
+            ]
+        sent, beside = lax.optimization_barrier((sent, beside))
+        relayed = jnp.where(first, sent[1], sent[0])
+        if number == 0:
+            (normed_own,) = beside
+        elif number == 1:
+            crossing, (taps, gain, shift, counts, scal) = beside[:3], beside[3:8]
+        if number == final:
+            normed_b, wide_cot, weight = beside[:3]
+            late_kinds, late_pieces = sent_kinds, sent
         else:
-            square_done = from_x
-        if number + 1 < len(shifts):
-            for k, arrived in zip(shifts[number + 1], sent[-len(shifts[number + 1]) :]):
+            kinds += sent_kinds
+            pieces += sent[: len(sent_kinds)]
+            for k, arrived in zip(onward, sent[len(sent_kinds) :]):
                 along[k] = arrived
-    features, start_noise, cotangent, kernel, bn_gain, bn_shift, _ = lax.optimization_barrier(
-        (features, start_noise, cotangent, kernel, bn_gain, bn_shift, square_done)
-    )
-    packed = jnp.concatenate([features, start_noise, cotangent], axis=0)
-    partner, near, far = across(
-        packed, jnp.where(first, packed[:, :HALO], packed[:, rows - HALO :])
-    )
-    whole = jnp.concatenate(
-        [
-            jnp.where(first, far, near),
-            jnp.where(first, packed, partner),
-            jnp.where(first, partner, packed),
-            jnp.where(first, near, far),
-        ],
-        axis=1,
-    )
-    wide_features, wide_noise, wide_cot = whole[0], whole[1], whole[2]
+    late_kinds.append((shifts[final], 3))
+    late_pieces.append(lax.ppermute(relayed, "tm", corner))
+    weight = place_late(scal, late_kinds, late_pieces, block.shape[0], weight)
 
     place_of = jnp.arange(half_width, dtype=jnp.int32)
     source = (2 * (place_of // slice_width) + core) * slice_width + place_of % slice_width
     chosen = (jnp.arange(width, dtype=jnp.int32)[:, None] == source[None, :]).astype(BF16)
-    cot = jnp.dot(wide_cot[HALO - EDGE : -(HALO - EDGE)], chosen, preferred_element_type=F32).astype(BF16)
-
-    def mine_of(array):
-        parts = array.reshape(array.shape[0], chips, 2, slice_width)
-        return lax.dynamic_index_in_dim(parts, core, 2, keepdims=False).reshape(-1, half_width)
-
-    channel = mine_of(jnp.concatenate([kernel, bn_gain[None], bn_shift[None]], axis=0))
-    gain, shift = channel[taps_n : taps_n + 1], channel[taps_n + 1 :]
-    taps = jnp.broadcast_to(channel[:taps_n, None], (taps_n, 8, half_width))
-
-    frame_ids = chip * chip_rows - HALO + jnp.arange(whole.shape[1], dtype=jnp.int32)
-    live = ((frame_ids >= 0) & (frame_ids < end)).astype(F32)
-    summed = wide_features.astype(F32) + noise_scale * wide_noise.astype(F32) * live[:, None]
-    normed_b = normalize(summed)[0].astype(BF16)
-
-    relayed, normed_b, taps, gain, shift = lax.optimization_barrier(
-        (relayed, normed_b, taps, gain, shift)
-    )
-    late_pieces.append(lax.ppermute(relayed, "tm", corner))
-    kinds, pieces = kinds + late_kinds[:1], pieces + late_pieces[:1]
-    weight = place(scal, kinds, pieces, block.shape[0], chips)
-    weight = place_late(scal, late_kinds[1:], late_pieces[1:], block.shape[0], weight)
+    cot = jnp.dot(wide_cot, chosen, preferred_element_type=F32).astype(BF16)
 
     value, gate, glu, conv, stats = forward(
         scal, normed_b, weight, taps, chip_rows, chips, True
     )
-    scaled, grad, inv, sums = batch(scal, counts, peers_of(stats), conv, cot, gain, shift, chips)
+    gathered, base = peers_of(stats), jnp.stack([features[0], start_noise[0]])
+    base, _ = lax.optimization_barrier((base, stats))
+    partner, near, far = across(base, jnp.where(first, base[:, :HALO], base[:, rows - HALO :]))
+    wide_features, wide_noise = (
+        assemble(base[n], partner[n], near[n], far[n]) for n in range(2)
+    )
+    scaled, grad, inv, sums = batch(scal, counts, gathered, conv, cot, gain, shift, chips)
+    sums, wide_features, wide_noise = lax.optimization_barrier((sums, wide_features, wide_noise))
     mine, other, grad_conv, totals = backward(
         scal, peers_of(sums), scaled, grad, inv, gain, taps, value, gate, weight
     )

time: 206 us -> 209 us (1.015)
  waiting for transfers between devices: 51.6 us -> 62.4 us
  local copies, waits for them, and re-layouts: 17.1 us -> 10.6 us
  starting transfers between devices: 47.8 us -> 51 us
  other arithmetic: 10.7 us -> 8.34 us
    ppermute x2 -> x3, waiting for transfers between devices: 0.01 us -> 12.1 us  [across(): lax.ppermute(edge, 'tm', near_pairs)]
    ppermute x2, waiting for transfers between devices: 15.6 us -> 5.12 us  [on_device(): sent.append(lax.ppermute(relayed, 'tm', corner))]
    ppermute x3, waiting for transfers between devices: 2.55 us -> 9.61 us  [on_device(): lax.ppermute(blocks, 'tm', swap_x)]
    ppermute x3, waiting for transfers between devices: 7.01 us -> 1.46 us  [on_device(): lax.ppermute(blocks, 'tm', swap_y)]
    ppermute x1, waiting for transfers between devices: 0.01 us -> 4.89 us  [on_device(): late_pieces.append(lax.ppermute(relayed, 'tm', corner))]
    select_n x6 -> x12, other arithmetic: 3.81 us -> 0.46 us  [the longest x3 0.22 us: assemble(): jnp.where(first, own, partner)]
    ppermute x2, starting transfers between devices: 0.6 us -> 3.56 us  [on_device(): sent.append(lax.ppermute(relayed, 'tm', corner))]
    all_to_all x3, starting transfers between devices: 15.2 us -> 17.7 us  [peers_of(): lax.all_to_all(array, 'tm', 0, 0, axis_index_groups=cores, tiled=True)]
  transfers between devices with their start and end apart: 24 -> 27, of which waited for: 11 -> 14; matrix products, arithmetic and copies ran while one was open for 10% -> 6% of each run, Pallas kernels for 7% -> 9%
where the time goes in v6:
time: 209 us; the launch traced here: 208 us
  waiting for transfers between devices  62.4 us (30%)
  Pallas kernels  60.7 us (29%)
  starting transfers between devices  51 us (24%)
  blocking collectives  10.9 us (5%)
  local copies, waits for them, and re-layouts  10.6 us (5%)
  other arithmetic  8.34 us (4%)
    all_to_all x3, starting transfers between devices, peers_of(): lax.all_to_all(array, 'tm', 0, 0, axis_index_groups=cores, tiled=True)  17.7 us
    pallas_call x2, Pallas kernels, forward(): pl.pallas_call(functools.partial(forward_kernel, keep), grid=(steps,), in...  15.5 us
    all_to_all x3, waiting for transfers between devices, peers_of(): lax.all_to_all(array, 'tm', 0, 0, axis_index_groups=cores, tiled=True)  14.9 us
    ppermute x3, waiting for transfers between devices, across(): lax.ppermute(edge, 'tm', near_pairs)  12.1 us
    all_to_all x1, blocking collectives, peers_of(): lax.all_to_all(array, 'tm', 0, 0, axis_index_groups=cores, tiled=True)  10.9 us
    ppermute x3, waiting for transfers between devices, on_device(): lax.ppermute(along[k - 1 if from_before else k + 1], 'tm', forth if from_...  9.85 us
    ppermute x3, waiting for transfers between devices, on_device(): lax.ppermute(blocks, 'tm', swap_x)  9.61 us
    pallas_call x1, Pallas kernels, backward(): pl.pallas_call(backward_kernel, grid=(steps,), in_specs=[pl.BlockSpec(mem...  8.2 us
  transfers between devices with their start and end apart: 27, of which 14 were waited for; matrix products, arithmetic and copies ran while one was open for 6% of the time, Pallas kernels for 9%

profile of v6, /device:TPU:0, one launch (start us, length us, event | category | flops | bytes accessed | tf_op | source)
XLA Modules:
  0.0 207.8 jit_solution(7753606776677715124)
XLA Ops:
  2.9 1.4 fusion.3
  4.3 1.4 multiply_reduce_fusion
  9.6 2.6 %collective-permute-start.1 = (bf16[96,1536]{1,0:T(8,128)(2,1)S(1)}, bf16[96,1536]{1,0:T(8,128)(2,1)S(1)}, u32[]{:S(2)}, u32[]{:S(2)}) collective-permute-start(bf16[96,1536]{1,0:T(8,128)(2,1)S(1)} %pad_maximum_fusion.6.refs_0_), channel_id=1, source_target_pairs={{0,2},{1,3},{2,0},{3,1},{4,6},{5,7},{6,4},{7,5},{8,10},{9,11},{10,... | collective-permute-start | bytes 884744 | tf_op jit(solution)/shard_map/ppermute | solution.py:711
  12.2 1.5 collective-permute-start.2
  13.7 1.6 collective-permute-start.3
  15.3 2.2 %collective-permute-start.4 = (bf16[96,1536]{1,0:T(8,128)(2,1)S(1)}, bf16[96,1536]{1,0:T(8,128)(2,1)S(1)}, u32[]{:S(2)}, u32[]{:S(2)}) collective-permute-start(bf16[96,1536]{1,0:T(8,128)(2,1)S(1)} %pad_maximum_fusion.6.refs_0_), channel_id=1, source_target_pairs={{0,24},{1,25},{2,26},{3,27},{4,28},{5,29},{6,30},{7,31},{8,0},{9,1... | collective-permute-start | bytes 884744 | tf_op jit(solution)/shard_map/ppermute | solution.py:719
  17.5 2.3 %collective-permute-done.1.refs_1_ = bf16[96,1536]{1,0:T(8,128)(2,1)S(1)} collective-permute-done((bf16[96,1536]{1,0:T(8,128)(2,1)S(1)}, bf16[96,1536]{1,0:T(8,128)(2,1)S(1)}, u32[]{:S(2)}, u32[]{:S(2)}) %collective-permute-start.1) | collective-permute-done | bytes 294944 | tf_op jit(solution)/shard_map/ppermute | solution.py:711
  19.8 1.5 collective-permute-done.2.refs_2_
  21.3 4.2 %collective-permute-done.3 = bf16[96,1536]{1,0:T(8,128)(2,1)S(1)} collective-permute-done((bf16[96,1536]{1,0:T(8,128)(2,1)S(1)}, bf16[96,1536]{1,0:T(8,128)(2,1)S(1)}, u32[]{:S(2)}, u32[]{:S(2)}) %collective-permute-start.3) | collective-permute-done | bytes 294944 | tf_op jit(solution)/shard_map/ppermute | solution.py:719
  25.4 4.7 %collective-permute-done.4 = bf16[96,1536]{1,0:T(8,128)(2,1)S(1)} collective-permute-done((bf16[96,1536]{1,0:T(8,128)(2,1)S(1)}, bf16[96,1536]{1,0:T(8,128)(2,1)S(1)}, u32[]{:S(2)}, u32[]{:S(2)}) %collective-permute-start.4) | collective-permute-done | bytes 294944 | tf_op jit(solution)/shard_map/ppermute | solution.py:719
  31.3 1.3 collective-permute-start.10
  33.4 4.1 %collective-permute-start.9 = (bf16[2,128,1536]{2,1,0:T(8,128)(2,1)S(1)}, bf16[2,128,1536]{2,1,0:T(8,128)(2,1)S(1)}, u32[]{:S(2)}, u32[]{:S(2)}) collective-permute-start(bf16[2,128,1536]{2,1,0:T(8,128)(2,1)S(1)} %pad_maximum_fusion.4), channel_id=1, source_target_pairs={{0,1},{1,0},{2,3},{3,2},{4,5},{5,4},{6,7},{7,6},{8,9},{9,8},{10,11... | collective-permute-start | bytes 2359304 | tf_op jit(solution)/shard_map/ppermute | solution.py:657
  37.5 12.1 %collective-permute-done.10 = bf16[48,1536]{1,0:T(8,128)(2,1)S(1)} collective-permute-done((bf16[48,1536]{1,0:T(8,128)(2,1)S(1)}, bf16[48,1536]{1,0:T(8,128)(2,1)S(1)}, u32[]{:S(2)}, u32[]{:S(2)}) %collective-permute-start.10) | collective-permute-done | bytes 147488 | tf_op jit(solution)/shard_map/ppermute | solution.py:658
  49.6 1.1 collective-permute-start.8
  52.3 5.1 %collective-permute-done.7.refs_6_ = bf16[96,1536]{1,0:T(8,128)(2,1)S(1)} collective-permute-done((bf16[96,1536]{1,0:T(8,128)(2,1)S(1)}, bf16[96,1536]{1,0:T(8,128)(2,1)S(1)}, u32[]{:S(2)}, u32[]{:S(2)}) %collective-permute-start.7) | collective-permute-done | bytes 294944 | tf_op jit(solution)/shard_map/ppermute | solution.py:714
  58.5 1.0 broadcast_in_dim.9.taps
  59.8 2.5 %collective-permute-start.14 = (bf16[192,1536]{1,0:T(8,128)(2,1)S(1)}, bf16[192,1536]{1,0:T(8,128)(2,1)S(1)}, u32[]{:S(2)}, u32[]{:S(2)}) collective-permute-start(bf16[192,1536]{1,0:T(8,128)(2,1)S(1)} %broadcast_select_fusion), channel_id=1, source_target_pairs={{0,2},{1,5},{2,0},{3,7},{4,6},{5,1},{6,4},{7,3},{8,10},{9,13},{10,... | collective-permute-start | bytes 1769480 | tf_op jit(solution)/shard_map/ppermute | solution.py:714
  62.6 4.2 %place_weights.1.refs_4_ = bf16[1536,1536]{1,0:T(8,128)(2,1)} custom-call(s32[6]{0:T(128)} %stack.38.scal, bf16[96,1536]{1,0:T(8,128)(2,1)} %copy-done.10, bf16[96,1536]{1,0:T(8,128)(2,1)} %copy-done.6, bf16[96,1536]{1,0:T(8,128)(2,1)} %copy-done.7, bf16[192,1536]{1,0:T(8,128)(2,1)} %copy-done.5, bf16[192,1536]{1,0:T(8,128)(2,1)} %copy-done.2, ...), custom_call_target="tpu_custom_call" | custom-call | bytes 9437184 | tf_op jit(solution)/shard_map/place_weights/pallas_call | solution.py:124
  66.9 1.0 pad_maximum_fusion.nb
  67.9 7.3 %collective-permute-done.12.refs_0_ = bf16[96,1536]{1,0:T(8,128)(2,1)S(1)} collective-permute-done((bf16[96,1536]{1,0:T(8,128)(2,1)S(1)}, bf16[96,1536]{1,0:T(8,128)(2,1)S(1)}, u32[]{:S(2)}, u32[]{:S(2)}) %collective-permute-start.12) | collective-permute-done | bytes 294944 | tf_op jit(solution)/shard_map/ppermute | solution.py:711
  75.3 1.8 collective-permute-start.15
  77.2 4.9 %collective-permute-done.15.refs_3_ = bf16[96,1536]{1,0:T(8,128)(2,1)S(1)} collective-permute-done((bf16[96,1536]{1,0:T(8,128)(2,1)S(1)}, bf16[96,1536]{1,0:T(8,128)(2,1)S(1)}, u32[]{:S(2)}, u32[]{:S(2)}) %collective-permute-start.15) | collective-permute-done | bytes 294944 | tf_op jit(solution)/shard_map/ppermute | solution.py:756
  82.8 2.5 %place_last_weights.1.value_w.gate_w = bf16[1536,1536]{1,0:T(8,128)(2,1)} custom-call(s32[6]{0:T(128)} %stack.38.scal, bf16[96,1536]{1,0:T(8,128)(2,1)} %copy-done.8, bf16[96,1536]{1,0:T(8,128)(2,1)} %copy-done.9, bf16[192,1536]{1,0:T(8,128)(2,1)} %copy-done.14, bf16[96,1536]{1,0:T(8,128)(2,1)} %copy-done.19, ...), custom_call_target="tpu_custom_call", output_to_operand_aliasing={{}: (5, {})} | custom-call | bytes 2949120 | tf_op jit(solution)/shard_map/place_last_weights/pallas_call | solution.py:139
  85.3 7.8 %project_glu_conv.2 = (f32[256,768]{1,0:T(8,128)}, f32[256,768]{1,0:T(8,128)}, bf16[320,768]{1,0:T(8,128)(2,1)}, f32[288,768]{1,0:T(8,128)}, f32[16,2,768]{2,1,0:T(2,128)}) custom-call(s32[6]{0:T(128)} %stack.38.scal, bf16[320,1536]{1,0:T(8,128)(2,1)} %pad_maximum_fusion.nb, bf16[1536,1536]{1,0:T(8,128)(2,1)} %place_last_weights.1.value_w.gate_w, ...), custom_call_target="tpu_custom_call" | custom-call | flops 1509949440 | bytes 7176192 | tf_op jit(solution)/shard_map/project_glu_conv/pallas_call | solution.py:183
  93.9 1.3 collective-permute-start.17
  95.2 8.0 %all-to-all-start = ((f32[16,2,768]{2,1,0:T(2,128)}), f32[16,2,768]{2,1,0:T(2,128)S(1)}, u32[]{:S(2)}, u32[]{:S(2)}) async-start(f32[16,2,768]{2,1,0:T(2,128)} %get-tuple-element.79), calls=%async_computation | async-start | bytes 196608 | tf_op jit(solution)/shard_map/all_to_all | solution.py:663
  103.2 1.9 fusion.2.cot
  105.1 5.8 %all-to-all-done.stats = f32[16,2,768]{2,1,0:T(2,128)S(1)} async-done(((f32[16,2,768]{2,1,0:T(2,128)}), f32[16,2,768]{2,1,0:T(2,128)S(1)}, u32[]{:S(2)}, u32[]{:S(2)}) %all-to-all-start) | async-done | bytes 98336 | tf_op jit(solution)/shard_map/all_to_all | solution.py:663
  111.5 3.9 %batch_norm_swish.1 = (f32[288,768]{1,0:T(8,128)}, f32[288,768]{1,0:T(8,128)}, f32[1,768]{1,0:T(1,128)}, f32[16,2,768]{2,1,0:T(2,128)}) custom-call(s32[6]{0:T(128)} %stack.38.scal, f32[2,16]{1,0:T(2,128)} %pad_maximum_fusion.8.counts, f32[16,2,768]{2,1,0:T(2,128)} %copy-done.16, f32[288,768]{1,0:T(8,128)} %get-tuple-element.80.conv, ...), custom_call_target="tpu_custom_call" | custom-call | flops 8847360 | bytes 3538944 | tf_op jit(solution)/shard_map/batch_norm_swish/pallas_call | solution.py:263
  115.6 1.4 pad_maximum_fusion.1
  117.0 10.9 %all_to_all.25.sums = f32[16,2,768]{2,1,0:T(2,128)} all-to-all(f32[16,2,768]{2,1,0:T(2,128)S(1)} %copy-done.24), channel_id=1, replica_groups={{0,2,4,6,8,10,12,14,16,18,20,22,24,26,28,30},{1,3,5,7,9,11,13,15,17,19,..., dimensions={0} | all-to-all | bytes 196608 | tf_op jit(solution)/shard_map/all_to_all | solution.py:663
  128.0 8.2 %grad_conv_project_back.1 = (f32[128,1536]{1,0:T(8,128)}, f32[128,1536]{1,0:T(8,128)}, bf16[256,768]{1,0:T(8,128)(2,1)}, f32[2,768]{1,0:T(2,128)}) custom-call(s32[6]{0:T(128)} %stack.38.scal, f32[16,2,768]{2,1,0:T(2,128)} %all_to_all.25.sums, f32[288,768]{1,0:T(8,128)} %get-tuple-element.87.scaled, f32[288,768]{1,0:T(8,128)} %get-tuple-element.88.grad, ...), custom_call_target="tpu_custom_call" | custom-call | flops 1207959552 | bytes 9142272 | tf_op jit(solution)/shard_map/grad_conv_project_back/pallas_call | solution.py:338
  136.2 2.5 %collective-permute-done.19.other = f32[128,1536]{1,0:T(8,128)S(1)} collective-permute-done((f32[128,1536]{1,0:T(8,128)}, f32[128,1536]{1,0:T(8,128)S(1)}, u32[]{:S(2)}, u32[]{:S(2)}) %collective-permute-start.19) | collective-permute-done | bytes 786464 | tf_op jit(solution)/shard_map/ppermute | solution.py:778
  139.6 3.2 %direction.1 = (f32[128,1536]{1,0:T(8,128)}, f32[32,1536]{1,0:T(8,128)}, f32[32,1,128]{2,1,0:T(1,128)}) custom-call(s32[6]{0:T(128)} %stack.38.scal, f32[128,1536]{1,0:T(8,128)} %get-tuple-element.92.mine, f32[128,1536]{1,0:T(8,128)} %copy-done.12, bf16[128,1536]{1,0:T(8,128)(2,1)} %bitcast.64, bf16[128,1536]{1,0:T(8,128)(2,1)} %bitcast.62), custom_call_target="tpu_custom_call" | custom-call | flops 5898240 | bytes 3145728 | tf_op jit(solution)/shard_map/direction/pallas_call | solution.py:568
  143.0 1.3 collective-permute-start.21
  145.0 7.0 %all-to-all-start.2 = ((f32[32,1,128]{2,1,0:T(1,128)}), f32[32,1,128]{2,1,0:T(1,128)S(1)}, u32[]{:S(2)}, u32[]{:S(2)}) async-start(f32[32,1,128]{2,1,0:T(1,128)} %get-tuple-element.94), calls=%async_computation.2 | async-start | bytes 32768 | tf_op jit(solution)/shard_map/all_to_all | solution.py:780
  151.9 4.9 %tap_grad.1.taps_before = f32[31,768]{1,0:T(8,128)} custom-call(bf16[256,768]{1,0:T(8,128)(2,1)} %get-tuple-element.95.grad_conv, bf16[320,768]{1,0:T(8,128)(2,1)} %get-tuple-element.96.glu), custom_call_target="tpu_custom_call" | custom-call | flops 12189696 | bytes 983040 | tf_op jit(solution)/shard_map/tap_grad/pallas_call | solution.py:386
  156.9 2.0 all-to-all-done.2.squares
  160.5 4.5 %ascend.1 = (f32[128,1536]{1,0:T(8,128)}, bf16[320,1536]{1,0:T(8,128)(2,1)}) custom-call(s32[6]{0:T(128)} %stack.38.scal, f32[32,1,128]{2,1,0:T(1,128)} %copy-done.25, bf16[320,1536]{1,0:T(8,128)(2,1)} %get-tuple-element.98.features, bf16[320,1536]{1,0:T(8,128)(2,1)} %get-tuple-element.99.noise, f32[128,1536]{1,0:T(8,128)} %get-tuple-element.100.mine, ...), custom_call_target="tpu_custom_call" | custom-call | flops 14745600 | bytes 3932160 | tf_op jit(solution)/shard_map/ascend/pallas_call | solution.py:612
  165.0 7.7 %project_glu_conv.3 = (bf16[320,768]{1,0:T(8,128)(2,1)}, f32[288,768]{1,0:T(8,128)}, f32[16,2,768]{2,1,0:T(2,128)}) custom-call(s32[6]{0:T(128)} %stack.38.scal, bf16[320,1536]{1,0:T(8,128)(2,1)} %get-tuple-element.103.nb, bf16[1536,1536]{1,0:T(8,128)(2,1)} %place_last_weights.1.value_w.gate_w, bf16[1536,1536]{1,0:T(8,128)(2,1)} %place_last_weights.1.value_w.gate_w, ...), custom_call_target="tpu_custom_call" | custom-call | flops 1509949440 | bytes 7176192 | tf_op jit(solution)/shard_map/project_glu_conv/pallas_call | solution.py:183
  172.7 4.7 %all-to-all-start.3 = ((f32[16,2,768]{2,1,0:T(2,128)}), f32[16,2,768]{2,1,0:T(2,128)S(1)}, u32[]{:S(2)}, u32[]{:S(2)}) async-start(f32[16,2,768]{2,1,0:T(2,128)} %get-tuple-element.104.stats.local_stats), calls=%async_computation.3 | async-start | bytes 196608 | tf_op jit(solution)/shard_map/all_to_all | solution.py:663
  177.4 5.7 %raw_taps.1 = (f32[31,768]{1,0:T(8,128)}, f32[31,768]{1,0:T(8,128)}) custom-call(s32[6]{0:T(128)} %stack.38.scal, f32[288,768]{1,0:T(8,128)} %get-tuple-element.105.conv, bf16[320,768]{1,0:T(8,128)(2,1)} %get-tuple-element.106.glu, f32[16,2,768]{2,1,0:T(2,128)} %get-tuple-element.104.stats.local_stats), custom_call_target="tpu_custom_call" | custom-call | flops 13713408 | bytes 1966080 | tf_op jit(solution)/shard_map/raw_taps/pallas_call | solution.py:419
  183.1 2.0 all-to-all-done.3.stats
  185.7 6.3 %batch_norm_swish_taps.1 = (bf16[16,48,128]{2,1,0:T(8,128)(2,1)}, f32[1,768]{1,0:T(1,128)}) custom-call(s32[6]{0:T(128)} %stack.38.scal, f32[2,16]{1,0:T(2,128)} %pad_maximum_fusion.8.counts, f32[16,2,768]{2,1,0:T(2,128)} %copy-done.15, f32[288,768]{1,0:T(8,128)} %get-tuple-element.105.conv, bf16[288,768]{1,0:T(8,128)(2,1)} %fusion.2.cot, ...), custom_call_target="tpu_custom_call" | custom-call | flops 22118400 | bytes 2211840 | tf_op jit(solution)/shard_map/batch_norm_swish_taps/pallas_call | solution.py:479
  192.1 4.9 %all-to-all-start.4 = ((bf16[16,48,128]{2,1,0:T(8,128)(2,1)}), bf16[16,48,128]{2,1,0:T(8,128)(2,1)S(1)}, u32[]{:S(2)}, u32[]{:S(2)}) async-start(bf16[16,48,128]{2,1,0:T(8,128)(2,1)} %get-tuple-element.110), calls=%async_computation.4 | async-start | bytes 393216 | tf_op jit(solution)/shard_map/all_to_all | solution.py:663
  197.0 1.3 fusion.17.known
  198.3 7.1 %all-to-all-done.4.received = bf16[16,48,128]{2,1,0:T(8,128)(2,1)S(1)} async-done(((bf16[16,48,128]{2,1,0:T(8,128)(2,1)}), bf16[16,48,128]{2,1,0:T(8,128)(2,1)S(1)}, u32[]{:S(2)}, u32[]{:S(2)}) %all-to-all-start.4) | async-done | bytes 196640 | tf_op jit(solution)/shard_map/all_to_all | solution.py:663
  206.2 1.7 finish.1
  (126 shorter events, 17.4 us)
Async XLA Ops:
  0.6 5.1 %copy-start.1 = (bf16[1,128,1536]{2,1,0:T(8,128)(2,1)S(1)}, bf16[1,128,1536]{2,1,0:T(8,128)(2,1)}, u32[]{:S(2)}) copy-start(bf16[1,128,1536]{2,1,0:T(8,128)(2,1)} %param.8) | copy-start | bytes 1179652
  0.6 5.1 %copy-start = (bf16[1,128,1536]{2,1,0:T(8,128)(2,1)S(1)}, bf16[1,128,1536]{2,1,0:T(8,128)(2,1)}, u32[]{:S(2)}) copy-start(bf16[1,128,1536]{2,1,0:T(8,128)(2,1)} %param.9) | copy-start | bytes 1179652
  0.7 5.5 %copy-start.23 = (f32[31,1536]{1,0:T(8,128)S(1)}, f32[31,1536]{1,0:T(8,128)}, u32[]{:S(2)}) copy-start(f32[31,1536]{1,0:T(8,128)} %param.12) | copy-start | bytes 571396
  1.7 7.8 %collective-permute-start = (bf16[48,1536]{1,0:T(8,128)(2,1)S(1)}, bf16[48,1536]{1,0:T(8,128)(2,1)S(1)}, u32[]{:S(2)}, u32[]{:S(2)}) collective-permute-start(bf16[48,1536]{1,0:T(8,128)(2,1)S(1)} %dynamic-slice_bitcast_fusion), channel_id=1, source_target_pairs={{0,1},{1,0},{2,3},{3,2},{4,5},{5,4},{6,7},{7,6},{8,9},{9,8},{10,11... | collective-permute-start | bytes 442376 | tf_op jit(solution)/shard_map/ppermute | solution.py:671
  4.3 2.8 %copy-start.26 = (f32[1536]{0:T(1024)S(1)}, f32[1536]{0:T(1024)}, u32[]{:S(2)}) copy-start(f32[1536]{0:T(1024)} %param.13) | copy-start | bytes 18436
  4.3 2.9 %copy-start.27 = (f32[1536]{0:T(1024)S(1)}, f32[1536]{0:T(1024)}, u32[]{:S(2)}) copy-start(f32[1536]{0:T(1024)} %param.14) | copy-start | bytes 18436
  6.1 3.4 %copy-start.20 = (bf16[96,1536]{1,0:T(8,128)(2,1)S(1)}, bf16[96,1536]{1,0:T(8,128)(2,1)}, u32[]{:S(2)}) copy-start(bf16[96,1536]{1,0:T(8,128)(2,1)} %param.11) | copy-start | bytes 884740
  7.0 10.5 %copy-start.4 = (bf16[1,128,1536]{2,1,0:T(8,128)(2,1)S(1)}, bf16[1,128,1536]{2,1,0:T(8,128)(2,1)}, u32[]{:S(2)}) copy-start(bf16[1,128,1536]{2,1,0:T(8,128)(2,1)} %param.10) | copy-start | bytes 1179652
  9.5 27.9 %copy-start.10 = (bf16[96,1536]{1,0:T(8,128)(2,1)}, bf16[96,1536]{1,0:T(8,128)(2,1)S(1)}, u32[]{:S(2)}) copy-start(bf16[96,1536]{1,0:T(8,128)(2,1)S(1)} %pad_maximum_fusion.6.refs_0_) | copy-start | bytes 884740
  9.6 10.2 %collective-permute-start.1 = (bf16[96,1536]{1,0:T(8,128)(2,1)S(1)}, bf16[96,1536]{1,0:T(8,128)(2,1)S(1)}, u32[]{:S(2)}, u32[]{:S(2)}) collective-permute-start(bf16[96,1536]{1,0:T(8,128)(2,1)S(1)} %pad_maximum_fusion.6.refs_0_), channel_id=1, source_target_pairs={{0,2},{1,3},{2,0},{3,1},{4,6},{5,7},{6,4},{7,5},{8,10},{9,11},{10,... | collective-permute-start | bytes 884744 | tf_op jit(solution)/shard_map/ppermute | solution.py:711
  12.2 9.1 %collective-permute-start.2 = (bf16[96,1536]{1,0:T(8,128)(2,1)S(1)}, bf16[96,1536]{1,0:T(8,128)(2,1)S(1)}, u32[]{:S(2)}, u32[]{:S(2)}) collective-permute-start(bf16[96,1536]{1,0:T(8,128)(2,1)S(1)} %pad_maximum_fusion.6.refs_0_), channel_id=1, source_target_pairs={{0,4},{1,5},{2,6},{3,7},{4,0},{5,1},{6,2},{7,3},{8,12},{9,13},{10,... | collective-permute-start | bytes 884744 | tf_op jit(solution)/shard_map/ppermute | solution.py:711
  13.7 11.7 %collective-permute-start.3 = (bf16[96,1536]{1,0:T(8,128)(2,1)S(1)}, bf16[96,1536]{1,0:T(8,128)(2,1)S(1)}, u32[]{:S(2)}, u32[]{:S(2)}) collective-permute-start(bf16[96,1536]{1,0:T(8,128)(2,1)S(1)} %pad_maximum_fusion.6.refs_0_), channel_id=1, source_target_pairs={{0,8},{1,9},{2,10},{3,11},{4,12},{5,13},{6,14},{7,15},{8,16},{9,17... | collective-permute-start | bytes 884744 | tf_op jit(solution)/shard_map/ppermute | solution.py:719
  15.3 14.8 %collective-permute-start.4 = (bf16[96,1536]{1,0:T(8,128)(2,1)S(1)}, bf16[96,1536]{1,0:T(8,128)(2,1)S(1)}, u32[]{:S(2)}, u32[]{:S(2)}) collective-permute-start(bf16[96,1536]{1,0:T(8,128)(2,1)S(1)} %pad_maximum_fusion.6.refs_0_), channel_id=1, source_target_pairs={{0,24},{1,25},{2,26},{3,27},{4,28},{5,29},{6,30},{7,31},{8,0},{9,1... | collective-permute-start | bytes 884744 | tf_op jit(solution)/shard_map/ppermute | solution.py:719
  19.8 17.7 %copy-start.6 = (bf16[96,1536]{1,0:T(8,128)(2,1)}, bf16[96,1536]{1,0:T(8,128)(2,1)S(1)}, u32[]{:S(2)}) copy-start(bf16[96,1536]{1,0:T(8,128)(2,1)S(1)} %collective-permute-done.1.refs_1_) | copy-start | bytes 884740
  21.3 16.2 %copy-start.7 = (bf16[96,1536]{1,0:T(8,128)(2,1)}, bf16[96,1536]{1,0:T(8,128)(2,1)S(1)}, u32[]{:S(2)}) copy-start(bf16[96,1536]{1,0:T(8,128)(2,1)S(1)} %collective-permute-done.2.refs_2_) | copy-start | bytes 884740
  30.2 29.4 %copy-start.5 = (bf16[192,1536]{1,0:T(8,128)(2,1)}, bf16[192,1536]{1,0:T(8,128)(2,1)S(1)}, u32[]{:S(2)}) copy-start(bf16[192,1536]{1,0:T(8,128)(2,1)S(1)} %constant_dynamic-update-slice_fusion.refs_3_) | copy-start | bytes 1769476
  30.2 28.3 %collective-permute-start.5 = (bf16[192,1536]{1,0:T(8,128)(2,1)S(1)}, bf16[192,1536]{1,0:T(8,128)(2,1)S(1)}, u32[]{:S(2)}, u32[]{:S(2)}) collective-permute-start(bf16[192,1536]{1,0:T(8,128)(2,1)S(1)} %constant_dynamic-update-slice_fusion.refs_3_), channel_id=1, source_target_pairs={{0,2},{1,3},{2,0},{3,1},{4,6},{5,7},{6,4},{7,5},{8,10},{9,11},{10,... | collective-permute-start | bytes 1769480 | tf_op jit(solution)/shard_map/ppermute | solution.py:711
  30.8 27.7 %collective-permute-start.6 = (bf16[192,1536]{1,0:T(8,128)(2,1)S(1)}, bf16[192,1536]{1,0:T(8,128)(2,1)S(1)}, u32[]{:S(2)}, u32[]{:S(2)}) collective-permute-start(bf16[192,1536]{1,0:T(8,128)(2,1)S(1)} %constant_dynamic-update-slice_fusion.refs_3_), channel_id=1, source_target_pairs={{0,4},{1,5},{2,6},{3,7},{4,0},{5,1},{6,2},{7,3},{8,12},{9,13},{10,... | collective-permute-start | bytes 1769480 | tf_op jit(solution)/shard_map/ppermute | solution.py:711
  31.3 18.3 %collective-permute-start.10 = (bf16[48,1536]{1,0:T(8,128)(2,1)S(1)}, bf16[48,1536]{1,0:T(8,128)(2,1)S(1)}, u32[]{:S(2)}, u32[]{:S(2)}) collective-permute-start(bf16[48,1536]{1,0:T(8,128)(2,1)S(1)} %pad_maximum_fusion.7), channel_id=1, source_target_pairs={{2,0},{4,2},{6,4},{8,6},{10,8},{12,10},{14,12},{16,14},{18,16},{20... | collective-permute-start | bytes 442376 | tf_op jit(solution)/shard_map/ppermute | solution.py:658
  32.6 18.1 %collective-permute-start.11 = (bf16[48,1536]{1,0:T(8,128)(2,1)S(1)}, bf16[48,1536]{1,0:T(8,128)(2,1)S(1)}, u32[]{:S(2)}, u32[]{:S(2)}) collective-permute-start(bf16[48,1536]{1,0:T(8,128)(2,1)S(1)} %pad_maximum_fusion.7), channel_id=1, source_target_pairs={{2,1},{4,3},{6,5},{8,7},{10,9},{12,11},{14,13},{16,15},{18,17},{20... | collective-permute-start | bytes 442376 | tf_op jit(solution)/shard_map/ppermute | solution.py:659
  33.4 25.1 %collective-permute-start.9 = (bf16[2,128,1536]{2,1,0:T(8,128)(2,1)S(1)}, bf16[2,128,1536]{2,1,0:T(8,128)(2,1)S(1)}, u32[]{:S(2)}, u32[]{:S(2)}) collective-permute-start(bf16[2,128,1536]{2,1,0:T(8,128)(2,1)S(1)} %pad_maximum_fusion.4), channel_id=1, source_target_pairs={{0,1},{1,0},{2,3},{3,2},{4,5},{5,4},{6,7},{7,6},{8,9},{9,8},{10,11... | collective-permute-start | bytes 2359304 | tf_op jit(solution)/shard_map/ppermute | solution.py:657
  49.6 8.8 %collective-permute-start.8 = (bf16[96,1536]{1,0:T(8,128)(2,1)S(1)}, bf16[96,1536]{1,0:T(8,128)(2,1)S(1)}, u32[]{:S(2)}, u32[]{:S(2)}) collective-permute-start(bf16[96,1536]{1,0:T(8,128)(2,1)S(1)} %collective-permute-done.3), channel_id=1, source_target_pairs={{0,8},{1,9},{2,10},{3,11},{4,12},{5,13},{6,14},{7,15},{8,16},{9,17... | collective-permute-start | bytes 884744 | tf_op jit(solution)/shard_map/ppermute | solution.py:719
  50.7 6.7 %collective-permute-start.7 = (bf16[96,1536]{1,0:T(8,128)(2,1)S(1)}, bf16[96,1536]{1,0:T(8,128)(2,1)S(1)}, u32[]{:S(2)}, u32[]{:S(2)}) collective-permute-start(bf16[96,1536]{1,0:T(8,128)(2,1)S(1)} %broadcast_select_fusion.2), channel_id=1, source_target_pairs={{0,2},{1,5},{2,0},{3,7},{4,6},{5,1},{6,4},{7,3},{8,10},{9,13},{10,... | collective-permute-start | bytes 884744 | tf_op jit(solution)/shard_map/ppermute | solution.py:714
  57.4 2.2 %copy-start.18 = (bf16[96,1536]{1,0:T(8,128)(2,1)}, bf16[96,1536]{1,0:T(8,128)(2,1)S(1)}, u32[]{:S(2)}) copy-start(bf16[96,1536]{1,0:T(8,128)(2,1)S(1)} %collective-permute-done.7.refs_6_) | copy-start | bytes 884740
  58.4 4.0 %copy-start.17 = (bf16[96,1536]{1,0:T(8,128)(2,1)}, bf16[96,1536]{1,0:T(8,128)(2,1)S(1)}, u32[]{:S(2)}) copy-start(bf16[96,1536]{1,0:T(8,128)(2,1)S(1)} %collective-permute-done.8.refs_7_) | copy-start | bytes 884740
  58.4 1.2 copy-start.2
  58.5 1.3 copy-start.3
  59.8 15.5 %collective-permute-start.14 = (bf16[192,1536]{1,0:T(8,128)(2,1)S(1)}, bf16[192,1536]{1,0:T(8,128)(2,1)S(1)}, u32[]{:S(2)}, u32[]{:S(2)}) collective-permute-start(bf16[192,1536]{1,0:T(8,128)(2,1)S(1)} %broadcast_select_fusion), channel_id=1, source_target_pairs={{0,2},{1,5},{2,0},{3,7},{4,6},{5,1},{6,4},{7,3},{8,10},{9,13},{10,... | collective-permute-start | bytes 1769480 | tf_op jit(solution)/shard_map/ppermute | solution.py:714
  62.4 12.9 %collective-permute-start.12 = (bf16[96,1536]{1,0:T(8,128)(2,1)S(1)}, bf16[96,1536]{1,0:T(8,128)(2,1)S(1)}, u32[]{:S(2)}, u32[]{:S(2)}) collective-permute-start(bf16[96,1536]{1,0:T(8,128)(2,1)S(1)} %collective-permute-done.8.refs_7_), channel_id=1, source_target_pairs={{0,2},{1,3},{2,0},{3,1},{4,6},{5,7},{6,4},{7,5},{8,10},{9,11},{10,... | collective-permute-start | bytes 884744 | tf_op jit(solution)/shard_map/ppermute | solution.py:711
  62.5 12.8 %collective-permute-start.13 = (bf16[96,1536]{1,0:T(8,128)(2,1)S(1)}, bf16[96,1536]{1,0:T(8,128)(2,1)S(1)}, u32[]{:S(2)}, u32[]{:S(2)}) collective-permute-start(bf16[96,1536]{1,0:T(8,128)(2,1)S(1)} %collective-permute-done.8.refs_7_), channel_id=1, source_target_pairs={{0,4},{1,5},{2,6},{3,7},{4,0},{5,1},{6,2},{7,3},{8,12},{9,13},{10,... | collective-permute-start | bytes 884744 | tf_op jit(solution)/shard_map/ppermute | solution.py:711
  75.3 6.9 %copy-start.8 = (bf16[96,1536]{1,0:T(8,128)(2,1)}, bf16[96,1536]{1,0:T(8,128)(2,1)S(1)}, u32[]{:S(2)}) copy-start(bf16[96,1536]{1,0:T(8,128)(2,1)S(1)} %collective-permute-done.12.refs_0_) | copy-start | bytes 884740
  75.3 6.9 %copy-start.9 = (bf16[96,1536]{1,0:T(8,128)(2,1)}, bf16[96,1536]{1,0:T(8,128)(2,1)S(1)}, u32[]{:S(2)}) copy-start(bf16[96,1536]{1,0:T(8,128)(2,1)S(1)} %collective-permute-done.13.refs_1_) | copy-start | bytes 884740
  75.3 6.8 %copy-start.14 = (bf16[192,1536]{1,0:T(8,128)(2,1)}, bf16[192,1536]{1,0:T(8,128)(2,1)S(1)}, u32[]{:S(2)}) copy-start(bf16[192,1536]{1,0:T(8,128)(2,1)S(1)} %collective-permute-done.14.refs_2_) | copy-start | bytes 1769476
  75.3 6.8 %collective-permute-start.15 = (bf16[96,1536]{1,0:T(8,128)(2,1)S(1)}, bf16[96,1536]{1,0:T(8,128)(2,1)S(1)}, u32[]{:S(2)}, u32[]{:S(2)}) collective-permute-start(bf16[96,1536]{1,0:T(8,128)(2,1)S(1)} %broadcast_select_fusion.1), channel_id=1, source_target_pairs={{0,2},{1,5},{2,0},{3,7},{4,6},{5,1},{6,4},{7,3},{8,10},{9,13},{10,... | collective-permute-start | bytes 884744 | tf_op jit(solution)/shard_map/ppermute | solution.py:756
  93.1 22.4 %collective-permute-start.18 = (bf16[2,128,1536]{2,1,0:T(8,128)(2,1)S(1)}, bf16[2,128,1536]{2,1,0:T(8,128)(2,1)S(1)}, u32[]{:S(2)}, u32[]{:S(2)}) collective-permute-start(bf16[2,128,1536]{2,1,0:T(8,128)(2,1)S(1)} %pad_maximum_fusion.5), channel_id=1, source_target_pairs={{0,1},{1,0},{2,3},{3,2},{4,5},{5,4},{6,7},{7,6},{8,9},{9,8},{10,11... | collective-permute-start | bytes 2359304 | tf_op jit(solution)/shard_map/ppermute | solution.py:657
  93.2 22.2 %collective-permute-start.16 = (bf16[2,32,1536]{2,1,0:T(8,128)(2,1)S(1)}, bf16[2,32,1536]{2,1,0:T(8,128)(2,1)S(1)}, u32[]{:S(2)}, u32[]{:S(2)}) collective-permute-start(bf16[2,32,1536]{2,1,0:T(8,128)(2,1)S(1)} %slice_select_fusion), channel_id=1, source_target_pairs={{2,1},{4,3},{6,5},{8,7},{10,9},{12,11},{14,13},{16,15},{18,17},{20... | collective-permute-start | bytes 589832 | tf_op jit(solution)/shard_map/ppermute | solution.py:659
  93.9 21.5 %collective-permute-start.17 = (bf16[2,32,1536]{2,1,0:T(8,128)(2,1)S(1)}, bf16[2,32,1536]{2,1,0:T(8,128)(2,1)S(1)}, u32[]{:S(2)}, u32[]{:S(2)}) collective-permute-start(bf16[2,32,1536]{2,1,0:T(8,128)(2,1)S(1)} %slice_select_fusion), channel_id=1, source_target_pairs={{2,0},{4,2},{6,4},{8,6},{10,8},{12,10},{14,12},{16,14},{18,16},{20... | collective-permute-start | bytes 589832 | tf_op jit(solution)/shard_map/ppermute | solution.py:658
  95.2 15.7 %all-to-all-start = ((f32[16,2,768]{2,1,0:T(2,128)}), f32[16,2,768]{2,1,0:T(2,128)S(1)}, u32[]{:S(2)}, u32[]{:S(2)}) async-start(f32[16,2,768]{2,1,0:T(2,128)} %get-tuple-element.79), calls=%async_computation | async-start | bytes 196608 | tf_op jit(solution)/shard_map/all_to_all | solution.py:663
  115.6 1.4 copy-start.24
  136.2 2.6 %collective-permute-start.19 = (f32[128,1536]{1,0:T(8,128)}, f32[128,1536]{1,0:T(8,128)S(1)}, u32[]{:S(2)}, u32[]{:S(2)}) collective-permute-start(f32[128,1536]{1,0:T(8,128)} %get-tuple-element.93), channel_id=1, source_target_pairs={{0,1},{1,0},{2,3},{3,2},{4,5},{5,4},{6,7},{7,6},{8,9},{9,8},{10,11... | collective-permute-start | bytes 2359304 | tf_op jit(solution)/shard_map/ppermute | solution.py:778
  142.8 16.0 %collective-permute-start.20 = (f32[128,1536]{1,0:T(8,128)}, f32[128,1536]{1,0:T(8,128)S(1)}, u32[]{:S(2)}, u32[]{:S(2)}) collective-permute-start(f32[128,1536]{1,0:T(8,128)} %get-tuple-element.100.mine), channel_id=1, source_target_pairs={{0,1},{1,0},{2,3},{3,2},{4,5},{5,4},{6,7},{7,6},{8,9},{9,8},{10,11... | collective-permute-start | bytes 2359304 | tf_op jit(solution)/shard_map/ppermute | solution.py:657
  143.0 15.8 %collective-permute-start.21 = (f32[32,1536]{1,0:T(8,128)}, f32[32,1536]{1,0:T(8,128)S(1)}, u32[]{:S(2)}, u32[]{:S(2)}) collective-permute-start(f32[32,1536]{1,0:T(8,128)} %get-tuple-element.101), channel_id=1, source_target_pairs={{2,0},{4,2},{6,4},{8,6},{10,8},{12,10},{14,12},{16,14},{18,16},{20... | collective-permute-start | bytes 589832 | tf_op jit(solution)/shard_map/ppermute | solution.py:658
  144.3 14.6 %collective-permute-start.22 = (f32[32,1536]{1,0:T(8,128)}, f32[32,1536]{1,0:T(8,128)S(1)}, u32[]{:S(2)}, u32[]{:S(2)}) collective-permute-start(f32[32,1536]{1,0:T(8,128)} %get-tuple-element.101), channel_id=1, source_target_pairs={{2,1},{4,3},{6,5},{8,7},{10,9},{12,11},{14,13},{16,15},{18,17},{20... | collective-permute-start | bytes 589832 | tf_op jit(solution)/shard_map/ppermute | solution.py:659
  145.0 13.9 %all-to-all-start.2 = ((f32[32,1,128]{2,1,0:T(1,128)}), f32[32,1,128]{2,1,0:T(1,128)S(1)}, u32[]{:S(2)}, u32[]{:S(2)}) async-start(f32[32,1,128]{2,1,0:T(1,128)} %get-tuple-element.94), calls=%async_computation.2 | async-start | bytes 32768 | tf_op jit(solution)/shard_map/all_to_all | solution.py:780
  159.6 0.9 copy-start.11
  172.7 12.4 %all-to-all-start.3 = ((f32[16,2,768]{2,1,0:T(2,128)}), f32[16,2,768]{2,1,0:T(2,128)S(1)}, u32[]{:S(2)}, u32[]{:S(2)}) async-start(f32[16,2,768]{2,1,0:T(2,128)} %get-tuple-element.104.stats.local_stats), calls=%async_computation.3 | async-start | bytes 196608 | tf_op jit(solution)/shard_map/all_to_all | solution.py:663
  177.4 19.6 %copy-start.28 = (f32[2,768]{1,0:T(2,128)S(1)}, f32[2,768]{1,0:T(2,128)}, u32[]{:S(2)}) copy-start(f32[2,768]{1,0:T(2,128)} %get-tuple-element.112) | copy-start | bytes 18436
  192.1 13.4 %all-to-all-start.4 = ((bf16[16,48,128]{2,1,0:T(8,128)(2,1)}), bf16[16,48,128]{2,1,0:T(8,128)(2,1)S(1)}, u32[]{:S(2)}, u32[]{:S(2)}) async-start(bf16[16,48,128]{2,1,0:T(8,128)(2,1)} %get-tuple-element.110), calls=%async_computation.4 | async-start | bytes 393216 | tf_op jit(solution)/shard_map/all_to_all | solution.py:663
  (8 other events, 5.6 us)

commit v7 on v6

--- a/solution.py
+++ b/solution.py
@@ -678,14 +678,16 @@
         parts = array.reshape(array.shape[0], chips, 2, slice_width)
         return lax.dynamic_index_in_dim(parts, core, 2, keepdims=False).reshape(-1, half_width)
 
-    def prepare_first():
+    def prepare_first(after):
+        ours, noise, _ = lax.optimization_barrier((features[0], start_noise[0], after))
         own_ids = chip * chip_rows + core * rows + jnp.arange(rows, dtype=jnp.int32)
         own_live = (own_ids < end).astype(F32)[:, None]
-        summed = features[0].astype(F32) + noise_scale * start_noise[0].astype(F32) * own_live
+        summed = ours.astype(F32) + noise_scale * noise.astype(F32) * own_live
         return [normalize(summed)[0].astype(BF16)]
 
-    def prepare_second():
-        channel = mine_of(jnp.concatenate([kernel, bn_gain[None], bn_shift[None]], axis=0))
+    def prepare_second(after):
+        own_taps, own_gain, own_shift, _ = lax.optimization_barrier((kernel, bn_gain, bn_shift, after))
+        channel = mine_of(jnp.concatenate([own_taps, own_gain[None], own_shift[None]], axis=0))
         taps = jnp.broadcast_to(channel[:taps_n, None], (taps_n, 8, half_width))
         return [taps, channel[taps_n : taps_n + 1], channel[taps_n + 1 :], counts, scal]
 
@@ -719,17 +721,17 @@
             sent.append(lax.ppermute(along[k - 1 if from_before else k + 1], "tm", forth if from_before else back))
         beside = []
         if number == 0:
-            beside = prepare_first()
+            beside = prepare_first(sent[0])
         elif number == 1:
-            both = jnp.stack([normed_own, cot_own])
+            both, *_ = lax.optimization_barrier((jnp.stack([normed_own, cot_own]), *sent[2:]))
             edge = jnp.concatenate(
                 [
-                    jnp.where(first, normed_own[:HALO], normed_own[rows - HALO :]),
-                    jnp.where(first, cot_own[:EDGE], cot_own[rows - EDGE :]),
+                    jnp.where(first, both[0, :HALO], both[0, rows - HALO :]),
+                    jnp.where(first, both[1, :EDGE], both[1, rows - EDGE :]),
                 ],
                 axis=0,
             )
-            beside = [*across(both, edge), *prepare_second()]
+            beside = [*across(both, edge), *prepare_second(sent[-1])]
         if number == final:
             (partner, near, far), ready = (beside or crossing)[:3], beside[3:]
             beside = [
@@ -756,16 +758,16 @@
     late_pieces.append(lax.ppermute(relayed, "tm", corner))
     weight = place_late(scal, late_kinds, late_pieces, block.shape[0], weight)
 
+    value, gate, glu, conv, stats = forward(
+        scal, normed_b, weight, taps, chip_rows, chips, True
+    )
     place_of = jnp.arange(half_width, dtype=jnp.int32)
     source = (2 * (place_of // slice_width) + core) * slice_width + place_of % slice_width
     chosen = (jnp.arange(width, dtype=jnp.int32)[:, None] == source[None, :]).astype(BF16)
+    chosen, _ = lax.optimization_barrier((chosen, stats))
     cot = jnp.dot(wide_cot, chosen, preferred_element_type=F32).astype(BF16)
-
-    value, gate, glu, conv, stats = forward(
-        scal, normed_b, weight, taps, chip_rows, chips, True
-    )
     gathered, base = peers_of(stats), jnp.stack([features[0], start_noise[0]])
-    base, _ = lax.optimization_barrier((base, stats))
+    base, _ = lax.optimization_barrier((base, cot))
     partner, near, far = across(base, jnp.where(first, base[:, :HALO], base[:, rows - HALO :]))
     wide_features, wide_noise = (
         assemble(base[n], partner[n], near[n], far[n]) for n in range(2)

time: 209 us -> 208 us (level)
  waiting for transfers between devices: 62.4 us -> 44.8 us
  blocking collectives: 10.9 us -> 27.6 us
  starting transfers between devices: 51 us -> 41.5 us
  other arithmetic: 8.34 us -> 16.5 us
    all_to_all x1 -> x2, blocking collectives: 10.9 us -> 27.6 us  [peers_of(): lax.all_to_all(array, 'tm', 0, 0, axis_index_groups=cores, tiled=True)]
    all_to_all x3 -> x2, starting transfers between devices: 17.7 us -> 9.62 us  [peers_of(): lax.all_to_all(array, 'tm', 0, 0, axis_index_groups=cores, tiled=True)]
    ppermute x3, waiting for transfers between devices: 12.1 us -> 6.07 us  [across(): lax.ppermute(edge, 'tm', near_pairs)]
    all_to_all x3 -> x2, waiting for transfers between devices: 14.9 us -> 9.15 us  [peers_of(): lax.all_to_all(array, 'tm', 0, 0, axis_index_groups=cores, tiled=True)]
    ppermute x3, starting transfers between devices: 4.26 us -> 0.21 us  [across(): lax.ppermute(array, 'tm', swap)]
    ppermute x2, waiting for transfers between devices: 5.12 us -> 1.75 us  [on_device(): sent.append(lax.ppermute(relayed, 'tm', corner))]
    ppermute x3, waiting for transfers between devices: 9.85 us -> 12.6 us  [on_device(): lax.ppermute(along[k - 1 if from_before else k + 1], 'tm', forth if from_...]
    ppermute x3, waiting for transfers between devices: 9.61 us -> 7.08 us  [on_device(): lax.ppermute(blocks, 'tm', swap_x)]
  transfers between devices with their start and end apart: 27 -> 26, of which waited for: 14 -> 12; matrix products, arithmetic and copies ran while one was open for 6% -> 8% of each run, Pallas kernels for 9% -> 9%
where the time goes in v7:
time: 208 us; the launch traced here: 206 us
  Pallas kernels  60.7 us (29%)
  waiting for transfers between devices  44.8 us (22%)
  starting transfers between devices  41.5 us (20%)
  blocking collectives  27.6 us (13%)
  other arithmetic  16.5 us (8%)
  local copies, waits for them, and re-layouts  11.3 us (5%)
    all_to_all x2, blocking collectives, peers_of(): lax.all_to_all(array, 'tm', 0, 0, axis_index_groups=cores, tiled=True)  27.6 us
    pallas_call x2, Pallas kernels, forward(): pl.pallas_call(functools.partial(forward_kernel, keep), grid=(steps,), in...  15.5 us
    ppermute x3, waiting for transfers between devices, on_device(): lax.ppermute(along[k - 1 if from_before else k + 1], 'tm', forth if from_...  12.6 us
    all_to_all x2, starting transfers between devices, peers_of(): lax.all_to_all(array, 'tm', 0, 0, axis_index_groups=cores, tiled=True)  9.62 us
    all_to_all x2, waiting for transfers between devices, peers_of(): lax.all_to_all(array, 'tm', 0, 0, axis_index_groups=cores, tiled=True)  9.15 us
    pallas_call x1, Pallas kernels, backward(): pl.pallas_call(backward_kernel, grid=(steps,), in_specs=[pl.BlockSpec(mem...  8.21 us
    ppermute x3, waiting for transfers between devices, on_device(): lax.ppermute(blocks, 'tm', swap_x)  7.08 us
    all_to_all x1, starting transfers between devices, on_device(): squares = lax.all_to_all(squares, 'tm', 0, 0, tiled=True)  6.78 us
  transfers between devices with their start and end apart: 26, of which 12 were waited for; matrix products, arithmetic and copies ran while one was open for 8% of the time, Pallas kernels for 9%

profile of v7, /device:TPU:0, one launch (start us, length us, event | category | flops | bytes accessed | tf_op | source)
XLA Modules:
  0.0 206.0 jit_solution(10683202730793995150)
XLA Ops:
  4.5 2.6 %collective-permute-start.1 = (bf16[96,1536]{1,0:T(8,128)(2,1)S(1)}, bf16[96,1536]{1,0:T(8,128)(2,1)S(1)}, u32[]{:S(2)}, u32[]{:S(2)}) collective-permute-start(bf16[96,1536]{1,0:T(8,128)(2,1)S(1)} %pad_maximum_fusion.6.refs_0_), channel_id=1, source_target_pairs={{0,2},{1,3},{2,0},{3,1},{4,6},{5,7},{6,4},{7,5},{8,10},{9,11},{10,... | collective-permute-start | bytes 884744 | tf_op jit(solution)/shard_map/ppermute | solution.py:713
  7.7 1.6 collective-permute-start.2
  9.3 1.6 collective-permute-start.3
  10.9 2.2 %collective-permute-start.4 = (bf16[96,1536]{1,0:T(8,128)(2,1)S(1)}, bf16[96,1536]{1,0:T(8,128)(2,1)S(1)}, u32[]{:S(2)}, u32[]{:S(2)}) collective-permute-start(bf16[96,1536]{1,0:T(8,128)(2,1)S(1)} %pad_maximum_fusion.6.refs_0_), channel_id=1, source_target_pairs={{0,24},{1,25},{2,26},{3,27},{4,28},{5,29},{6,30},{7,31},{8,0},{9,1... | collective-permute-start | bytes 884744 | tf_op jit(solution)/shard_map/ppermute | solution.py:721
  13.1 1.7 collective-permute-done.1.refs_1_
  14.8 1.5 fusion.1
  17.0 4.0 %collective-permute-done.3 = bf16[96,1536]{1,0:T(8,128)(2,1)S(1)} collective-permute-done((bf16[96,1536]{1,0:T(8,128)(2,1)S(1)}, bf16[96,1536]{1,0:T(8,128)(2,1)S(1)}, u32[]{:S(2)}, u32[]{:S(2)}) %collective-permute-start.3) | collective-permute-done | bytes 294944 | tf_op jit(solution)/shard_map/ppermute | solution.py:721
  21.0 4.8 %collective-permute-done.4 = bf16[96,1536]{1,0:T(8,128)(2,1)S(1)} collective-permute-done((bf16[96,1536]{1,0:T(8,128)(2,1)S(1)}, bf16[96,1536]{1,0:T(8,128)(2,1)S(1)}, u32[]{:S(2)}, u32[]{:S(2)}) %collective-permute-start.4) | collective-permute-done | bytes 294944 | tf_op jit(solution)/shard_map/ppermute | solution.py:721
  25.7 1.1 collective-permute-start.8
  29.0 1.5 collective-permute-start.5
  32.0 3.9 %collective-permute-done.8.refs_7_ = bf16[96,1536]{1,0:T(8,128)(2,1)S(1)} collective-permute-done((bf16[96,1536]{1,0:T(8,128)(2,1)S(1)}, bf16[96,1536]{1,0:T(8,128)(2,1)S(1)}, u32[]{:S(2)}, u32[]{:S(2)}) %collective-permute-start.8) | collective-permute-done | bytes 294944 | tf_op jit(solution)/shard_map/ppermute | solution.py:721
  35.9 1.7 collective-permute-done.7.refs_6_
  37.6 1.1 select_bitcast_fusion.10
  40.3 1.3 collective-permute-start.10
  41.6 1.3 collective-permute-start.11
  45.6 6.1 %collective-permute-done.10 = bf16[48,1536]{1,0:T(8,128)(2,1)} collective-permute-done((bf16[48,1536]{1,0:T(8,128)(2,1)}, bf16[48,1536]{1,0:T(8,128)(2,1)}, u32[]{:S(2)}, u32[]{:S(2)}) %collective-permute-start.10) | collective-permute-done | bytes 147488 | tf_op jit(solution)/shard_map/ppermute | solution.py:658
  53.8 1.1 bitcast_select_fusion.1
  55.0 2.3 %collective-permute-start.14 = (bf16[192,1536]{1,0:T(8,128)(2,1)S(1)}, bf16[192,1536]{1,0:T(8,128)(2,1)S(1)}, u32[]{:S(2)}, u32[]{:S(2)}) collective-permute-start(bf16[192,1536]{1,0:T(8,128)(2,1)S(1)} %broadcast_select_fusion), channel_id=1, source_target_pairs={{0,2},{1,5},{2,0},{3,7},{4,6},{5,1},{6,4},{7,3},{8,10},{9,13},{10,... | collective-permute-start | bytes 1769480 | tf_op jit(solution)/shard_map/ppermute | solution.py:716
  59.3 1.5 collective-permute-start.13
  60.9 4.3 %place_weights.1.refs_4_ = bf16[1536,1536]{1,0:T(8,128)(2,1)} custom-call(s32[6]{0:T(128)} %stack.38.scal, bf16[96,1536]{1,0:T(8,128)(2,1)} %copy-done.10, bf16[96,1536]{1,0:T(8,128)(2,1)} %copy-done.6, bf16[96,1536]{1,0:T(8,128)(2,1)} %copy-done.7, bf16[192,1536]{1,0:T(8,128)(2,1)} %constant_dynamic-update-slice_fusion.refs_3_, ...), custom_call_target="tpu_custom_call" | custom-call | bytes 9437184 | tf_op jit(solution)/shard_map/place_weights/pallas_call | solution.py:124
  66.2 5.4 %collective-permute-done.12.refs_0_ = bf16[96,1536]{1,0:T(8,128)(2,1)S(1)} collective-permute-done((bf16[96,1536]{1,0:T(8,128)(2,1)S(1)}, bf16[96,1536]{1,0:T(8,128)(2,1)S(1)}, u32[]{:S(2)}, u32[]{:S(2)}) %collective-permute-start.12) | collective-permute-done | bytes 294944 | tf_op jit(solution)/shard_map/ppermute | solution.py:713
  71.6 2.1 %collective-permute-start.15 = (bf16[96,1536]{1,0:T(8,128)(2,1)S(1)}, bf16[96,1536]{1,0:T(8,128)(2,1)S(1)}, u32[]{:S(2)}, u32[]{:S(2)}) collective-permute-start(bf16[96,1536]{1,0:T(8,128)(2,1)S(1)} %broadcast_select_fusion.1), channel_id=1, source_target_pairs={{0,2},{1,5},{2,0},{3,7},{4,6},{5,1},{6,4},{7,3},{8,10},{9,13},{10,... | collective-permute-start | bytes 884744 | tf_op jit(solution)/shard_map/ppermute | solution.py:758
  74.9 3.5 %collective-permute-done.15.refs_3_ = bf16[96,1536]{1,0:T(8,128)(2,1)S(1)} collective-permute-done((bf16[96,1536]{1,0:T(8,128)(2,1)S(1)}, bf16[96,1536]{1,0:T(8,128)(2,1)S(1)}, u32[]{:S(2)}, u32[]{:S(2)}) %collective-permute-start.15) | collective-permute-done | bytes 294944 | tf_op jit(solution)/shard_map/ppermute | solution.py:758
  79.1 2.5 %place_last_weights.1.value_w.gate_w = bf16[1536,1536]{1,0:T(8,128)(2,1)} custom-call(s32[6]{0:T(128)} %stack.38.scal, bf16[96,1536]{1,0:T(8,128)(2,1)} %copy-done.8, bf16[96,1536]{1,0:T(8,128)(2,1)} %copy-done.9, bf16[192,1536]{1,0:T(8,128)(2,1)} %copy-done.14, bf16[96,1536]{1,0:T(8,128)(2,1)} %copy-done.19, ...), custom_call_target="tpu_custom_call", output_to_operand_aliasing={{}: (5, {})} | custom-call | bytes 2949120 | tf_op jit(solution)/shard_map/place_last_weights/pallas_call | solution.py:139
  81.6 7.8 %project_glu_conv.2 = (f32[256,768]{1,0:T(8,128)}, f32[256,768]{1,0:T(8,128)}, bf16[320,768]{1,0:T(8,128)(2,1)}, f32[288,768]{1,0:T(8,128)}, f32[16,2,768]{2,1,0:T(2,128)}) custom-call(s32[6]{0:T(128)} %stack.38.scal, bf16[320,1536]{1,0:T(8,128)(2,1)} %pad_maximum_fusion.nb, bf16[1536,1536]{1,0:T(8,128)(2,1)} %place_last_weights.1.value_w.gate_w, ...), custom_call_target="tpu_custom_call" | custom-call | flops 1509949440 | bytes 7176192 | tf_op jit(solution)/shard_map/project_glu_conv/pallas_call | solution.py:183
  89.4 1.6 convolution_convert_fusion.cot
  91.8 1.3 collective-permute-start.17
  93.1 16.7 %all_to_all.25.stats = f32[16,2,768]{2,1,0:T(2,128)} all-to-all(f32[16,2,768]{2,1,0:T(2,128)S(1)} %copy-done.24), channel_id=1, replica_groups={{0,2,4,6,8,10,12,14,16,18,20,22,24,26,28,30},{1,3,5,7,9,11,13,15,17,19,..., dimensions={0} | all-to-all | bytes 196608 | tf_op jit(solution)/shard_map/all_to_all | solution.py:663
  109.7 3.9 %batch_norm_swish.1 = (f32[288,768]{1,0:T(8,128)}, f32[288,768]{1,0:T(8,128)}, f32[1,768]{1,0:T(1,128)}, f32[16,2,768]{2,1,0:T(2,128)}) custom-call(s32[6]{0:T(128)} %stack.38.scal, f32[2,16]{1,0:T(2,128)} %pad_maximum_fusion.8.counts, f32[16,2,768]{2,1,0:T(2,128)} %all_to_all.25.stats, f32[288,768]{1,0:T(8,128)} %get-tuple-element.93.conv, ...), custom_call_target="tpu_custom_call" | custom-call | flops 8847360 | bytes 3538944 | tf_op jit(solution)/shard_map/batch_norm_swish/pallas_call | solution.py:263
  113.8 1.4 pad_maximum_fusion.1
  115.2 10.9 %all_to_all.26.sums = f32[16,2,768]{2,1,0:T(2,128)} all-to-all(f32[16,2,768]{2,1,0:T(2,128)S(1)} %copy-done.23), channel_id=1, replica_groups={{0,2,4,6,8,10,12,14,16,18,20,22,24,26,28,30},{1,3,5,7,9,11,13,15,17,19,..., dimensions={0} | all-to-all | bytes 196608 | tf_op jit(solution)/shard_map/all_to_all | solution.py:663
  126.2 8.2 %grad_conv_project_back.1 = (f32[128,1536]{1,0:T(8,128)}, f32[128,1536]{1,0:T(8,128)}, bf16[256,768]{1,0:T(8,128)(2,1)}, f32[2,768]{1,0:T(2,128)}) custom-call(s32[6]{0:T(128)} %stack.38.scal, f32[16,2,768]{2,1,0:T(2,128)} %all_to_all.26.sums, f32[288,768]{1,0:T(8,128)} %get-tuple-element.101.scaled, f32[288,768]{1,0:T(8,128)} %get-tuple-element.102.grad, ...), custom_call_target="tpu_custom_call" | custom-call | flops 1207959552 | bytes 9142272 | tf_op jit(solution)/shard_map/grad_conv_project_back/pallas_call | solution.py:338
  134.5 2.5 %collective-permute-done.19.other = f32[128,1536]{1,0:T(8,128)S(1)} collective-permute-done((f32[128,1536]{1,0:T(8,128)}, f32[128,1536]{1,0:T(8,128)S(1)}, u32[]{:S(2)}, u32[]{:S(2)}) %collective-permute-start.19) | collective-permute-done | bytes 786464 | tf_op jit(solution)/shard_map/ppermute | solution.py:780
  137.8 3.3 %direction.1 = (f32[128,1536]{1,0:T(8,128)}, f32[32,1536]{1,0:T(8,128)}, f32[32,1,128]{2,1,0:T(1,128)}) custom-call(s32[6]{0:T(128)} %stack.38.scal, f32[128,1536]{1,0:T(8,128)} %get-tuple-element.106.mine, f32[128,1536]{1,0:T(8,128)} %copy-done.12, bf16[128,1536]{1,0:T(8,128)(2,1)} %bitcast.65, bf16[128,1536]{1,0:T(8,128)(2,1)} %bitcast.60), custom_call_target="tpu_custom_call" | custom-call | flops 5898240 | bytes 3145728 | tf_op jit(solution)/shard_map/direction/pallas_call | solution.py:568
  141.2 1.3 collective-permute-start.21
  143.2 6.8 %all-to-all-start.2 = ((f32[32,1,128]{2,1,0:T(1,128)}), f32[32,1,128]{2,1,0:T(1,128)S(1)}, u32[]{:S(2)}, u32[]{:S(2)}) async-start(f32[32,1,128]{2,1,0:T(1,128)} %get-tuple-element.108), calls=%async_computation.2 | async-start | bytes 32768 | tf_op jit(solution)/shard_map/all_to_all | solution.py:782
  150.0 4.9 %tap_grad.1.taps_before = f32[31,768]{1,0:T(8,128)} custom-call(bf16[256,768]{1,0:T(8,128)(2,1)} %get-tuple-element.109.grad_conv, bf16[320,768]{1,0:T(8,128)(2,1)} %get-tuple-element.110.glu), custom_call_target="tpu_custom_call" | custom-call | flops 12189696 | bytes 983040 | tf_op jit(solution)/shard_map/tap_grad/pallas_call | solution.py:386
  154.9 2.1 %all-to-all-done.2.squares = f32[32,1,128]{2,1,0:T(1,128)S(1)} async-done(((f32[32,1,128]{2,1,0:T(1,128)}), f32[32,1,128]{2,1,0:T(1,128)S(1)}, u32[]{:S(2)}, u32[]{:S(2)}) %all-to-all-start.2) | async-done | bytes 16416 | tf_op jit(solution)/shard_map/all_to_all | solution.py:782
  158.7 4.5 %ascend.1 = (f32[128,1536]{1,0:T(8,128)}, bf16[320,1536]{1,0:T(8,128)(2,1)}) custom-call(s32[6]{0:T(128)} %stack.38.scal, f32[32,1,128]{2,1,0:T(1,128)} %copy-done.25, bf16[320,1536]{1,0:T(8,128)(2,1)} %get-tuple-element.112.features, bf16[320,1536]{1,0:T(8,128)(2,1)} %get-tuple-element.113.noise, f32[128,1536]{1,0:T(8,128)} %get-tuple-element.114.mine, ...), custom_call_target="tpu_custom_call" | custom-call | flops 14745600 | bytes 3932160 | tf_op jit(solution)/shard_map/ascend/pallas_call | solution.py:612
  163.2 7.7 %project_glu_conv.3 = (bf16[320,768]{1,0:T(8,128)(2,1)}, f32[288,768]{1,0:T(8,128)}, f32[16,2,768]{2,1,0:T(2,128)}) custom-call(s32[6]{0:T(128)} %stack.38.scal, bf16[320,1536]{1,0:T(8,128)(2,1)} %get-tuple-element.117.nb, bf16[1536,1536]{1,0:T(8,128)(2,1)} %place_last_weights.1.value_w.gate_w, bf16[1536,1536]{1,0:T(8,128)(2,1)} %place_last_weights.1.value_w.gate_w, ...), custom_call_target="tpu_custom_call" | custom-call | flops 1509949440 | bytes 7176192 | tf_op jit(solution)/shard_map/project_glu_conv/pallas_call | solution.py:183
  170.9 4.7 %all-to-all-start.3 = ((f32[16,2,768]{2,1,0:T(2,128)}), f32[16,2,768]{2,1,0:T(2,128)S(1)}, u32[]{:S(2)}, u32[]{:S(2)}) async-start(f32[16,2,768]{2,1,0:T(2,128)} %get-tuple-element.118.stats.local_stats), calls=%async_computation.3 | async-start | bytes 196608 | tf_op jit(solution)/shard_map/all_to_all | solution.py:663
  175.7 5.6 %raw_taps.1 = (f32[31,768]{1,0:T(8,128)}, f32[31,768]{1,0:T(8,128)}) custom-call(s32[6]{0:T(128)} %stack.38.scal, f32[288,768]{1,0:T(8,128)} %get-tuple-element.119.conv, bf16[320,768]{1,0:T(8,128)(2,1)} %get-tuple-element.120.glu, f32[16,2,768]{2,1,0:T(2,128)} %get-tuple-element.118.stats.local_stats), custom_call_target="tpu_custom_call" | custom-call | flops 13713408 | bytes 1966080 | tf_op jit(solution)/shard_map/raw_taps/pallas_call | solution.py:419
  181.3 2.0 all-to-all-done.3.stats
  184.0 6.3 %batch_norm_swish_taps.1 = (bf16[16,48,128]{2,1,0:T(8,128)(2,1)}, f32[1,768]{1,0:T(1,128)}) custom-call(s32[6]{0:T(128)} %stack.38.scal, f32[2,16]{1,0:T(2,128)} %pad_maximum_fusion.8.counts, f32[16,2,768]{2,1,0:T(2,128)} %copy-done.15, f32[288,768]{1,0:T(8,128)} %get-tuple-element.119.conv, bf16[288,768]{1,0:T(8,128)(2,1)} %convolution_convert_fusion.cot, ...), custom_call_target="tpu_custom_call" | custom-call | flops 22118400 | bytes 2211840 | tf_op jit(solution)/shard_map/batch_norm_swish_taps/pallas_call | solution.py:479
  190.3 4.9 %all-to-all-start.4 = ((bf16[16,48,128]{2,1,0:T(8,128)(2,1)}), bf16[16,48,128]{2,1,0:T(8,128)(2,1)S(1)}, u32[]{:S(2)}, u32[]{:S(2)}) async-start(bf16[16,48,128]{2,1,0:T(8,128)(2,1)} %get-tuple-element.124), calls=%async_computation.4 | async-start | bytes 393216 | tf_op jit(solution)/shard_map/all_to_all | solution.py:663
  195.2 1.4 fusion.15.known
  196.6 7.1 %all-to-all-done.4.received = bf16[16,48,128]{2,1,0:T(8,128)(2,1)S(1)} async-done(((bf16[16,48,128]{2,1,0:T(8,128)(2,1)}), bf16[16,48,128]{2,1,0:T(8,128)(2,1)S(1)}, u32[]{:S(2)}, u32[]{:S(2)}) %all-to-all-start.4) | async-done | bytes 196640 | tf_op jit(solution)/shard_map/all_to_all | solution.py:663
  204.4 1.7 finish.1
  (126 shorter events, 24.8 us)
Async XLA Ops:
  0.6 15.7 %copy-start = (bf16[1,128,1536]{2,1,0:T(8,128)(2,1)S(1)}, bf16[1,128,1536]{2,1,0:T(8,128)(2,1)}, u32[]{:S(2)}) copy-start(bf16[1,128,1536]{2,1,0:T(8,128)(2,1)} %param.9) | copy-start | bytes 1179652
  0.6 15.7 %copy-start.1 = (bf16[1,128,1536]{2,1,0:T(8,128)(2,1)S(1)}, bf16[1,128,1536]{2,1,0:T(8,128)(2,1)}, u32[]{:S(2)}) copy-start(bf16[1,128,1536]{2,1,0:T(8,128)(2,1)} %param.8) | copy-start | bytes 1179652
  1.7 1.9 collective-permute-start
  4.5 23.1 %copy-start.10 = (bf16[96,1536]{1,0:T(8,128)(2,1)}, bf16[96,1536]{1,0:T(8,128)(2,1)S(1)}, u32[]{:S(2)}) copy-start(bf16[96,1536]{1,0:T(8,128)(2,1)S(1)} %pad_maximum_fusion.6.refs_0_) | copy-start | bytes 884740
  4.5 10.2 %collective-permute-start.1 = (bf16[96,1536]{1,0:T(8,128)(2,1)S(1)}, bf16[96,1536]{1,0:T(8,128)(2,1)S(1)}, u32[]{:S(2)}, u32[]{:S(2)}) collective-permute-start(bf16[96,1536]{1,0:T(8,128)(2,1)S(1)} %pad_maximum_fusion.6.refs_0_), channel_id=1, source_target_pairs={{0,2},{1,3},{2,0},{3,1},{4,6},{5,7},{6,4},{7,5},{8,10},{9,11},{10,... | collective-permute-start | bytes 884744 | tf_op jit(solution)/shard_map/ppermute | solution.py:713
  7.7 9.3 %collective-permute-start.2 = (bf16[96,1536]{1,0:T(8,128)(2,1)S(1)}, bf16[96,1536]{1,0:T(8,128)(2,1)S(1)}, u32[]{:S(2)}, u32[]{:S(2)}) collective-permute-start(bf16[96,1536]{1,0:T(8,128)(2,1)S(1)} %pad_maximum_fusion.6.refs_0_), channel_id=1, source_target_pairs={{0,4},{1,5},{2,6},{3,7},{4,0},{5,1},{6,2},{7,3},{8,12},{9,13},{10,... | collective-permute-start | bytes 884744 | tf_op jit(solution)/shard_map/ppermute | solution.py:713
  9.3 11.7 %collective-permute-start.3 = (bf16[96,1536]{1,0:T(8,128)(2,1)S(1)}, bf16[96,1536]{1,0:T(8,128)(2,1)S(1)}, u32[]{:S(2)}, u32[]{:S(2)}) collective-permute-start(bf16[96,1536]{1,0:T(8,128)(2,1)S(1)} %pad_maximum_fusion.6.refs_0_), channel_id=1, source_target_pairs={{0,8},{1,9},{2,10},{3,11},{4,12},{5,13},{6,14},{7,15},{8,16},{9,17... | collective-permute-start | bytes 884744 | tf_op jit(solution)/shard_map/ppermute | solution.py:721
  10.9 14.9 %collective-permute-start.4 = (bf16[96,1536]{1,0:T(8,128)(2,1)S(1)}, bf16[96,1536]{1,0:T(8,128)(2,1)S(1)}, u32[]{:S(2)}, u32[]{:S(2)}) collective-permute-start(bf16[96,1536]{1,0:T(8,128)(2,1)S(1)} %pad_maximum_fusion.6.refs_0_), channel_id=1, source_target_pairs={{0,24},{1,25},{2,26},{3,27},{4,28},{5,29},{6,30},{7,31},{8,0},{9,1... | collective-permute-start | bytes 884744 | tf_op jit(solution)/shard_map/ppermute | solution.py:721
  14.8 12.9 %copy-start.6 = (bf16[96,1536]{1,0:T(8,128)(2,1)}, bf16[96,1536]{1,0:T(8,128)(2,1)S(1)}, u32[]{:S(2)}) copy-start(bf16[96,1536]{1,0:T(8,128)(2,1)S(1)} %collective-permute-done.1.refs_1_) | copy-start | bytes 884740
  16.3 14.7 %copy-start.4 = (bf16[1,128,1536]{2,1,0:T(8,128)(2,1)S(1)}, bf16[1,128,1536]{2,1,0:T(8,128)(2,1)}, u32[]{:S(2)}) copy-start(bf16[1,128,1536]{2,1,0:T(8,128)(2,1)} %param.10) | copy-start | bytes 1179652
  17.0 21.7 %copy-start.7 = (bf16[96,1536]{1,0:T(8,128)(2,1)}, bf16[96,1536]{1,0:T(8,128)(2,1)S(1)}, u32[]{:S(2)}) copy-start(bf16[96,1536]{1,0:T(8,128)(2,1)S(1)} %collective-permute-done.2.refs_2_) | copy-start | bytes 884740
  25.7 10.1 %collective-permute-start.8 = (bf16[96,1536]{1,0:T(8,128)(2,1)S(1)}, bf16[96,1536]{1,0:T(8,128)(2,1)S(1)}, u32[]{:S(2)}, u32[]{:S(2)}) collective-permute-start(bf16[96,1536]{1,0:T(8,128)(2,1)S(1)} %collective-permute-done.3), channel_id=1, source_target_pairs={{0,8},{1,9},{2,10},{3,11},{4,12},{5,13},{6,14},{7,15},{8,16},{9,17... | collective-permute-start | bytes 884744 | tf_op jit(solution)/shard_map/ppermute | solution.py:721
  27.6 15.3 %copy-start.22 = (f32[31,1536]{1,0:T(8,128)S(1)}, f32[31,1536]{1,0:T(8,128)}, u32[]{:S(2)}) copy-start(f32[31,1536]{1,0:T(8,128)} %param.12) | copy-start | bytes 571396
  27.7 9.9 %collective-permute-start.7 = (bf16[96,1536]{1,0:T(8,128)(2,1)S(1)}, bf16[96,1536]{1,0:T(8,128)(2,1)S(1)}, u32[]{:S(2)}, u32[]{:S(2)}) collective-permute-start(bf16[96,1536]{1,0:T(8,128)(2,1)S(1)} %broadcast_select_fusion.2), channel_id=1, source_target_pairs={{0,2},{1,5},{2,0},{3,7},{4,6},{5,1},{6,4},{7,3},{8,10},{9,13},{10,... | collective-permute-start | bytes 884744 | tf_op jit(solution)/shard_map/ppermute | solution.py:716
  29.0 22.7 %collective-permute-start.5 = (bf16[192,1536]{1,0:T(8,128)(2,1)}, bf16[192,1536]{1,0:T(8,128)(2,1)S(1)}, u32[]{:S(2)}, u32[]{:S(2)}) collective-permute-start(bf16[192,1536]{1,0:T(8,128)(2,1)} %constant_dynamic-update-slice_fusion.refs_3_), channel_id=1, source_target_pairs={{0,2},{1,3},{2,0},{3,1},{4,6},{5,7},{6,4},{7,5},{8,10},{9,11},{10,... | collective-permute-start | bytes 1769480 | tf_op jit(solution)/shard_map/ppermute | solution.py:713
  30.5 21.2 %collective-permute-start.6 = (bf16[192,1536]{1,0:T(8,128)(2,1)}, bf16[192,1536]{1,0:T(8,128)(2,1)S(1)}, u32[]{:S(2)}, u32[]{:S(2)}) collective-permute-start(bf16[192,1536]{1,0:T(8,128)(2,1)} %constant_dynamic-update-slice_fusion.refs_3_), channel_id=1, source_target_pairs={{0,4},{1,5},{2,6},{3,7},{4,0},{5,1},{6,2},{7,3},{8,12},{9,13},{10,... | collective-permute-start | bytes 1769480 | tf_op jit(solution)/shard_map/ppermute | solution.py:713
  31.0 12.8 %copy-start.26 = (f32[1536]{0:T(1024)S(1)}, f32[1536]{0:T(1024)}, u32[]{:S(2)}) copy-start(f32[1536]{0:T(1024)} %param.13) | copy-start | bytes 18436
  31.0 12.9 %copy-start.27 = (f32[1536]{0:T(1024)S(1)}, f32[1536]{0:T(1024)}, u32[]{:S(2)}) copy-start(f32[1536]{0:T(1024)} %param.14) | copy-start | bytes 18436
  35.9 5.7 %copy-start.16 = (bf16[96,1536]{1,0:T(8,128)(2,1)}, bf16[96,1536]{1,0:T(8,128)(2,1)S(1)}, u32[]{:S(2)}) copy-start(bf16[96,1536]{1,0:T(8,128)(2,1)S(1)} %collective-permute-done.8.refs_7_) | copy-start | bytes 884740
  37.6 4.0 %copy-start.18 = (bf16[96,1536]{1,0:T(8,128)(2,1)}, bf16[96,1536]{1,0:T(8,128)(2,1)S(1)}, u32[]{:S(2)}) copy-start(bf16[96,1536]{1,0:T(8,128)(2,1)S(1)} %collective-permute-done.7.refs_6_) | copy-start | bytes 884740
  38.7 13.0 %collective-permute-start.9 = (bf16[2,128,1536]{2,1,0:T(8,128)(2,1)}, bf16[2,128,1536]{2,1,0:T(8,128)(2,1)}, u32[]{:S(2)}, u32[]{:S(2)}) collective-permute-start(bf16[2,128,1536]{2,1,0:T(8,128)(2,1)} %pad_maximum_fusion.4), channel_id=1, source_target_pairs={{0,1},{1,0},{2,3},{3,2},{4,5},{5,4},{6,7},{7,6},{8,9},{9,8},{10,11... | collective-permute-start | bytes 2359304 | tf_op jit(solution)/shard_map/ppermute | solution.py:657
  40.3 11.4 %collective-permute-start.10 = (bf16[48,1536]{1,0:T(8,128)(2,1)}, bf16[48,1536]{1,0:T(8,128)(2,1)}, u32[]{:S(2)}, u32[]{:S(2)}) collective-permute-start(bf16[48,1536]{1,0:T(8,128)(2,1)} %pad_maximum_fusion.7), channel_id=1, source_target_pairs={{2,0},{4,2},{6,4},{8,6},{10,8},{12,10},{14,12},{16,14},{18,16},{20... | collective-permute-start | bytes 442376 | tf_op jit(solution)/shard_map/ppermute | solution.py:658
  41.6 10.1 %collective-permute-start.11 = (bf16[48,1536]{1,0:T(8,128)(2,1)}, bf16[48,1536]{1,0:T(8,128)(2,1)}, u32[]{:S(2)}, u32[]{:S(2)}) collective-permute-start(bf16[48,1536]{1,0:T(8,128)(2,1)} %pad_maximum_fusion.7), channel_id=1, source_target_pairs={{2,1},{4,3},{6,5},{8,7},{10,9},{12,11},{14,13},{16,15},{18,17},{20... | collective-permute-start | bytes 442376 | tf_op jit(solution)/shard_map/ppermute | solution.py:659
  43.8 8.9 %copy-start.5 = (bf16[1,128,1536]{2,1,0:T(8,128)(2,1)S(1)}, bf16[1,128,1536]{2,1,0:T(8,128)(2,1)}, u32[]{:S(2)}) copy-start(bf16[1,128,1536]{2,1,0:T(8,128)(2,1)} %param.10) | copy-start | bytes 1179652
  51.7 3.2 %copy-start.2 = (bf16[192,1536]{1,0:T(8,128)(2,1)}, bf16[192,1536]{1,0:T(8,128)(2,1)S(1)}, u32[]{:S(2)}) copy-start(bf16[192,1536]{1,0:T(8,128)(2,1)S(1)} %collective-permute-done.5.refs_4_) | copy-start | bytes 1769476
  51.7 3.2 %copy-start.3 = (bf16[192,1536]{1,0:T(8,128)(2,1)}, bf16[192,1536]{1,0:T(8,128)(2,1)S(1)}, u32[]{:S(2)}) copy-start(bf16[192,1536]{1,0:T(8,128)(2,1)S(1)} %collective-permute-done.6.refs_5_) | copy-start | bytes 1769476
  53.8 5.4 %copy-start.17 = (bf16[96,1536]{1,0:T(8,128)(2,1)S(1)}, bf16[96,1536]{1,0:T(8,128)(2,1)}, u32[]{:S(2)}) copy-start(bf16[96,1536]{1,0:T(8,128)(2,1)} %copy-done.16) | copy-start | bytes 884740
  55.0 16.5 %collective-permute-start.14 = (bf16[192,1536]{1,0:T(8,128)(2,1)S(1)}, bf16[192,1536]{1,0:T(8,128)(2,1)S(1)}, u32[]{:S(2)}, u32[]{:S(2)}) collective-permute-start(bf16[192,1536]{1,0:T(8,128)(2,1)S(1)} %broadcast_select_fusion), channel_id=1, source_target_pairs={{0,2},{1,5},{2,0},{3,7},{4,6},{5,1},{6,4},{7,3},{8,10},{9,13},{10,... | collective-permute-start | bytes 1769480 | tf_op jit(solution)/shard_map/ppermute | solution.py:716
  59.2 12.4 %collective-permute-start.12 = (bf16[96,1536]{1,0:T(8,128)(2,1)S(1)}, bf16[96,1536]{1,0:T(8,128)(2,1)S(1)}, u32[]{:S(2)}, u32[]{:S(2)}) collective-permute-start(bf16[96,1536]{1,0:T(8,128)(2,1)S(1)} %copy-done.17), channel_id=1, source_target_pairs={{0,2},{1,3},{2,0},{3,1},{4,6},{5,7},{6,4},{7,5},{8,10},{9,11},{10,... | collective-permute-start | bytes 884744 | tf_op jit(solution)/shard_map/ppermute | solution.py:713
  59.3 12.3 %collective-permute-start.13 = (bf16[96,1536]{1,0:T(8,128)(2,1)S(1)}, bf16[96,1536]{1,0:T(8,128)(2,1)S(1)}, u32[]{:S(2)}, u32[]{:S(2)}) collective-permute-start(bf16[96,1536]{1,0:T(8,128)(2,1)S(1)} %copy-done.17), channel_id=1, source_target_pairs={{0,4},{1,5},{2,6},{3,7},{4,0},{5,1},{6,2},{7,3},{8,12},{9,13},{10,... | collective-permute-start | bytes 884744 | tf_op jit(solution)/shard_map/ppermute | solution.py:713
  71.6 3.3 %copy-start.8 = (bf16[96,1536]{1,0:T(8,128)(2,1)}, bf16[96,1536]{1,0:T(8,128)(2,1)S(1)}, u32[]{:S(2)}) copy-start(bf16[96,1536]{1,0:T(8,128)(2,1)S(1)} %collective-permute-done.12.refs_0_) | copy-start | bytes 884740
  71.6 3.3 %copy-start.9 = (bf16[96,1536]{1,0:T(8,128)(2,1)}, bf16[96,1536]{1,0:T(8,128)(2,1)S(1)}, u32[]{:S(2)}) copy-start(bf16[96,1536]{1,0:T(8,128)(2,1)S(1)} %collective-permute-done.13.refs_1_) | copy-start | bytes 884740
  71.6 3.3 %copy-start.14 = (bf16[192,1536]{1,0:T(8,128)(2,1)}, bf16[192,1536]{1,0:T(8,128)(2,1)S(1)}, u32[]{:S(2)}) copy-start(bf16[192,1536]{1,0:T(8,128)(2,1)S(1)} %collective-permute-done.14.refs_2_) | copy-start | bytes 1769476
  71.6 6.8 %collective-permute-start.15 = (bf16[96,1536]{1,0:T(8,128)(2,1)S(1)}, bf16[96,1536]{1,0:T(8,128)(2,1)S(1)}, u32[]{:S(2)}, u32[]{:S(2)}) collective-permute-start(bf16[96,1536]{1,0:T(8,128)(2,1)S(1)} %broadcast_select_fusion.1), channel_id=1, source_target_pairs={{0,2},{1,5},{2,0},{3,7},{4,6},{5,1},{6,4},{7,3},{8,10},{9,13},{10,... | collective-permute-start | bytes 884744 | tf_op jit(solution)/shard_map/ppermute | solution.py:758
  89.4 3.7 %copy-start.24 = (f32[16,2,768]{2,1,0:T(2,128)S(1)}, f32[16,2,768]{2,1,0:T(2,128)}, u32[]{:S(2)}) copy-start(f32[16,2,768]{2,1,0:T(2,128)} %get-tuple-element.92) | copy-start | bytes 294916
  91.0 22.6 %collective-permute-start.18 = (bf16[2,128,1536]{2,1,0:T(8,128)(2,1)S(1)}, bf16[2,128,1536]{2,1,0:T(8,128)(2,1)S(1)}, u32[]{:S(2)}, u32[]{:S(2)}) collective-permute-start(bf16[2,128,1536]{2,1,0:T(8,128)(2,1)S(1)} %pad_maximum_fusion.5), channel_id=1, source_target_pairs={{0,1},{1,0},{2,3},{3,2},{4,5},{5,4},{6,7},{7,6},{8,9},{9,8},{10,11... | collective-permute-start | bytes 2359304 | tf_op jit(solution)/shard_map/ppermute | solution.py:657
  91.1 22.6 %collective-permute-start.16 = (bf16[2,32,1536]{2,1,0:T(8,128)(2,1)S(1)}, bf16[2,32,1536]{2,1,0:T(8,128)(2,1)S(1)}, u32[]{:S(2)}, u32[]{:S(2)}) collective-permute-start(bf16[2,32,1536]{2,1,0:T(8,128)(2,1)S(1)} %slice_select_fusion), channel_id=1, source_target_pairs={{2,1},{4,3},{6,5},{8,7},{10,9},{12,11},{14,13},{16,15},{18,17},{20... | collective-permute-start | bytes 589832 | tf_op jit(solution)/shard_map/ppermute | solution.py:659
  91.8 21.9 %collective-permute-start.17 = (bf16[2,32,1536]{2,1,0:T(8,128)(2,1)S(1)}, bf16[2,32,1536]{2,1,0:T(8,128)(2,1)S(1)}, u32[]{:S(2)}, u32[]{:S(2)}) collective-permute-start(bf16[2,32,1536]{2,1,0:T(8,128)(2,1)S(1)} %slice_select_fusion), channel_id=1, source_target_pairs={{2,0},{4,2},{6,4},{8,6},{10,8},{12,10},{14,12},{16,14},{18,16},{20... | collective-permute-start | bytes 589832 | tf_op jit(solution)/shard_map/ppermute | solution.py:658
  113.8 1.4 copy-start.23
  134.4 2.6 %collective-permute-start.19 = (f32[128,1536]{1,0:T(8,128)}, f32[128,1536]{1,0:T(8,128)S(1)}, u32[]{:S(2)}, u32[]{:S(2)}) collective-permute-start(f32[128,1536]{1,0:T(8,128)} %get-tuple-element.107), channel_id=1, source_target_pairs={{0,1},{1,0},{2,3},{3,2},{4,5},{5,4},{6,7},{7,6},{8,9},{9,8},{10,11... | collective-permute-start | bytes 2359304 | tf_op jit(solution)/shard_map/ppermute | solution.py:780
  141.1 16.0 %collective-permute-start.20 = (f32[128,1536]{1,0:T(8,128)}, f32[128,1536]{1,0:T(8,128)S(1)}, u32[]{:S(2)}, u32[]{:S(2)}) collective-permute-start(f32[128,1536]{1,0:T(8,128)} %get-tuple-element.114.mine), channel_id=1, source_target_pairs={{0,1},{1,0},{2,3},{3,2},{4,5},{5,4},{6,7},{7,6},{8,9},{9,8},{10,11... | collective-permute-start | bytes 2359304 | tf_op jit(solution)/shard_map/ppermute | solution.py:657
  141.2 15.8 %collective-permute-start.21 = (f32[32,1536]{1,0:T(8,128)}, f32[32,1536]{1,0:T(8,128)S(1)}, u32[]{:S(2)}, u32[]{:S(2)}) collective-permute-start(f32[32,1536]{1,0:T(8,128)} %get-tuple-element.115), channel_id=1, source_target_pairs={{2,0},{4,2},{6,4},{8,6},{10,8},{12,10},{14,12},{16,14},{18,16},{20... | collective-permute-start | bytes 589832 | tf_op jit(solution)/shard_map/ppermute | solution.py:658
  142.5 14.6 %collective-permute-start.22 = (f32[32,1536]{1,0:T(8,128)}, f32[32,1536]{1,0:T(8,128)S(1)}, u32[]{:S(2)}, u32[]{:S(2)}) collective-permute-start(f32[32,1536]{1,0:T(8,128)} %get-tuple-element.115), channel_id=1, source_target_pairs={{2,1},{4,3},{6,5},{8,7},{10,9},{12,11},{14,13},{16,15},{18,17},{20... | collective-permute-start | bytes 589832 | tf_op jit(solution)/shard_map/ppermute | solution.py:659
  143.2 13.9 %all-to-all-start.2 = ((f32[32,1,128]{2,1,0:T(1,128)}), f32[32,1,128]{2,1,0:T(1,128)S(1)}, u32[]{:S(2)}, u32[]{:S(2)}) async-start(f32[32,1,128]{2,1,0:T(1,128)} %get-tuple-element.108), calls=%async_computation.2 | async-start | bytes 32768 | tf_op jit(solution)/shard_map/all_to_all | solution.py:782
  157.8 0.9 copy-start.11
  170.9 12.4 %all-to-all-start.3 = ((f32[16,2,768]{2,1,0:T(2,128)}), f32[16,2,768]{2,1,0:T(2,128)S(1)}, u32[]{:S(2)}, u32[]{:S(2)}) async-start(f32[16,2,768]{2,1,0:T(2,128)} %get-tuple-element.118.stats.local_stats), calls=%async_computation.3 | async-start | bytes 196608 | tf_op jit(solution)/shard_map/all_to_all | solution.py:663
  175.7 19.5 %copy-start.28 = (f32[2,768]{1,0:T(2,128)S(1)}, f32[2,768]{1,0:T(2,128)}, u32[]{:S(2)}) copy-start(f32[2,768]{1,0:T(2,128)} %get-tuple-element.126) | copy-start | bytes 18436
  190.3 13.4 %all-to-all-start.4 = ((bf16[16,48,128]{2,1,0:T(8,128)(2,1)}), bf16[16,48,128]{2,1,0:T(8,128)(2,1)S(1)}, u32[]{:S(2)}, u32[]{:S(2)}) async-start(bf16[16,48,128]{2,1,0:T(8,128)(2,1)} %get-tuple-element.124), calls=%async_computation.4 | async-start | bytes 393216 | tf_op jit(solution)/shard_map/all_to_all | solution.py:663
  (7 other events, 4.9 us)

commit v8 on v7

--- a/solution.py
+++ b/solution.py
@@ -754,6 +754,8 @@
             pieces += sent[: len(sent_kinds)]
             for k, arrived in zip(onward, sent[len(sent_kinds) :]):
                 along[k] = arrived
+    base, _ = lax.optimization_barrier((jnp.stack([features[0], start_noise[0]]), relayed))
+    base_crossing = across(base, jnp.where(first, base[:, :HALO], base[:, rows - HALO :]))
     late_kinds.append((shifts[final], 3))
     late_pieces.append(lax.ppermute(relayed, "tm", corner))
     weight = place_late(scal, late_kinds, late_pieces, block.shape[0], weight)
@@ -761,19 +763,17 @@
     value, gate, glu, conv, stats = forward(
         scal, normed_b, weight, taps, chip_rows, chips, True
     )
+    stats, base_crossing = lax.optimization_barrier((stats, base_crossing))
     place_of = jnp.arange(half_width, dtype=jnp.int32)
     source = (2 * (place_of // slice_width) + core) * slice_width + place_of % slice_width
     chosen = (jnp.arange(width, dtype=jnp.int32)[:, None] == source[None, :]).astype(BF16)
-    chosen, _ = lax.optimization_barrier((chosen, stats))
     cot = jnp.dot(wide_cot, chosen, preferred_element_type=F32).astype(BF16)
-    gathered, base = peers_of(stats), jnp.stack([features[0], start_noise[0]])
-    base, _ = lax.optimization_barrier((base, cot))
-    partner, near, far = across(base, jnp.where(first, base[:, :HALO], base[:, rows - HALO :]))
+    gathered = peers_of(stats)
+    partner, near, far = base_crossing
     wide_features, wide_noise = (
         assemble(base[n], partner[n], near[n], far[n]) for n in range(2)
     )
     scaled, grad, inv, sums = batch(scal, counts, gathered, conv, cot, gain, shift, chips)
-    sums, wide_features, wide_noise = lax.optimization_barrier((sums, wide_features, wide_noise))
     mine, other, grad_conv, totals = backward(
         scal, peers_of(sums), scaled, grad, inv, gain, taps, value, gate, weight
     )

time: 208 us -> 207 us (level)
  blocking collectives: 27.6 us -> 11.8 us
  starting transfers between devices: 41.5 us -> 48.6 us
  local copies, waits for them, and re-layouts: 11.3 us -> 15.9 us
  waiting for transfers between devices: 44.8 us -> 48.6 us
    all_to_all x2 -> x1, blocking collectives: 27.6 us -> 11.8 us  [peers_of(): lax.all_to_all(array, 'tm', 0, 0, axis_index_groups=cores, tiled=True)]
    all_to_all x2 -> x3, starting transfers between devices: 9.62 us -> 16.5 us  [peers_of(): lax.all_to_all(array, 'tm', 0, 0, axis_index_groups=cores, tiled=True)]
    all_to_all x2 -> x3, waiting for transfers between devices: 9.15 us -> 15 us  [peers_of(): lax.all_to_all(array, 'tm', 0, 0, axis_index_groups=cores, tiled=True)]
    ppermute x3, waiting for transfers between devices: 6.07 us -> 1.98 us  [across(): lax.ppermute(edge, 'tm', near_pairs)]
    ppermute x1, waiting for transfers between devices: 3.53 us -> 6.05 us  [on_device(): late_pieces.append(lax.ppermute(relayed, 'tm', corner))]
    ppermute x3, waiting for transfers between devices: 0.01 us -> 2.41 us  [on_device(): lax.ppermute(blocks, 'tm', swap_y)]
  transfers between devices with their start and end apart: 26 -> 27, of which waited for: 12 -> 14; matrix products, arithmetic and copies ran while one was open for 8% -> 11% of each run, Pallas kernels for 9% -> 12%
where the time goes in v8:
time: 207 us; the launch traced here: 205 us
  Pallas kernels  60.6 us (29%)
  starting transfers between devices  48.6 us (23%)
  waiting for transfers between devices  48.6 us (23%)
  other arithmetic  16.2 us (8%)
  local copies, waits for them, and re-layouts  15.9 us (8%)
  blocking collectives  11.8 us (6%)
    all_to_all x3, starting transfers between devices, peers_of(): lax.all_to_all(array, 'tm', 0, 0, axis_index_groups=cores, tiled=True)  16.5 us
    pallas_call x2, Pallas kernels, forward(): pl.pallas_call(functools.partial(forward_kernel, keep), grid=(steps,), in...  15.5 us
    all_to_all x3, waiting for transfers between devices, peers_of(): lax.all_to_all(array, 'tm', 0, 0, axis_index_groups=cores, tiled=True)  15 us
    ppermute x3, waiting for transfers between devices, on_device(): lax.ppermute(along[k - 1 if from_before else k + 1], 'tm', forth if from_...  12.7 us
    all_to_all x1, blocking collectives, peers_of(): lax.all_to_all(array, 'tm', 0, 0, axis_index_groups=cores, tiled=True)  11.8 us
    pallas_call x1, Pallas kernels, backward(): pl.pallas_call(backward_kernel, grid=(steps,), in_specs=[pl.BlockSpec(mem...  8.2 us
    all_to_all x1, starting transfers between devices, on_device(): squares = lax.all_to_all(squares, 'tm', 0, 0, tiled=True)  6.96 us
    pallas_call x1, Pallas kernels, last(): pl.pallas_call(functools.partial(last_kernel, taps_n), grid=(steps,), in_...  6.37 us
  transfers between devices with their start and end apart: 27, of which 14 were waited for; matrix products, arithmetic and copies ran while one was open for 11% of the time, Pallas kernels for 12%

profile of v8, /device:TPU:0, one launch (start us, length us, event | category | flops | bytes accessed | tf_op | source)
XLA Modules:
  0.0 205.4 jit_solution(7502068065993499193)
XLA Ops:
  4.4 2.6 %collective-permute-start.1 = (bf16[96,1536]{1,0:T(8,128)(2,1)S(1)}, bf16[96,1536]{1,0:T(8,128)(2,1)S(1)}, u32[]{:S(2)}, u32[]{:S(2)}) collective-permute-start(bf16[96,1536]{1,0:T(8,128)(2,1)S(1)} %pad_maximum_fusion.6.refs_0_), channel_id=1, source_target_pairs={{0,2},{1,3},{2,0},{3,1},{4,6},{5,7},{6,4},{7,5},{8,10},{9,11},{10,... | collective-permute-start | bytes 884744 | tf_op jit(solution)/shard_map/ppermute | solution.py:713
  7.8 1.2 pad_maximum_fusion.5
  9.0 1.6 collective-permute-start.2
  10.5 1.6 collective-permute-start.3
  12.1 2.2 %collective-permute-start.4 = (bf16[96,1536]{1,0:T(8,128)(2,1)S(1)}, bf16[96,1536]{1,0:T(8,128)(2,1)S(1)}, u32[]{:S(2)}, u32[]{:S(2)}) collective-permute-start(bf16[96,1536]{1,0:T(8,128)(2,1)S(1)} %pad_maximum_fusion.6.refs_0_), channel_id=1, source_target_pairs={{0,24},{1,25},{2,26},{3,27},{4,28},{5,29},{6,30},{7,31},{8,0},{9,1... | collective-permute-start | bytes 884744 | tf_op jit(solution)/shard_map/ppermute | solution.py:721
  15.7 2.4 %collective-permute-done.2.refs_2_ = bf16[96,1536]{1,0:T(8,128)(2,1)S(1)} collective-permute-done((bf16[96,1536]{1,0:T(8,128)(2,1)S(1)}, bf16[96,1536]{1,0:T(8,128)(2,1)S(1)}, u32[]{:S(2)}, u32[]{:S(2)}) %collective-permute-start.2) | collective-permute-done | bytes 294944 | tf_op jit(solution)/shard_map/ppermute | solution.py:713
  18.1 4.2 %collective-permute-done.3 = bf16[96,1536]{1,0:T(8,128)(2,1)S(1)} collective-permute-done((bf16[96,1536]{1,0:T(8,128)(2,1)S(1)}, bf16[96,1536]{1,0:T(8,128)(2,1)S(1)}, u32[]{:S(2)}, u32[]{:S(2)}) %collective-permute-start.3) | collective-permute-done | bytes 294944 | tf_op jit(solution)/shard_map/ppermute | solution.py:721
  22.3 4.7 %collective-permute-done.4 = bf16[96,1536]{1,0:T(8,128)(2,1)S(1)} collective-permute-done((bf16[96,1536]{1,0:T(8,128)(2,1)S(1)}, bf16[96,1536]{1,0:T(8,128)(2,1)S(1)}, u32[]{:S(2)}, u32[]{:S(2)}) %collective-permute-start.4) | collective-permute-done | bytes 294944 | tf_op jit(solution)/shard_map/ppermute | solution.py:721
  26.9 1.1 collective-permute-start.8
  30.2 1.5 collective-permute-start.5
  33.2 3.9 %collective-permute-done.8.refs_7_ = bf16[96,1536]{1,0:T(8,128)(2,1)S(1)} collective-permute-done((bf16[96,1536]{1,0:T(8,128)(2,1)S(1)}, bf16[96,1536]{1,0:T(8,128)(2,1)S(1)}, u32[]{:S(2)}, u32[]{:S(2)}) %collective-permute-start.8) | collective-permute-done | bytes 294944 | tf_op jit(solution)/shard_map/ppermute | solution.py:721
  37.1 1.8 collective-permute-done.7.refs_6_
  41.5 1.3 collective-permute-start.10
  42.8 1.3 collective-permute-start.11
  44.1 1.6 concatenate.37
  51.0 2.0 collective-permute-done.10
  55.1 1.1 bitcast_select_fusion.1
  56.3 2.3 %collective-permute-start.14 = (bf16[192,1536]{1,0:T(8,128)(2,1)S(1)}, bf16[192,1536]{1,0:T(8,128)(2,1)S(1)}, u32[]{:S(2)}, u32[]{:S(2)}) collective-permute-start(bf16[192,1536]{1,0:T(8,128)(2,1)S(1)} %broadcast_select_fusion), channel_id=1, source_target_pairs={{0,2},{1,5},{2,0},{3,7},{4,6},{5,1},{6,4},{7,3},{8,10},{9,13},{10,... | collective-permute-start | bytes 1769480 | tf_op jit(solution)/shard_map/ppermute | solution.py:716
  60.5 1.5 collective-permute-start.13
  62.0 4.2 %place_weights.1.refs_4_ = bf16[1536,1536]{1,0:T(8,128)(2,1)} custom-call(s32[6]{0:T(128)} %stack.38.scal, bf16[96,1536]{1,0:T(8,128)(2,1)} %copy-done.9, bf16[96,1536]{1,0:T(8,128)(2,1)} %copy-done.5, bf16[96,1536]{1,0:T(8,128)(2,1)} %copy-done.6, bf16[192,1536]{1,0:T(8,128)(2,1)} %constant_dynamic-update-slice_fusion.refs_3_, bf16[192,1536]{1,0:T(8,128)(2,1)} %copy-done.2, ...), custom_call_target="tpu_custom_call" | custom-call | bytes 9437184 | tf_op jit(solution)/shard_map/place_weights/pallas_call | solution.py:124
  67.3 5.5 %collective-permute-done.12.refs_0_ = bf16[96,1536]{1,0:T(8,128)(2,1)S(1)} collective-permute-done((bf16[96,1536]{1,0:T(8,128)(2,1)S(1)}, bf16[96,1536]{1,0:T(8,128)(2,1)S(1)}, u32[]{:S(2)}, u32[]{:S(2)}) %collective-permute-start.12) | collective-permute-done | bytes 294944 | tf_op jit(solution)/shard_map/ppermute | solution.py:713
  73.0 2.0 collective-permute-start.15
  75.1 1.3 collective-permute-start.17
  77.1 6.0 %collective-permute-done.15.refs_3_ = bf16[96,1536]{1,0:T(8,128)(2,1)S(1)} collective-permute-done((bf16[96,1536]{1,0:T(8,128)(2,1)S(1)}, bf16[96,1536]{1,0:T(8,128)(2,1)S(1)}, u32[]{:S(2)}, u32[]{:S(2)}) %collective-permute-start.15) | collective-permute-done | bytes 294944 | tf_op jit(solution)/shard_map/ppermute | solution.py:760
  83.8 2.5 %place_last_weights.1.value_w.gate_w = bf16[1536,1536]{1,0:T(8,128)(2,1)} custom-call(s32[6]{0:T(128)} %stack.38.scal, bf16[96,1536]{1,0:T(8,128)(2,1)} %copy-done.7, bf16[96,1536]{1,0:T(8,128)(2,1)} %copy-done.8, bf16[192,1536]{1,0:T(8,128)(2,1)} %copy-done.15, bf16[96,1536]{1,0:T(8,128)(2,1)} %copy-done.21, ...), custom_call_target="tpu_custom_call", output_to_operand_aliasing={{}: (5, {})} | custom-call | bytes 2949120 | tf_op jit(solution)/shard_map/place_last_weights/pallas_call | solution.py:139
  86.3 7.8 %project_glu_conv.2 = (f32[256,768]{1,0:T(8,128)}, f32[256,768]{1,0:T(8,128)}, bf16[320,768]{1,0:T(8,128)(2,1)}, f32[288,768]{1,0:T(8,128)}, f32[16,2,768]{2,1,0:T(2,128)}) custom-call(s32[6]{0:T(128)} %stack.38.scal, bf16[320,1536]{1,0:T(8,128)(2,1)} %pad_maximum_fusion.nb, bf16[1536,1536]{1,0:T(8,128)(2,1)} %place_last_weights.1.value_w.gate_w, ...), custom_call_target="tpu_custom_call" | custom-call | flops 1509949440 | bytes 7176192 | tf_op jit(solution)/shard_map/project_glu_conv/pallas_call | solution.py:183
  95.1 5.4 %all-to-all-start = ((f32[16,2,768]{2,1,0:T(2,128)}), f32[16,2,768]{2,1,0:T(2,128)S(1)}, u32[]{:S(2)}, u32[]{:S(2)}) async-start(f32[16,2,768]{2,1,0:T(2,128)} %get-tuple-element.94), calls=%async_computation | async-start | bytes 196608 | tf_op jit(solution)/shard_map/all_to_all | solution.py:663
  100.5 1.9 fusion.2.cot
  102.4 5.8 %all-to-all-done.stats = f32[16,2,768]{2,1,0:T(2,128)S(1)} async-done(((f32[16,2,768]{2,1,0:T(2,128)}), f32[16,2,768]{2,1,0:T(2,128)S(1)}, u32[]{:S(2)}, u32[]{:S(2)}) %all-to-all-start) | async-done | bytes 98336 | tf_op jit(solution)/shard_map/all_to_all | solution.py:663
  108.9 3.9 %batch_norm_swish.1 = (f32[288,768]{1,0:T(8,128)}, f32[288,768]{1,0:T(8,128)}, f32[1,768]{1,0:T(1,128)}, f32[16,2,768]{2,1,0:T(2,128)}) custom-call(s32[6]{0:T(128)} %stack.38.scal, f32[2,16]{1,0:T(2,128)} %pad_maximum_fusion.8.counts, f32[16,2,768]{2,1,0:T(2,128)} %copy-done.17, f32[288,768]{1,0:T(8,128)} %get-tuple-element.95.conv, ...), custom_call_target="tpu_custom_call" | custom-call | flops 8847360 | bytes 3538944 | tf_op jit(solution)/shard_map/batch_norm_swish/pallas_call | solution.py:263
  112.8 11.8 %all_to_all.25.sums = f32[16,2,768]{2,1,0:T(2,128)} all-to-all(f32[16,2,768]{2,1,0:T(2,128)} %get-tuple-element.99), channel_id=1, replica_groups={{0,2,4,6,8,10,12,14,16,18,20,22,24,26,28,30},{1,3,5,7,9,11,13,15,17,19,..., dimensions={0} | all-to-all | bytes 196608 | tf_op jit(solution)/shard_map/all_to_all | solution.py:663
  124.6 8.2 %grad_conv_project_back.1 = (f32[128,1536]{1,0:T(8,128)}, f32[128,1536]{1,0:T(8,128)}, bf16[256,768]{1,0:T(8,128)(2,1)}, f32[2,768]{1,0:T(2,128)}) custom-call(s32[6]{0:T(128)} %stack.38.scal, f32[16,2,768]{2,1,0:T(2,128)} %all_to_all.25.sums, f32[288,768]{1,0:T(8,128)} %get-tuple-element.100.scaled, f32[288,768]{1,0:T(8,128)} %get-tuple-element.101.grad, ...), custom_call_target="tpu_custom_call" | custom-call | flops 1207959552 | bytes 9142272 | tf_op jit(solution)/shard_map/grad_conv_project_back/pallas_call | solution.py:338
  132.9 2.5 %collective-permute-done.19.other = f32[128,1536]{1,0:T(8,128)S(1)} collective-permute-done((f32[128,1536]{1,0:T(8,128)}, f32[128,1536]{1,0:T(8,128)S(1)}, u32[]{:S(2)}, u32[]{:S(2)}) %collective-permute-start.19) | collective-permute-done | bytes 786464 | tf_op jit(solution)/shard_map/ppermute | solution.py:780
  136.3 3.2 %direction.1 = (f32[128,1536]{1,0:T(8,128)}, f32[32,1536]{1,0:T(8,128)}, f32[32,1,128]{2,1,0:T(1,128)}) custom-call(s32[6]{0:T(128)} %stack.38.scal, f32[128,1536]{1,0:T(8,128)} %get-tuple-element.105.mine, f32[128,1536]{1,0:T(8,128)} %copy-done.11, bf16[128,1536]{1,0:T(8,128)(2,1)} %bitcast.63, bf16[128,1536]{1,0:T(8,128)(2,1)} %bitcast.58), custom_call_target="tpu_custom_call" | custom-call | flops 5898240 | bytes 3145728 | tf_op jit(solution)/shard_map/direction/pallas_call | solution.py:568
  139.7 1.3 collective-permute-start.21
  141.7 7.0 %all-to-all-start.2 = ((f32[32,1,128]{2,1,0:T(1,128)}), f32[32,1,128]{2,1,0:T(1,128)S(1)}, u32[]{:S(2)}, u32[]{:S(2)}) async-start(f32[32,1,128]{2,1,0:T(1,128)} %get-tuple-element.107), calls=%async_computation.2 | async-start | bytes 32768 | tf_op jit(solution)/shard_map/all_to_all | solution.py:782
  148.7 1.5 pad_maximum_fusion.1
  150.2 4.9 %tap_grad.1.taps_before = f32[31,768]{1,0:T(8,128)} custom-call(bf16[256,768]{1,0:T(8,128)(2,1)} %get-tuple-element.108.grad_conv, bf16[320,768]{1,0:T(8,128)(2,1)} %get-tuple-element.109.glu), custom_call_target="tpu_custom_call" | custom-call | flops 12189696 | bytes 983040 | tf_op jit(solution)/shard_map/tap_grad/pallas_call | solution.py:386
  156.6 4.4 %ascend.1 = (f32[128,1536]{1,0:T(8,128)}, bf16[320,1536]{1,0:T(8,128)(2,1)}) custom-call(s32[6]{0:T(128)} %stack.38.scal, f32[32,1,128]{2,1,0:T(1,128)} %copy-done.25, bf16[320,1536]{1,0:T(8,128)(2,1)} %get-tuple-element.149.features, bf16[320,1536]{1,0:T(8,128)(2,1)} %get-tuple-element.150.noise, f32[128,1536]{1,0:T(8,128)} %get-tuple-element.114.mine, ...), custom_call_target="tpu_custom_call" | custom-call | flops 14745600 | bytes 3932160 | tf_op jit(solution)/shard_map/ascend/pallas_call | solution.py:612
  161.1 7.7 %project_glu_conv.3 = (bf16[320,768]{1,0:T(8,128)(2,1)}, f32[288,768]{1,0:T(8,128)}, f32[16,2,768]{2,1,0:T(2,128)}) custom-call(s32[6]{0:T(128)} %stack.38.scal, bf16[320,1536]{1,0:T(8,128)(2,1)} %get-tuple-element.117.nb, bf16[1536,1536]{1,0:T(8,128)(2,1)} %place_last_weights.1.value_w.gate_w, bf16[1536,1536]{1,0:T(8,128)(2,1)} %place_last_weights.1.value_w.gate_w, ...), custom_call_target="tpu_custom_call" | custom-call | flops 1509949440 | bytes 7176192 | tf_op jit(solution)/shard_map/project_glu_conv/pallas_call | solution.py:183
  168.7 6.2 %all-to-all-start.3 = ((f32[16,2,768]{2,1,0:T(2,128)}), f32[16,2,768]{2,1,0:T(2,128)S(1)}, u32[]{:S(2)}, u32[]{:S(2)}) async-start(f32[16,2,768]{2,1,0:T(2,128)} %get-tuple-element.118.stats.local_stats), calls=%async_computation.3 | async-start | bytes 196608 | tf_op jit(solution)/shard_map/all_to_all | solution.py:663
  175.0 5.6 %raw_taps.1 = (f32[31,768]{1,0:T(8,128)}, f32[31,768]{1,0:T(8,128)}) custom-call(s32[6]{0:T(128)} %stack.38.scal, f32[288,768]{1,0:T(8,128)} %get-tuple-element.119.conv, bf16[320,768]{1,0:T(8,128)(2,1)} %get-tuple-element.120.glu, f32[16,2,768]{2,1,0:T(2,128)} %get-tuple-element.118.stats.local_stats), custom_call_target="tpu_custom_call" | custom-call | flops 13713408 | bytes 1966080 | tf_op jit(solution)/shard_map/raw_taps/pallas_call | solution.py:419
  180.6 2.0 all-to-all-done.3.stats
  183.3 6.4 %batch_norm_swish_taps.1 = (bf16[16,48,128]{2,1,0:T(8,128)(2,1)}, f32[1,768]{1,0:T(1,128)}) custom-call(s32[6]{0:T(128)} %stack.38.scal, f32[2,16]{1,0:T(2,128)} %pad_maximum_fusion.8.counts, f32[16,2,768]{2,1,0:T(2,128)} %copy-done.16, f32[288,768]{1,0:T(8,128)} %get-tuple-element.119.conv, bf16[288,768]{1,0:T(8,128)(2,1)} %fusion.2.cot, ...), custom_call_target="tpu_custom_call" | custom-call | flops 22118400 | bytes 2211840 | tf_op jit(solution)/shard_map/batch_norm_swish_taps/pallas_call | solution.py:479
  189.7 4.9 %all-to-all-start.4 = ((bf16[16,48,128]{2,1,0:T(8,128)(2,1)}), bf16[16,48,128]{2,1,0:T(8,128)(2,1)S(1)}, u32[]{:S(2)}, u32[]{:S(2)}) async-start(bf16[16,48,128]{2,1,0:T(8,128)(2,1)} %get-tuple-element.124), calls=%async_computation.4 | async-start | bytes 393216 | tf_op jit(solution)/shard_map/all_to_all | solution.py:663
  194.6 1.3 fusion.17.known
  195.9 7.1 %all-to-all-done.4.received = bf16[16,48,128]{2,1,0:T(8,128)(2,1)S(1)} async-done(((bf16[16,48,128]{2,1,0:T(8,128)(2,1)}), bf16[16,48,128]{2,1,0:T(8,128)(2,1)S(1)}, u32[]{:S(2)}, u32[]{:S(2)}) %all-to-all-start.4) | async-done | bytes 196640 | tf_op jit(solution)/shard_map/all_to_all | solution.py:663
  203.8 1.7 finish.1
  (126 shorter events, 29.6 us)
Async XLA Ops:
  0.6 14.1 %copy-start = (bf16[1,128,1536]{2,1,0:T(8,128)(2,1)S(1)}, bf16[1,128,1536]{2,1,0:T(8,128)(2,1)}, u32[]{:S(2)}) copy-start(bf16[1,128,1536]{2,1,0:T(8,128)(2,1)} %param.9) | copy-start | bytes 1179652
  0.6 14.0 %copy-start.1 = (bf16[1,128,1536]{2,1,0:T(8,128)(2,1)S(1)}, bf16[1,128,1536]{2,1,0:T(8,128)(2,1)}, u32[]{:S(2)}) copy-start(bf16[1,128,1536]{2,1,0:T(8,128)(2,1)} %param.8) | copy-start | bytes 1179652
  1.7 1.8 collective-permute-start
  4.4 11.2 %copy-start.9 = (bf16[96,1536]{1,0:T(8,128)(2,1)}, bf16[96,1536]{1,0:T(8,128)(2,1)S(1)}, u32[]{:S(2)}) copy-start(bf16[96,1536]{1,0:T(8,128)(2,1)S(1)} %pad_maximum_fusion.6.refs_0_) | copy-start | bytes 884740
  4.4 10.2 %collective-permute-start.1 = (bf16[96,1536]{1,0:T(8,128)(2,1)S(1)}, bf16[96,1536]{1,0:T(8,128)(2,1)S(1)}, u32[]{:S(2)}, u32[]{:S(2)}) collective-permute-start(bf16[96,1536]{1,0:T(8,128)(2,1)S(1)} %pad_maximum_fusion.6.refs_0_), channel_id=1, source_target_pairs={{0,2},{1,3},{2,0},{3,1},{4,6},{5,7},{6,4},{7,5},{8,10},{9,11},{10,... | collective-permute-start | bytes 884744 | tf_op jit(solution)/shard_map/ppermute | solution.py:713
  9.0 9.1 %collective-permute-start.2 = (bf16[96,1536]{1,0:T(8,128)(2,1)S(1)}, bf16[96,1536]{1,0:T(8,128)(2,1)S(1)}, u32[]{:S(2)}, u32[]{:S(2)}) collective-permute-start(bf16[96,1536]{1,0:T(8,128)(2,1)S(1)} %pad_maximum_fusion.6.refs_0_), channel_id=1, source_target_pairs={{0,4},{1,5},{2,6},{3,7},{4,0},{5,1},{6,2},{7,3},{8,12},{9,13},{10,... | collective-permute-start | bytes 884744 | tf_op jit(solution)/shard_map/ppermute | solution.py:713
  10.5 11.7 %collective-permute-start.3 = (bf16[96,1536]{1,0:T(8,128)(2,1)S(1)}, bf16[96,1536]{1,0:T(8,128)(2,1)S(1)}, u32[]{:S(2)}, u32[]{:S(2)}) collective-permute-start(bf16[96,1536]{1,0:T(8,128)(2,1)S(1)} %pad_maximum_fusion.6.refs_0_), channel_id=1, source_target_pairs={{0,8},{1,9},{2,10},{3,11},{4,12},{5,13},{6,14},{7,15},{8,16},{9,17... | collective-permute-start | bytes 884744 | tf_op jit(solution)/shard_map/ppermute | solution.py:721
  12.1 14.8 %collective-permute-start.4 = (bf16[96,1536]{1,0:T(8,128)(2,1)S(1)}, bf16[96,1536]{1,0:T(8,128)(2,1)S(1)}, u32[]{:S(2)}, u32[]{:S(2)}) collective-permute-start(bf16[96,1536]{1,0:T(8,128)(2,1)S(1)} %pad_maximum_fusion.6.refs_0_), channel_id=1, source_target_pairs={{0,24},{1,25},{2,26},{3,27},{4,28},{5,29},{6,30},{7,31},{8,0},{9,1... | collective-permute-start | bytes 884744 | tf_op jit(solution)/shard_map/ppermute | solution.py:721
  14.7 14.2 %copy-start.5 = (bf16[96,1536]{1,0:T(8,128)(2,1)}, bf16[96,1536]{1,0:T(8,128)(2,1)S(1)}, u32[]{:S(2)}) copy-start(bf16[96,1536]{1,0:T(8,128)(2,1)S(1)} %collective-permute-done.1.refs_1_) | copy-start | bytes 884740
  15.0 17.2 %copy-start.4 = (bf16[1,128,1536]{2,1,0:T(8,128)(2,1)S(1)}, bf16[1,128,1536]{2,1,0:T(8,128)(2,1)}, u32[]{:S(2)}) copy-start(bf16[1,128,1536]{2,1,0:T(8,128)(2,1)} %param.10) | copy-start | bytes 1179652
  18.1 12.1 %copy-start.6 = (bf16[96,1536]{1,0:T(8,128)(2,1)}, bf16[96,1536]{1,0:T(8,128)(2,1)S(1)}, u32[]{:S(2)}) copy-start(bf16[96,1536]{1,0:T(8,128)(2,1)S(1)} %collective-permute-done.2.refs_2_) | copy-start | bytes 884740
  26.9 10.1 %collective-permute-start.8 = (bf16[96,1536]{1,0:T(8,128)(2,1)S(1)}, bf16[96,1536]{1,0:T(8,128)(2,1)S(1)}, u32[]{:S(2)}, u32[]{:S(2)}) collective-permute-start(bf16[96,1536]{1,0:T(8,128)(2,1)S(1)} %collective-permute-done.3), channel_id=1, source_target_pairs={{0,8},{1,9},{2,10},{3,11},{4,12},{5,13},{6,14},{7,15},{8,16},{9,17... | collective-permute-start | bytes 884744 | tf_op jit(solution)/shard_map/ppermute | solution.py:721
  28.8 15.3 %copy-start.24 = (f32[31,1536]{1,0:T(8,128)S(1)}, f32[31,1536]{1,0:T(8,128)}, u32[]{:S(2)}) copy-start(f32[31,1536]{1,0:T(8,128)} %param.12) | copy-start | bytes 571396
  28.9 9.9 %collective-permute-start.7 = (bf16[96,1536]{1,0:T(8,128)(2,1)S(1)}, bf16[96,1536]{1,0:T(8,128)(2,1)S(1)}, u32[]{:S(2)}, u32[]{:S(2)}) collective-permute-start(bf16[96,1536]{1,0:T(8,128)(2,1)S(1)} %broadcast_select_fusion.2), channel_id=1, source_target_pairs={{0,2},{1,5},{2,0},{3,7},{4,6},{5,1},{6,4},{7,3},{8,10},{9,13},{10,... | collective-permute-start | bytes 884744 | tf_op jit(solution)/shard_map/ppermute | solution.py:716
  30.2 22.7 %collective-permute-start.5 = (bf16[192,1536]{1,0:T(8,128)(2,1)}, bf16[192,1536]{1,0:T(8,128)(2,1)S(1)}, u32[]{:S(2)}, u32[]{:S(2)}) collective-permute-start(bf16[192,1536]{1,0:T(8,128)(2,1)} %constant_dynamic-update-slice_fusion.refs_3_), channel_id=1, source_target_pairs={{0,2},{1,3},{2,0},{3,1},{4,6},{5,7},{6,4},{7,5},{8,10},{9,11},{10,... | collective-permute-start | bytes 1769480 | tf_op jit(solution)/shard_map/ppermute | solution.py:713
  31.7 21.2 %collective-permute-start.6 = (bf16[192,1536]{1,0:T(8,128)(2,1)}, bf16[192,1536]{1,0:T(8,128)(2,1)S(1)}, u32[]{:S(2)}, u32[]{:S(2)}) collective-permute-start(bf16[192,1536]{1,0:T(8,128)(2,1)} %constant_dynamic-update-slice_fusion.refs_3_), channel_id=1, source_target_pairs={{0,4},{1,5},{2,6},{3,7},{4,0},{5,1},{6,2},{7,3},{8,12},{9,13},{10,... | collective-permute-start | bytes 1769480 | tf_op jit(solution)/shard_map/ppermute | solution.py:713
  32.2 14.6 %copy-start.26 = (f32[1536]{0:T(1024)S(1)}, f32[1536]{0:T(1024)}, u32[]{:S(2)}) copy-start(f32[1536]{0:T(1024)} %param.13) | copy-start | bytes 18436
  32.2 14.7 %copy-start.27 = (f32[1536]{0:T(1024)S(1)}, f32[1536]{0:T(1024)}, u32[]{:S(2)}) copy-start(f32[1536]{0:T(1024)} %param.14) | copy-start | bytes 18436
  37.1 7.0 %copy-start.18 = (bf16[96,1536]{1,0:T(8,128)(2,1)}, bf16[96,1536]{1,0:T(8,128)(2,1)S(1)}, u32[]{:S(2)}) copy-start(bf16[96,1536]{1,0:T(8,128)(2,1)S(1)} %collective-permute-done.8.refs_7_) | copy-start | bytes 884740
  38.8 2.7 %copy-start.20 = (bf16[96,1536]{1,0:T(8,128)(2,1)}, bf16[96,1536]{1,0:T(8,128)(2,1)S(1)}, u32[]{:S(2)}) copy-start(bf16[96,1536]{1,0:T(8,128)(2,1)S(1)} %collective-permute-done.7.refs_6_) | copy-start | bytes 884740
  39.9 13.1 %collective-permute-start.9 = (bf16[2,128,1536]{2,1,0:T(8,128)(2,1)}, bf16[2,128,1536]{2,1,0:T(8,128)(2,1)}, u32[]{:S(2)}, u32[]{:S(2)}) collective-permute-start(bf16[2,128,1536]{2,1,0:T(8,128)(2,1)} %pad_maximum_fusion.4), channel_id=1, source_target_pairs={{0,1},{1,0},{2,3},{3,2},{4,5},{5,4},{6,7},{7,6},{8,9},{9,8},{10,11... | collective-permute-start | bytes 2359304 | tf_op jit(solution)/shard_map/ppermute | solution.py:657
  41.5 11.5 %collective-permute-start.10 = (bf16[48,1536]{1,0:T(8,128)(2,1)}, bf16[48,1536]{1,0:T(8,128)(2,1)}, u32[]{:S(2)}, u32[]{:S(2)}) collective-permute-start(bf16[48,1536]{1,0:T(8,128)(2,1)} %pad_maximum_fusion.7), channel_id=1, source_target_pairs={{2,0},{4,2},{6,4},{8,6},{10,8},{12,10},{14,12},{16,14},{18,16},{20... | collective-permute-start | bytes 442376 | tf_op jit(solution)/shard_map/ppermute | solution.py:658
  42.8 10.2 %collective-permute-start.11 = (bf16[48,1536]{1,0:T(8,128)(2,1)}, bf16[48,1536]{1,0:T(8,128)(2,1)}, u32[]{:S(2)}, u32[]{:S(2)}) collective-permute-start(bf16[48,1536]{1,0:T(8,128)(2,1)} %pad_maximum_fusion.7), channel_id=1, source_target_pairs={{2,1},{4,3},{6,5},{8,7},{10,9},{12,11},{14,13},{16,15},{18,17},{20... | collective-permute-start | bytes 442376 | tf_op jit(solution)/shard_map/ppermute | solution.py:659
  52.9 3.2 %copy-start.2 = (bf16[192,1536]{1,0:T(8,128)(2,1)}, bf16[192,1536]{1,0:T(8,128)(2,1)S(1)}, u32[]{:S(2)}) copy-start(bf16[192,1536]{1,0:T(8,128)(2,1)S(1)} %collective-permute-done.5.refs_4_) | copy-start | bytes 1769476
  53.0 3.2 %copy-start.3 = (bf16[192,1536]{1,0:T(8,128)(2,1)}, bf16[192,1536]{1,0:T(8,128)(2,1)S(1)}, u32[]{:S(2)}) copy-start(bf16[192,1536]{1,0:T(8,128)(2,1)S(1)} %collective-permute-done.6.refs_5_) | copy-start | bytes 1769476
  55.1 5.4 %copy-start.19 = (bf16[96,1536]{1,0:T(8,128)(2,1)S(1)}, bf16[96,1536]{1,0:T(8,128)(2,1)}, u32[]{:S(2)}) copy-start(bf16[96,1536]{1,0:T(8,128)(2,1)} %copy-done.18) | copy-start | bytes 884740
  56.3 16.5 %collective-permute-start.14 = (bf16[192,1536]{1,0:T(8,128)(2,1)S(1)}, bf16[192,1536]{1,0:T(8,128)(2,1)S(1)}, u32[]{:S(2)}, u32[]{:S(2)}) collective-permute-start(bf16[192,1536]{1,0:T(8,128)(2,1)S(1)} %broadcast_select_fusion), channel_id=1, source_target_pairs={{0,2},{1,5},{2,0},{3,7},{4,6},{5,1},{6,4},{7,3},{8,10},{9,13},{10,... | collective-permute-start | bytes 1769480 | tf_op jit(solution)/shard_map/ppermute | solution.py:716
  60.4 12.4 %collective-permute-start.12 = (bf16[96,1536]{1,0:T(8,128)(2,1)S(1)}, bf16[96,1536]{1,0:T(8,128)(2,1)S(1)}, u32[]{:S(2)}, u32[]{:S(2)}) collective-permute-start(bf16[96,1536]{1,0:T(8,128)(2,1)S(1)} %copy-done.19), channel_id=1, source_target_pairs={{0,2},{1,3},{2,0},{3,1},{4,6},{5,7},{6,4},{7,5},{8,10},{9,11},{10,... | collective-permute-start | bytes 884744 | tf_op jit(solution)/shard_map/ppermute | solution.py:713
  60.5 12.3 %collective-permute-start.13 = (bf16[96,1536]{1,0:T(8,128)(2,1)S(1)}, bf16[96,1536]{1,0:T(8,128)(2,1)S(1)}, u32[]{:S(2)}, u32[]{:S(2)}) collective-permute-start(bf16[96,1536]{1,0:T(8,128)(2,1)S(1)} %copy-done.19), channel_id=1, source_target_pairs={{0,4},{1,5},{2,6},{3,7},{4,0},{5,1},{6,2},{7,3},{8,12},{9,13},{10,... | collective-permute-start | bytes 884744 | tf_op jit(solution)/shard_map/ppermute | solution.py:713
  72.8 10.3 %copy-start.7 = (bf16[96,1536]{1,0:T(8,128)(2,1)}, bf16[96,1536]{1,0:T(8,128)(2,1)S(1)}, u32[]{:S(2)}) copy-start(bf16[96,1536]{1,0:T(8,128)(2,1)S(1)} %collective-permute-done.12.refs_0_) | copy-start | bytes 884740
  72.8 10.3 %copy-start.8 = (bf16[96,1536]{1,0:T(8,128)(2,1)}, bf16[96,1536]{1,0:T(8,128)(2,1)S(1)}, u32[]{:S(2)}) copy-start(bf16[96,1536]{1,0:T(8,128)(2,1)S(1)} %collective-permute-done.13.refs_1_) | copy-start | bytes 884740
  72.8 10.3 %copy-start.15 = (bf16[192,1536]{1,0:T(8,128)(2,1)}, bf16[192,1536]{1,0:T(8,128)(2,1)S(1)}, u32[]{:S(2)}) copy-start(bf16[192,1536]{1,0:T(8,128)(2,1)S(1)} %collective-permute-done.14.refs_2_) | copy-start | bytes 1769476
  72.9 21.3 %collective-permute-start.16 = (bf16[2,128,1536]{2,1,0:T(8,128)(2,1)S(1)}, bf16[2,128,1536]{2,1,0:T(8,128)(2,1)S(1)}, u32[]{:S(2)}, u32[]{:S(2)}) collective-permute-start(bf16[2,128,1536]{2,1,0:T(8,128)(2,1)S(1)} %pad_maximum_fusion.5), channel_id=1, source_target_pairs={{0,1},{1,0},{2,3},{3,2},{4,5},{5,4},{6,7},{7,6},{8,9},{9,8},{10,11... | collective-permute-start | bytes 2359304 | tf_op jit(solution)/shard_map/ppermute | solution.py:657
  73.0 10.1 %collective-permute-start.15 = (bf16[96,1536]{1,0:T(8,128)(2,1)S(1)}, bf16[96,1536]{1,0:T(8,128)(2,1)S(1)}, u32[]{:S(2)}, u32[]{:S(2)}) collective-permute-start(bf16[96,1536]{1,0:T(8,128)(2,1)S(1)} %broadcast_select_fusion.1), channel_id=1, source_target_pairs={{0,2},{1,5},{2,0},{3,7},{4,6},{5,1},{6,4},{7,3},{8,10},{9,13},{10,... | collective-permute-start | bytes 884744 | tf_op jit(solution)/shard_map/ppermute | solution.py:760
  75.1 19.1 %collective-permute-start.17 = (bf16[2,32,1536]{2,1,0:T(8,128)(2,1)S(1)}, bf16[2,32,1536]{2,1,0:T(8,128)(2,1)S(1)}, u32[]{:S(2)}, u32[]{:S(2)}) collective-permute-start(bf16[2,32,1536]{2,1,0:T(8,128)(2,1)S(1)} %slice_select_fusion), channel_id=1, source_target_pairs={{2,0},{4,2},{6,4},{8,6},{10,8},{12,10},{14,12},{16,14},{18,16},{20... | collective-permute-start | bytes 589832 | tf_op jit(solution)/shard_map/ppermute | solution.py:658
  76.4 17.8 %collective-permute-start.18 = (bf16[2,32,1536]{2,1,0:T(8,128)(2,1)S(1)}, bf16[2,32,1536]{2,1,0:T(8,128)(2,1)S(1)}, u32[]{:S(2)}, u32[]{:S(2)}) collective-permute-start(bf16[2,32,1536]{2,1,0:T(8,128)(2,1)S(1)} %slice_select_fusion), channel_id=1, source_target_pairs={{2,1},{4,3},{6,5},{8,7},{10,9},{12,11},{14,13},{16,15},{18,17},{20... | collective-permute-start | bytes 589832 | tf_op jit(solution)/shard_map/ppermute | solution.py:659
  94.2 1.0 copy-start.13
  95.1 13.1 %all-to-all-start = ((f32[16,2,768]{2,1,0:T(2,128)}), f32[16,2,768]{2,1,0:T(2,128)S(1)}, u32[]{:S(2)}, u32[]{:S(2)}) async-start(f32[16,2,768]{2,1,0:T(2,128)} %get-tuple-element.94), calls=%async_computation | async-start | bytes 196608 | tf_op jit(solution)/shard_map/all_to_all | solution.py:663
  132.8 6.8 %copy-start.14 = (bf16[2,128,1536]{2,1,0:T(8,128)(2,1)S(1)}, bf16[2,128,1536]{2,1,0:T(8,128)(2,1)}, u32[]{:S(2)}) copy-start(bf16[2,128,1536]{2,1,0:T(8,128)(2,1)} %copy-done.13) | copy-start | bytes 2359300
  132.9 2.6 %collective-permute-start.19 = (f32[128,1536]{1,0:T(8,128)}, f32[128,1536]{1,0:T(8,128)S(1)}, u32[]{:S(2)}, u32[]{:S(2)}) collective-permute-start(f32[128,1536]{1,0:T(8,128)} %get-tuple-element.106), channel_id=1, source_target_pairs={{0,1},{1,0},{2,3},{3,2},{4,5},{5,4},{6,7},{7,6},{8,9},{9,8},{10,11... | collective-permute-start | bytes 2359304 | tf_op jit(solution)/shard_map/ppermute | solution.py:780
  139.5 16.2 %collective-permute-start.20 = (f32[128,1536]{1,0:T(8,128)}, f32[128,1536]{1,0:T(8,128)S(1)}, u32[]{:S(2)}, u32[]{:S(2)}) collective-permute-start(f32[128,1536]{1,0:T(8,128)} %get-tuple-element.114.mine), channel_id=1, source_target_pairs={{0,1},{1,0},{2,3},{3,2},{4,5},{5,4},{6,7},{7,6},{8,9},{9,8},{10,11... | collective-permute-start | bytes 2359304 | tf_op jit(solution)/shard_map/ppermute | solution.py:657
  139.7 15.8 %collective-permute-start.21 = (f32[32,1536]{1,0:T(8,128)}, f32[32,1536]{1,0:T(8,128)S(1)}, u32[]{:S(2)}, u32[]{:S(2)}) collective-permute-start(f32[32,1536]{1,0:T(8,128)} %get-tuple-element.115), channel_id=1, source_target_pairs={{2,0},{4,2},{6,4},{8,6},{10,8},{12,10},{14,12},{16,14},{18,16},{20... | collective-permute-start | bytes 589832 | tf_op jit(solution)/shard_map/ppermute | solution.py:658
  141.0 14.6 %collective-permute-start.22 = (f32[32,1536]{1,0:T(8,128)}, f32[32,1536]{1,0:T(8,128)S(1)}, u32[]{:S(2)}, u32[]{:S(2)}) collective-permute-start(f32[32,1536]{1,0:T(8,128)} %get-tuple-element.115), channel_id=1, source_target_pairs={{2,1},{4,3},{6,5},{8,7},{10,9},{12,11},{14,13},{16,15},{18,17},{20... | collective-permute-start | bytes 589832 | tf_op jit(solution)/shard_map/ppermute | solution.py:659
  141.7 13.9 %all-to-all-start.2 = ((f32[32,1,128]{2,1,0:T(1,128)}), f32[32,1,128]{2,1,0:T(1,128)S(1)}, u32[]{:S(2)}, u32[]{:S(2)}) async-start(f32[32,1,128]{2,1,0:T(1,128)} %get-tuple-element.107), calls=%async_computation.2 | async-start | bytes 32768 | tf_op jit(solution)/shard_map/all_to_all | solution.py:782
  155.6 1.0 copy-start.10
  168.7 13.9 %all-to-all-start.3 = ((f32[16,2,768]{2,1,0:T(2,128)}), f32[16,2,768]{2,1,0:T(2,128)S(1)}, u32[]{:S(2)}, u32[]{:S(2)}) async-start(f32[16,2,768]{2,1,0:T(2,128)} %get-tuple-element.118.stats.local_stats), calls=%async_computation.3 | async-start | bytes 196608 | tf_op jit(solution)/shard_map/all_to_all | solution.py:663
  175.0 19.6 %copy-start.28 = (f32[2,768]{1,0:T(2,128)S(1)}, f32[2,768]{1,0:T(2,128)}, u32[]{:S(2)}) copy-start(f32[2,768]{1,0:T(2,128)} %get-tuple-element.126) | copy-start | bytes 18436
  189.7 13.4 %all-to-all-start.4 = ((bf16[16,48,128]{2,1,0:T(8,128)(2,1)}), bf16[16,48,128]{2,1,0:T(8,128)(2,1)S(1)}, u32[]{:S(2)}, u32[]{:S(2)}) async-start(bf16[16,48,128]{2,1,0:T(8,128)(2,1)} %get-tuple-element.124), calls=%async_computation.4 | async-start | bytes 393216 | tf_op jit(solution)/shard_map/all_to_all | solution.py:663
  (8 other events, 5.6 us)

commit v9 on v8

--- a/solution.py
+++ b/solution.py
@@ -555,9 +555,10 @@
                 - normed * jnp.mean(grad * normed, axis=-1, keepdims=True)
             )
         )
-        out[at] = moved
+        out[0, at] = moved
+        out[1, at] = summed
         total = total + jnp.sum(moved * moved)
-    edge[...] = jnp.where(scal[2] == 0, out[:HALO], out[rows - HALO :])
+    edge[...] = jnp.where(scal[2] == 0, out[:, :HALO], out[:, rows - HALO :])
     for peer in range(squares.shape[0]):
         squares[peer] = total
 
@@ -569,8 +570,8 @@
         direction_kernel,
         in_specs=[pl.BlockSpec(memory_space=pltpu.SMEM)] + [vmem] * 4,
         out_shape=[
-            jax.ShapeDtypeStruct((rows, width), F32),
-            jax.ShapeDtypeStruct((HALO, width), F32),
+            jax.ShapeDtypeStruct((2, rows, width), F32),
+            jax.ShapeDtypeStruct((2, HALO, width), F32),
             jax.ShapeDtypeStruct((peers, 1, 128), F32),
         ],
         compiler_params=params(),
@@ -579,9 +580,9 @@
     )(scal, mine, other, features, noise)
 
 
-def ascend_kernel(scal, squares, features, noise, mine, partner, near, far, own_noise, perturbation, normed_out):
+def ascend_kernel(scal, squares, mine, partner, near, far, noise, perturbation, normed_out):
     start, end, core = scal[0], scal[1], scal[2]
-    rows, width = mine.shape
+    _, rows, width = mine.shape
     total = squares[0]
     for index in range(1, squares.shape[0]):
         total = total + squares[index]
@@ -591,35 +592,35 @@
     block = 32
     is_first = core == 0
 
-    def place(row, moved):
-        at = slice(row, row + block)
-        live = live_rows(start - HALO + row, block, end)
-        summed = features[at].astype(F32) + (noise_scale * noise[at].astype(F32) * live + moved * rate)
-        normed_out[at] = normalize(summed)[0].astype(BF16)
-
-    place(0, jnp.where(is_first, far[...], near[...]))
+    def place_rows(row, one, two, at):
+        moved = jnp.where(is_first, one[0, at], two[0, at])
+        summed = jnp.where(is_first, one[1, at], two[1, at]) + moved * rate
+        normed_out[row : row + block] = normalize(summed)[0].astype(BF16)
+
+    place_rows(0, far, near, slice(0, HALO))
     for row in range(0, rows, block):
         at = slice(row, row + block)
-        place(HALO + row, jnp.where(is_first, mine[at], partner[at]))
-        place(HALO + rows + row, jnp.where(is_first, partner[at], mine[at]))
+        place_rows(HALO + row, mine, partner, at)
+        place_rows(HALO + rows + row, partner, mine, at)
         live = live_rows(start + core * rows + row, block, end)
-        perturbation[at] = noise_scale * own_noise[at].astype(F32) * live + mine[at] * rate
-    place(HALO + 2 * rows, jnp.where(is_first, near[...], far[...]))
-
-
-def ascend(scal, squares, features, noise, mine, partner, near, far, own_noise):
+        perturbation[at] = noise_scale * noise[at].astype(F32) * live + mine[0, at] * rate
+    place_rows(HALO + 2 * rows, near, far, slice(0, HALO))
+
+
+def ascend(scal, squares, mine, partner, near, far, noise):
+    _, rows, width = mine.shape
     vmem = pl.BlockSpec(memory_space=pltpu.VMEM)
     return pl.pallas_call(
         ascend_kernel,
-        in_specs=[pl.BlockSpec(memory_space=pltpu.SMEM)] + [vmem] * 8,
+        in_specs=[pl.BlockSpec(memory_space=pltpu.SMEM)] + [vmem] * 6,
         out_shape=[
-            jax.ShapeDtypeStruct(mine.shape, F32),
-            jax.ShapeDtypeStruct(features.shape, BF16),
-        ],
-        compiler_params=params(),
-        cost_estimate=cost(30 * features.size, 8 * features.size),
+            jax.ShapeDtypeStruct((rows, width), F32),
+            jax.ShapeDtypeStruct((2 * (rows + HALO), width), BF16),
+        ],
+        compiler_params=params(),
+        cost_estimate=cost(60 * rows * width, 30 * rows * width),
         name="ascend",
-    )(scal, squares, features, noise, mine, partner, near, far, own_noise)
+    )(scal, squares, mine, partner, near, far, noise)
 
 
 def on_device(on_dp, features, start_noise, cotangent, in_weight, kernel, bn_gain, bn_shift, ends):
@@ -754,8 +755,6 @@
             pieces += sent[: len(sent_kinds)]
             for k, arrived in zip(onward, sent[len(sent_kinds) :]):
                 along[k] = arrived
-    base, _ = lax.optimization_barrier((jnp.stack([features[0], start_noise[0]]), relayed))
-    base_crossing = across(base, jnp.where(first, base[:, :HALO], base[:, rows - HALO :]))
     late_kinds.append((shifts[final], 3))
     late_pieces.append(lax.ppermute(relayed, "tm", corner))
     weight = place_late(scal, late_kinds, late_pieces, block.shape[0], weight)
@@ -763,16 +762,11 @@
     value, gate, glu, conv, stats = forward(
         scal, normed_b, weight, taps, chip_rows, chips, True
     )
-    stats, base_crossing = lax.optimization_barrier((stats, base_crossing))
     place_of = jnp.arange(half_width, dtype=jnp.int32)
     source = (2 * (place_of // slice_width) + core) * slice_width + place_of % slice_width
     chosen = (jnp.arange(width, dtype=jnp.int32)[:, None] == source[None, :]).astype(BF16)
     cot = jnp.dot(wide_cot, chosen, preferred_element_type=F32).astype(BF16)
     gathered = peers_of(stats)
-    partner, near, far = base_crossing
-    wide_features, wide_noise = (
-        assemble(base[n], partner[n], near[n], far[n]) for n in range(2)
-    )
     scaled, grad, inv, sums = batch(scal, counts, gathered, conv, cot, gain, shift, chips)
     mine, other, grad_conv, totals = backward(
         scal, peers_of(sums), scaled, grad, inv, gain, taps, value, gate, weight
@@ -783,9 +777,7 @@
     partner, near, far = across(moved, edge)
     taps_before = tap_grad(taps_n, grad_conv, glu)
     squares, taps_before = lax.optimization_barrier((squares, taps_before))
-    perturbation, normed_b = ascend(
-        scal, squares, wide_features, wide_noise, moved, partner, near, far, start_noise[0]
-    )
+    perturbation, normed_b = ascend(scal, squares, moved, partner, near, far, start_noise[0])
 
     glu, conv, stats = forward(scal, normed_b, weight, taps, chip_rows, chips, False)
     alone, crossed = raw_taps(taps_n, scal, conv, glu, stats)

time: 207 us -> 205 us (level)
  waiting for transfers between devices: 48.6 us -> 57.2 us
  starting transfers between devices: 48.6 us -> 43.3 us
  local copies, waits for them, and re-layouts: 15.9 us -> 13.3 us
  other arithmetic: 16.2 us -> 13.8 us
    all_to_all x1, waiting for transfers between devices: 0.45 us -> 8.28 us  [on_device(): squares = lax.all_to_all(squares, 'tm', 0, 0, tiled=True)]
    ppermute x3 -> x2, waiting for transfers between devices: 1.98 us -> 5.29 us  [across(): lax.ppermute(edge, 'tm', near_pairs)]
    all_to_all x3, starting transfers between devices: 16.5 us -> 13.4 us  [peers_of(): lax.all_to_all(array, 'tm', 0, 0, axis_index_groups=cores, tiled=True)]
    ppermute x3, waiting for transfers between devices: 2.41 us -> 0.01 us  [on_device(): lax.ppermute(blocks, 'tm', swap_y)]
    unnamed x59 -> x51, local copies, waits for them, and re-layouts: 6.36 us -> 6.45 us
  transfers between devices with their start and end apart: 27 -> 24, of which waited for: 14 -> 13; matrix products, arithmetic and copies ran while one was open for 11% -> 9% of each run, Pallas kernels for 12% -> 7%
where the time goes in v9:
time: 205 us; the launch traced here: 204 us
  Pallas kernels  60.9 us (30%)
  waiting for transfers between devices  57.2 us (28%)
  starting transfers between devices  43.3 us (21%)
  other arithmetic  13.8 us (7%)
  local copies, waits for them, and re-layouts  13.3 us (6%)
  blocking collectives  11.8 us (6%)
    pallas_call x2, Pallas kernels, forward(): pl.pallas_call(functools.partial(forward_kernel, keep), grid=(steps,), in...  15.5 us
    all_to_all x3, waiting for transfers between devices, peers_of(): lax.all_to_all(array, 'tm', 0, 0, axis_index_groups=cores, tiled=True)  15 us
    all_to_all x3, starting transfers between devices, peers_of(): lax.all_to_all(array, 'tm', 0, 0, axis_index_groups=cores, tiled=True)  13.4 us
    ppermute x3, waiting for transfers between devices, on_device(): lax.ppermute(along[k - 1 if from_before else k + 1], 'tm', forth if from_...  12.6 us
    all_to_all x1, blocking collectives, peers_of(): lax.all_to_all(array, 'tm', 0, 0, axis_index_groups=cores, tiled=True)  11.8 us
    all_to_all x1, waiting for transfers between devices, on_device(): squares = lax.all_to_all(squares, 'tm', 0, 0, tiled=True)  8.28 us
    pallas_call x1, Pallas kernels, backward(): pl.pallas_call(backward_kernel, grid=(steps,), in_specs=[pl.BlockSpec(mem...  8.23 us
    ppermute x3, waiting for transfers between devices, on_device(): lax.ppermute(blocks, 'tm', swap_x)  7.15 us
  transfers between devices with their start and end apart: 24, of which 13 were waited for; matrix products, arithmetic and copies ran while one was open for 9% of the time, Pallas kernels for 7%

profile of v9, /device:TPU:0, one launch (start us, length us, event | category | flops | bytes accessed | tf_op | source)
XLA Modules:
  0.0 204.0 jit_solution(14027679688355300838)
XLA Ops:
  4.4 2.6 %collective-permute-start.1 = (bf16[96,1536]{1,0:T(8,128)(2,1)S(1)}, bf16[96,1536]{1,0:T(8,128)(2,1)S(1)}, u32[]{:S(2)}, u32[]{:S(2)}) collective-permute-start(bf16[96,1536]{1,0:T(8,128)(2,1)S(1)} %pad_maximum_fusion.3.refs_0_), channel_id=1, source_target_pairs={{0,2},{1,3},{2,0},{3,1},{4,6},{5,7},{6,4},{7,5},{8,10},{9,11},{10,... | collective-permute-start | bytes 884744 | tf_op jit(solution)/shard_map/ppermute | solution.py:714
  7.7 1.5 collective-permute-start.2
  9.2 1.6 collective-permute-start.3
  10.8 2.2 %collective-permute-start.4 = (bf16[96,1536]{1,0:T(8,128)(2,1)S(1)}, bf16[96,1536]{1,0:T(8,128)(2,1)S(1)}, u32[]{:S(2)}, u32[]{:S(2)}) collective-permute-start(bf16[96,1536]{1,0:T(8,128)(2,1)S(1)} %pad_maximum_fusion.3.refs_0_), channel_id=1, source_target_pairs={{0,24},{1,25},{2,26},{3,27},{4,28},{5,29},{6,30},{7,31},{8,0},{9,1... | collective-permute-start | bytes 884744 | tf_op jit(solution)/shard_map/ppermute | solution.py:722
  13.0 1.7 collective-permute-done.1.refs_1_
  14.7 1.5 fusion.3
  16.9 4.0 %collective-permute-done.3 = bf16[96,1536]{1,0:T(8,128)(2,1)S(1)} collective-permute-done((bf16[96,1536]{1,0:T(8,128)(2,1)S(1)}, bf16[96,1536]{1,0:T(8,128)(2,1)S(1)}, u32[]{:S(2)}, u32[]{:S(2)}) %collective-permute-start.3) | collective-permute-done | bytes 294944 | tf_op jit(solution)/shard_map/ppermute | solution.py:722
  20.9 4.7 %collective-permute-done.4 = bf16[96,1536]{1,0:T(8,128)(2,1)S(1)} collective-permute-done((bf16[96,1536]{1,0:T(8,128)(2,1)S(1)}, bf16[96,1536]{1,0:T(8,128)(2,1)S(1)}, u32[]{:S(2)}, u32[]{:S(2)}) %collective-permute-start.4) | collective-permute-done | bytes 294944 | tf_op jit(solution)/shard_map/ppermute | solution.py:722
  25.6 1.1 collective-permute-start.8
  28.9 1.5 collective-permute-start.5
  31.8 3.9 %collective-permute-done.8.refs_7_ = bf16[96,1536]{1,0:T(8,128)(2,1)S(1)} collective-permute-done((bf16[96,1536]{1,0:T(8,128)(2,1)S(1)}, bf16[96,1536]{1,0:T(8,128)(2,1)S(1)}, u32[]{:S(2)}, u32[]{:S(2)}) %collective-permute-start.8) | collective-permute-done | bytes 294944 | tf_op jit(solution)/shard_map/ppermute | solution.py:722
  35.7 1.8 collective-permute-done.7.refs_6_
  37.5 1.1 select_bitcast_fusion.2
  40.1 1.3 collective-permute-start.10
  41.4 1.3 collective-permute-start.11
  42.7 1.8 concatenate.31
  46.3 5.3 %collective-permute-done.10 = bf16[48,1536]{1,0:T(8,128)(2,1)} collective-permute-done((bf16[48,1536]{1,0:T(8,128)(2,1)}, bf16[48,1536]{1,0:T(8,128)(2,1)}, u32[]{:S(2)}, u32[]{:S(2)}) %collective-permute-start.10) | collective-permute-done | bytes 147488 | tf_op jit(solution)/shard_map/ppermute | solution.py:659
  54.9 2.3 %collective-permute-start.14 = (bf16[192,1536]{1,0:T(8,128)(2,1)S(1)}, bf16[192,1536]{1,0:T(8,128)(2,1)S(1)}, u32[]{:S(2)}, u32[]{:S(2)}) collective-permute-start(bf16[192,1536]{1,0:T(8,128)(2,1)S(1)} %broadcast_select_fusion), channel_id=1, source_target_pairs={{0,2},{1,5},{2,0},{3,7},{4,6},{5,1},{6,4},{7,3},{8,10},{9,13},{10,... | collective-permute-start | bytes 1769480 | tf_op jit(solution)/shard_map/ppermute | solution.py:717
  59.1 1.5 collective-permute-start.13
  60.6 4.3 %place_weights.1.refs_4_ = bf16[1536,1536]{1,0:T(8,128)(2,1)} custom-call(s32[6]{0:T(128)} %stack.35.scal, bf16[96,1536]{1,0:T(8,128)(2,1)} %copy-done.10, bf16[96,1536]{1,0:T(8,128)(2,1)} %copy-done.6, bf16[96,1536]{1,0:T(8,128)(2,1)} %copy-done.7, bf16[192,1536]{1,0:T(8,128)(2,1)} %constant_dynamic-update-slice_fusion.refs_3_, ...), custom_call_target="tpu_custom_call" | custom-call | bytes 9437184 | tf_op jit(solution)/shard_map/place_weights/pallas_call | solution.py:124
  65.9 5.5 %collective-permute-done.12.refs_0_ = bf16[96,1536]{1,0:T(8,128)(2,1)S(1)} collective-permute-done((bf16[96,1536]{1,0:T(8,128)(2,1)S(1)}, bf16[96,1536]{1,0:T(8,128)(2,1)S(1)}, u32[]{:S(2)}, u32[]{:S(2)}) %collective-permute-start.12) | collective-permute-done | bytes 294944 | tf_op jit(solution)/shard_map/ppermute | solution.py:714
  71.5 2.1 %collective-permute-start.15 = (bf16[96,1536]{1,0:T(8,128)(2,1)S(1)}, bf16[96,1536]{1,0:T(8,128)(2,1)S(1)}, u32[]{:S(2)}, u32[]{:S(2)}) collective-permute-start(bf16[96,1536]{1,0:T(8,128)(2,1)S(1)} %broadcast_select_fusion.1), channel_id=1, source_target_pairs={{0,2},{1,5},{2,0},{3,7},{4,6},{5,1},{6,4},{7,3},{8,10},{9,13},{10,... | collective-permute-start | bytes 884744 | tf_op jit(solution)/shard_map/ppermute | solution.py:759
  73.6 4.7 %collective-permute-done.15.refs_3_ = bf16[96,1536]{1,0:T(8,128)(2,1)S(1)} collective-permute-done((bf16[96,1536]{1,0:T(8,128)(2,1)S(1)}, bf16[96,1536]{1,0:T(8,128)(2,1)S(1)}, u32[]{:S(2)}, u32[]{:S(2)}) %collective-permute-start.15) | collective-permute-done | bytes 294944 | tf_op jit(solution)/shard_map/ppermute | solution.py:759
  79.0 2.5 %place_last_weights.1.value_w.gate_w = bf16[1536,1536]{1,0:T(8,128)(2,1)} custom-call(s32[6]{0:T(128)} %stack.35.scal, bf16[96,1536]{1,0:T(8,128)(2,1)} %copy-done.8, bf16[96,1536]{1,0:T(8,128)(2,1)} %copy-done.9, bf16[192,1536]{1,0:T(8,128)(2,1)} %copy-done.13, bf16[96,1536]{1,0:T(8,128)(2,1)} %copy-done.20, ...), custom_call_target="tpu_custom_call", output_to_operand_aliasing={{}: (5, {})} | custom-call | bytes 2949120 | tf_op jit(solution)/shard_map/place_last_weights/pallas_call | solution.py:139
  81.5 7.8 %project_glu_conv.2 = (f32[256,768]{1,0:T(8,128)}, f32[256,768]{1,0:T(8,128)}, bf16[320,768]{1,0:T(8,128)(2,1)}, f32[288,768]{1,0:T(8,128)}, f32[16,2,768]{2,1,0:T(2,128)}) custom-call(s32[6]{0:T(128)} %stack.35.scal, bf16[320,1536]{1,0:T(8,128)(2,1)} %pad_maximum_fusion.nb, bf16[1536,1536]{1,0:T(8,128)(2,1)} %place_last_weights.1.value_w.gate_w, ...), custom_call_target="tpu_custom_call" | custom-call | flops 1509949440 | bytes 7176192 | tf_op jit(solution)/shard_map/project_glu_conv/pallas_call | solution.py:183
  89.3 4.9 %all-to-all-start = ((f32[16,2,768]{2,1,0:T(2,128)}), f32[16,2,768]{2,1,0:T(2,128)S(1)}, u32[]{:S(2)}, u32[]{:S(2)}) async-start(f32[16,2,768]{2,1,0:T(2,128)} %get-tuple-element.87), calls=%async_computation | async-start | bytes 196608 | tf_op jit(solution)/shard_map/all_to_all | solution.py:664
  94.2 1.9 fusion.2.cot
  96.1 5.8 %all-to-all-done.stats = f32[16,2,768]{2,1,0:T(2,128)S(1)} async-done(((f32[16,2,768]{2,1,0:T(2,128)}), f32[16,2,768]{2,1,0:T(2,128)S(1)}, u32[]{:S(2)}, u32[]{:S(2)}) %all-to-all-start) | async-done | bytes 98336 | tf_op jit(solution)/shard_map/all_to_all | solution.py:664
  102.5 3.9 %batch_norm_swish.1 = (f32[288,768]{1,0:T(8,128)}, f32[288,768]{1,0:T(8,128)}, f32[1,768]{1,0:T(1,128)}, f32[16,2,768]{2,1,0:T(2,128)}) custom-call(s32[6]{0:T(128)} %stack.35.scal, f32[2,16]{1,0:T(2,128)} %pad_maximum_fusion.5.counts, f32[16,2,768]{2,1,0:T(2,128)} %copy-done.17, f32[288,768]{1,0:T(8,128)} %get-tuple-element.88.conv, ...), custom_call_target="tpu_custom_call" | custom-call | flops 8847360 | bytes 3538944 | tf_op jit(solution)/shard_map/batch_norm_swish/pallas_call | solution.py:263
  106.4 11.8 %all_to_all.25.sums = f32[16,2,768]{2,1,0:T(2,128)} all-to-all(f32[16,2,768]{2,1,0:T(2,128)} %get-tuple-element.92), channel_id=1, replica_groups={{0,2,4,6,8,10,12,14,16,18,20,22,24,26,28,30},{1,3,5,7,9,11,13,15,17,19,..., dimensions={0} | all-to-all | bytes 196608 | tf_op jit(solution)/shard_map/all_to_all | solution.py:664
  118.2 8.2 %grad_conv_project_back.1 = (f32[128,1536]{1,0:T(8,128)}, f32[128,1536]{1,0:T(8,128)}, bf16[256,768]{1,0:T(8,128)(2,1)}, f32[2,768]{1,0:T(2,128)}) custom-call(s32[6]{0:T(128)} %stack.35.scal, f32[16,2,768]{2,1,0:T(2,128)} %all_to_all.25.sums, f32[288,768]{1,0:T(8,128)} %get-tuple-element.93.scaled, f32[288,768]{1,0:T(8,128)} %get-tuple-element.94.grad, ...), custom_call_target="tpu_custom_call" | custom-call | flops 1207959552 | bytes 9142272 | tf_op jit(solution)/shard_map/grad_conv_project_back/pallas_call | solution.py:338
  126.6 2.5 %collective-permute-done.16.other = f32[128,1536]{1,0:T(8,128)S(1)} collective-permute-done((f32[128,1536]{1,0:T(8,128)}, f32[128,1536]{1,0:T(8,128)S(1)}, u32[]{:S(2)}, u32[]{:S(2)}) %collective-permute-start.16) | collective-permute-done | bytes 786464 | tf_op jit(solution)/shard_map/ppermute | solution.py:774
  129.9 3.5 %direction.1 = (f32[2,128,1536]{2,1,0:T(8,128)}, f32[2,32,1536]{2,1,0:T(8,128)}, f32[32,1,128]{2,1,0:T(1,128)}) custom-call(s32[6]{0:T(128)} %stack.35.scal, f32[128,1536]{1,0:T(8,128)} %get-tuple-element.98.mine, f32[128,1536]{1,0:T(8,128)} %copy-done.11, bf16[128,1536]{1,0:T(8,128)(2,1)} %bitcast.48, bf16[128,1536]{1,0:T(8,128)(2,1)} %bitcast.43), custom_call_target="tpu_custom_call" | custom-call | flops 5898240 | bytes 3145728 | tf_op jit(solution)/shard_map/direction/pallas_call | solution.py:569
  133.6 1.3 collective-permute-start.18
  135.5 6.9 %all-to-all-start.2 = ((f32[32,1,128]{2,1,0:T(1,128)}), f32[32,1,128]{2,1,0:T(1,128)S(1)}, u32[]{:S(2)}, u32[]{:S(2)}) async-start(f32[32,1,128]{2,1,0:T(1,128)} %get-tuple-element.100), calls=%async_computation.2 | async-start | bytes 32768 | tf_op jit(solution)/shard_map/all_to_all | solution.py:776
  142.5 4.9 %tap_grad.1.taps_before = f32[31,768]{1,0:T(8,128)} custom-call(bf16[256,768]{1,0:T(8,128)(2,1)} %get-tuple-element.101.grad_conv, bf16[320,768]{1,0:T(8,128)(2,1)} %get-tuple-element.102.glu), custom_call_target="tpu_custom_call" | custom-call | flops 12189696 | bytes 983040 | tf_op jit(solution)/shard_map/tap_grad/pallas_call | solution.py:386
  147.4 8.3 %all-to-all-done.2.squares = f32[32,1,128]{2,1,0:T(1,128)S(1)} async-done(((f32[32,1,128]{2,1,0:T(1,128)}), f32[32,1,128]{2,1,0:T(1,128)S(1)}, u32[]{:S(2)}, u32[]{:S(2)}) %all-to-all-start.2) | async-done | bytes 16416 | tf_op jit(solution)/shard_map/all_to_all | solution.py:776
  156.6 1.2 copy-done.4
  157.8 4.4 %ascend.1 = (f32[128,1536]{1,0:T(8,128)}, bf16[320,1536]{1,0:T(8,128)(2,1)}) custom-call(s32[6]{0:T(128)} %stack.35.scal, f32[32,1,128]{2,1,0:T(1,128)} %copy-done.21, f32[2,128,1536]{2,1,0:T(8,128)} %get-tuple-element.104.mine, f32[2,128,1536]{2,1,0:T(8,128)} %copy-done.4, f32[2,32,1536]{2,1,0:T(8,128)} %copy-done.15, f32[2,32,1536]{2,1,0:T(8,128)} %copy-done.16, ...), custom_call_target="tpu_custom_call" | custom-call | flops 11796480 | bytes 5898240 | tf_op jit(solution)/shard_map/ascend/pallas_call | solution.py:613
  162.3 7.8 %project_glu_conv.3 = (bf16[320,768]{1,0:T(8,128)(2,1)}, f32[288,768]{1,0:T(8,128)}, f32[16,2,768]{2,1,0:T(2,128)}) custom-call(s32[6]{0:T(128)} %stack.35.scal, bf16[320,1536]{1,0:T(8,128)(2,1)} %get-tuple-element.107.nb, bf16[1536,1536]{1,0:T(8,128)(2,1)} %place_last_weights.1.value_w.gate_w, bf16[1536,1536]{1,0:T(8,128)(2,1)} %place_last_weights.1.value_w.gate_w, ...), custom_call_target="tpu_custom_call" | custom-call | flops 1509949440 | bytes 7176192 | tf_op jit(solution)/shard_map/project_glu_conv/pallas_call | solution.py:183
  170.0 3.5 %all-to-all-start.3 = ((f32[16,2,768]{2,1,0:T(2,128)}), f32[16,2,768]{2,1,0:T(2,128)S(1)}, u32[]{:S(2)}, u32[]{:S(2)}) async-start(f32[16,2,768]{2,1,0:T(2,128)} %get-tuple-element.108.stats.local_stats), calls=%async_computation.3 | async-start | bytes 196608 | tf_op jit(solution)/shard_map/all_to_all | solution.py:664
  173.5 5.6 %raw_taps.1 = (f32[31,768]{1,0:T(8,128)}, f32[31,768]{1,0:T(8,128)}) custom-call(s32[6]{0:T(128)} %stack.35.scal, f32[288,768]{1,0:T(8,128)} %get-tuple-element.109.conv, bf16[320,768]{1,0:T(8,128)(2,1)} %get-tuple-element.110.glu, f32[16,2,768]{2,1,0:T(2,128)} %get-tuple-element.108.stats.local_stats), custom_call_target="tpu_custom_call" | custom-call | flops 13713408 | bytes 1966080 | tf_op jit(solution)/shard_map/raw_taps/pallas_call | solution.py:419
  179.2 2.0 all-to-all-done.3.stats
  181.8 6.3 %batch_norm_swish_taps.1 = (bf16[16,48,128]{2,1,0:T(8,128)(2,1)}, f32[1,768]{1,0:T(1,128)}) custom-call(s32[6]{0:T(128)} %stack.35.scal, f32[2,16]{1,0:T(2,128)} %pad_maximum_fusion.5.counts, f32[16,2,768]{2,1,0:T(2,128)} %copy-done.14, f32[288,768]{1,0:T(8,128)} %get-tuple-element.109.conv, bf16[288,768]{1,0:T(8,128)(2,1)} %fusion.2.cot, ...), custom_call_target="tpu_custom_call" | custom-call | flops 22118400 | bytes 2211840 | tf_op jit(solution)/shard_map/batch_norm_swish_taps/pallas_call | solution.py:479
  188.1 4.9 %all-to-all-start.4 = ((bf16[16,48,128]{2,1,0:T(8,128)(2,1)}), bf16[16,48,128]{2,1,0:T(8,128)(2,1)S(1)}, u32[]{:S(2)}, u32[]{:S(2)}) async-start(bf16[16,48,128]{2,1,0:T(8,128)(2,1)} %get-tuple-element.114), calls=%async_computation.4 | async-start | bytes 393216 | tf_op jit(solution)/shard_map/all_to_all | solution.py:664
  193.1 1.4 fusion.17.known
  194.4 7.2 %all-to-all-done.4.received = bf16[16,48,128]{2,1,0:T(8,128)(2,1)S(1)} async-done(((bf16[16,48,128]{2,1,0:T(8,128)(2,1)}), bf16[16,48,128]{2,1,0:T(8,128)(2,1)S(1)}, u32[]{:S(2)}, u32[]{:S(2)}) %all-to-all-start.4) | async-done | bytes 196640 | tf_op jit(solution)/shard_map/all_to_all | solution.py:664
  202.3 1.7 finish.1
  (107 shorter events, 22.9 us)
Async XLA Ops:
  0.6 15.6 %copy-start = (bf16[1,128,1536]{2,1,0:T(8,128)(2,1)S(1)}, bf16[1,128,1536]{2,1,0:T(8,128)(2,1)}, u32[]{:S(2)}) copy-start(bf16[1,128,1536]{2,1,0:T(8,128)(2,1)} %param.9) | copy-start | bytes 1179652
  0.6 15.6 %copy-start.1 = (bf16[1,128,1536]{2,1,0:T(8,128)(2,1)S(1)}, bf16[1,128,1536]{2,1,0:T(8,128)(2,1)}, u32[]{:S(2)}) copy-start(bf16[1,128,1536]{2,1,0:T(8,128)(2,1)} %param.8) | copy-start | bytes 1179652
  1.7 1.8 collective-permute-start
  4.4 23.1 %copy-start.10 = (bf16[96,1536]{1,0:T(8,128)(2,1)}, bf16[96,1536]{1,0:T(8,128)(2,1)S(1)}, u32[]{:S(2)}) copy-start(bf16[96,1536]{1,0:T(8,128)(2,1)S(1)} %pad_maximum_fusion.3.refs_0_) | copy-start | bytes 884740
  4.4 10.2 %collective-permute-start.1 = (bf16[96,1536]{1,0:T(8,128)(2,1)S(1)}, bf16[96,1536]{1,0:T(8,128)(2,1)S(1)}, u32[]{:S(2)}, u32[]{:S(2)}) collective-permute-start(bf16[96,1536]{1,0:T(8,128)(2,1)S(1)} %pad_maximum_fusion.3.refs_0_), channel_id=1, source_target_pairs={{0,2},{1,3},{2,0},{3,1},{4,6},{5,7},{6,4},{7,5},{8,10},{9,11},{10,... | collective-permute-start | bytes 884744 | tf_op jit(solution)/shard_map/ppermute | solution.py:714
  7.7 9.2 %collective-permute-start.2 = (bf16[96,1536]{1,0:T(8,128)(2,1)S(1)}, bf16[96,1536]{1,0:T(8,128)(2,1)S(1)}, u32[]{:S(2)}, u32[]{:S(2)}) collective-permute-start(bf16[96,1536]{1,0:T(8,128)(2,1)S(1)} %pad_maximum_fusion.3.refs_0_), channel_id=1, source_target_pairs={{0,4},{1,5},{2,6},{3,7},{4,0},{5,1},{6,2},{7,3},{8,12},{9,13},{10,... | collective-permute-start | bytes 884744 | tf_op jit(solution)/shard_map/ppermute | solution.py:714
  9.2 11.7 %collective-permute-start.3 = (bf16[96,1536]{1,0:T(8,128)(2,1)S(1)}, bf16[96,1536]{1,0:T(8,128)(2,1)S(1)}, u32[]{:S(2)}, u32[]{:S(2)}) collective-permute-start(bf16[96,1536]{1,0:T(8,128)(2,1)S(1)} %pad_maximum_fusion.3.refs_0_), channel_id=1, source_target_pairs={{0,8},{1,9},{2,10},{3,11},{4,12},{5,13},{6,14},{7,15},{8,16},{9,17... | collective-permute-start | bytes 884744 | tf_op jit(solution)/shard_map/ppermute | solution.py:722
  10.8 14.8 %collective-permute-start.4 = (bf16[96,1536]{1,0:T(8,128)(2,1)S(1)}, bf16[96,1536]{1,0:T(8,128)(2,1)S(1)}, u32[]{:S(2)}, u32[]{:S(2)}) collective-permute-start(bf16[96,1536]{1,0:T(8,128)(2,1)S(1)} %pad_maximum_fusion.3.refs_0_), channel_id=1, source_target_pairs={{0,24},{1,25},{2,26},{3,27},{4,28},{5,29},{6,30},{7,31},{8,0},{9,1... | collective-permute-start | bytes 884744 | tf_op jit(solution)/shard_map/ppermute | solution.py:722
  14.7 12.8 %copy-start.6 = (bf16[96,1536]{1,0:T(8,128)(2,1)}, bf16[96,1536]{1,0:T(8,128)(2,1)S(1)}, u32[]{:S(2)}) copy-start(bf16[96,1536]{1,0:T(8,128)(2,1)S(1)} %collective-permute-done.1.refs_1_) | copy-start | bytes 884740
  16.2 14.7 %copy-start.5 = (bf16[1,128,1536]{2,1,0:T(8,128)(2,1)S(1)}, bf16[1,128,1536]{2,1,0:T(8,128)(2,1)}, u32[]{:S(2)}) copy-start(bf16[1,128,1536]{2,1,0:T(8,128)(2,1)} %param.10) | copy-start | bytes 1179652
  16.9 12.0 %copy-start.7 = (bf16[96,1536]{1,0:T(8,128)(2,1)}, bf16[96,1536]{1,0:T(8,128)(2,1)S(1)}, u32[]{:S(2)}) copy-start(bf16[96,1536]{1,0:T(8,128)(2,1)S(1)} %collective-permute-done.2.refs_2_) | copy-start | bytes 884740
  25.6 10.1 %collective-permute-start.8 = (bf16[96,1536]{1,0:T(8,128)(2,1)S(1)}, bf16[96,1536]{1,0:T(8,128)(2,1)S(1)}, u32[]{:S(2)}, u32[]{:S(2)}) collective-permute-start(bf16[96,1536]{1,0:T(8,128)(2,1)S(1)} %collective-permute-done.3), channel_id=1, source_target_pairs={{0,8},{1,9},{2,10},{3,11},{4,12},{5,13},{6,14},{7,15},{8,16},{9,17... | collective-permute-start | bytes 884744 | tf_op jit(solution)/shard_map/ppermute | solution.py:722
  27.5 9.9 %collective-permute-start.7 = (bf16[96,1536]{1,0:T(8,128)(2,1)S(1)}, bf16[96,1536]{1,0:T(8,128)(2,1)S(1)}, u32[]{:S(2)}, u32[]{:S(2)}) collective-permute-start(bf16[96,1536]{1,0:T(8,128)(2,1)S(1)} %broadcast_select_fusion.2), channel_id=1, source_target_pairs={{0,2},{1,5},{2,0},{3,7},{4,6},{5,1},{6,4},{7,3},{8,10},{9,13},{10,... | collective-permute-start | bytes 884744 | tf_op jit(solution)/shard_map/ppermute | solution.py:717
  28.9 22.8 %collective-permute-start.5 = (bf16[192,1536]{1,0:T(8,128)(2,1)}, bf16[192,1536]{1,0:T(8,128)(2,1)S(1)}, u32[]{:S(2)}, u32[]{:S(2)}) collective-permute-start(bf16[192,1536]{1,0:T(8,128)(2,1)} %constant_dynamic-update-slice_fusion.refs_3_), channel_id=1, source_target_pairs={{0,2},{1,3},{2,0},{3,1},{4,6},{5,7},{6,4},{7,5},{8,10},{9,11},{10,... | collective-permute-start | bytes 1769480 | tf_op jit(solution)/shard_map/ppermute | solution.py:714
  30.4 21.3 %collective-permute-start.6 = (bf16[192,1536]{1,0:T(8,128)(2,1)}, bf16[192,1536]{1,0:T(8,128)(2,1)S(1)}, u32[]{:S(2)}, u32[]{:S(2)}) collective-permute-start(bf16[192,1536]{1,0:T(8,128)(2,1)} %constant_dynamic-update-slice_fusion.refs_3_), channel_id=1, source_target_pairs={{0,4},{1,5},{2,6},{3,7},{4,0},{5,1},{6,2},{7,3},{8,12},{9,13},{10,... | collective-permute-start | bytes 1769480 | tf_op jit(solution)/shard_map/ppermute | solution.py:714
  30.9 13.7 %copy-start.22 = (f32[1536]{0:T(1024)S(1)}, f32[1536]{0:T(1024)}, u32[]{:S(2)}) copy-start(f32[1536]{0:T(1024)} %param.13) | copy-start | bytes 18436
  30.9 13.8 %copy-start.23 = (f32[1536]{0:T(1024)S(1)}, f32[1536]{0:T(1024)}, u32[]{:S(2)}) copy-start(f32[1536]{0:T(1024)} %param.14) | copy-start | bytes 18436
  35.7 23.4 %copy-start.18 = (bf16[96,1536]{1,0:T(8,128)(2,1)}, bf16[96,1536]{1,0:T(8,128)(2,1)S(1)}, u32[]{:S(2)}) copy-start(bf16[96,1536]{1,0:T(8,128)(2,1)S(1)} %collective-permute-done.8.refs_7_) | copy-start | bytes 884740
  37.5 5.3 %copy-start.19 = (bf16[96,1536]{1,0:T(8,128)(2,1)}, bf16[96,1536]{1,0:T(8,128)(2,1)S(1)}, u32[]{:S(2)}) copy-start(bf16[96,1536]{1,0:T(8,128)(2,1)S(1)} %collective-permute-done.7.refs_6_) | copy-start | bytes 884740
  38.5 13.1 %collective-permute-start.9 = (bf16[2,128,1536]{2,1,0:T(8,128)(2,1)}, bf16[2,128,1536]{2,1,0:T(8,128)(2,1)}, u32[]{:S(2)}, u32[]{:S(2)}) collective-permute-start(bf16[2,128,1536]{2,1,0:T(8,128)(2,1)} %pad_maximum_fusion.2), channel_id=1, source_target_pairs={{0,1},{1,0},{2,3},{3,2},{4,5},{5,4},{6,7},{7,6},{8,9},{9,8},{10,11... | collective-permute-start | bytes 2359304 | tf_op jit(solution)/shard_map/ppermute | solution.py:658
  40.1 11.5 %collective-permute-start.10 = (bf16[48,1536]{1,0:T(8,128)(2,1)}, bf16[48,1536]{1,0:T(8,128)(2,1)}, u32[]{:S(2)}, u32[]{:S(2)}) collective-permute-start(bf16[48,1536]{1,0:T(8,128)(2,1)} %pad_maximum_fusion.4), channel_id=1, source_target_pairs={{2,0},{4,2},{6,4},{8,6},{10,8},{12,10},{14,12},{16,14},{18,16},{20... | collective-permute-start | bytes 442376 | tf_op jit(solution)/shard_map/ppermute | solution.py:659
  41.4 10.2 %collective-permute-start.11 = (bf16[48,1536]{1,0:T(8,128)(2,1)}, bf16[48,1536]{1,0:T(8,128)(2,1)}, u32[]{:S(2)}, u32[]{:S(2)}) collective-permute-start(bf16[48,1536]{1,0:T(8,128)(2,1)} %pad_maximum_fusion.4), channel_id=1, source_target_pairs={{2,1},{4,3},{6,5},{8,7},{10,9},{12,11},{14,13},{16,15},{18,17},{20... | collective-permute-start | bytes 442376 | tf_op jit(solution)/shard_map/ppermute | solution.py:660
  51.6 3.2 %copy-start.2 = (bf16[192,1536]{1,0:T(8,128)(2,1)}, bf16[192,1536]{1,0:T(8,128)(2,1)S(1)}, u32[]{:S(2)}) copy-start(bf16[192,1536]{1,0:T(8,128)(2,1)S(1)} %collective-permute-done.5.refs_4_) | copy-start | bytes 1769476
  51.7 3.2 %copy-start.3 = (bf16[192,1536]{1,0:T(8,128)(2,1)}, bf16[192,1536]{1,0:T(8,128)(2,1)S(1)}, u32[]{:S(2)}) copy-start(bf16[192,1536]{1,0:T(8,128)(2,1)S(1)} %collective-permute-done.6.refs_5_) | copy-start | bytes 1769476
  54.9 16.5 %collective-permute-start.14 = (bf16[192,1536]{1,0:T(8,128)(2,1)S(1)}, bf16[192,1536]{1,0:T(8,128)(2,1)S(1)}, u32[]{:S(2)}, u32[]{:S(2)}) collective-permute-start(bf16[192,1536]{1,0:T(8,128)(2,1)S(1)} %broadcast_select_fusion), channel_id=1, source_target_pairs={{0,2},{1,5},{2,0},{3,7},{4,6},{5,1},{6,4},{7,3},{8,10},{9,13},{10,... | collective-permute-start | bytes 1769480 | tf_op jit(solution)/shard_map/ppermute | solution.py:717
  59.0 12.4 %collective-permute-start.12 = (bf16[96,1536]{1,0:T(8,128)(2,1)S(1)}, bf16[96,1536]{1,0:T(8,128)(2,1)S(1)}, u32[]{:S(2)}, u32[]{:S(2)}) collective-permute-start(bf16[96,1536]{1,0:T(8,128)(2,1)S(1)} %collective-permute-done.8.refs_7_), channel_id=1, source_target_pairs={{0,2},{1,3},{2,0},{3,1},{4,6},{5,7},{6,4},{7,5},{8,10},{9,11},{10,... | collective-permute-start | bytes 884744 | tf_op jit(solution)/shard_map/ppermute | solution.py:714
  59.1 12.3 %collective-permute-start.13 = (bf16[96,1536]{1,0:T(8,128)(2,1)S(1)}, bf16[96,1536]{1,0:T(8,128)(2,1)S(1)}, u32[]{:S(2)}, u32[]{:S(2)}) collective-permute-start(bf16[96,1536]{1,0:T(8,128)(2,1)S(1)} %collective-permute-done.8.refs_7_), channel_id=1, source_target_pairs={{0,4},{1,5},{2,6},{3,7},{4,0},{5,1},{6,2},{7,3},{8,12},{9,13},{10,... | collective-permute-start | bytes 884744 | tf_op jit(solution)/shard_map/ppermute | solution.py:714
  71.4 6.9 %copy-start.8 = (bf16[96,1536]{1,0:T(8,128)(2,1)}, bf16[96,1536]{1,0:T(8,128)(2,1)S(1)}, u32[]{:S(2)}) copy-start(bf16[96,1536]{1,0:T(8,128)(2,1)S(1)} %collective-permute-done.12.refs_0_) | copy-start | bytes 884740
  71.4 6.9 %copy-start.9 = (bf16[96,1536]{1,0:T(8,128)(2,1)}, bf16[96,1536]{1,0:T(8,128)(2,1)S(1)}, u32[]{:S(2)}) copy-start(bf16[96,1536]{1,0:T(8,128)(2,1)S(1)} %collective-permute-done.13.refs_1_) | copy-start | bytes 884740
  71.4 6.8 %copy-start.13 = (bf16[192,1536]{1,0:T(8,128)(2,1)}, bf16[192,1536]{1,0:T(8,128)(2,1)S(1)}, u32[]{:S(2)}) copy-start(bf16[192,1536]{1,0:T(8,128)(2,1)S(1)} %collective-permute-done.14.refs_2_) | copy-start | bytes 1769476
  71.5 6.8 %collective-permute-start.15 = (bf16[96,1536]{1,0:T(8,128)(2,1)S(1)}, bf16[96,1536]{1,0:T(8,128)(2,1)S(1)}, u32[]{:S(2)}, u32[]{:S(2)}) collective-permute-start(bf16[96,1536]{1,0:T(8,128)(2,1)S(1)} %broadcast_select_fusion.1), channel_id=1, source_target_pairs={{0,2},{1,5},{2,0},{3,7},{4,6},{5,1},{6,4},{7,3},{8,10},{9,13},{10,... | collective-permute-start | bytes 884744 | tf_op jit(solution)/shard_map/ppermute | solution.py:759
  78.3 0.7 copy-start.20
  89.3 12.6 %all-to-all-start = ((f32[16,2,768]{2,1,0:T(2,128)}), f32[16,2,768]{2,1,0:T(2,128)S(1)}, u32[]{:S(2)}, u32[]{:S(2)}) async-start(f32[16,2,768]{2,1,0:T(2,128)} %get-tuple-element.87), calls=%async_computation | async-start | bytes 196608 | tf_op jit(solution)/shard_map/all_to_all | solution.py:664
  101.9 0.6 copy-start.17
  126.5 2.6 %collective-permute-start.16 = (f32[128,1536]{1,0:T(8,128)}, f32[128,1536]{1,0:T(8,128)S(1)}, u32[]{:S(2)}, u32[]{:S(2)}) collective-permute-start(f32[128,1536]{1,0:T(8,128)} %get-tuple-element.99), channel_id=1, source_target_pairs={{0,1},{1,0},{2,3},{3,2},{4,5},{5,4},{6,7},{7,6},{8,9},{9,8},{10,11... | collective-permute-start | bytes 2359304 | tf_op jit(solution)/shard_map/ppermute | solution.py:774
  129.0 0.9 copy-start.11
  133.4 22.3 %collective-permute-start.17 = (f32[2,128,1536]{2,1,0:T(8,128)}, f32[2,128,1536]{2,1,0:T(8,128)S(1)}, u32[]{:S(2)}, u32[]{:S(2)}) collective-permute-start(f32[2,128,1536]{2,1,0:T(8,128)} %get-tuple-element.104.mine), channel_id=1, source_target_pairs={{0,1},{1,0},{2,3},{3,2},{4,5},{5,4},{6,7},{7,6},{8,9},{9,8},{10,11... | collective-permute-start | bytes 4718600 | tf_op jit(solution)/shard_map/ppermute | solution.py:658
  133.6 22.2 %collective-permute-start.18 = (f32[2,32,1536]{2,1,0:T(8,128)}, f32[2,32,1536]{2,1,0:T(8,128)S(1)}, u32[]{:S(2)}, u32[]{:S(2)}) collective-permute-start(f32[2,32,1536]{2,1,0:T(8,128)} %get-tuple-element.105), channel_id=1, source_target_pairs={{2,0},{4,2},{6,4},{8,6},{10,8},{12,10},{14,12},{16,14},{18,16},{20... | collective-permute-start | bytes 1179656 | tf_op jit(solution)/shard_map/ppermute | solution.py:659
  134.8 20.9 %collective-permute-start.19 = (f32[2,32,1536]{2,1,0:T(8,128)}, f32[2,32,1536]{2,1,0:T(8,128)S(1)}, u32[]{:S(2)}, u32[]{:S(2)}) collective-permute-start(f32[2,32,1536]{2,1,0:T(8,128)} %get-tuple-element.105), channel_id=1, source_target_pairs={{2,1},{4,3},{6,5},{8,7},{10,9},{12,11},{14,13},{16,15},{18,17},{20... | collective-permute-start | bytes 1179656 | tf_op jit(solution)/shard_map/ppermute | solution.py:660
  135.5 20.2 %all-to-all-start.2 = ((f32[32,1,128]{2,1,0:T(1,128)}), f32[32,1,128]{2,1,0:T(1,128)S(1)}, u32[]{:S(2)}, u32[]{:S(2)}) async-start(f32[32,1,128]{2,1,0:T(1,128)} %get-tuple-element.100), calls=%async_computation.2 | async-start | bytes 32768 | tf_op jit(solution)/shard_map/all_to_all | solution.py:776
  155.7 0.8 copy-start.15
  155.7 0.9 copy-start.16
  156.6 1.2 copy-start.4
  170.0 11.1 %all-to-all-start.3 = ((f32[16,2,768]{2,1,0:T(2,128)}), f32[16,2,768]{2,1,0:T(2,128)S(1)}, u32[]{:S(2)}, u32[]{:S(2)}) async-start(f32[16,2,768]{2,1,0:T(2,128)} %get-tuple-element.108.stats.local_stats), calls=%async_computation.3 | async-start | bytes 196608 | tf_op jit(solution)/shard_map/all_to_all | solution.py:664
  173.5 19.5 %copy-start.24 = (f32[2,768]{1,0:T(2,128)S(1)}, f32[2,768]{1,0:T(2,128)}, u32[]{:S(2)}) copy-start(f32[2,768]{1,0:T(2,128)} %get-tuple-element.116) | copy-start | bytes 18436
  181.2 0.6 copy-start.14
  188.1 13.5 %all-to-all-start.4 = ((bf16[16,48,128]{2,1,0:T(8,128)(2,1)}), bf16[16,48,128]{2,1,0:T(8,128)(2,1)S(1)}, u32[]{:S(2)}, u32[]{:S(2)}) async-start(bf16[16,48,128]{2,1,0:T(8,128)(2,1)} %get-tuple-element.114), calls=%async_computation.4 | async-start | bytes 393216 | tf_op jit(solution)/shard_map/all_to_all | solution.py:664
  201.6 0.7 copy-start.12
  (1 other events, 0.6 us)

commit v10 on v4

--- a/solution.py
+++ b/solution.py
@@ -72,7 +72,7 @@
 def correlate(taps_n, left, shifted, first):
     rows = left.shape[0]
     lanes = slice(0, 128)
-    most = 16
+    most = 32
     totals = [None] * taps_n
     for tile in range(0, rows // 8, most):
         part = left[8 * tile : 8 * (tile + most)].reshape(most, 8, 128)

time: 205 us -> 206 us (level)
  no operation moved by 1% of the time
where the time goes in v10:
time: 206 us; the launch traced here: 205 us
  Pallas kernels  60 us (29%)
  starting transfers between devices  52.7 us (26%)
  waiting for transfers between devices  52.6 us (26%)
  local copies, waits for them, and re-layouts  13.7 us (7%)
  blocking collectives  11.8 us (6%)
  other arithmetic  9.4 us (5%)
  matrix products  2.98 us (1%)
    all_to_all x3, starting transfers between devices, peers_of(): lax.all_to_all(array, 'tm', 0, 0, axis_index_groups=cores, tiled=True)  19.5 us
    pallas_call x2, Pallas kernels, forward(): pl.pallas_call(functools.partial(forward_kernel, keep), grid=(steps,), in...  15.6 us
    ppermute x3, waiting for transfers between devices, on_device(): lax.ppermute(block, 'tm', [(i, (i + 8 * k) % shards) for i in range(shard...  15.1 us
    ppermute x3, waiting for transfers between devices, on_device(): from_x = lax.ppermute(blocks, 'tm', swap_x)  14.9 us
    all_to_all x3, waiting for transfers between devices, peers_of(): lax.all_to_all(array, 'tm', 0, 0, axis_index_groups=cores, tiled=True)  13.6 us
    all_to_all x1, blocking collectives, peers_of(): lax.all_to_all(array, 'tm', 0, 0, axis_index_groups=cores, tiled=True)  11.8 us
    pallas_call x1, Pallas kernels, backward(): pl.pallas_call(backward_kernel, grid=(steps,), in_specs=[pl.BlockSpec(mem...  8.23 us
    pallas_call x1, Pallas kernels, last(): pl.pallas_call(functools.partial(last_kernel, taps_n), grid=(steps,), in_...  6.97 us
  transfers between devices with their start and end apart: 24, of which 14 were waited for; matrix products, arithmetic and copies ran while one was open for 9% of the time, Pallas kernels for 5%

profile of v10, /device:TPU:0, one launch (start us, length us, event | category | flops | bytes accessed | tf_op | source)
XLA Modules:
  0.0 205.0 jit_solution(15412505605879405469)
XLA Ops:
  0.7 1.0 dynamic-slice_bitcast_fusion
  2.2 1.0 collective-permute-done
  3.2 0.9 bitcast_select_fusion.1
  4.8 2.9 %collective-permute-start.3 = (bf16[96,1536]{1,0:T(8,128)(2,1)}, bf16[96,1536]{1,0:T(8,128)(2,1)S(1)}, u32[]{:S(2)}, u32[]{:S(2)}) collective-permute-start(bf16[96,1536]{1,0:T(8,128)(2,1)} %pad_maximum_fusion.2.refs_0_), channel_id=1, source_target_pairs={{0,2},{1,3},{2,0},{3,1},{4,6},{5,7},{6,4},{7,5},{8,10},{9,11},{10,... | collective-permute-start | bytes 884744 | tf_op jit(solution)/shard_map/ppermute | solution.py:648
  7.7 1.5 collective-permute-start.2
  10.5 3.7 %collective-permute-start.8 = (bf16[96,1536]{1,0:T(8,128)(2,1)}, bf16[96,1536]{1,0:T(8,128)(2,1)S(1)}, u32[]{:S(2)}, u32[]{:S(2)}) collective-permute-start(bf16[96,1536]{1,0:T(8,128)(2,1)} %pad_maximum_fusion.2.refs_0_), channel_id=1, source_target_pairs={{0,24},{1,25},{2,26},{3,27},{4,28},{5,29},{6,30},{7,31},{8,0},{9,1... | collective-permute-start | bytes 884744 | tf_op jit(solution)/shard_map/ppermute | solution.py:639
  14.1 1.0 collective-permute-start.1
  15.2 1.5 collective-permute-done.2.refs_2_
  17.9 4.0 %collective-permute-done.8 = bf16[96,1536]{1,0:T(8,128)(2,1)S(1)} collective-permute-done((bf16[96,1536]{1,0:T(8,128)(2,1)}, bf16[96,1536]{1,0:T(8,128)(2,1)S(1)}, u32[]{:S(2)}, u32[]{:S(2)}) %collective-permute-start.8) | collective-permute-done | bytes 294944 | tf_op jit(solution)/shard_map/ppermute | solution.py:639
  21.9 7.2 %collective-permute-done.7 = bf16[96,1536]{1,0:T(8,128)(2,1)S(1)} collective-permute-done((bf16[96,1536]{1,0:T(8,128)(2,1)}, bf16[96,1536]{1,0:T(8,128)(2,1)S(1)}, u32[]{:S(2)}, u32[]{:S(2)}) %collective-permute-start.7) | collective-permute-done | bytes 294944 | tf_op jit(solution)/shard_map/ppermute | solution.py:639
  29.9 1.0 constant_dynamic-update-slice_fusion
  31.6 1.3 collective-permute-start.10
  32.9 1.4 collective-permute-start.9
  35.5 3.9 %collective-permute-done.1.refs_8_ = bf16[96,1536]{1,0:T(8,128)(2,1)} collective-permute-done((bf16[96,1536]{1,0:T(8,128)(2,1)}, bf16[96,1536]{1,0:T(8,128)(2,1)}, u32[]{:S(2)}, u32[]{:S(2)}) %collective-permute-start.1) | collective-permute-done | bytes 294944 | tf_op jit(solution)/shard_map/ppermute | solution.py:639
  42.2 1.4 collective-permute-start.6
  43.6 4.4 %collective-permute-start.5 = (bf16[96,1536]{1,0:T(8,128)(2,1)}, bf16[96,1536]{1,0:T(8,128)(2,1)S(1)}, u32[]{:S(2)}, u32[]{:S(2)}) collective-permute-start(bf16[96,1536]{1,0:T(8,128)(2,1)} %collective-permute-done.1.refs_8_), channel_id=1, source_target_pairs={{0,4},{1,5},{2,6},{3,7},{4,0},{5,1},{6,2},{7,3},{8,12},{9,13},{10,... | collective-permute-start | bytes 884744 | tf_op jit(solution)/shard_map/ppermute | solution.py:649
  48.0 1.1 broadcast_select_fusion.4
  49.2 10.8 %collective-permute-done.12.refs_5_ = bf16[192,1536]{1,0:T(8,128)(2,1)S(1)} collective-permute-done((bf16[192,1536]{1,0:T(8,128)(2,1)S(1)}, bf16[192,1536]{1,0:T(8,128)(2,1)S(1)}, u32[]{:S(2)}, u32[]{:S(2)}) %collective-permute-start.12) | collective-permute-done | bytes 589856 | tf_op jit(solution)/shard_map/ppermute | solution.py:648
  60.0 1.8 collective-permute-start.14
  61.8 4.1 %collective-permute-done.6.refs_9_ = bf16[96,1536]{1,0:T(8,128)(2,1)S(1)} collective-permute-done((bf16[96,1536]{1,0:T(8,128)(2,1)}, bf16[96,1536]{1,0:T(8,128)(2,1)S(1)}, u32[]{:S(2)}, u32[]{:S(2)}) %collective-permute-start.6) | collective-permute-done | bytes 294944 | tf_op jit(solution)/shard_map/ppermute | solution.py:648
  69.3 1.5 multiply_convert_fusion.nb
  70.8 1.0 broadcast_in_dim.9.taps
  71.7 2.1 %collective-permute-start.15 = (bf16[96,1536]{1,0:T(8,128)(2,1)S(1)}, bf16[96,1536]{1,0:T(8,128)(2,1)S(1)}, u32[]{:S(2)}, u32[]{:S(2)}) collective-permute-start(bf16[96,1536]{1,0:T(8,128)(2,1)S(1)} %broadcast_select_fusion.5), channel_id=1, source_target_pairs={{0,2},{1,5},{2,0},{3,7},{4,6},{5,1},{6,4},{7,3},{8,10},{9,13},{10,... | collective-permute-start | bytes 884744 | tf_op jit(solution)/shard_map/ppermute | solution.py:693
  74.5 4.1 %collective-permute-done.15.refs_11_ = bf16[96,1536]{1,0:T(8,128)(2,1)S(1)} collective-permute-done((bf16[96,1536]{1,0:T(8,128)(2,1)S(1)}, bf16[96,1536]{1,0:T(8,128)(2,1)S(1)}, u32[]{:S(2)}, u32[]{:S(2)}) %collective-permute-start.15) | collective-permute-done | bytes 294944 | tf_op jit(solution)/shard_map/ppermute | solution.py:693
  79.3 4.8 %place_weights.1.value_w.gate_w = bf16[1536,1536]{1,0:T(8,128)(2,1)} custom-call(s32[6]{0:T(128)} %stack.26.scal, bf16[96,1536]{1,0:T(8,128)(2,1)} %pad_maximum_fusion.2.refs_0_, bf16[96,1536]{1,0:T(8,128)(2,1)} %copy-done.7, bf16[96,1536]{1,0:T(8,128)(2,1)} %copy-done.8, bf16[96,1536]{1,0:T(8,128)(2,1)} %collective-permute-done.4.refs_3_, ...), custom_call_target="tpu_custom_call" | custom-call | bytes 9437184 | tf_op jit(solution)/shard_map/place_weights/pallas_call | solution.py:104
  84.1 7.9 %project_glu_conv.2 = (f32[256,768]{1,0:T(8,128)}, f32[256,768]{1,0:T(8,128)}, bf16[320,768]{1,0:T(8,128)(2,1)}, f32[288,768]{1,0:T(8,128)}, f32[16,2,768]{2,1,0:T(2,128)}) custom-call(s32[6]{0:T(128)} %stack.26.scal, bf16[320,1536]{1,0:T(8,128)(2,1)} %multiply_convert_fusion.nb, bf16[1536,1536]{1,0:T(8,128)(2,1)} %place_weights.1.value_w.gate_w, ...), custom_call_target="tpu_custom_call" | custom-call | flops 1509949440 | bytes 7176192 | tf_op jit(solution)/shard_map/project_glu_conv/pallas_call | solution.py:146
  92.0 8.0 %all-to-all-start = ((f32[16,2,768]{2,1,0:T(2,128)}), f32[16,2,768]{2,1,0:T(2,128)}, u32[]{:S(2)}, u32[]{:S(2)}) async-start(f32[16,2,768]{2,1,0:T(2,128)} %get-tuple-element.56), calls=%async_computation | async-start | bytes 196608 | tf_op jit(solution)/shard_map/all_to_all | solution.py:626
  99.9 3.0 %fusion.3.cot = bf16[288,768]{1,0:T(8,128)(2,1)} fusion(s32[768]{0:T(1024)S(1)} %fusion.21, bf16[3,32,1536]{2,1,0:T(8,128)(2,1)S(1)} %copy-done.14, bf16[3,128,1536]{2,1,0:T(8,128)(2,1)} %copy-done.1, bf16[3,128,1536]{2,1,0:T(8,128)(2,1)} %copy-done, bf16[3,32,1536]{2,1,0:T(8,128)(2,1)S(1)} %copy-done.12), kind=kOutput, calls=%fused_computation.8 | convolution fusion | flops 684417024 | bytes 3394560 | tf_op jit(solution)/shard_map/dot_general | solution.py:675
  102.9 4.7 %all-to-all-done.stats = f32[16,2,768]{2,1,0:T(2,128)} async-done(((f32[16,2,768]{2,1,0:T(2,128)}), f32[16,2,768]{2,1,0:T(2,128)}, u32[]{:S(2)}, u32[]{:S(2)}) %all-to-all-start) | async-done | bytes 98336 | tf_op jit(solution)/shard_map/all_to_all | solution.py:626
  107.7 3.9 %batch_norm_swish.1 = (f32[288,768]{1,0:T(8,128)}, f32[288,768]{1,0:T(8,128)}, f32[1,768]{1,0:T(1,128)}, f32[16,2,768]{2,1,0:T(2,128)}) custom-call(s32[6]{0:T(128)} %stack.26.scal, f32[2,16]{1,0:T(2,128)} %pad_maximum_fusion.3.counts, f32[16,2,768]{2,1,0:T(2,128)} %all-to-all-done.stats, f32[288,768]{1,0:T(8,128)} %get-tuple-element.57.conv, ...), custom_call_target="tpu_custom_call" | custom-call | flops 8847360 | bytes 3538944 | tf_op jit(solution)/shard_map/batch_norm_swish/pallas_call | solution.py:226
  111.6 11.8 %all_to_all.25.sums = f32[16,2,768]{2,1,0:T(2,128)} all-to-all(f32[16,2,768]{2,1,0:T(2,128)} %get-tuple-element.60), channel_id=1, replica_groups={{0,2,4,6,8,10,12,14,16,18,20,22,24,26,28,30},{1,3,5,7,9,11,13,15,17,19,..., dimensions={0} | all-to-all | bytes 196608 | tf_op jit(solution)/shard_map/all_to_all | solution.py:626
  123.4 8.2 %grad_conv_project_back.1 = (f32[128,1536]{1,0:T(8,128)}, f32[128,1536]{1,0:T(8,128)}, bf16[256,768]{1,0:T(8,128)(2,1)}, f32[2,768]{1,0:T(2,128)}) custom-call(s32[6]{0:T(128)} %stack.26.scal, f32[16,2,768]{2,1,0:T(2,128)} %all_to_all.25.sums, f32[288,768]{1,0:T(8,128)} %get-tuple-element.61.scaled, f32[288,768]{1,0:T(8,128)} %get-tuple-element.62.grad, ...), custom_call_target="tpu_custom_call" | custom-call | flops 1207959552 | bytes 9142272 | tf_op jit(solution)/shard_map/grad_conv_project_back/pallas_call | solution.py:301
  132.3 2.1 %collective-permute-done.16.other = f32[128,1536]{1,0:T(8,128)S(1)} collective-permute-done((f32[128,1536]{1,0:T(8,128)}, f32[128,1536]{1,0:T(8,128)S(1)}, u32[]{:S(2)}, u32[]{:S(2)}) %collective-permute-start.16) | collective-permute-done | bytes 786464 | tf_op jit(solution)/shard_map/ppermute | solution.py:703
  135.3 3.2 %direction.1 = (f32[128,1536]{1,0:T(8,128)}, f32[32,1536]{1,0:T(8,128)}, f32[32,1,128]{2,1,0:T(1,128)}) custom-call(s32[6]{0:T(128)} %stack.26.scal, f32[128,1536]{1,0:T(8,128)} %get-tuple-element.66.mine, f32[128,1536]{1,0:T(8,128)} %copy-done.15, bf16[128,1536]{1,0:T(8,128)(2,1)} %bitcast.50, bf16[128,1536]{1,0:T(8,128)(2,1)} %bitcast.48), custom_call_target="tpu_custom_call" | custom-call | flops 5898240 | bytes 3145728 | tf_op jit(solution)/shard_map/direction/pallas_call | solution.py:531
  139.5 1.3 collective-permute-start.18
  140.8 6.6 %all-to-all-start.2 = ((f32[32,1,128]{2,1,0:T(1,128)}), f32[32,1,128]{2,1,0:T(1,128)S(1)}, u32[]{:S(2)}, u32[]{:S(2)}) async-start(f32[32,1,128]{2,1,0:T(1,128)} %get-tuple-element.68), calls=%async_computation.2 | async-start | bytes 32768 | tf_op jit(solution)/shard_map/all_to_all | solution.py:705
  147.4 1.4 slice_bitcast_fusion
  148.8 5.2 %tap_grad.1.taps_before = f32[31,768]{1,0:T(8,128)} custom-call(bf16[256,768]{1,0:T(8,128)(2,1)} %get-tuple-element.69.grad_conv, bf16[320,768]{1,0:T(8,128)(2,1)} %get-tuple-element.70.glu), custom_call_target="tpu_custom_call" | custom-call | flops 12189696 | bytes 983040 | tf_op jit(solution)/shard_map/tap_grad/pallas_call | solution.py:349
  155.1 4.5 %ascend.1 = (f32[128,1536]{1,0:T(8,128)}, bf16[320,1536]{1,0:T(8,128)(2,1)}) custom-call(s32[6]{0:T(128)} %stack.26.scal, f32[32,1,128]{2,1,0:T(1,128)} %copy-done.24, bf16[320,1536]{1,0:T(8,128)(2,1)} %get-tuple-element.88.features, bf16[320,1536]{1,0:T(8,128)(2,1)} %get-tuple-element.87.noise, f32[128,1536]{1,0:T(8,128)} %get-tuple-element.72.mine, ...), custom_call_target="tpu_custom_call" | custom-call | flops 14745600 | bytes 3932160 | tf_op jit(solution)/shard_map/ascend/pallas_call | solution.py:575
  159.6 7.7 %project_glu_conv.3 = (bf16[320,768]{1,0:T(8,128)(2,1)}, f32[288,768]{1,0:T(8,128)}, f32[16,2,768]{2,1,0:T(2,128)}) custom-call(s32[6]{0:T(128)} %stack.26.scal, bf16[320,1536]{1,0:T(8,128)(2,1)} %get-tuple-element.75.nb, bf16[1536,1536]{1,0:T(8,128)(2,1)} %place_weights.1.value_w.gate_w, bf16[1536,1536]{1,0:T(8,128)(2,1)} %place_weights.1.value_w.gate_w, ...), custom_call_target="tpu_custom_call" | custom-call | flops 1509949440 | bytes 7176192 | tf_op jit(solution)/shard_map/project_glu_conv/pallas_call | solution.py:146
  167.3 6.4 %all-to-all-start.3 = ((f32[16,2,768]{2,1,0:T(2,128)}), f32[16,2,768]{2,1,0:T(2,128)S(1)}, u32[]{:S(2)}, u32[]{:S(2)}) async-start(f32[16,2,768]{2,1,0:T(2,128)} %get-tuple-element.76.stats.local_stats), calls=%async_computation.3 | async-start | bytes 196608 | tf_op jit(solution)/shard_map/all_to_all | solution.py:626
  173.7 5.9 %raw_taps.1 = (f32[31,768]{1,0:T(8,128)}, f32[31,768]{1,0:T(8,128)}) custom-call(s32[6]{0:T(128)} %stack.26.scal, f32[288,768]{1,0:T(8,128)} %get-tuple-element.77.conv, bf16[320,768]{1,0:T(8,128)(2,1)} %get-tuple-element.78.glu, f32[16,2,768]{2,1,0:T(2,128)} %get-tuple-element.76.stats.local_stats), custom_call_target="tpu_custom_call" | custom-call | flops 13713408 | bytes 1966080 | tf_op jit(solution)/shard_map/raw_taps/pallas_call | solution.py:382
  179.6 1.7 all-to-all-done.3.stats
  182.0 7.0 %batch_norm_swish_taps.1 = (bf16[16,48,128]{2,1,0:T(8,128)(2,1)}, f32[1,768]{1,0:T(1,128)}) custom-call(s32[6]{0:T(128)} %stack.26.scal, f32[2,16]{1,0:T(2,128)} %pad_maximum_fusion.3.counts, f32[16,2,768]{2,1,0:T(2,128)} %copy-done.18, f32[288,768]{1,0:T(8,128)} %get-tuple-element.77.conv, bf16[288,768]{1,0:T(8,128)(2,1)} %fusion.3.cot, ...), custom_call_target="tpu_custom_call" | custom-call | flops 22118400 | bytes 2211840 | tf_op jit(solution)/shard_map/batch_norm_swish_taps/pallas_call | solution.py:442
  188.9 5.2 %all-to-all-start.4 = ((bf16[16,48,128]{2,1,0:T(8,128)(2,1)}), bf16[16,48,128]{2,1,0:T(8,128)(2,1)S(1)}, u32[]{:S(2)}, u32[]{:S(2)}) async-start(bf16[16,48,128]{2,1,0:T(8,128)(2,1)} %get-tuple-element.82), calls=%async_computation.4 | async-start | bytes 393216 | tf_op jit(solution)/shard_map/all_to_all | solution.py:626
  194.2 1.3 fusion.23.known
  195.5 7.2 %all-to-all-done.4.received = bf16[16,48,128]{2,1,0:T(8,128)(2,1)S(1)} async-done(((bf16[16,48,128]{2,1,0:T(8,128)(2,1)}), bf16[16,48,128]{2,1,0:T(8,128)(2,1)S(1)}, u32[]{:S(2)}, u32[]{:S(2)}) %all-to-all-start.4) | async-done | bytes 196640 | tf_op jit(solution)/shard_map/all_to_all | solution.py:626
  203.3 1.7 finish.1
  (109 shorter events, 18.2 us)
Async XLA Ops:
  0.6 29.2 %copy-start.6 = (bf16[1,128,1536]{2,1,0:T(8,128)(2,1)S(1)}, bf16[1,128,1536]{2,1,0:T(8,128)(2,1)}, u32[]{:S(2)}) copy-start(bf16[1,128,1536]{2,1,0:T(8,128)(2,1)} %param.8) | copy-start | bytes 1179652
  1.6 1.5 collective-permute-start
  2.2 27.7 %copy-start.2 = (bf16[1,128,1536]{2,1,0:T(8,128)(2,1)S(1)}, bf16[1,128,1536]{2,1,0:T(8,128)(2,1)}, u32[]{:S(2)}) copy-start(bf16[1,128,1536]{2,1,0:T(8,128)(2,1)} %param.9) | copy-start | bytes 1179652
  4.8 10.4 %collective-permute-start.3 = (bf16[96,1536]{1,0:T(8,128)(2,1)}, bf16[96,1536]{1,0:T(8,128)(2,1)S(1)}, u32[]{:S(2)}, u32[]{:S(2)}) collective-permute-start(bf16[96,1536]{1,0:T(8,128)(2,1)} %pad_maximum_fusion.2.refs_0_), channel_id=1, source_target_pairs={{0,2},{1,3},{2,0},{3,1},{4,6},{5,7},{6,4},{7,5},{8,10},{9,11},{10,... | collective-permute-start | bytes 884744 | tf_op jit(solution)/shard_map/ppermute | solution.py:648
  7.7 9.0 %collective-permute-start.2 = (bf16[96,1536]{1,0:T(8,128)(2,1)}, bf16[96,1536]{1,0:T(8,128)(2,1)S(1)}, u32[]{:S(2)}, u32[]{:S(2)}) collective-permute-start(bf16[96,1536]{1,0:T(8,128)(2,1)} %pad_maximum_fusion.2.refs_0_), channel_id=1, source_target_pairs={{0,4},{1,5},{2,6},{3,7},{4,0},{5,1},{6,2},{7,3},{8,12},{9,13},{10,... | collective-permute-start | bytes 884744 | tf_op jit(solution)/shard_map/ppermute | solution.py:649
  10.5 11.4 %collective-permute-start.8 = (bf16[96,1536]{1,0:T(8,128)(2,1)}, bf16[96,1536]{1,0:T(8,128)(2,1)S(1)}, u32[]{:S(2)}, u32[]{:S(2)}) collective-permute-start(bf16[96,1536]{1,0:T(8,128)(2,1)} %pad_maximum_fusion.2.refs_0_), channel_id=1, source_target_pairs={{0,24},{1,25},{2,26},{3,27},{4,28},{5,29},{6,30},{7,31},{8,0},{9,1... | collective-permute-start | bytes 884744 | tf_op jit(solution)/shard_map/ppermute | solution.py:639
  14.1 15.0 %collective-permute-start.7 = (bf16[96,1536]{1,0:T(8,128)(2,1)}, bf16[96,1536]{1,0:T(8,128)(2,1)S(1)}, u32[]{:S(2)}, u32[]{:S(2)}) collective-permute-start(bf16[96,1536]{1,0:T(8,128)(2,1)} %pad_maximum_fusion.2.refs_0_), channel_id=1, source_target_pairs={{0,8},{1,9},{2,10},{3,11},{4,12},{5,13},{6,14},{7,15},{8,16},{9,17... | collective-permute-start | bytes 884744 | tf_op jit(solution)/shard_map/ppermute | solution.py:639
  14.1 25.2 %collective-permute-start.1 = (bf16[96,1536]{1,0:T(8,128)(2,1)}, bf16[96,1536]{1,0:T(8,128)(2,1)}, u32[]{:S(2)}, u32[]{:S(2)}) collective-permute-start(bf16[96,1536]{1,0:T(8,128)(2,1)} %pad_maximum_fusion.2.refs_0_), channel_id=1, source_target_pairs={{0,16},{1,17},{2,18},{3,19},{4,20},{5,21},{6,22},{7,23},{8,24},{9,... | collective-permute-start | bytes 884744 | tf_op jit(solution)/shard_map/ppermute | solution.py:639
  15.2 14.0 %copy-start.7 = (bf16[96,1536]{1,0:T(8,128)(2,1)}, bf16[96,1536]{1,0:T(8,128)(2,1)S(1)}, u32[]{:S(2)}) copy-start(bf16[96,1536]{1,0:T(8,128)(2,1)S(1)} %collective-permute-done.3.refs_1_) | copy-start | bytes 884740
  16.7 12.5 %copy-start.8 = (bf16[96,1536]{1,0:T(8,128)(2,1)}, bf16[96,1536]{1,0:T(8,128)(2,1)S(1)}, u32[]{:S(2)}) copy-start(bf16[96,1536]{1,0:T(8,128)(2,1)S(1)} %collective-permute-done.2.refs_2_) | copy-start | bytes 884740
  17.5 16.8 %copy-start.25 = (f32[1536]{0:T(1024)S(1)}, f32[1536]{0:T(1024)}, u32[]{:S(2)}) copy-start(f32[1536]{0:T(1024)} %param.13) | copy-start | bytes 18436
  17.5 16.9 %copy-start.26 = (f32[1536]{0:T(1024)S(1)}, f32[1536]{0:T(1024)}, u32[]{:S(2)}) copy-start(f32[1536]{0:T(1024)} %param.14) | copy-start | bytes 18436
  17.5 24.5 %collective-permute-start.4 = (bf16[96,1536]{1,0:T(8,128)(2,1)}, bf16[96,1536]{1,0:T(8,128)(2,1)}, u32[]{:S(2)}, u32[]{:S(2)}) collective-permute-start(bf16[96,1536]{1,0:T(8,128)(2,1)} %broadcast_select_fusion.6), channel_id=1, source_target_pairs={{0,2},{1,5},{2,0},{3,7},{4,6},{5,1},{6,4},{7,3},{8,10},{9,13},{10,... | collective-permute-start | bytes 884744 | tf_op jit(solution)/shard_map/ppermute | solution.py:653
  29.2 10.1 %copy-start.3 = (bf16[192,1536]{1,0:T(8,128)(2,1)}, bf16[192,1536]{1,0:T(8,128)(2,1)S(1)}, u32[]{:S(2)}) copy-start(bf16[192,1536]{1,0:T(8,128)(2,1)S(1)} %pad_maximum_fusion.1.refs_4_) | copy-start | bytes 1769476
  29.2 5.3 %copy-start.23 = (f32[31,1536]{1,0:T(8,128)S(1)}, f32[31,1536]{1,0:T(8,128)}, u32[]{:S(2)}) copy-start(f32[31,1536]{1,0:T(8,128)} %param.12) | copy-start | bytes 571396
  29.2 19.9 %collective-permute-start.13 = (bf16[192,1536]{1,0:T(8,128)(2,1)S(1)}, bf16[192,1536]{1,0:T(8,128)(2,1)S(1)}, u32[]{:S(2)}, u32[]{:S(2)}) collective-permute-start(bf16[192,1536]{1,0:T(8,128)(2,1)S(1)} %pad_maximum_fusion.1.refs_4_), channel_id=1, source_target_pairs={{0,4},{1,5},{2,6},{3,7},{4,0},{5,1},{6,2},{7,3},{8,12},{9,13},{10,... | collective-permute-start | bytes 1769480 | tf_op jit(solution)/shard_map/ppermute | solution.py:649
  31.6 10.5 %collective-permute-start.10 = (bf16[3,32,1536]{2,1,0:T(8,128)(2,1)}, bf16[3,32,1536]{2,1,0:T(8,128)(2,1)}, u32[]{:S(2)}, u32[]{:S(2)}) collective-permute-start(bf16[3,32,1536]{2,1,0:T(8,128)(2,1)} %slice_select_fusion), channel_id=1, source_target_pairs={{2,0},{4,2},{6,4},{8,6},{10,8},{12,10},{14,12},{16,14},{18,16},{20... | collective-permute-start | bytes 884744 | tf_op jit(solution)/shard_map/ppermute | solution.py:621
  32.9 10.7 %collective-permute-start.9 = (bf16[3,32,1536]{2,1,0:T(8,128)(2,1)}, bf16[3,32,1536]{2,1,0:T(8,128)(2,1)}, u32[]{:S(2)}, u32[]{:S(2)}) collective-permute-start(bf16[3,32,1536]{2,1,0:T(8,128)(2,1)} %slice_select_fusion), channel_id=1, source_target_pairs={{2,1},{4,3},{6,5},{8,7},{10,9},{12,11},{14,13},{16,15},{18,17},{20... | collective-permute-start | bytes 884744 | tf_op jit(solution)/shard_map/ppermute | solution.py:622
  39.3 20.6 %collective-permute-start.12 = (bf16[192,1536]{1,0:T(8,128)(2,1)S(1)}, bf16[192,1536]{1,0:T(8,128)(2,1)S(1)}, u32[]{:S(2)}, u32[]{:S(2)}) collective-permute-start(bf16[192,1536]{1,0:T(8,128)(2,1)S(1)} %pad_maximum_fusion.1.refs_4_), channel_id=1, source_target_pairs={{0,2},{1,3},{2,0},{3,1},{4,6},{5,7},{6,4},{7,5},{8,10},{9,11},{10,... | collective-permute-start | bytes 1769480 | tf_op jit(solution)/shard_map/ppermute | solution.py:648
  42.0 23.9 %collective-permute-start.11 = (bf16[3,128,1536]{2,1,0:T(8,128)(2,1)S(1)}, bf16[3,128,1536]{2,1,0:T(8,128)(2,1)S(1)}, u32[]{:S(2)}, u32[]{:S(2)}) collective-permute-start(bf16[3,128,1536]{2,1,0:T(8,128)(2,1)S(1)} %constant_dynamic-update-slice_fusion), channel_id=1, source_target_pairs={{0,1},{1,0},{2,3},{3,2},{4,5},{5,4},{6,7},{7,6},{8,9},{9,8},{10,11... | collective-permute-start | bytes 3538952 | tf_op jit(solution)/shard_map/ppermute | solution.py:620
  42.2 23.7 %collective-permute-start.6 = (bf16[96,1536]{1,0:T(8,128)(2,1)}, bf16[96,1536]{1,0:T(8,128)(2,1)S(1)}, u32[]{:S(2)}, u32[]{:S(2)}) collective-permute-start(bf16[96,1536]{1,0:T(8,128)(2,1)} %collective-permute-done.1.refs_8_), channel_id=1, source_target_pairs={{0,2},{1,3},{2,0},{3,1},{4,6},{5,7},{6,4},{7,5},{8,10},{9,11},{10,... | collective-permute-start | bytes 884744 | tf_op jit(solution)/shard_map/ppermute | solution.py:648
  43.6 22.3 %collective-permute-start.5 = (bf16[96,1536]{1,0:T(8,128)(2,1)}, bf16[96,1536]{1,0:T(8,128)(2,1)S(1)}, u32[]{:S(2)}, u32[]{:S(2)}) collective-permute-start(bf16[96,1536]{1,0:T(8,128)(2,1)} %collective-permute-done.1.refs_8_), channel_id=1, source_target_pairs={{0,4},{1,5},{2,6},{3,7},{4,0},{5,1},{6,2},{7,3},{8,12},{9,13},{10,... | collective-permute-start | bytes 884744 | tf_op jit(solution)/shard_map/ppermute | solution.py:649
  49.1 17.6 %copy-start.11 = (bf16[3,32,1536]{2,1,0:T(8,128)(2,1)}, bf16[3,32,1536]{2,1,0:T(8,128)(2,1)S(1)}, u32[]{:S(2)}) copy-start(bf16[3,32,1536]{2,1,0:T(8,128)(2,1)S(1)} %get-tuple-element.91) | copy-start | bytes 884740
  49.1 17.6 %copy-start.13 = (bf16[3,32,1536]{2,1,0:T(8,128)(2,1)}, bf16[3,32,1536]{2,1,0:T(8,128)(2,1)S(1)}, u32[]{:S(2)}) copy-start(bf16[3,32,1536]{2,1,0:T(8,128)(2,1)S(1)} %get-tuple-element.92) | copy-start | bytes 884740
  49.1 16.9 %copy-start.4 = (bf16[192,1536]{1,0:T(8,128)(2,1)}, bf16[192,1536]{1,0:T(8,128)(2,1)S(1)}, u32[]{:S(2)}) copy-start(bf16[192,1536]{1,0:T(8,128)(2,1)S(1)} %collective-permute-done.13.refs_6_) | copy-start | bytes 1769476
  59.9 6.1 %copy-start.5 = (bf16[192,1536]{1,0:T(8,128)(2,1)}, bf16[192,1536]{1,0:T(8,128)(2,1)S(1)}, u32[]{:S(2)}) copy-start(bf16[192,1536]{1,0:T(8,128)(2,1)S(1)} %collective-permute-done.12.refs_5_) | copy-start | bytes 1769476
  60.0 14.5 %collective-permute-start.14 = (bf16[192,1536]{1,0:T(8,128)(2,1)S(1)}, bf16[192,1536]{1,0:T(8,128)(2,1)S(1)}, u32[]{:S(2)}, u32[]{:S(2)}) collective-permute-start(bf16[192,1536]{1,0:T(8,128)(2,1)S(1)} %broadcast_select_fusion.2), channel_id=1, source_target_pairs={{0,2},{1,5},{2,0},{3,7},{4,6},{5,1},{6,4},{7,3},{8,10},{9,13},{10,... | collective-permute-start | bytes 1769480 | tf_op jit(solution)/shard_map/ppermute | solution.py:653
  65.8 0.7 copy-start.9
  65.8 0.9 copy-start.10
  66.7 1.0 copy-start
  66.7 1.5 copy-start.1
  69.3 1.5 copy-start.19
  71.7 6.8 %collective-permute-start.15 = (bf16[96,1536]{1,0:T(8,128)(2,1)S(1)}, bf16[96,1536]{1,0:T(8,128)(2,1)S(1)}, u32[]{:S(2)}, u32[]{:S(2)}) collective-permute-start(bf16[96,1536]{1,0:T(8,128)(2,1)S(1)} %broadcast_select_fusion.5), channel_id=1, source_target_pairs={{0,2},{1,5},{2,0},{3,7},{4,6},{5,1},{6,4},{7,3},{8,10},{9,13},{10,... | collective-permute-start | bytes 884744 | tf_op jit(solution)/shard_map/ppermute | solution.py:693
  74.5 4.1 %copy-start.17 = (bf16[192,1536]{1,0:T(8,128)(2,1)}, bf16[192,1536]{1,0:T(8,128)(2,1)S(1)}, u32[]{:S(2)}) copy-start(bf16[192,1536]{1,0:T(8,128)(2,1)S(1)} %collective-permute-done.14.refs_7_) | copy-start | bytes 1769476
  78.6 0.7 copy-start.20
  84.1 15.9 %copy-start.12 = (bf16[3,32,1536]{2,1,0:T(8,128)(2,1)S(1)}, bf16[3,32,1536]{2,1,0:T(8,128)(2,1)}, u32[]{:S(2)}) copy-start(bf16[3,32,1536]{2,1,0:T(8,128)(2,1)} %copy-done.11) | copy-start | bytes 884740
  84.1 15.9 %copy-start.14 = (bf16[3,32,1536]{2,1,0:T(8,128)(2,1)S(1)}, bf16[3,32,1536]{2,1,0:T(8,128)(2,1)}, u32[]{:S(2)}) copy-start(bf16[3,32,1536]{2,1,0:T(8,128)(2,1)} %copy-done.13) | copy-start | bytes 884740
  92.0 15.7 %all-to-all-start = ((f32[16,2,768]{2,1,0:T(2,128)}), f32[16,2,768]{2,1,0:T(2,128)}, u32[]{:S(2)}, u32[]{:S(2)}) async-start(f32[16,2,768]{2,1,0:T(2,128)} %get-tuple-element.56), calls=%async_computation | async-start | bytes 196608 | tf_op jit(solution)/shard_map/all_to_all | solution.py:626
  131.6 2.8 %collective-permute-start.16 = (f32[128,1536]{1,0:T(8,128)}, f32[128,1536]{1,0:T(8,128)S(1)}, u32[]{:S(2)}, u32[]{:S(2)}) collective-permute-start(f32[128,1536]{1,0:T(8,128)} %get-tuple-element.67), channel_id=1, source_target_pairs={{0,1},{1,0},{2,3},{3,2},{4,5},{5,4},{6,7},{7,6},{8,9},{9,8},{10,11... | collective-permute-start | bytes 2359304 | tf_op jit(solution)/shard_map/ppermute | solution.py:703
  134.4 0.9 copy-start.15
  138.5 15.9 %collective-permute-start.17 = (f32[128,1536]{1,0:T(8,128)}, f32[128,1536]{1,0:T(8,128)}, u32[]{:S(2)}, u32[]{:S(2)}) collective-permute-start(f32[128,1536]{1,0:T(8,128)} %get-tuple-element.72.mine), channel_id=1, source_target_pairs={{0,1},{1,0},{2,3},{3,2},{4,5},{5,4},{6,7},{7,6},{8,9},{9,8},{10,11... | collective-permute-start | bytes 2359304 | tf_op jit(solution)/shard_map/ppermute | solution.py:620
  138.9 15.5 %collective-permute-start.19 = (f32[32,1536]{1,0:T(8,128)}, f32[32,1536]{1,0:T(8,128)S(1)}, u32[]{:S(2)}, u32[]{:S(2)}) collective-permute-start(f32[32,1536]{1,0:T(8,128)} %get-tuple-element.73), channel_id=1, source_target_pairs={{2,1},{4,3},{6,5},{8,7},{10,9},{12,11},{14,13},{16,15},{18,17},{20... | collective-permute-start | bytes 589832 | tf_op jit(solution)/shard_map/ppermute | solution.py:622
  139.5 14.8 %collective-permute-start.18 = (f32[32,1536]{1,0:T(8,128)}, f32[32,1536]{1,0:T(8,128)S(1)}, u32[]{:S(2)}, u32[]{:S(2)}) collective-permute-start(f32[32,1536]{1,0:T(8,128)} %get-tuple-element.73), channel_id=1, source_target_pairs={{2,0},{4,2},{6,4},{8,6},{10,8},{12,10},{14,12},{16,14},{18,16},{20... | collective-permute-start | bytes 589832 | tf_op jit(solution)/shard_map/ppermute | solution.py:621
  140.8 13.5 %all-to-all-start.2 = ((f32[32,1,128]{2,1,0:T(1,128)}), f32[32,1,128]{2,1,0:T(1,128)S(1)}, u32[]{:S(2)}, u32[]{:S(2)}) async-start(f32[32,1,128]{2,1,0:T(1,128)} %get-tuple-element.68), calls=%async_computation.2 | async-start | bytes 32768 | tf_op jit(solution)/shard_map/all_to_all | solution.py:705
  154.3 0.7 copy-start.22
  167.3 14.0 %all-to-all-start.3 = ((f32[16,2,768]{2,1,0:T(2,128)}), f32[16,2,768]{2,1,0:T(2,128)S(1)}, u32[]{:S(2)}, u32[]{:S(2)}) async-start(f32[16,2,768]{2,1,0:T(2,128)} %get-tuple-element.76.stats.local_stats), calls=%async_computation.3 | async-start | bytes 196608 | tf_op jit(solution)/shard_map/all_to_all | solution.py:626
  173.7 20.5 %copy-start.27 = (f32[2,768]{1,0:T(2,128)S(1)}, f32[2,768]{1,0:T(2,128)}, u32[]{:S(2)}) copy-start(f32[2,768]{1,0:T(2,128)} %get-tuple-element.84) | copy-start | bytes 18436
  188.9 13.7 %all-to-all-start.4 = ((bf16[16,48,128]{2,1,0:T(8,128)(2,1)}), bf16[16,48,128]{2,1,0:T(8,128)(2,1)S(1)}, u32[]{:S(2)}, u32[]{:S(2)}) async-start(bf16[16,48,128]{2,1,0:T(8,128)(2,1)} %get-tuple-element.82), calls=%async_computation.4 | async-start | bytes 393216 | tf_op jit(solution)/shard_map/all_to_all | solution.py:626
  (4 other events, 2.6 us)
